TPU v7x, 32 devices: a whole 2x2x4 slice. The times are simulated.
32 devices in a mesh: dp: 4 (over x, core), fsdp: 8 (over z, y).
Axes of the slice: x: 2, y: 2, z: 4, core: 2. Of those that a mesh axis runs over, the one named last changes fastest.
Arguments:
- tokens: bfloat16 [8192, 2048], P(('dp', 'fsdp')), may hold values from -16 to 16
- cotangent: bfloat16 [8192, 2048], P(('dp', 'fsdp')), may hold values from -6 to 6
- destination: int32 [8192], P(('dp', 'fsdp')), may hold values from 0 to 8191, as said below
- lengths: int32 [32, 4], P(('dp', 'fsdp')), may hold values from 1 to 128, 256 in all within a row
- norm_gain: bfloat16 [2048], P('fsdp'), may hold values from 0.5 to 1.5
- in_weight: bfloat16 [2048, 8192], P('fsdp'), may hold values from -0.125 to 0.125
- conv_weight: bfloat16 [4, 4096], P(None, 'fsdp'), may hold values from -3 to 3
- conv_bias: bfloat16 [4096], P('fsdp'), may hold values from -3 to 3
- select_weight: bfloat16 [160, 4096], P(None, 'fsdp'), may hold values from -0.09375 to 0.09375
- step_weight: bfloat16 [128, 4096], P(None, 'fsdp'), may hold values from -0.5 to 0.5
- step_bias: bfloat16 [4096], P('fsdp'), may hold values from -6.875 to -2.296875
- decay_log: bfloat16 [16, 4096], P(None, 'fsdp'), may hold values from 0 to 2.765625
- skip_gain: bfloat16 [4096], P('fsdp'), may hold values from 0.5 to 1.5
- out_weight: bfloat16 [4096, 2048], P('fsdp'), may hold values from -0.25 to 0.25
Outputs:
- layer_output: bfloat16 [8192, 2048], P(('dp', 'fsdp'))
- mixer_output: bfloat16 [8192, 2048], P(('dp', 'fsdp'))
- input_grad: bfloat16 [8192, 2048], P(('dp', 'fsdp'))
- input_rms: float32 [], replicated
- grad_norm_gain: float32 [2048], P('fsdp')
- grad_in_weight: float32 [2048, 8192], P('fsdp')
- grad_conv_weight: float32 [4, 4096], P(None, 'fsdp')
- grad_conv_bias: float32 [4096], P('fsdp')
- grad_select_weight: float32 [160, 4096], P(None, 'fsdp')
- grad_step_weight: float32 [128, 4096], P(None, 'fsdp')
- grad_step_bias: float32 [4096], P('fsdp')
- grad_decay_log: float32 [16, 4096], P(None, 'fsdp')
- grad_skip_gain: float32 [4096], P('fsdp')
- grad_out_weight: float32 [4096, 2048], P('fsdp')
Inputs may be any that keep to these rules, and one draw needn't show every extreme that they name: `destination`: a permutation of the 8192 row positions; the 256 tokens of each device's block go exactly 8 to each row. `lengths`: the last entry of each row counts padding positions.
All inputs are finite; a program needn't handle non-finite values.
Results may differ from a plain program's by a relative error of at most 0.012.
Values may be sent and summed in bfloat16 or wider, within the bound.
A program may use at most 512 MiB of HBM per device.

v0:
```python
from functools import partial
import math

import jax
import jax.numpy as jnp
from jax import lax
from jax.sharding import PartitionSpec as P

DI = 4096
N = 16
R = 128
KC = 4
MICRO = 2
SCAN_BLOCK = 16


eps = 1e-05


def silu_slope(value):
    sigma = jax.nn.sigmoid(value)
    return sigma * (1.0 + value * (1.0 - sigma))


def delayed(values, lag, fill):
    if lag == 0:
        return values
    front = jnp.full((lag,) + values.shape[1:], fill, values.dtype)
    return jnp.concatenate([front, values[:-lag]], axis=0)


def advance(rate, state, item):
    delta, bmat, signal, keep = item
    decay = jnp.exp(delta[None, :] * rate) * keep
    return decay * state + bmat[:, None] * (delta * signal)[None, :]


def forward_block(rate, state, items):

    def token_step(carry, item):
        step_row, write_row, read_row, signal_row, keep_row = item
        carry = advance(rate, carry, (step_row, write_row, signal_row, keep_row))
        return (carry, jnp.sum(read_row[:, None] * carry, axis=0))

    final, output = lax.scan(token_step, state, items)
    return (final, (output, state))


def backward_block(rate, carried, items):
    later, rate_grad = carried
    delta, bmat, cmat, signal, keep, entry_state, out_grad = items

    def rebuild(carry, item):
        carry = advance(rate, carry, item)
        return (carry, carry)

    _, states = lax.scan(rebuild, entry_state, (delta, bmat, signal, keep))
    previous = jnp.concatenate([entry_state[None], states[:-1]], axis=0)

    def token_back(carry, item):
        flowing, total = carry
        step_row, write_row, read_row, signal_row, keep_row, here, before, grad_row = item
        decay = jnp.exp(step_row[None, :] * rate) * keep_row
        state_grad = read_row[:, None] * grad_row[None, :] + flowing
        decay_grad = state_grad * before * decay
        delta_grad = jnp.sum(
            decay_grad * rate + state_grad * write_row[:, None] * signal_row[None, :], axis=0
        )
        total = total + decay_grad * step_row[None, :]
        bmat_grad = jnp.sum(state_grad * (step_row * signal_row)[None, :], axis=1)
        signal_grad = jnp.sum(state_grad * write_row[:, None], axis=0) * step_row
        cmat_grad = jnp.sum(here * grad_row[None, :], axis=1)
        return ((decay * state_grad, total), (delta_grad, bmat_grad, cmat_grad, signal_grad))

    steps_in = (delta, bmat, cmat, signal, keep, states, previous, out_grad)
    (flowing, rate_grad), outputs = lax.scan(token_back, (later, rate_grad), steps_in, reverse=True)
    return ((flowing, rate_grad), outputs)


def pack_full(pieces, kinds, shards):
    columns = []
    for piece, kind in zip(pieces, kinds):
        if kind == 0:
            columns.append(piece.reshape(shards, -1))
        else:
            height = piece.shape[0]
            columns.append(piece.reshape(height, shards, -1).transpose(1, 0, 2).reshape(shards, -1))
    return jnp.concatenate(columns, axis=1)


def unpack_full(stacked, shapes, kinds, shards):
    pieces = []
    offset = 0
    for shape, kind in zip(shapes, kinds):
        size = math.prod(shape)
        block = stacked[:, offset : offset + size]
        offset = offset + size
        if kind == 0:
            pieces.append(block.reshape((shards * shape[0],) + tuple(shape[1:])))
        else:
            pieces.append(
                block.reshape(shards, shape[0], shape[1])
                .transpose(1, 0, 2)
                .reshape(shape[0], shards * shape[1])
            )
    return pieces


def unpack_local(flat, shapes):
    pieces = []
    offset = 0
    for shape in shapes:
        size = math.prod(shape)
        pieces.append(flat[0, offset : offset + size].reshape(shape))
        offset = offset + size
    return pieces


def per_device(
    tokens,
    cotangent,
    destination,
    lengths,
    norm_gain,
    in_weight,
    conv_weight,
    conv_bias,
    select_weight,
    step_weight,
    step_bias,
    decay_log,
    skip_gain,
    out_weight,
):
    row_count = lax.axis_size(("dp", "fsdp"))
    shards = lax.axis_size("fsdp")
    tok_dev = tokens.shape[0]
    width = tokens.shape[1]
    pair = tok_dev // row_count
    order = jnp.argsort(destination)
    sorted_dest = destination[order]
    send_place = (sorted_dest % tok_dev).reshape(row_count, pair)
    got_place = lax.all_to_all(
        send_place, ("dp", "fsdp"), split_axis=0, concat_axis=0, tiled=True
    ).reshape(tok_dev)
    arrival = jnp.argsort(got_place)
    dealt = (
        lax.all_to_all(
            tokens[order].reshape(row_count, pair, width),
            ("dp", "fsdp"),
            split_axis=0,
            concat_axis=0,
            tiled=True,
        ),
        lax.all_to_all(
            cotangent[order].reshape(row_count, pair, width),
            ("dp", "fsdp"),
            split_axis=0,
            concat_axis=0,
            tiled=True,
        ),
    )
    x_rows = dealt[0].reshape(tok_dev, width)[arrival].astype(jnp.float32)
    dy_rows = dealt[1].reshape(tok_dev, width)[arrival]
    seg_lengths = lengths[0]
    ends = jnp.cumsum(seg_lengths)
    begins = ends - seg_lengths
    positions = jnp.arange(tok_dev, dtype=jnp.int32)
    keep = 1.0 - jnp.any(positions[:, None] == begins[None, :], axis=1).astype(jnp.float32)
    segment = jnp.sum((positions[:, None] >= ends[None, :]).astype(jnp.int32), axis=1)
    valid = (positions < ends[-2]).astype(jnp.float32)
    square_rows = jnp.sum(x_rows * x_rows, axis=1)
    totals = lax.psum((jnp.sum(square_rows * valid), jnp.sum(valid)), ("dp", "fsdp"))
    input_rms = jnp.sqrt(totals[0] / (totals[1] * width))
    local_pieces = [
        norm_gain,
        in_weight,
        out_weight,
        conv_bias,
        step_bias,
        skip_gain,
        conv_weight,
        select_weight,
        step_weight,
        decay_log,
    ]
    kinds = [0, 0, 0, 0, 0, 0, 1, 1, 1, 1]
    shapes = [piece.shape for piece in local_pieces]
    packed = jnp.concatenate([piece.reshape(1, -1) for piece in local_pieces], axis=1)
    shared = unpack_full(lax.all_gather(packed, "fsdp", axis=0, tiled=True), shapes, kinds, shards)
    micro_len = tok_dev // MICRO
    blocks = micro_len // SCAN_BLOCK
    state = jnp.zeros((N, DI), jnp.float32)
    tail_x = jnp.zeros((KC - 1, DI), jnp.float32)
    tail_seg = jnp.full((KC - 1,), -1, jnp.int32)
    saved = []
    for index in range(MICRO):
        weights = shared
        (
            gain_full,
            in_full,
            out_full,
            conv_bias_full,
            step_bias_full,
            skip_full,
            conv_full,
            select_full,
            step_full,
            decay_full,
        ) = weights
        start = index * micro_len
        rows_x = x_rows[start : start + micro_len]
        rstd = lax.rsqrt(jnp.mean(rows_x * rows_x, axis=1, keepdims=True) + eps)
        normed = (rows_x * rstd * gain_full.astype(jnp.float32)[None]).astype(jnp.bfloat16)
        proj = jnp.dot(normed, in_full, preferred_element_type=jnp.float32)
        x_in = proj[:, :DI]
        gate = proj[:, DI:]
        seg_here = segment[start : start + micro_len]
        ext_x = jnp.concatenate([tail_x, x_in], axis=0)
        ext_seg = jnp.concatenate([tail_seg, seg_here], axis=0)
        conv = jnp.zeros_like(x_in) + conv_bias_full.astype(jnp.float32)[None]
        for lag in range(KC):
            begin = KC - 1 - lag
            same = (ext_seg[begin : begin + micro_len] == seg_here).astype(jnp.float32)
            conv = (
                conv
                + conv_full[KC - 1 - lag].astype(jnp.float32)[None]
                * ext_x[begin : begin + micro_len]
                * same[:, None]
            )
        tail_x = ext_x[micro_len:]
        tail_seg = ext_seg[micro_len:]
        act = jax.nn.silu(conv).astype(jnp.bfloat16)
        dbl = lax.dot_general(
            act, select_full, (((1,), (1,)), ((), ())), preferred_element_type=jnp.float32
        )
        step_low = dbl[:, :R].astype(jnp.bfloat16)
        bmat = dbl[:, R : R + N]
        cmat = dbl[:, R + N :]
        pre = (
            jnp.dot(step_low, step_full, preferred_element_type=jnp.float32)
            + step_bias_full.astype(jnp.float32)[None]
        )
        delta = jax.nn.softplus(pre)
        rate = -jnp.exp(decay_full.astype(jnp.float32))
        signal = act.astype(jnp.float32)
        items = (
            delta.reshape(blocks, SCAN_BLOCK, DI),
            bmat.reshape(blocks, SCAN_BLOCK, N),
            cmat.reshape(blocks, SCAN_BLOCK, N),
            signal.reshape(blocks, SCAN_BLOCK, DI),
            keep[start : start + micro_len].reshape(blocks, SCAN_BLOCK),
        )
        state, (outputs, entry_states) = lax.scan(partial(forward_block, rate), state, items)
        scan_out = outputs.reshape(micro_len, DI) + skip_full.astype(jnp.float32)[None] * signal
        gated = (scan_out * jax.nn.silu(gate)).astype(jnp.bfloat16)
        mixed = jnp.dot(gated, out_full, preferred_element_type=jnp.float32)
        saved.append(
            (
                rstd,
                normed,
                x_in,
                gate,
                conv,
                act,
                bmat,
                cmat,
                step_low,
                pre,
                delta,
                entry_states,
                scan_out,
                gated,
                mixed,
            )
        )
    later = jnp.zeros((N, DI), jnp.float32)
    rate_grad = jnp.zeros((N, DI), jnp.float32)
    head_grad = jnp.zeros((KC - 1, DI), jnp.float32)
    head_seg = jnp.full((KC - 1,), -1, jnp.int32)
    skip_grad = jnp.zeros((DI,), jnp.float32)
    gain_grad = jnp.zeros((width,), jnp.float32)
    results_back = [None] * MICRO
    for index in reversed(range(MICRO)):
        weights = shared
        (
            gain_full,
            in_full,
            out_full,
            conv_bias_full,
            step_bias_full,
            skip_full,
            conv_full,
            select_full,
            step_full,
            decay_full,
        ) = weights
        (
            rstd,
            normed,
            x_in,
            gate,
            conv,
            act,
            bmat,
            cmat,
            step_low,
            pre,
            delta,
            entry_states,
            scan_out,
            gated,
            mixed,
        ) = saved[index]
        start = index * micro_len
        rows_x = x_rows[start : start + micro_len]
        dy_here = dy_rows[start : start + micro_len]
        seg_here = segment[start : start + micro_len]
        rate = -jnp.exp(decay_full.astype(jnp.float32))
        gated_grad = lax.dot_general(
            dy_here, out_full, (((1,), (1,)), ((), ())), preferred_element_type=jnp.float32
        )
        scan_grad = gated_grad * jax.nn.silu(gate)
        gate_grad = gated_grad * scan_out * silu_slope(gate)
        signal = act.astype(jnp.float32)
        skip_grad = skip_grad + jnp.sum(scan_grad * signal, axis=0)
        items = (
            delta.reshape(blocks, SCAN_BLOCK, DI),
            bmat.reshape(blocks, SCAN_BLOCK, N),
            cmat.reshape(blocks, SCAN_BLOCK, N),
            signal.reshape(blocks, SCAN_BLOCK, DI),
            keep[start : start + micro_len].reshape(blocks, SCAN_BLOCK),
            entry_states,
            scan_grad.reshape(blocks, SCAN_BLOCK, DI),
        )
        (later, rate_grad), (delta_grad, bmat_grad, cmat_grad, signal_grad) = lax.scan(
            partial(backward_block, rate), (later, rate_grad), items, reverse=True
        )
        pre_grad = (delta_grad.reshape(micro_len, DI) * jax.nn.sigmoid(pre)).astype(jnp.bfloat16)
        low_grad = lax.dot_general(
            pre_grad, step_full, (((1,), (1,)), ((), ())), preferred_element_type=jnp.float32
        )
        dbl_grad = jnp.concatenate(
            [low_grad, bmat_grad.reshape(micro_len, N), cmat_grad.reshape(micro_len, N)], axis=1
        ).astype(jnp.bfloat16)
        act_grad = (
            signal_grad.reshape(micro_len, DI) + skip_full.astype(jnp.float32)[None] * scan_grad
        )
        act_grad = act_grad + jnp.dot(dbl_grad, select_full, preferred_element_type=jnp.float32)
        conv_grad = act_grad * silu_slope(conv)
        ext_grad = jnp.concatenate([conv_grad, head_grad], axis=0)
        ext_seg = jnp.concatenate([seg_here, head_seg], axis=0)
        in_grad = jnp.zeros_like(conv_grad)
        for lag in range(KC):
            same = (ext_seg[lag : lag + micro_len] == seg_here).astype(jnp.float32)
            in_grad = (
                in_grad
                + conv_full[KC - 1 - lag].astype(jnp.float32)[None]
                * ext_grad[lag : lag + micro_len]
                * same[:, None]
            )
        head_grad = conv_grad[: KC - 1]
        head_seg = seg_here[: KC - 1]
        proj_grad = jnp.concatenate([in_grad, gate_grad], axis=1).astype(jnp.bfloat16)
        normed_grad = lax.dot_general(
            proj_grad, in_full, (((1,), (1,)), ((), ())), preferred_element_type=jnp.float32
        )
        hat = rows_x * rstd
        gain_grad = gain_grad + jnp.sum(normed_grad * hat, axis=0)
        hat_grad = normed_grad * gain_full.astype(jnp.float32)[None]
        row_grad = dy_here.astype(jnp.float32) + rstd * (
            hat_grad - hat * jnp.mean(hat_grad * hat, axis=1, keepdims=True)
        )
        results_back[index] = (pre_grad, dbl_grad, conv_grad, proj_grad, row_grad)

    def joined(position, source):
        return jnp.concatenate([entry[position] for entry in source], axis=0)

    normed_all = joined(1, saved)
    x_in_all = joined(2, saved)
    act_all = joined(5, saved)
    step_low_all = joined(8, saved)
    gated_all = joined(13, saved)
    mixed_all = joined(14, saved)
    pre_grad_all = joined(0, results_back)
    dbl_grad_all = joined(1, results_back)
    conv_grad_all = joined(2, results_back)
    proj_grad_all = joined(3, results_back)
    row_grad_all = joined(4, results_back)
    contract = (((0,), (0,)), ((), ()))
    in_grad_full = lax.dot_general(
        normed_all, proj_grad_all, contract, preferred_element_type=jnp.float32
    )
    out_grad_full = lax.dot_general(
        gated_all, dy_rows, contract, preferred_element_type=jnp.float32
    )
    select_grad_full = lax.dot_general(
        dbl_grad_all, act_all, contract, preferred_element_type=jnp.float32
    )
    step_grad_full = lax.dot_general(
        step_low_all, pre_grad_all, contract, preferred_element_type=jnp.float32
    )
    step_bias_grad = jnp.sum(pre_grad_all.astype(jnp.float32), axis=0)
    conv_bias_grad = jnp.sum(conv_grad_all, axis=0)
    tap_grads = []
    for tap in range(KC):
        lag = KC - 1 - tap
        same = (delayed(segment, lag, -1) == segment).astype(jnp.float32)
        tap_grads.append(
            jnp.sum(conv_grad_all * delayed(x_in_all, lag, 0.0) * same[:, None], axis=0)
        )
    conv_weight_grad = jnp.stack(tap_grads, axis=0)
    decay_grad_full = rate_grad * rate
    full_grads = [
        gain_grad,
        in_grad_full,
        out_grad_full,
        conv_bias_grad,
        step_bias_grad,
        skip_grad,
        conv_weight_grad,
        select_grad_full,
        step_grad_full,
        decay_grad_full,
    ]
    stacked = pack_full(full_grads, kinds, shards)
    received = lax.all_to_all(stacked, "fsdp", split_axis=0, concat_axis=0, tiled=True)
    owned = jnp.sum(received, axis=0, keepdims=True)
    summed = lax.psum(owned, "dp")
    local_grads = unpack_local(summed, shapes)

    def outgoing(values):
        return values[got_place].reshape(row_count, pair, width)

    layer_rows = (x_rows + mixed_all).astype(jnp.bfloat16)
    mixer_rows = mixed_all.astype(jnp.bfloat16)
    grad_rows = row_grad_all.astype(jnp.bfloat16)
    back = (
        lax.all_to_all(
            outgoing(layer_rows), ("dp", "fsdp"), split_axis=0, concat_axis=0, tiled=True
        ),
        lax.all_to_all(
            outgoing(mixer_rows), ("dp", "fsdp"), split_axis=0, concat_axis=0, tiled=True
        ),
        lax.all_to_all(
            outgoing(grad_rows), ("dp", "fsdp"), split_axis=0, concat_axis=0, tiled=True
        ),
    )
    undo = jnp.argsort(order)
    layer_output = back[0].reshape(tok_dev, width)[undo]
    mixer_output = back[1].reshape(tok_dev, width)[undo]
    input_grad = back[2].reshape(tok_dev, width)[undo]
    return (
        layer_output,
        mixer_output,
        input_grad,
        input_rms,
        local_grads[0],
        local_grads[1],
        local_grads[6],
        local_grads[3],
        local_grads[7],
        local_grads[8],
        local_grads[4],
        local_grads[9],
        local_grads[5],
        local_grads[2],
    )


def solution(mesh):
    return jax.shard_map(
        per_device,
        mesh=mesh,
        in_specs=(
            P(("dp", "fsdp"), None),
            P(("dp", "fsdp"), None),
            P(("dp", "fsdp")),
            P(("dp", "fsdp"), None),
            P("fsdp"),
            P("fsdp", None),
            P(None, "fsdp"),
            P("fsdp"),
            P(None, "fsdp"),
            P(None, "fsdp"),
            P("fsdp"),
            P(None, "fsdp"),
            P("fsdp"),
            P("fsdp", None),
        ),
        out_specs=(
            P(("dp", "fsdp"), None),
            P(("dp", "fsdp"), None),
            P(("dp", "fsdp"), None),
            P(),
            P("fsdp"),
            P("fsdp", None),
            P(None, "fsdp"),
            P("fsdp"),
            P(None, "fsdp"),
            P(None, "fsdp"),
            P("fsdp"),
            P(None, "fsdp"),
            P("fsdp"),
            P("fsdp", None),
        ),
        check_vma=False,
    )
```

profile of v0, /device:TPU:21, one launch (start us, length us, event | category | flops | bytes accessed | tf_op | source)
XLA Modules:
  0.0 7942.5 jit_solution(515035873564955539)
XLA Ops:
  61.8 135.5 %all-to-all-done.1 = s32[32,1,8]{2,1,0:T(1,128)S(1)} async-done(((s32[32,1,8]{2,1,0:T(1,128)}), s32[32,1,8]{2,1,0:T(1,128)S(1)}, u32[]{:S(2)}, u32[]{:S(2)}) %all-to-all-start.1) | async-done | bytes 1056 | tf_op jit(solution)/shard_map/all_to_all | solution.py:143
  298.0 1763.0 %all-gather.3.cloned.1.call-done = bf16[8,1,3305216]{2,1,0:T(2,128)(2,1)} async-done(((bf16[1,1,3305216]{2,1,0:T(2,128)(2,1)}), bf16[8,1,3305216]{2,1,0:T(2,128)(2,1)}) %all-gather.3.cloned.1.call-update) | async-done | bytes 52883472 | tf_op jit(solution)/shard_map/all_gather | solution.py:190
  2157.5 83.5 %reshape.525 = bf16[2048,8192]{1,0:T(8,128)(2,1)} reshape(bf16[8,2097152]{1,0:T(8,128)(2,1)} %slice.395) | data formatting | bytes 67108864 | tf_op jit(solution)/shard_map/reshape | solution.py:99
  2342.7 265.2 %while.277 = (s32[]{:T(128)}, f32[16,4096]{1,0:T(8,128)S(1)}, f32[8,16,4096]{2,1,0:T(8,128)}, f32[8,16,4096]{2,1,0:T(8,128)}, f32[8,16,4096]{2,1,0:T(8,128)}, /*...) while((s32[]{:T(128)}, f32[16,4096]{1,0:T(8,128)S(1)}, ...), condition=%wide.region_10.11_spmd, body=%wide.region_6.10_spmd.sunk | while | flops 458756 | bytes 4084630 | solution.py:254
  2612.7 265.0 %while.279 = (s32[]{:T(128)}, f32[16,4096]{1,0:T(8,128)S(1)}, f32[8,16,4096]{2,1,0:T(8,128)}, f32[8,16,4096]{2,1,0:T(8,128)}, f32[8,16,4096]{2,1,0:T(8,128)}, /*...) while((s32[]{:T(128)}, f32[16,4096]{1,0:T(8,128)S(1)}, ...), condition=%wide.region_16.17_spmd, body=%wide.region_12.16_spmd.sunk | while | flops 458756 | bytes 4084630 | solution.py:254
  2880.9 829.4 %while.282 = (s32[]{:T(128)}, f32[16,4096]{1,0:T(8,128)S(1)}, f32[16,4096]{1,0:T(8,128)S(1)}, f32[8,16,4096]{2,1,0:T(8,128)}, bf16[8,16,16]{2,1,0:T(8,128)(2,1)S...) while((s32[]{:T(128)}, f32[16,4096]{1,0:T(8,128)S(1)}, ...), condition=%wide.region_27.28_spmd, body=%wide.region_18.27_spmd.sunk | while | flops 2625512 | bytes 23780592 | solution.py:336
  2924.8 58.9 while.289
  3028.5 58.9 while.289
  3132.1 58.9 while.289
  3235.8 58.9 while.289
  3339.5 58.9 while.289
  3443.1 58.9 while.289
  3546.8 58.9 while.289
  3650.5 58.9 while.289
  3713.4 829.6 %while.285 = (s32[]{:T(128)}, f32[16,4096]{1,0:T(8,128)S(1)}, f32[16,4096]{1,0:T(8,128)S(1)}, f32[8,16,4096]{2,1,0:T(8,128)}, bf16[8,16,16]{2,1,0:T(8,128)(2,1)S...) while((s32[]{:T(128)}, f32[16,4096]{1,0:T(8,128)S(1)}, ...), condition=%wide.region_37.38_spmd, body=%wide.region_28.37_spmd.sunk | while | flops 2625512 | bytes 23780592 | solution.py:336
  3757.3 58.9 while.291
  4068.3 58.9 while.291
  4172.0 58.9 while.291
  4648.0 59.4 reshape.562
  4843.0 86.0 %all_to_all.31 = f32[8,1,3305216]{2,1,0:T(1,128)} reshape(f32[8,3305216]{1,0:T(8,128)} %constant_dynamic-update-slice_fusion.10) | data formatting | bytes 211533824 | tf_op jit(solution)/shard_map/all_to_all | solution.py:427
  4951.0 2257.8 %all-to-all-done.6 = f32[8,1,3305216]{2,1,0:T(1,128)} async-done(((f32[8,1,3305216]{2,1,0:T(1,128)}), f32[8,1,3305216]{2,1,0:T(1,128)}, u32[]{:S(2)}, u32[]{:S(2)}) %all-to-all-start.6) | async-done | bytes 105766944 | tf_op jit(solution)/shard_map/all_to_all | solution.py:427
  7208.8 244.1 %reduce_sum.329 = f32[3305216]{0:T(1024)} reduce(f32[8,1,3305216]{2,1,0:T(1,128)} %all-to-all-done.6, f32[]{:T(128)} %constant.351.clone.1), dimensions={0,1}, to_apply=%region_56.57 | reduce | flops 23136512 | bytes 118987776 | tf_op jit(solution)/shard_map/reduce_sum | solution.py:428
  7642.2 130.2 %all-reduce.12.cloned.1.call-done = f32[1,3305216]{1,0:T(1,128)} async-done(((f32[1,3305216]{1,0:T(1,128)}), f32[1,3305216]{1,0:T(1,128)}) %all-reduce.12.cloned.1.call-update) | async-done | bytes 13220880 | tf_op jit(solution)/shard_map/psum | solution.py:429
  7772.4 90.9 %slice_reduce_fusion = f32[2097152]{0:T(1024)} fusion(f32[1,3305216]{1,0:T(1,128)} %all-reduce.12.cloned.1.call-done), kind=kLoop, calls=%fused_computation.118 | loop fusion | bytes 16777216 | tf_op jit(solution)/shard_map/slice | solution.py:114
  (5478 shorter events, 4348.8 us)
Async XLA Ops:
  7.2 52.3 copy-start
  7.2 2053.8 %all-gather.3.cloned.1.call-start = ((), (), s32[]{:S(2)}) async-start(), calls=%async_computation.8 | async-start | bytes 118987776 | tf_op jit(solution)/shard_map/all_gather | solution.py:190
  53.3 144.0 %all-to-all-start.1 = ((s32[32,1,8]{2,1,0:T(1,128)}), s32[32,1,8]{2,1,0:T(1,128)S(1)}, u32[]{:S(2)}, u32[]{:S(2)}) async-start(s32[32,1,8]{2,1,0:T(1,128)} %bitcast.86), calls=%async_computation.1 | async-start | bytes 32768 | tf_op jit(solution)/shard_map/all_to_all | solution.py:143
  61.8 142.4 %copy-start.7 = (bf16[256,2048]{1,0:T(8,128)(2,1)S(1)}, bf16[256,2048]{1,0:T(8,128)(2,1)}, u32[]{:S(2)}) copy-start(bf16[256,2048]{1,0:T(8,128)(2,1)} %param.35) | copy-start | bytes 3145732
  197.3 42.2 copy-start.56
  197.3 30.9 all-to-all-start
  228.2 65.7 all-to-all-start.4
  244.8 51.4 copy-start.34
  298.0 1943.0 %copy-start.69 = (f32[128]{0:T(128)}, f32[128]{0:T(128)S(1)}, u32[]{:S(2)}) copy-start(f32[128]{0:T(128)S(1)} %get-tuple-element.2234) | copy-start | bytes 1540
  298.0 1943.0 %copy-start.72 = (f32[128]{0:T(128)}, f32[128]{0:T(128)S(1)}, u32[]{:S(2)}) copy-start(f32[128]{0:T(128)S(1)} %get-tuple-element.2235) | copy-start | bytes 1540
  2157.4 83.5 %copy-start.59 = (f32[1,2,8,128]{3,1,2,0:T(2,128)}, f32[1,2,8,128]{3,1,2,0:T(2,128)S(1)}, u32[]{:S(2)}) copy-start(f32[1,2,8,128]{3,1,2,0:T(2,128)S(1)} %copy.95) | copy-start | bytes 24580
  2157.5 83.5 %copy-start.12 = (f32[256,2048]{1,0:T(8,128)S(1)}, f32[256,2048]{1,0:T(8,128)}, u32[]{:S(2)}) copy-start(f32[256,2048]{1,0:T(8,128)} %convert_element_type.227) | copy-start | bytes 6291460
  2258.0 54.2 copy-start.47
  2258.0 54.2 copy-start.49
  2258.0 54.2 copy-start.51
  2258.1 54.2 copy-start.53
  2279.4 54.8 copy-start.13
  2342.6 265.4 %copy-start.18 = (bf16[128,4096]{1,0:T(8,128)(2,1)S(1)}, bf16[128,4096]{1,0:T(8,128)(2,1)}, u32[]{:S(2)}) copy-start(bf16[128,4096]{1,0:T(8,128)(2,1)} %get-tuple-element.2140) | copy-start | bytes 3145732
  4648.0 59.4 copy-start.27
  4929.1 2279.7 %all-to-all-start.6 = ((f32[8,1,3305216]{2,1,0:T(1,128)}), f32[8,1,3305216]{2,1,0:T(1,128)}, u32[]{:S(2)}, u32[]{:S(2)}) async-start(f32[8,1,3305216]{2,1,0:T(1,128)} %all_to_all.31), calls=%async_computation.6 | async-start | bytes 211533824 | tf_op jit(solution)/shard_map/all_to_all | solution.py:427
  4942.4 2830.0 %all-reduce.12.cloned.1.call-start = ((), (), s32[]{:S(2)}) async-start(), calls=%async_computation.7 | async-start | bytes 26441728 | tf_op jit(solution)/shard_map/psum | solution.py:429
  7516.2 32.9 all-to-all-start.2
  7549.1 30.3 all-to-all-start.3
  7579.4 60.5 all-to-all-start.5
  (86 other events, 866.1 us)
Sparse Core Ops, SparseCore 0:
  46.3 2014.5 all-gather.2
  7503.6 268.7 all-reduce.11
where the time goes:
time: 7970 us; the launch traced here: 7940 us
  waiting for transfers between devices  4390 us (55%)
  local copies, waits for them, and re-layouts  1740 us (22%)
  other arithmetic  1500 us (19%)
  matrix products  169 us (2%)
    all_to_all x1, waiting for transfers between devices, per_device(): lax.all_to_all(stacked, 'fsdp', split_axis=0, concat_axis=0, tiled=True)  2260 us
    all_gather x1, waiting for transfers between devices, per_device(): lax.all_gather(packed, 'fsdp', axis=0, tiled=True)  1760 us
    reduce_sum x256, other arithmetic, token_back(): signal_grad = jnp.sum(state_grad * write_row[:, None], axis=0) * step_row  542 us
    dynamic_slice x768, local copies, waits for them, and re-layouts, forward_block(): final, output = lax.scan(token_step, state, items)  452 us
    dynamic_update_slice x256, other arithmetic, backward_block(): _, states = lax.scan(rebuild, entry_state, (delta, bmat, signal, keep))  373 us
    dynamic_update_slice x768, local copies, waits for them, and re-layouts, forward_block(): final, output = lax.scan(token_step, state, items)  300 us
    reduce_sum x1, other arithmetic, per_device(): owned = jnp.sum(received, axis=0, keepdims=True)  244 us
    reduce_sum x256, other arithmetic, token_step(): return (carry, jnp.sum(read_row[:, None] * carry, axis=0))  199 us

commit v1 on v0

v1 whole, which is shorter than its diff:
```python
import functools
import math

import jax
import jax.numpy as jnp
from jax import lax
from jax.experimental import pallas as pl
from jax.experimental.pallas import tpu as pltpu
from jax.sharding import PartitionSpec as P

EPS = 1e-05
TB = 16
LOG2E = math.log2(math.e)
RESET = 1.0e4
BF16 = jnp.bfloat16
F32 = jnp.float32


def silu_slope(value):
    sigma = jax.nn.sigmoid(value)
    return sigma * (1.0 + value * (1.0 - sigma))


def fwd_kernel(chunks, lanes, delta_ref, act_ref, big_ref, bt_ref, cw_ref, rate_ref, skip_ref,
               y_ref, s_ref, carry, d_s, u_s, sc):
    n, ch = rate_ref.shape

    @pl.when(pl.program_id(1) == 0)
    def _():
        carry[...] = jnp.zeros_like(carry)

    def chunk(i, _):
        base = pl.multiple_of(i * TB, TB)
        dl = delta_ref[pl.ds(base, TB), :]
        ac = act_ref[pl.ds(base, TB), :].astype(F32)
        d_s[...] = dl + big_ref[pl.ds(base, TB), :]
        u_s[...] = dl * ac
        bt = bt_ref[i]
        for lo in range(0, ch, lanes):
            cs = pl.ds(lo, lanes)
            rate = rate_ref[:, cs]
            s = carry[:, cs]
            for t in range(TB):
                dec = jnp.exp2(d_s[t : t + 1, cs] * rate)
                s = dec * s + bt[:, t : t + 1] * u_s[t : t + 1, cs]
                sc[t * n : (t + 1) * n, cs] = s.astype(BF16)
            carry[:, cs] = s
        states = sc[...]
        y = jnp.dot(cw_ref[i], states, preferred_element_type=F32)
        y_ref[pl.ds(base, TB), :] = y + skip_ref[...] * ac
        s_ref[pl.ds(pl.multiple_of(base * n, TB * n), TB * n), :] = states
        return 0

    lax.fori_loop(0, chunks, chunk, 0)


def block_coef(m):
    t, n = m.shape
    eye = jnp.eye(TB, dtype=m.dtype)
    spread = m.reshape(t // TB, TB, 1, n) * eye[None, :, :, None]
    return spread.reshape(t // TB, TB, TB * n).astype(BF16)


def turned(m):
    t, n = m.shape
    return m.reshape(t // TB, TB, n).transpose(0, 2, 1)


def scan_forward(delta, act, big, bmat, cmat, rate2, skip, row_len, tblk=64, lanes=512):
    t, ch = delta.shape
    n = bmat.shape[1]
    nb = row_len // tblk
    k = tblk // TB
    at = lambda r, j: (r * nb + j, 0)
    at3 = lambda r, j: (r * nb + j, 0, 0)
    zero = lambda r, j: (0, 0)
    return pl.pallas_call(
        functools.partial(fwd_kernel, k, min(lanes, ch)),
        grid=(t // row_len, nb),
        in_specs=[
            pl.BlockSpec((tblk, ch), at),
            pl.BlockSpec((tblk, ch), at),
            pl.BlockSpec((tblk, 1), at),
            pl.BlockSpec((k, n, TB), at3),
            pl.BlockSpec((k, TB, TB * n), at3),
            pl.BlockSpec((n, ch), zero),
            pl.BlockSpec((1, ch), zero),
        ],
        out_specs=[pl.BlockSpec((tblk, ch), at), pl.BlockSpec((tblk * n, ch), at)],
        out_shape=[jax.ShapeDtypeStruct((t, ch), F32), jax.ShapeDtypeStruct((t * n, ch), BF16)],
        scratch_shapes=[
            pltpu.VMEM((n, ch), F32),
            pltpu.VMEM((TB, ch), F32),
            pltpu.VMEM((TB, ch), F32),
            pltpu.VMEM((TB * n, ch), BF16),
        ],
        compiler_params=pltpu.CompilerParams(vmem_limit_bytes=24 * 2**20),
        cost_estimate=pl.CostEstimate(flops=t * n * ch * 40, bytes_accessed=t * ch * 44, transcendentals=t * n * ch),
    )(delta, act, big, turned(bmat), block_coef(cmat), rate2, skip)


def bwd_kernel(chunks, lanes, delta_ref, act_ref, big_ref, gy_ref, ct_ref, bw_ref, rate_ref, s_ref, sp_ref,
               dd_ref, da_ref, db_ref, dc_ref, dl_ref, carry, d_s, u_s, g_s, h_s):
    n, ch = rate_ref.shape

    @pl.when(pl.program_id(1) == 0)
    def _():
        carry[...] = jnp.zeros_like(carry)

    @pl.when((pl.program_id(0) == 0) & (pl.program_id(1) == 0))
    def _():
        dl_ref[...] = jnp.zeros_like(dl_ref)

    row = lax.broadcasted_iota(jnp.int32, (TB, TB * n), 0)
    col = lax.broadcasted_iota(jnp.int32, (TB, TB * n), 1)
    ones = jnp.where(row == col // n, 1.0, 0.0).astype(BF16)
    nt = (((1,), (1,)), ((), ()))

    def chunk(back, _):
        i = chunks - 1 - back
        base = pl.multiple_of(i * TB, TB)
        sbase = pl.multiple_of(i * TB * n, TB * n)
        dl = delta_ref[pl.ds(base, TB), :]
        ac = act_ref[pl.ds(base, TB), :].astype(F32)
        d_s[...] = dl + big_ref[pl.ds(base, TB), :]
        u_s[...] = dl * ac
        ct = ct_ref[i]
        before = pl.multiple_of(jnp.maximum(sbase - n, 0), n)
        for lo in range(0, ch, lanes):
            cs = pl.ds(lo, lanes)
            rate = rate_ref[:, cs]
            flow = carry[:, cs]
            acc = dl_ref[:, cs]
            for t in reversed(range(TB)):
                dr = d_s[t : t + 1, cs]
                dec = jnp.exp2(dr * rate)
                g = ct[:, t : t + 1] * gy_ref[pl.ds(base + t, 1), cs] + flow
                flow = dec * g
                if t > 0:
                    prev = s_ref[pl.ds(sbase + (t - 1) * n, n), cs]
                else:
                    prev = jnp.where(i > 0, s_ref[pl.ds(before, n), cs], sp_ref[:, cs])
                h = flow * prev.astype(F32)
                acc = acc + h * dr
                g_s[t * n : (t + 1) * n, cs] = g.astype(BF16)
                h_s[t * n : (t + 1) * n, cs] = (h * rate).astype(BF16)
            carry[:, cs] = flow
            dl_ref[:, cs] = acc
        gb = g_s[...]
        du = jnp.dot(bw_ref[i], gb, preferred_element_type=F32)
        hr = jnp.dot(ones, h_s[...], preferred_element_type=F32)
        dd_ref[pl.ds(base, TB), :] = hr * (1.0 / LOG2E) + du * ac
        da_ref[pl.ds(base, TB), :] = du * dl
        db_ref[pl.ds(sbase, TB * n), :] = lax.dot_general(
            gb, u_s[...].astype(BF16), nt, preferred_element_type=F32
        )
        dc_ref[pl.ds(sbase, TB * n), :] = lax.dot_general(
            s_ref[pl.ds(sbase, TB * n), :], gy_ref[pl.ds(base, TB), :].astype(BF16), nt, preferred_element_type=F32
        )
        return 0

    lax.fori_loop(0, chunks, chunk, 0)


def scan_backward(delta, act, big, gy, bmat, cmat, rate2, states, row_len, tblk=64, lanes=512):
    t, ch = delta.shape
    n = bmat.shape[1]
    nb = row_len // tblk
    k = tblk // TB
    at = lambda r, j: (r * nb + nb - 1 - j, 0)
    at3 = lambda r, j: (r * nb + nb - 1 - j, 0, 0)
    zero = lambda r, j: (0, 0)
    entry = lambda r, j: (jnp.maximum((r * nb + nb - 1 - j) * tblk - 1, 0), 0)
    dd, da, db, dc, dl = pl.pallas_call(
        functools.partial(bwd_kernel, k, min(lanes, ch)),
        grid=(t // row_len, nb),
        in_specs=[
            pl.BlockSpec((tblk, ch), at),
            pl.BlockSpec((tblk, ch), at),
            pl.BlockSpec((tblk, 1), at),
            pl.BlockSpec((tblk, ch), at),
            pl.BlockSpec((k, n, TB), at3),
            pl.BlockSpec((k, TB, TB * n), at3),
            pl.BlockSpec((n, ch), zero),
            pl.BlockSpec((tblk * n, ch), at),
            pl.BlockSpec((n, ch), entry),
        ],
        out_specs=[
            pl.BlockSpec((tblk, ch), at),
            pl.BlockSpec((tblk, ch), at),
            pl.BlockSpec((tblk * n, TB), at),
            pl.BlockSpec((tblk * n, TB), at),
            pl.BlockSpec((n, ch), zero),
        ],
        out_shape=[
            jax.ShapeDtypeStruct((t, ch), F32),
            jax.ShapeDtypeStruct((t, ch), F32),
            jax.ShapeDtypeStruct((t * n, TB), F32),
            jax.ShapeDtypeStruct((t * n, TB), F32),
            jax.ShapeDtypeStruct((n, ch), F32),
        ],
        scratch_shapes=[
            pltpu.VMEM((n, ch), F32),
            pltpu.VMEM((TB, ch), F32),
            pltpu.VMEM((TB, ch), F32),
            pltpu.VMEM((TB * n, ch), BF16),
            pltpu.VMEM((TB * n, ch), BF16),
        ],
        compiler_params=pltpu.CompilerParams(vmem_limit_bytes=32 * 2**20),
        cost_estimate=pl.CostEstimate(flops=t * n * ch * 80, bytes_accessed=t * ch * 60, transcendentals=t * n * ch),
    )(delta, act, big, gy, turned(cmat), block_coef(bmat), rate2, states, states)

    def diagonal(m):
        m = m.reshape(t // TB, TB, n, TB)
        return jnp.sum(m * jnp.eye(TB, dtype=m.dtype)[None, :, None, :], axis=3).reshape(t, n)

    return dd, da, diagonal(db), diagonal(dc), dl


def ring_order(count):
    half = count // 2
    if count % 2:
        return list(range(count))
    return [2 * p if p < half else 2 * (count - 1 - p) + 1 for p in range(count)]


def ring_step(value, count, by):
    order = ring_order(count)
    pairs = [(order[p], order[(p + by) % count]) for p in range(count)]
    return lax.ppermute(value, "fsdp", pairs)


def ring_gather(block, count, down):
    blocks = [None] * count
    blocks[0] = block
    here = block
    for hop in range(1, down + 1):
        here = ring_step(here, count, -1)
        blocks[hop] = here
    here = block
    for hop in range(1, count - down):
        here = ring_step(here, count, 1)
        blocks[count - hop] = here
    return blocks


def ring_reduce(part, count, down, dtype):
    total = part(0).astype(F32)
    if down:
        moving = part(count - down).astype(dtype)
        for hop in range(down):
            moving = ring_step(moving, count, -1)
            if hop < down - 1:
                moving = (moving.astype(F32) + part(count - down + hop + 1).astype(F32)).astype(dtype)
        total = total + moving.astype(F32)
    up = count - 1 - down
    if up:
        moving = part(up).astype(dtype)
        for hop in range(up):
            moving = ring_step(moving, count, 1)
            if hop < up - 1:
                moving = (moving.astype(F32) + part(up - hop - 1).astype(F32)).astype(dtype)
        total = total + moving.astype(F32)
    return total


def swap(value, count, mask):
    return lax.ppermute(value, "dp", [(i, i ^ mask) for i in range(count)])


def masks_of(count):
    return [1 << b for b in range(count.bit_length() - 1)]


def group_gather(block, count):
    blocks = {0: block}
    for mask in reversed(masks_of(count)):
        keys = sorted(blocks)
        got = swap(jnp.stack([blocks[m] for m in keys]), count, mask)
        for place, m in enumerate(keys):
            blocks[m | mask] = got[place]
    return [blocks[m] for m in range(count)]


def group_reduce(blocks, count, dtype):
    held = {m: b for m, b in enumerate(blocks)}
    for mask in masks_of(count):
        keep = [m for m in sorted(held) if not m & mask]
        got = swap(jnp.stack([held[m | mask].astype(dtype) for m in keep]), count, mask)
        held = {m: held[m].astype(F32) + got[place].astype(F32) for place, m in enumerate(keep)}
    return held[0]


def group_sum(blocks, count):
    held = {m: b for m, b in enumerate(blocks)}
    masks = masks_of(count)
    keep = [m for m in sorted(held) if not m & 1]
    got = swap(jnp.stack([held[m | 1] for m in keep]), count, 1)
    held = {m: held[m] + got[place] for place, m in enumerate(keep)}
    for mask in masks[1:]:
        keys = sorted(held)
        got = swap(jnp.stack([held[m] for m in keys]), count, mask)
        held = {m: held[m] + got[keys.index(m ^ mask)] for m in keys}
    keys = sorted(held)
    got = swap(jnp.stack([held[m] for m in keys]), count, 1)
    for place, m in enumerate(keys):
        held[m | 1] = got[place]
    return [held[m] for m in range(count)]


def per_device(
    tokens,
    cotangent,
    destination,
    lengths,
    norm_gain,
    in_weight,
    conv_weight,
    conv_bias,
    select_weight,
    step_weight,
    step_bias,
    decay_log,
    skip_gain,
    out_weight,
):
    n_dp = lax.axis_size("dp")
    n_f = lax.axis_size("fsdp")
    rows = n_dp * n_f
    tok = tokens.shape[0]
    width = tokens.shape[1]
    pair = tok // rows
    inner = conv_bias.shape[0] * n_f
    cs = conv_bias.shape[0] // n_dp
    ch = cs * n_f
    taps = conv_weight.shape[0]
    n = decay_log.shape[0]
    rank_of = step_weight.shape[0]
    dcols = width // n_f
    group = n_dp * tok
    both = ("dp", "fsdp")
    me_d = lax.axis_index("dp")
    me_f = lax.axis_index("fsdp")
    order = ring_order(n_f)
    place_of = jnp.asarray([order.index(f) for f in range(n_f)], jnp.int32)
    order_arr = jnp.asarray(order, jnp.int32)
    q = place_of[me_f]
    at_ring = [order_arr[(q + k) % n_f] for k in range(n_f)]
    flat_dot = lambda a, b: jnp.dot(a, b, preferred_element_type=F32)
    nt_dot = lambda a, b: lax.dot_general(a, b, (((1,), (1,)), ((), ())), preferred_element_type=F32)
    tn_dot = lambda a, b: lax.dot_general(a, b, (((0,), (0,)), ((), ())), preferred_element_type=F32)

    rank = jnp.sum((destination[None, :] < destination[:, None]).astype(jnp.int32), axis=1)
    slots = jnp.arange(tok, dtype=jnp.int32)
    to_send = (rank[None, :] == slots[:, None]).astype(BF16)
    from_send = (rank[:, None] == slots[None, :]).astype(BF16)
    spot = jnp.sum(
        jnp.where(rank[None, :] == slots[:, None], (destination % tok)[None, :], 0), axis=1
    )
    tag = jnp.broadcast_to(spot[:, None], (tok, 128)).astype(BF16)
    payload = jnp.concatenate([flat_dot(to_send, tokens).astype(BF16), tag], axis=1)
    got_x = lax.all_to_all(payload.reshape(rows, pair, width + 128), both, 0, 0, tiled=True)
    got_x = got_x.reshape(tok, width + 128)
    got_dy = lax.all_to_all(
        flat_dot(to_send, cotangent).astype(BF16).reshape(rows, pair, width), both, 0, 0, tiled=True
    ).reshape(tok, width)
    got_spot = got_x[:, width].astype(jnp.int32)
    to_row = (got_spot[None, :] == slots[:, None]).astype(BF16)
    from_row = (got_spot[:, None] == slots[None, :]).astype(BF16)
    x_own = flat_dot(to_row, got_x[:, :width]).astype(BF16)
    dy_own = flat_dot(to_row, got_dy).astype(BF16)

    def ring_columns(value):
        return jnp.concatenate(
            [lax.dynamic_slice_in_dim(value, at_ring[k] * dcols, dcols, 1) for k in range(n_f)], axis=1
        )

    def plain_columns(value):
        return jnp.concatenate(
            [lax.dynamic_slice_in_dim(value, ((place_of[f] - q) % n_f) * dcols, dcols, 1) for f in range(n_f)],
            axis=1,
        )

    x_all = jnp.concatenate(group_gather(ring_columns(x_own), n_dp), axis=0)
    dy_all = jnp.concatenate(group_gather(dy_own, n_dp), axis=0)

    lens = group_gather(jnp.broadcast_to(lengths, (8, lengths.shape[1])), n_dp)
    positions = jnp.arange(tok, dtype=jnp.int32)
    starts, segments = [], []
    for m in range(n_dp):
        total = jnp.int32(0)
        start = jnp.zeros((tok,), jnp.bool_)
        segment = jnp.zeros((tok,), jnp.int32)
        for s in range(lengths.shape[1]):
            start = start | (positions == total)
            total = total + lens[m][0, s]
            segment = segment + (positions >= total).astype(jnp.int32)
            if m == 0 and s == lengths.shape[1] - 2:
                valid = (positions < total).astype(F32)
        starts.append(start)
        segments.append(segment + m * (lengths.shape[1] + 1))
    big = jnp.where(jnp.concatenate(starts), RESET, 0.0).astype(F32)[:, None]
    segment = jnp.concatenate(segments)
    x_own32 = x_own.astype(F32)
    square = jnp.sum(x_own32 * x_own32, axis=1)
    totals = lax.psum(jnp.stack([jnp.sum(square * valid), jnp.sum(valid)]), both)
    input_rms = jnp.sqrt(totals[0] / (totals[1] * width))

    def mine(shard):
        return lax.dynamic_slice_in_dim(shard.reshape(-1, n_dp * cs), me_d * cs, cs, 1)

    smalls = [conv_weight, conv_bias, step_bias, skip_gain, decay_log, select_weight, step_weight]
    heights = [math.prod(s.shape) // (n_dp * cs) for s in smalls]
    gain_rows = dcols // cs
    used = sum(heights) + gain_rows
    filler = -used % 16
    small_block = jnp.concatenate(
        [mine(s) for s in smalls] + [norm_gain.reshape(gain_rows, cs), jnp.zeros((filler, cs), BF16)], axis=0
    )

    def my_columns(half):
        return jnp.concatenate(
            [
                lax.dynamic_slice_in_dim(in_weight, half * inner + f * n_dp * cs + me_d * cs, cs, 1)
                for f in range(n_f)
            ],
            axis=1,
        )

    small_ring = ring_gather(small_block, n_f, n_f // 2)
    wx = jnp.concatenate(ring_gather(my_columns(0), n_f, n_f // 2), axis=0)
    wg = jnp.concatenate(ring_gather(my_columns(1), n_f, n_f - 1 - n_f // 2), axis=0)
    wo_ring = ring_gather(lax.dynamic_slice_in_dim(out_weight, me_d * cs, cs, 0), n_f, n_f // 2)
    wo = jnp.zeros((n_f * cs, width), BF16)
    for k in range(n_f):
        wo = lax.dynamic_update_slice_in_dim(wo, wo_ring[k], at_ring[k] * cs, 0)
    small = jnp.zeros((used + filler, ch), BF16)
    for k in range(n_f):
        small = lax.dynamic_update_slice_in_dim(small, small_ring[k], at_ring[k] * cs, 1)
    gain = jnp.concatenate([b[used - gain_rows : used].reshape(dcols) for b in small_ring]).astype(F32)
    pieces, at = [], 0
    for height in heights:
        pieces.append(small[at : at + height])
        at += height
    conv_w, conv_b, step_b, skip, dlog, sel, stepw = pieces
    conv_w = conv_w.astype(F32)
    skip = skip.astype(F32)
    rate = -jnp.exp(dlog.astype(F32))

    x_all32 = x_all.astype(F32)
    rstd = lax.rsqrt(jnp.mean(x_all32 * x_all32, axis=1, keepdims=True) + EPS)
    normed = (x_all32 * rstd * gain[None]).astype(BF16)
    x_in = flat_dot(normed, wx)

    def shifted(values, lag):
        if lag == 0:
            return values
        edge = jnp.zeros((abs(lag),) + values.shape[1:], values.dtype)
        if lag > 0:
            return jnp.concatenate([edge, values[:-lag]], axis=0)
        return jnp.concatenate([values[-lag:], edge], axis=0)

    same = [(shifted(segment + 1, lag) == segment + 1).astype(F32)[:, None] for lag in range(taps)]
    same_next = [(shifted(segment + 1, -lag) == segment + 1).astype(F32)[:, None] for lag in range(taps)]
    conv = conv_b.astype(F32) + sum(
        conv_w[taps - 1 - lag][None] * shifted(x_in, lag) * same[lag] for lag in range(taps)
    )
    act = jax.nn.silu(conv).astype(BF16)
    dbl_part = nt_dot(act, sel)
    split = lambda value: [value[m * tok : (m + 1) * tok] for m in range(n_dp)]
    dbl = jnp.concatenate(group_sum(split(dbl_part), n_dp), axis=0)
    step_low = dbl[:, :rank_of].astype(BF16)
    bmat = dbl[:, rank_of : rank_of + n]
    cmat = dbl[:, rank_of + n :]
    pre = flat_dot(step_low, stepw) + step_b.astype(F32)
    delta = jax.nn.softplus(pre)
    rate2 = rate * LOG2E
    scan_out, states = scan_forward(delta, act, big, bmat, cmat, rate2, skip, tok)
    gate = flat_dot(normed, wg)
    gate_silu = jax.nn.silu(gate)
    gated = (scan_out * gate_silu).astype(BF16)
    mixed_part = flat_dot(gated, wo).astype(BF16)
    mixed = group_reduce(split(mixed_part), n_dp, BF16)

    gated_grad = nt_dot(dy_all, wo)
    scan_grad = gated_grad * gate_silu
    gate_grad = (gated_grad * scan_out * silu_slope(gate)).astype(BF16)
    wg_grad = tn_dot(normed, gate_grad).astype(BF16)
    wo_grad = tn_dot(gated, dy_all).astype(BF16)
    wg_own = ring_reduce(lambda k: wg_grad[k * dcols : (k + 1) * dcols], n_f, n_f // 2, BF16)
    wo_own = ring_reduce(
        lambda k: lax.dynamic_slice_in_dim(wo_grad, at_ring[k] * cs, cs, 0), n_f, n_f - 1 - n_f // 2, BF16
    )
    dd, da, bmat_grad, cmat_grad, decay_sum = scan_backward(
        delta, act, big, scan_grad, bmat, cmat, rate2, states, tok
    )
    pre_grad = (dd * jax.nn.sigmoid(pre)).astype(BF16)
    low_grad = nt_dot(pre_grad, stepw)
    dbl_grad = jnp.concatenate(
        group_sum(split(jnp.concatenate([low_grad, bmat_grad, cmat_grad], axis=1)), n_dp), axis=0
    ).astype(BF16)
    act32 = act.astype(F32)
    act_grad = da + skip * scan_grad + flat_dot(dbl_grad, sel)
    conv_grad = act_grad * silu_slope(conv)
    in_grad = sum(
        conv_w[taps - 1 - lag][None] * shifted(conv_grad, -lag) * same_next[lag] for lag in range(taps)
    ).astype(BF16)
    wx_grad = tn_dot(normed, in_grad).astype(BF16)
    wx_own = ring_reduce(lambda k: wx_grad[k * dcols : (k + 1) * dcols], n_f, n_f // 2, BF16)
    normed_grad_part = (nt_dot(in_grad, wx) + nt_dot(gate_grad, wg)).astype(BF16)
    normed_grad = group_reduce(split(normed_grad_part), n_dp, BF16)

    tap_grads = [
        jnp.sum(conv_grad * shifted(x_in, taps - 1 - tap) * same[taps - 1 - tap], axis=0) for tap in range(taps)
    ]
    small_grads = jnp.concatenate(
        [jnp.stack(tap_grads)]
        + [
            jnp.sum(conv_grad, axis=0, keepdims=True),
            jnp.sum(pre_grad.astype(F32), axis=0, keepdims=True),
            jnp.sum(scan_grad * act32, axis=0, keepdims=True),
            decay_sum * rate,
            tn_dot(dbl_grad, act),
            tn_dot(step_low, pre_grad),
            jnp.zeros((-sum(heights) % 16, ch), F32),
        ],
        axis=0,
    )
    small_own = ring_reduce(
        lambda k: lax.dynamic_slice_in_dim(small_grads, at_ring[k] * cs, cs, 1), n_f, n_f - 1 - n_f // 2, F32
    )

    def in_group_order(blocks):
        stacked = jnp.stack(blocks)
        return [lax.dynamic_index_in_dim(stacked, me_d ^ i, 0, keepdims=False) for i in range(n_dp)]

    def interleaved(blocks):
        parts = in_group_order(blocks)
        return jnp.concatenate(
            [p[:, f * cs : (f + 1) * cs] for f in range(parts[0].shape[1] // cs) for p in parts], axis=1
        )

    gx = interleaved(group_gather(wx_own.astype(BF16), n_dp))
    gg = interleaved(group_gather(wg_own.astype(BF16), n_dp))
    grad_in_weight = jnp.concatenate([gx, gg], axis=1).astype(F32)
    grad_out_weight = jnp.concatenate(in_group_order(group_gather(wo_own.astype(BF16), n_dp)), axis=0).astype(F32)
    small_full = interleaved(group_gather(small_own, n_dp))
    out_small, at = [], 0
    for height, s in zip(heights, smalls):
        out_small.append(small_full[at : at + height].reshape(s.shape))
        at += height
    grad_norm_gain = jnp.sum(grad_in_weight * in_weight.astype(F32), axis=1) / norm_gain.astype(F32)

    hat = x_all32[:tok] * rstd[:tok]
    hat_grad = normed_grad * gain[None]
    change = rstd[:tok] * (hat_grad - hat * jnp.mean(hat_grad * hat, axis=1, keepdims=True))
    row_grad = (dy_own.astype(F32) + plain_columns(change)).astype(BF16)
    layer = (x_own32 + mixed).astype(BF16)

    def returned(value):
        cols = value.shape[1]
        out = flat_dot(from_row, value).astype(BF16).reshape(rows, pair, cols)
        back = lax.all_to_all(out, both, 0, 0, tiled=True).reshape(tok, cols)
        return flat_dot(from_send, back).astype(BF16)

    ahead = returned(jnp.concatenate([layer, mixed.astype(BF16)], axis=1))
    layer_output = ahead[:, :width]
    mixer_output = ahead[:, width:]
    input_grad = returned(row_grad)
    return (
        layer_output,
        mixer_output,
        input_grad,
        input_rms,
        grad_norm_gain,
        grad_in_weight,
        out_small[0],
        out_small[1],
        out_small[5],
        out_small[6],
        out_small[2],
        out_small[4],
        out_small[3],
        grad_out_weight,
    )


def solution(mesh):
    return jax.shard_map(
        per_device,
        mesh=mesh,
        in_specs=(
            P(("dp", "fsdp"), None),
            P(("dp", "fsdp"), None),
            P(("dp", "fsdp")),
            P(("dp", "fsdp"), None),
            P("fsdp"),
            P("fsdp", None),
            P(None, "fsdp"),
            P("fsdp"),
            P(None, "fsdp"),
            P(None, "fsdp"),
            P("fsdp"),
            P(None, "fsdp"),
            P("fsdp"),
            P("fsdp", None),
        ),
        out_specs=(
            P(("dp", "fsdp"), None),
            P(("dp", "fsdp"), None),
            P(("dp", "fsdp"), None),
            P(),
            P("fsdp"),
            P("fsdp", None),
            P(None, "fsdp"),
            P("fsdp"),
            P(None, "fsdp"),
            P(None, "fsdp"),
            P("fsdp"),
            P(None, "fsdp"),
            P("fsdp"),
            P("fsdp", None),
        ),
        check_vma=False,
    )
```

time: 7970 us -> 976 us (0.12)
  waiting for transfers between devices: 4390 us -> 229 us
  local copies, waits for them, and re-layouts: 1740 us -> 226 us
  other arithmetic: 1500 us -> 92.1 us
  Pallas kernels: 0 us -> 89.5 us
    all_to_all x7 -> x4, waiting for transfers between devices: 2500 us -> 15.8 us  [the longest x2 15.8 us: returned(): back = lax.all_to_all(out, both, 0, 0, tiled=True).reshape(tok, cols)]
    all_gather x1 -> x0, waiting for transfers between devices: 1760 us -> none  [per_device(): lax.all_gather(packed, 'fsdp', axis=0, tiled=True)]
    reduce_sum x522 -> x9, other arithmetic: 1000 us -> 26.9 us  [the longest x1 8.21 us: per_device(): jnp.sum(conv_grad, axis=0, keepdims=True)]
    dynamic_slice x784 -> x20, local copies, waits for them, and re-layouts: 468 us -> 26.5 us  [the longest x10 19.4 us: in_group_order(): lax.dynamic_index_in_dim(stacked, me_d ^ i, 0, keepdims=False)]
    dynamic_update_slice x256 -> x0, other arithmetic: 373 us -> none  [backward_block(): _, states = lax.scan(rebuild, entry_state, (delta, bmat, signal, keep))]
    dynamic_update_slice x1328 -> x16, local copies, waits for them, and re-layouts: 344 us -> 14.6 us  [the longest x8 14.4 us: per_device(): wo = lax.dynamic_update_slice_in_dim(wo, wo_ring[k], at_ring[k] * cs, 0)]
    ppermute x0 -> x80, waiting for transfers between devices: none -> 214 us  [the longest x56 159 us: ring_step(): return lax.ppermute(value, 'fsdp', pairs)]
    slice x43 -> x22, local copies, waits for them, and re-layouts: 229 us -> 16.3 us  [the longest x4 4.86 us: group_gather(): blocks[m | mask] = got[place]]
where the time goes in v1:
time: 976 us; the launch traced here: 957 us
  waiting for transfers between devices  229 us (23%)
  local copies, waits for them, and re-layouts  226 us (23%)
  starting transfers between devices  116 us (12%)
  matrix products  103 us (11%)
  other arithmetic  92.1 us (9%)
  Pallas kernels  89.5 us (9%)
  blocking collectives  62.8 us (6%)
  between operations  38.2 us (4%)
    ppermute x56, waiting for transfers between devices, ring_step(): return lax.ppermute(value, 'fsdp', pairs)  159 us
    unnamed x324, local copies, waits for them, and re-layouts  131 us
    psum x1, blocking collectives, per_device(): lax.psum(jnp.stack([jnp.sum(square * valid), jnp.sum(valid)]), both)  62.8 us
    pallas_call x1, Pallas kernels, scan_backward(): pl.pallas_call(functools.partial(bwd_kernel, k, min(lanes, ch)), grid=(t...  62.2 us
    ppermute x24, waiting for transfers between devices, swap(): return lax.ppermute(value, 'dp', [(i, i ^ mask) for i in range(count)])  54.6 us
    dot_general x13, matrix products, per_device(): flat_dot = lambda a, b: jnp.dot(a, b, preferred_element_type=F32)  42.4 us
    ppermute x24, starting transfers between devices, swap(): return lax.ppermute(value, 'dp', [(i, i ^ mask) for i in range(count)])  40.8 us
    dot_general x5, matrix products, per_device(): lax.dot_general(a, b, (((1,), (1,)), ((), ())), preferred_element_type=F32)  38.7 us
  transfers between devices with their start and end apart: 84, of which 31 were waited for; matrix products, arithmetic and copies ran while one was open for 34% of the time, Pallas kernels for 0%

profile of v1, /device:TPU:21, one launch (start us, length us, event | category | flops | bytes accessed | tf_op | source)
XLA Modules:
  0.0 957.3 jit_solution(7613200176856770214)
XLA Ops:
  143.6 10.9 %collective-permute-done.10 = bf16[256,1024]{1,0:T(8,128)(2,1)} collective-permute-done((bf16[256,1024]{1,0:T(8,128)(2,1)}, bf16[256,1024]{1,0:T(8,128)(2,1)}, u32[]{:S(2)}, u32[]{:S(2)}) %collective-permute-start.10) | collective-permute-done | bytes 524320 | tf_op jit(solution)/shard_map/ppermute | solution.py:230
  154.8 11.1 %collective-permute-done.22 = bf16[256,1024]{1,0:T(8,128)(2,1)} collective-permute-done((bf16[256,1024]{1,0:T(8,128)(2,1)S(1)}, bf16[256,1024]{1,0:T(8,128)(2,1)}, u32[]{:S(2)}, u32[]{:S(2)}) %collective-permute-start.22) | collective-permute-done | bytes 524320 | tf_op jit(solution)/shard_map/ppermute | solution.py:230
  167.0 19.1 %all-to-all-start.2 = ((bf16[32,8,2048]{2,1,0:T(8,128)(2,1)}), bf16[32,8,2048]{2,1,0:T(8,128)(2,1)}, u32[]{:S(2)}, u32[]{:S(2)}) async-start(bf16[32,8,2048]{2,1,0:T(8,128)(2,1)} %fusion.4), calls=%async_computation.2 | async-start | bytes 2097152 | tf_op jit(solution)/shard_map/all_to_all | solution.py:364
  198.8 23.1 %collective-permute-done.30 = bf16[128,2048]{1,0:T(8,128)(2,1)} collective-permute-done((bf16[128,2048]{1,0:T(8,128)(2,1)}, bf16[128,2048]{1,0:T(8,128)(2,1)}, u32[]{:S(2)}, u32[]{:S(2)}) %collective-permute-start.30) | collective-permute-done | bytes 524320 | tf_op jit(solution)/shard_map/ppermute | solution.py:230
  225.3 8.0 collective-permute-done.12
  238.6 13.1 %collective-permute-start.8 = (bf16[2,256,2048]{2,1,0:T(8,128)(2,1)}, bf16[2,256,2048]{2,1,0:T(8,128)(2,1)}, u32[]{:S(2)}, u32[]{:S(2)}) collective-permute-start(bf16[2,256,2048]{2,1,0:T(8,128)(2,1)} %pad_maximum_fusion.1), channel_id=1, source_target_pairs={{0,8},{8,0},{16,24},{24,16},{1,9},{9,1},{17,25},{25,17},{2,10},{10... | collective-permute-start | bytes 6291464 | tf_op jit(solution)/shard_map/ppermute | solution.py:268
  268.6 12.8 %collective-permute-done.37 = bf16[1,256,2048]{2,1,0:T(8,128)(2,1)S(1)} collective-permute-done((bf16[1,256,2048]{2,1,0:T(8,128)(2,1)S(1)}, bf16[1,256,2048]{2,1,0:T(8,128)(2,1)S(1)}, u32[]{:S(2)}, u32[]{:S(2)}) %collective-permute-start.37) | collective-permute-done | bytes 1048608 | tf_op jit(solution)/shard_map/ppermute | solution.py:268
  299.3 9.8 %fusion.112 = f32[1024,1024]{1,0:T(8,128)} fusion(bf16[1024,2048]{1,0:T(8,128)(2,1)S(1)} %multiply_convert_fusion, bf16[2048,1024]{1,0:T(8,128)(2,1)} %constant_dynamic-update-slice_fusion.39), kind=kOutput, calls=%fused_computation.478 | convolution fusion | flops 4294967296 | bytes 12582912 | tf_op jit(solution)/shard_map/dot_general | solution.py:349
  310.5 17.4 %multiply_reduce_fusion.2 = (f32[1024]{0:T(1024)}, f32[1024,1024]{1,0:T(8,128)}, bf16[1024,1024]{1,0:T(8,128)(2,1)S(1)}, f32[1024,1024]{1,0:T(8,128)}, f32[1024,1024]{1,0:T(8,128)}) fusion(f32[1024,1024]{1,0:T(8,128)} %fusion.112, f32[1024]{0:T(1024)S(1)} %fusion.64, f32[1021,1024]{1,0:T(8,128)S(1)} %bitcast.323, f32[1024]{0:T(1024)S(1)} %bitcast.416, ...), kind=kOutput, calls=%fused_computation.14 | convolution fusion | flops 4336909312 | bytes 44052480 | tf_op jit(solution)/shard_map/dot_general | solution.py:350
  367.5 27.2 %shard_map.266 = (f32[1024,1024]{1,0:T(8,128)S(1)}, bf16[16384,1024]{1,0:T(8,128)(2,1)}) custom-call(f32[1024,1024]{1,0:T(8,128)S(1)} %get-tuple-element.195.delta_ref, bf16[1024,1024]{1,0:T(8,128)(2,1)S(1)} %get-tuple-element.37.act_ref, f32[1024,1]{1,0:T(8,128)S(1)} %broadcast_select_fusion.big_ref, f32[64,16,16]{2,1,0:T(8,128)S(1)} %bitcast.321, ...), custom_call_target="tpu_custom_call" | custom-call | flops 671088640 | bytes 46137344 | tf_op jit(solution)/shard_map/pallas_call | solution.py:77
  394.7 62.2 %shard_map.267 = (f32[1024,1024]{1,0:T(8,128)S(1)}, f32[1024,1024]{1,0:T(8,128)S(1)}, f32[16384,16]{1,0:T(8,128)}, f32[16384,16]{1,0:T(8,128)}, f32[16,1024]{1,0:T(8,128)S(1)}) custom-call(f32[1024,1024]{1,0:T(8,128)S(1)} %get-tuple-element.195.delta_ref, bf16[1024,1024]{1,0:T(8,128)(2,1)S(1)} %get-tuple-element.37.act_ref, ...), custom_call_target="tpu_custom_call" | custom-call | flops 1342177280 | bytes 62914560 | tf_op jit(solution)/shard_map/pallas_call | solution.py:174
  472.4 9.8 %convolution_convert_fusion.5 = bf16[1024,2048]{1,0:T(8,128)(2,1)} fusion(bf16[1024,1024]{1,0:T(8,128)(2,1)S(1)} %get-tuple-element.46, bf16[1024,2048]{1,0:T(8,128)(2,1)} %constant_dynamic-update-slice_fusion.118), kind=kOutput, calls=%fused_computation.33 | convolution fusion | flops 4297064448 | bytes 10485760 | tf_op jit(solution)/shard_map/dot_general | solution.py:349
  488.6 9.0 fusion.113
  538.2 8.2 fusion.92
  550.6 7.6 convolution_convert_fusion.4
  577.3 21.0 %collective-permute-done.63 = f32[320,128]{1,0:T(8,128)S(1)} collective-permute-done((f32[320,128]{1,0:T(8,128)S(1)}, f32[320,128]{1,0:T(8,128)S(1)}, u32[]{:S(2)}, u32[]{:S(2)}) %collective-permute-start.63) | collective-permute-done | bytes 163872 | tf_op jit(solution)/shard_map/ppermute | solution.py:230
  603.0 10.0 %collective-permute-done.64 = f32[320,128]{1,0:T(8,128)S(1)} collective-permute-done((f32[320,128]{1,0:T(8,128)S(1)}, f32[320,128]{1,0:T(8,128)S(1)}, u32[]{:S(2)}, u32[]{:S(2)}) %collective-permute-start.64) | collective-permute-done | bytes 163872 | tf_op jit(solution)/shard_map/ppermute | solution.py:230
  657.6 9.5 collective-permute-done.56
  668.8 9.5 collective-permute-done.46
  680.6 21.2 %collective-permute-done.78 = bf16[1,128,2048]{2,1,0:T(8,128)(2,1)S(1)} collective-permute-done((bf16[1,128,2048]{2,1,0:T(8,128)(2,1)S(1)}, bf16[1,128,2048]{2,1,0:T(8,128)(2,1)S(1)}, u32[]{:S(2)}, u32[]{:S(2)}) %collective-permute-start.78) | collective-permute-done | bytes 524320 | tf_op jit(solution)/shard_map/ppermute | solution.py:268
  703.0 10.1 %collective-permute-done.60 = bf16[1,256,1024]{1,2,0:T(8,128)(2,1)S(1)} collective-permute-done((bf16[1,256,1024]{1,2,0:T(8,128)(2,1)S(1)}, bf16[1,256,1024]{1,2,0:T(8,128)(2,1)S(1)}, u32[]{:S(2)}, u32[]{:S(2)}) %collective-permute-start.60) | collective-permute-done | bytes 524320 | tf_op jit(solution)/shard_map/ppermute | solution.py:268
  724.5 62.8 %psum.7 = f32[2]{0:T(128)S(1)} all-reduce(f32[2]{0:T(128)S(1)} %pad_maximum_fusion.34), channel_id=1, replica_groups=mesh['dp'=4,'fsdp'=8] {'dp','fsdp'}, use_global_device_ids=true, to_apply=%region_9.10 | all-reduce | flops 2 | bytes 16 | tf_op jit(solution)/shard_map/psum | solution.py:406
  926.5 7.9 multiply_reduce_fusion
  937.8 15.8 %all-to-all-done.1 = bf16[32,8,4096]{2,1,0:T(8,128)(2,1)S(1)} async-done(((bf16[32,8,4096]{2,1,0:T(8,128)(2,1)}), bf16[32,8,4096]{2,1,0:T(8,128)(2,1)S(1)}, u32[]{:S(2)}, u32[]{:S(2)}) %all-to-all-start.1) | async-done | bytes 2097184 | tf_op jit(solution)/shard_map/all_to_all | solution.py:563
  (702 shorter events, 502.1 us)
Async XLA Ops:
  15.6 109.7 %collective-permute-start.28 = (bf16[128,2048]{1,0:T(8,128)(2,1)}, bf16[128,2048]{1,0:T(8,128)(2,1)}, u32[]{:S(2)}, u32[]{:S(2)}) collective-permute-start(bf16[128,2048]{1,0:T(8,128)(2,1)} %get-tuple-element.44), channel_id=1, source_target_pairs={{0,1},{2,0},{4,2},{6,4},{7,6},{5,7},{3,5},{1,3},{8,9},{10,8},{12,1... | collective-permute-start | bytes 1572872 | tf_op jit(solution)/shard_map/ppermute | solution.py:230
  16.8 109.7 %collective-permute-start.32 = (bf16[128,2048]{1,0:T(8,128)(2,1)}, bf16[128,2048]{1,0:T(8,128)(2,1)}, u32[]{:S(2)}, u32[]{:S(2)}) collective-permute-start(bf16[128,2048]{1,0:T(8,128)(2,1)} %get-tuple-element.44), channel_id=1, source_target_pairs={{0,2},{2,4},{4,6},{6,7},{7,5},{5,3},{3,1},{1,0},{8,10},{10,12},{12... | collective-permute-start | bytes 1572872 | tf_op jit(solution)/shard_map/ppermute | solution.py:230
  29.3 97.5 %collective-permute-start.9 = (bf16[256,1024]{1,0:T(8,128)(2,1)}, bf16[256,1024]{1,0:T(8,128)(2,1)}, u32[]{:S(2)}, u32[]{:S(2)}) collective-permute-start(bf16[256,1024]{1,0:T(8,128)(2,1)} %get-tuple-element.72), channel_id=1, source_target_pairs={{0,1},{2,0},{4,2},{6,4},{7,6},{5,7},{3,5},{1,3},{8,9},{10,8},{12,1... | collective-permute-start | bytes 1572872 | tf_op jit(solution)/shard_map/ppermute | solution.py:230
  30.5 108.4 %collective-permute-start.13 = (bf16[256,1024]{1,0:T(8,128)(2,1)}, bf16[256,1024]{1,0:T(8,128)(2,1)}, u32[]{:S(2)}, u32[]{:S(2)}) collective-permute-start(bf16[256,1024]{1,0:T(8,128)(2,1)} %get-tuple-element.72), channel_id=1, source_target_pairs={{0,2},{2,4},{4,6},{6,7},{7,5},{5,3},{3,1},{1,0},{8,10},{10,12},{12... | collective-permute-start | bytes 1572872 | tf_op jit(solution)/shard_map/ppermute | solution.py:230
  32.8 134.2 %all-to-all-start = ((bf16[32,8,2176]{2,1,0:T(8,128)(2,1)}), bf16[32,8,2176]{2,1,0:T(8,128)(2,1)S(1)}, u32[]{:S(2)}, u32[]{:S(2)}) async-start(bf16[32,8,2176]{2,1,0:T(8,128)(2,1)} %maximum_bitcast_fusion), calls=%async_computation | async-start | bytes 2228224 | tf_op jit(solution)/shard_map/all_to_all | solution.py:362
  40.2 45.8 %collective-permute-start.16 = (s32[1,8,4]{1,2,0:T(4,128)S(1)}, s32[1,8,4]{1,2,0:T(4,128)S(1)}, u32[]{:S(2)}, u32[]{:S(2)}) collective-permute-start(s32[1,8,4]{1,2,0:T(4,128)S(1)} %stack_broadcast_in_dim.2), channel_id=1, source_target_pairs={{0,16},{8,24},{16,0},{24,8},{1,17},{9,25},{17,1},{25,9},{2,18},{10... | collective-permute-start | bytes 392 | tf_op jit(solution)/shard_map/ppermute | solution.py:268
  138.9 48.0 %collective-permute-start.33 = (bf16[128,2048]{1,0:T(8,128)(2,1)}, bf16[128,2048]{1,0:T(8,128)(2,1)}, u32[]{:S(2)}, u32[]{:S(2)}) collective-permute-start(bf16[128,2048]{1,0:T(8,128)(2,1)} %collective-permute-done.32), channel_id=1, source_target_pairs={{0,2},{2,4},{4,6},{6,7},{7,5},{5,3},{3,1},{1,0},{8,10},{10,12},{12... | collective-permute-start | bytes 1572872 | tf_op jit(solution)/shard_map/ppermute | solution.py:230
  140.2 48.1 %collective-permute-start.14 = (bf16[256,1024]{1,0:T(8,128)(2,1)}, bf16[256,1024]{1,0:T(8,128)(2,1)}, u32[]{:S(2)}, u32[]{:S(2)}) collective-permute-start(bf16[256,1024]{1,0:T(8,128)(2,1)} %collective-permute-done.13), channel_id=1, source_target_pairs={{0,2},{2,4},{4,6},{6,7},{7,5},{5,3},{3,1},{1,0},{8,10},{10,12},{12... | collective-permute-start | bytes 1572872 | tf_op jit(solution)/shard_map/ppermute | solution.py:230
  143.3 48.1 %collective-permute-start.25 = (bf16[256,1024]{1,0:T(8,128)(2,1)}, bf16[256,1024]{1,0:T(8,128)(2,1)}, u32[]{:S(2)}, u32[]{:S(2)}) collective-permute-start(bf16[256,1024]{1,0:T(8,128)(2,1)} %collective-permute-done.24), channel_id=1, source_target_pairs={{0,2},{2,4},{4,6},{6,7},{7,5},{5,3},{3,1},{1,0},{8,10},{10,12},{12... | collective-permute-start | bytes 1572872 | tf_op jit(solution)/shard_map/ppermute | solution.py:230
  167.0 90.2 %all-to-all-start.2 = ((bf16[32,8,2048]{2,1,0:T(8,128)(2,1)}), bf16[32,8,2048]{2,1,0:T(8,128)(2,1)}, u32[]{:S(2)}, u32[]{:S(2)}) async-start(bf16[32,8,2048]{2,1,0:T(8,128)(2,1)} %fusion.4), calls=%async_computation.2 | async-start | bytes 2097152 | tf_op jit(solution)/shard_map/all_to_all | solution.py:364
  188.3 48.7 %collective-permute-start.7 = (bf16[1,256,2048]{2,1,0:T(8,128)(2,1)S(1)}, bf16[1,256,2048]{2,1,0:T(8,128)(2,1)S(1)}, u32[]{:S(2)}, u32[]{:S(2)}) collective-permute-start(bf16[1,256,2048]{2,1,0:T(8,128)(2,1)S(1)} %bitcast.329), channel_id=1, source_target_pairs={{0,16},{8,24},{16,0},{24,8},{1,17},{9,25},{17,1},{25,9},{2,18},{10... | collective-permute-start | bytes 3145736 | tf_op jit(solution)/shard_map/ppermute | solution.py:268
  238.6 46.1 %collective-permute-start.8 = (bf16[2,256,2048]{2,1,0:T(8,128)(2,1)}, bf16[2,256,2048]{2,1,0:T(8,128)(2,1)}, u32[]{:S(2)}, u32[]{:S(2)}) collective-permute-start(bf16[2,256,2048]{2,1,0:T(8,128)(2,1)} %pad_maximum_fusion.1), channel_id=1, source_target_pairs={{0,8},{8,0},{16,24},{24,16},{1,9},{9,1},{17,25},{25,17},{2,10},{10... | collective-permute-start | bytes 6291464 | tf_op jit(solution)/shard_map/ppermute | solution.py:268
  498.7 75.5 %collective-permute-start.71 = (bf16[128,2048]{1,0:T(8,128)(2,1)}, bf16[128,2048]{1,0:T(8,128)(2,1)}, u32[]{:S(2)}, u32[]{:S(2)}) collective-permute-start(bf16[128,2048]{1,0:T(8,128)(2,1)} %get-tuple-element.53), channel_id=1, source_target_pairs={{0,1},{2,0},{4,2},{6,4},{7,6},{5,7},{3,5},{1,3},{8,9},{10,8},{12,1... | collective-permute-start | bytes 1572872 | tf_op jit(solution)/shard_map/ppermute | solution.py:230
  514.9 85.2 %collective-permute-start.57 = (bf16[256,1024]{0,1:T(8,128)(2,1)}, bf16[256,1024]{0,1:T(8,128)(2,1)}, u32[]{:S(2)}, u32[]{:S(2)}) collective-permute-start(bf16[256,1024]{0,1:T(8,128)(2,1)} %get-tuple-element.61), channel_id=1, source_target_pairs={{0,2},{2,4},{4,6},{6,7},{7,5},{5,3},{3,1},{1,0},{8,10},{10,12},{12... | collective-permute-start | bytes 1572872 | tf_op jit(solution)/shard_map/ppermute | solution.py:230
  520.6 53.7 %collective-permute-start.75 = (bf16[128,2048]{1,0:T(8,128)(2,1)}, bf16[128,2048]{1,0:T(8,128)(2,1)}, u32[]{:S(2)}, u32[]{:S(2)}) collective-permute-start(bf16[128,2048]{1,0:T(8,128)(2,1)} %add_convert_fusion.7), channel_id=1, source_target_pairs={{0,2},{2,4},{4,6},{6,7},{7,5},{5,3},{3,1},{1,0},{8,10},{10,12},{12... | collective-permute-start | bytes 1572872 | tf_op jit(solution)/shard_map/ppermute | solution.py:230
  573.0 43.2 %collective-permute-start.44 = (bf16[256,1024]{0,1:T(8,128)(2,1)S(1)}, bf16[256,1024]{0,1:T(8,128)(2,1)S(1)}, u32[]{:S(2)}, u32[]{:S(2)}) collective-permute-start(bf16[256,1024]{0,1:T(8,128)(2,1)S(1)} %get-tuple-element.66), channel_id=1, source_target_pairs={{0,1},{2,0},{4,2},{6,4},{7,6},{5,7},{3,5},{1,3},{8,9},{10,8},{12,1... | collective-permute-start | bytes 1572872 | tf_op jit(solution)/shard_map/ppermute | solution.py:230
  627.9 88.3 %collective-permute-start.42 = (bf16[2,256,2048]{2,1,0:T(8,128)(2,1)S(1)}, bf16[2,256,2048]{2,1,0:T(8,128)(2,1)S(1)}, u32[]{:S(2)}, u32[]{:S(2)}) collective-permute-start(bf16[2,256,2048]{2,1,0:T(8,128)(2,1)S(1)} %pad_maximum_fusion.4), channel_id=1, source_target_pairs={{0,8},{8,0},{16,24},{24,16},{1,9},{9,1},{17,25},{25,17},{2,10},{10... | collective-permute-start | bytes 6291464 | tf_op jit(solution)/shard_map/ppermute | solution.py:268
  667.1 51.9 %collective-permute-start.36 = (bf16[1,256,2048]{2,1,0:T(8,128)(2,1)S(1)}, bf16[1,256,2048]{2,1,0:T(8,128)(2,1)S(1)}, u32[]{:S(2)}, u32[]{:S(2)}) collective-permute-start(bf16[1,256,2048]{2,1,0:T(8,128)(2,1)S(1)} %fusion.16), channel_id=1, source_target_pairs={{0,16},{8,24},{16,0},{24,8},{1,17},{9,25},{17,1},{25,9},{2,18},{10... | collective-permute-start | bytes 3145736 | tf_op jit(solution)/shard_map/ppermute | solution.py:268
  713.1 83.9 %collective-permute-start.79 = (bf16[2,128,2048]{2,1,0:T(8,128)(2,1)}, bf16[2,128,2048]{2,1,0:T(8,128)(2,1)}, u32[]{:S(2)}, u32[]{:S(2)}) collective-permute-start(bf16[2,128,2048]{2,1,0:T(8,128)(2,1)} %pad_maximum_fusion.10), channel_id=1, source_target_pairs={{0,8},{8,0},{16,24},{24,16},{1,9},{9,1},{17,25},{25,17},{2,10},{10... | collective-permute-start | bytes 3145736 | tf_op jit(solution)/shard_map/ppermute | solution.py:268
  716.2 83.0 %collective-permute-start.61 = (bf16[2,256,1024]{1,2,0:T(8,128)(2,1)}, bf16[2,256,1024]{1,2,0:T(8,128)(2,1)}, u32[]{:S(2)}, u32[]{:S(2)}) collective-permute-start(bf16[2,256,1024]{1,2,0:T(8,128)(2,1)} %pad_maximum_fusion.9), channel_id=1, source_target_pairs={{0,8},{8,0},{16,24},{24,16},{1,9},{9,1},{17,25},{25,17},{2,10},{10... | collective-permute-start | bytes 3145736 | tf_op jit(solution)/shard_map/ppermute | solution.py:268
  718.8 74.2 %collective-permute-start.51 = (bf16[1,256,1024]{1,2,0:T(8,128)(2,1)}, bf16[1,256,1024]{1,2,0:T(8,128)(2,1)}, u32[]{:S(2)}, u32[]{:S(2)}) collective-permute-start(bf16[1,256,1024]{1,2,0:T(8,128)(2,1)} %fusion.23), channel_id=1, source_target_pairs={{0,16},{8,24},{16,0},{24,8},{1,17},{9,25},{17,1},{25,9},{2,18},{10... | collective-permute-start | bytes 1572872 | tf_op jit(solution)/shard_map/ppermute | solution.py:268
  723.3 91.8 %collective-permute-start.43 = (bf16[1,256,2048]{2,1,0:T(8,128)(2,1)}, bf16[1,256,2048]{2,1,0:T(8,128)(2,1)}, u32[]{:S(2)}, u32[]{:S(2)}) collective-permute-start(bf16[1,256,2048]{2,1,0:T(8,128)(2,1)} %fusion.17), channel_id=1, source_target_pairs={{0,16},{8,24},{16,0},{24,8},{1,17},{9,25},{17,1},{25,9},{2,18},{10... | collective-permute-start | bytes 3145736 | tf_op jit(solution)/shard_map/ppermute | solution.py:268
  823.0 78.3 %all-to-all-start.3 = ((bf16[32,8,2048]{2,1,0:T(8,128)(2,1)}), bf16[32,8,2048]{2,1,0:T(8,128)(2,1)S(1)}, u32[]{:S(2)}, u32[]{:S(2)}) async-start(bf16[32,8,2048]{2,1,0:T(8,128)(2,1)} %fusion.5), calls=%async_computation.3 | async-start | bytes 2097152 | tf_op jit(solution)/shard_map/all_to_all | solution.py:563
  901.3 52.2 %all-to-all-start.1 = ((bf16[32,8,4096]{2,1,0:T(8,128)(2,1)}), bf16[32,8,4096]{2,1,0:T(8,128)(2,1)S(1)}, u32[]{:S(2)}, u32[]{:S(2)}) async-start(bf16[32,8,4096]{2,1,0:T(8,128)(2,1)} %fusion.2), calls=%async_computation.1 | async-start | bytes 4194304 | tf_op jit(solution)/shard_map/all_to_all | solution.py:563
  (164 other events, 4400.2 us)

commit v2 on v1

--- a/solution.py
+++ b/solution.py
@@ -230,20 +230,6 @@
     return lax.ppermute(value, "fsdp", pairs)
 
 
-def ring_gather(block, count, down):
-    blocks = [None] * count
-    blocks[0] = block
-    here = block
-    for hop in range(1, down + 1):
-        here = ring_step(here, count, -1)
-        blocks[hop] = here
-    here = block
-    for hop in range(1, count - down):
-        here = ring_step(here, count, 1)
-        blocks[count - hop] = here
-    return blocks
-
-
 def ring_reduce(part, count, down, dtype):
     total = part(0).astype(F32)
     if down:
@@ -306,6 +292,297 @@
     for place, m in enumerate(keys):
         held[m | 1] = got[place]
     return [held[m] for m in range(count)]
+
+
+def mesh_at(index, n_f):
+    return (index // n_f, lax.rem(index, n_f))
+
+
+def ring_index(p, n_f):
+    if n_f % 2:
+        return p
+    return jnp.where(p < n_f // 2, 2 * p, 2 * (n_f - 1 - p) + 1)
+
+
+def ring_place(f, n_f):
+    if n_f % 2:
+        return f
+    return jnp.where(lax.rem(f, 2) == 0, f // 2, n_f - 1 - f // 2)
+
+
+def gather_kernel(n_dp, n_f, downs, send_ref, *refs):
+    streams = len(downs)
+    blocks = refs[:streams]
+    x_all, dy_all, x_own_ref, dy_own_ref, tag_ref = refs[streams : streams + 5]
+    outs = refs[streams + 5 : 2 * streams + 5]
+    got, x_own, dy_own, own_sem, deal_sem, loc_sem, pair_send, pair_recv, ring_send, ring_recv = refs[2 * streams + 5 :]
+    count = n_dp * n_f
+    me_d = lax.axis_index("dp")
+    me_f = lax.axis_index("fsdp")
+    me = me_d * n_f + me_f
+    q = ring_place(me_f, n_f)
+    below = ring_index(lax.rem(q + n_f - 1, n_f), n_f)
+    above = ring_index(lax.rem(q + 1, n_f), n_f)
+
+    barrier = pltpu.get_barrier_semaphore()
+
+    def greet(p, _):
+        pl.semaphore_signal(
+            barrier, inc=1, device_id=mesh_at(lax.rem(me + p, count), n_f), device_id_type=pl.DeviceIdType.MESH
+        )
+        return 0
+
+    lax.fori_loop(1, count, greet, 0)
+    own = pltpu.make_async_copy(send_ref.at[0], got.at[0], own_sem)
+    own.start()
+    locals_ = [
+        pltpu.make_async_copy(blocks[s], outs[s].at[me_f], loc_sem.at[s]) for s in range(streams)
+    ]
+    for c in locals_:
+        c.start()
+    pl.semaphore_wait(barrier, count - 1)
+
+    def deal(p, _):
+        pltpu.make_async_remote_copy(
+            src_ref=send_ref.at[p],
+            dst_ref=got.at[p],
+            send_sem=deal_sem.at[0],
+            recv_sem=deal_sem.at[1],
+            device_id=mesh_at(lax.rem(me + p, count), n_f),
+            device_id_type=pl.DeviceIdType.MESH,
+        ).start()
+        return 0
+
+    def hop(s, h, up):
+        k = lax.rem(q + (n_f - h if up else h), n_f)
+        index = ring_index(k, n_f)
+        src = blocks[s] if h == 0 else outs[s].at[index]
+        return pltpu.make_async_remote_copy(
+            src_ref=src,
+            dst_ref=outs[s].at[index],
+            send_sem=ring_send.at[s, int(up), h],
+            recv_sem=ring_recv.at[s, int(up), h],
+            device_id=(me_d, above if up else below),
+            device_id_type=pl.DeviceIdType.MESH,
+        )
+
+    hops = [[downs[s], n_f - 1 - downs[s]] for s in range(streams)]
+    for s in range(streams):
+        for up in (0, 1):
+            if hops[s][up]:
+                hop(s, 0, up).start()
+        if s == 1:
+            lax.fori_loop(1, count, deal, 0)
+
+    def advance(h):
+        for s in range(streams):
+            for up in (0, 1):
+                if h < hops[s][up]:
+                    hop(s, h - 1, up).wait_recv()
+                    hop(s, h, up).start()
+
+    own.wait()
+    rest = got.at[pl.ds(1, count - 1)]
+    pltpu.make_async_copy(send_ref.at[pl.ds(1, count - 1)], rest, deal_sem.at[1]).wait()
+    tok, width = x_own.shape
+    pair2 = got.shape[1]
+    total = count * pair2
+    tag = got[:, :, width : width + 128].astype(F32).reshape(total, 128)
+    reps = tok // 128
+    spots = jnp.concatenate([tag] * reps, axis=1)
+    lane = lax.broadcasted_iota(jnp.int32, (total, tok), 1).astype(F32)
+    row = lax.broadcasted_iota(jnp.int32, (total, tok), 0)
+    first = lax.rem(row, pair2) < pair2 // 2
+    match = spots == lane
+    x_pick = jnp.where(match & first, 1.0, 0.0).astype(BF16)
+    dy_pick = jnp.where(match & jnp.logical_not(first), 1.0, 0.0).astype(BF16)
+    tn = (((0,), (0,)), ((), ()))
+    tag_ref[...] = tag
+
+    def place(pick, out):
+        def part(j, _):
+            cols = pl.ds(pl.multiple_of(j * 256, 256), 256)
+            values = got[:, :, cols].reshape(total, 256)
+            out[:, cols] = lax.dot_general(pick, values, tn, preferred_element_type=F32).astype(BF16)
+            return 0
+
+        lax.fori_loop(0, width // 256, part, 0)
+
+    masks = list(reversed(masks_of(n_dp)))
+
+    def partner(mask):
+        return me_d + mask - 2 * mask * lax.rem(me_d // mask, 2)
+
+    def share(a, m, mask):
+        out = (x_all, dy_all)[a]
+        own_block = (x_own, dy_own)[a]
+        return pltpu.make_async_remote_copy(
+            src_ref=own_block if m == 0 else out.at[m],
+            dst_ref=out.at[m | mask],
+            send_sem=pair_send.at[a, m | mask],
+            recv_sem=pair_recv.at[a, m | mask],
+            device_id=(partner(mask), me_f),
+            device_id_type=pl.DeviceIdType.MESH,
+        )
+
+    copies = []
+
+    def keep(a):
+        own_block = (x_own, dy_own)[a]
+        for j, dst in enumerate(((x_all, dy_all)[a].at[0], (x_own_ref, dy_own_ref)[a])):
+            c = pltpu.make_async_copy(own_block, dst, loc_sem.at[streams + 2 * a + j])
+            c.start()
+            copies.append(c)
+
+    advance(1)
+    place(x_pick, x_own)
+    for mask in masks:
+        share(0, 0, mask).start()
+    keep(0)
+    place(dy_pick, dy_own)
+    for mask in masks:
+        share(1, 0, mask).start()
+    keep(1)
+
+    def relay(a):
+        held = [0]
+        for step, mask in enumerate(masks):
+            for m in held:
+                if m:
+                    share(a, m, mask).start()
+            for m in held:
+                share(a, m, mask).wait_recv()
+            held = held + [m | mask for m in held]
+
+    most = max(max(h) for h in hops)
+    for h in range(2, most):
+        advance(h)
+        if h == 2:
+            relay(0)
+    if most <= 2:
+        relay(0)
+    relay(1)
+    for s in range(streams):
+        for up in (0, 1):
+            if hops[s][up]:
+                hop(s, hops[s][up] - 1, up).wait_recv()
+    for s in range(streams):
+        for up in (0, 1):
+            for h in range(hops[s][up]):
+                hop(s, h, up).wait_send()
+    for a in (0, 1):
+        held = [0]
+        for mask in masks:
+            for m in held:
+                share(a, m, mask).wait_send()
+            held = held + [m | mask for m in held]
+    for c in locals_ + copies:
+        c.wait()
+    pltpu.make_async_copy(send_ref.at[pl.ds(1, count - 1)], rest, deal_sem.at[0]).wait()
+
+
+def gather_all(send, blocks, downs, n_dp, n_f, tok, width):
+    streams = len(blocks)
+    count, pair2, _ = send.shape
+    hops = max(max(d, n_f - 1 - d) for d in downs)
+    any_ = pl.BlockSpec(memory_space=pl.ANY)
+    row = jax.ShapeDtypeStruct((tok, width), BF16)
+    rows = jax.ShapeDtypeStruct((n_dp, tok, width), BF16)
+    return pl.pallas_call(
+        functools.partial(gather_kernel, n_dp, n_f, downs),
+        in_specs=[any_] * (1 + streams),
+        out_specs=[any_] * 4 + [pl.BlockSpec(memory_space=pltpu.VMEM)] + [any_] * streams,
+        out_shape=[rows, rows, row, row, jax.ShapeDtypeStruct((count * pair2, 128), F32)]
+        + [jax.ShapeDtypeStruct((n_f,) + b.shape, b.dtype) for b in blocks],
+        scratch_shapes=[
+            pltpu.VMEM(send.shape, BF16),
+            pltpu.VMEM((tok, width), BF16),
+            pltpu.VMEM((tok, width), BF16),
+            pltpu.SemaphoreType.DMA,
+            pltpu.SemaphoreType.DMA((2,)),
+            pltpu.SemaphoreType.DMA((streams + 4,)),
+            pltpu.SemaphoreType.DMA((2, n_dp)),
+            pltpu.SemaphoreType.DMA((2, n_dp)),
+            pltpu.SemaphoreType.DMA((streams, 2, hops)),
+            pltpu.SemaphoreType.DMA((streams, 2, hops)),
+        ],
+        compiler_params=pltpu.CompilerParams(
+            collective_id=0, has_side_effects=True, vmem_limit_bytes=32 * 2**20
+        ),
+        cost_estimate=pl.CostEstimate(flops=10**10, bytes_accessed=2 * 10**8, transcendentals=0),
+    )(send, *blocks)
+
+
+def columns_kernel(starts, cs, w_ref, *outs):
+    me_d = lax.axis_index("dp")
+    for o, out in enumerate(outs):
+        for j, start in enumerate(starts[o]):
+            out[:, j * cs : (j + 1) * cs] = w_ref[:, pl.ds(pl.multiple_of(start + me_d * cs, 128), cs)]
+
+
+def take_columns(w, halves, n_f, n_dp, cs):
+    inner = n_f * n_dp * cs
+    starts = [[h * inner + f * n_dp * cs for f in range(n_f)] for h in range(halves)]
+    me_d = lax.axis_index("dp")
+    if cs % 128:
+        return [
+            jnp.concatenate([lax.dynamic_slice_in_dim(w, s + me_d * cs, cs, 1) for s in group], axis=1)
+            for group in starts
+        ]
+    height = w.shape[0]
+    blk = min(height, 64)
+    return pl.pallas_call(
+        functools.partial(columns_kernel, starts, cs),
+        grid=(height // blk,),
+        in_specs=[pl.BlockSpec((blk, w.shape[1]), lambda i: (i, 0))],
+        out_specs=[pl.BlockSpec((blk, n_f * cs), lambda i: (i, 0))] * halves,
+        out_shape=[jax.ShapeDtypeStruct((height, n_f * cs), w.dtype)] * halves,
+    )(w)
+
+
+def spread_kernel(cs, x_ref, w_ref, out_ref, sum_ref):
+    me_d = lax.axis_index("dp")
+    total = jnp.zeros(sum_ref.shape, F32)
+    for i in range(x_ref.shape[0]):
+        m = me_d + i - 2 * ((me_d // 2 % 2) * (i // 2 % 2) * 2 + (me_d % 2) * (i % 2))
+        part = x_ref[m].astype(F32)
+        cols = slice(i * cs, (i + 1) * cs)
+        out_ref[:, cols] = part
+        product = part * w_ref[:, cols].astype(F32)
+        for j in range(0, cs, 128):
+            total = total + product[:, j : j + 128]
+
+    @pl.when(pl.program_id(0) == 0)
+    def _():
+        sum_ref[...] = jnp.zeros_like(sum_ref)
+
+    sum_ref[...] += total
+
+
+def spread_columns(rel, w, cs):
+    n_dp, height, cols = rel.shape
+    if cs % 128 or n_dp != 4:
+        me_d = lax.axis_index("dp")
+        parts = [lax.dynamic_index_in_dim(rel, me_d ^ i, 0, keepdims=False) for i in range(n_dp)]
+        out = jnp.concatenate(
+            [p[:, f * cs : (f + 1) * cs] for f in range(cols // cs) for p in parts], axis=1
+        ).astype(F32)
+        return out, jnp.sum(out * w.astype(F32), axis=1)
+    out, sums = pl.pallas_call(
+        functools.partial(spread_kernel, cs),
+        grid=(cols // cs,),
+        in_specs=[
+            pl.BlockSpec((n_dp, height, cs), lambda f: (0, 0, f)),
+            pl.BlockSpec((height, n_dp * cs), lambda f: (0, f)),
+        ],
+        out_specs=[
+            pl.BlockSpec((height, n_dp * cs), lambda f: (0, f)),
+            pl.BlockSpec((height, 128), lambda f: (0, 0)),
+        ],
+        out_shape=[jax.ShapeDtypeStruct((height, n_dp * cols), F32), jax.ShapeDtypeStruct((height, 128), F32)],
+        cost_estimate=pl.CostEstimate(flops=4 * height * cols * n_dp, bytes_accessed=8 * height * cols * n_dp, transcendentals=0),
+    )(rel, w)
+    return out, jnp.sum(sums, axis=1)
 
 
 def per_device(
@@ -350,39 +627,50 @@
     nt_dot = lambda a, b: lax.dot_general(a, b, (((1,), (1,)), ((), ())), preferred_element_type=F32)
     tn_dot = lambda a, b: lax.dot_general(a, b, (((0,), (0,)), ((), ())), preferred_element_type=F32)
 
+    me = me_d * n_f + me_f
+    row_to = destination // tok
+    in_row = destination % tok
     rank = jnp.sum((destination[None, :] < destination[:, None]).astype(jnp.int32), axis=1)
     slots = jnp.arange(tok, dtype=jnp.int32)
-    to_send = (rank[None, :] == slots[:, None]).astype(BF16)
+    rel_rank = ((row_to - me) % rows) * pair + rank % pair
+    to_send = rel_rank[None, :] == slots[:, None]
     from_send = (rank[:, None] == slots[None, :]).astype(BF16)
-    spot = jnp.sum(
-        jnp.where(rank[None, :] == slots[:, None], (destination % tok)[None, :], 0), axis=1
-    )
-    tag = jnp.broadcast_to(spot[:, None], (tok, 128)).astype(BF16)
-    payload = jnp.concatenate([flat_dot(to_send, tokens).astype(BF16), tag], axis=1)
-    got_x = lax.all_to_all(payload.reshape(rows, pair, width + 128), both, 0, 0, tiled=True)
-    got_x = got_x.reshape(tok, width + 128)
-    got_dy = lax.all_to_all(
-        flat_dot(to_send, cotangent).astype(BF16).reshape(rows, pair, width), both, 0, 0, tiled=True
-    ).reshape(tok, width)
-    got_spot = got_x[:, width].astype(jnp.int32)
-    to_row = (got_spot[None, :] == slots[:, None]).astype(BF16)
-    from_row = (got_spot[:, None] == slots[None, :]).astype(BF16)
-    x_own = flat_dot(to_row, got_x[:, :width]).astype(BF16)
-    dy_own = flat_dot(to_row, got_dy).astype(BF16)
-
-    def ring_columns(value):
-        return jnp.concatenate(
-            [lax.dynamic_slice_in_dim(value, at_ring[k] * dcols, dcols, 1) for k in range(n_f)], axis=1
-        )
-
-    def plain_columns(value):
-        return jnp.concatenate(
-            [lax.dynamic_slice_in_dim(value, ((place_of[f] - q) % n_f) * dcols, dcols, 1) for f in range(n_f)],
-            axis=1,
-        )
-
-    x_all = jnp.concatenate(group_gather(ring_columns(x_own), n_dp), axis=0)
-    dy_all = jnp.concatenate(group_gather(dy_own, n_dp), axis=0)
+    spot = jnp.sum(jnp.where(to_send, in_row[None, :], 0), axis=1)
+    tag = jnp.broadcast_to(spot[:, None], (tok, 128)).astype(BF16).reshape(rows, pair, 128)
+    to_send = to_send.astype(BF16)
+    sorted_x = flat_dot(to_send, tokens).astype(BF16).reshape(rows, pair, width)
+    sorted_dy = flat_dot(to_send, cotangent).astype(BF16).reshape(rows, pair, width)
+    payload = jnp.concatenate(
+        [jnp.concatenate([sorted_x, tag], axis=2), jnp.concatenate([sorted_dy, tag], axis=2)], axis=1
+    )
+
+    def mine(shard):
+        return lax.dynamic_slice_in_dim(shard.reshape(-1, n_dp * cs), me_d * cs, cs, 1)
+
+    smalls = [conv_weight, conv_bias, step_bias, skip_gain, decay_log, select_weight, step_weight]
+    heights = [math.prod(s.shape) // (n_dp * cs) for s in smalls]
+    gain_rows = dcols // cs
+    used = sum(heights) + gain_rows
+    filler = -used % 16
+    small_block = jnp.concatenate(
+        [mine(s) for s in smalls] + [norm_gain.reshape(gain_rows, cs), jnp.zeros((filler, cs), BF16)], axis=0
+    )
+    wx_block, wg_block = take_columns(in_weight, 2, n_f, n_dp, cs)
+    wo_block = lax.dynamic_slice_in_dim(out_weight, me_d * cs, cs, 0)
+    x_all, dy_all, x_own, dy_own, tags, small_all, wx, wg, wo = gather_all(
+        payload, [small_block, wx_block, wg_block, wo_block], [n_f // 2, n_f // 2, n_f - 1 - n_f // 2, n_f // 2],
+        n_dp, n_f, tok, width,
+    )
+    x_all = x_all.reshape(group, width)
+    dy_all = dy_all.reshape(group, width)
+    wx = wx.reshape(width, ch)
+    wg = wg.reshape(width, ch)
+    wo = wo.reshape(ch, width)
+    small = small_all.transpose(1, 0, 2).reshape(used + filler, ch)
+    gain = small_all[:, used - gain_rows : used].reshape(width).astype(F32)
+    tags = tags.reshape(rows, 2 * pair, 128)[:, :pair, 0].astype(jnp.int32)
+    tags = tags[(me - jnp.arange(rows, dtype=jnp.int32)) % rows].reshape(tok)
+    from_row = (tags[:, None] == slots[None, :]).astype(BF16)
 
     lens = group_gather(jnp.broadcast_to(lengths, (8, lengths.shape[1])), n_dp)
     positions = jnp.arange(tok, dtype=jnp.int32)
@@ -403,41 +691,8 @@
     segment = jnp.concatenate(segments)
     x_own32 = x_own.astype(F32)
     square = jnp.sum(x_own32 * x_own32, axis=1)
-    totals = lax.psum(jnp.stack([jnp.sum(square * valid), jnp.sum(valid)]), both)
-    input_rms = jnp.sqrt(totals[0] / (totals[1] * width))
-
-    def mine(shard):
-        return lax.dynamic_slice_in_dim(shard.reshape(-1, n_dp * cs), me_d * cs, cs, 1)
-
-    smalls = [conv_weight, conv_bias, step_bias, skip_gain, decay_log, select_weight, step_weight]
-    heights = [math.prod(s.shape) // (n_dp * cs) for s in smalls]
-    gain_rows = dcols // cs
-    used = sum(heights) + gain_rows
-    filler = -used % 16
-    small_block = jnp.concatenate(
-        [mine(s) for s in smalls] + [norm_gain.reshape(gain_rows, cs), jnp.zeros((filler, cs), BF16)], axis=0
-    )
-
-    def my_columns(half):
-        return jnp.concatenate(
-            [
-                lax.dynamic_slice_in_dim(in_weight, half * inner + f * n_dp * cs + me_d * cs, cs, 1)
-                for f in range(n_f)
-            ],
-            axis=1,
-        )
-
-    small_ring = ring_gather(small_block, n_f, n_f // 2)
-    wx = jnp.concatenate(ring_gather(my_columns(0), n_f, n_f // 2), axis=0)
-    wg = jnp.concatenate(ring_gather(my_columns(1), n_f, n_f - 1 - n_f // 2), axis=0)
-    wo_ring = ring_gather(lax.dynamic_slice_in_dim(out_weight, me_d * cs, cs, 0), n_f, n_f // 2)
-    wo = jnp.zeros((n_f * cs, width), BF16)
-    for k in range(n_f):
-        wo = lax.dynamic_update_slice_in_dim(wo, wo_ring[k], at_ring[k] * cs, 0)
-    small = jnp.zeros((used + filler, ch), BF16)
-    for k in range(n_f):
-        small = lax.dynamic_update_slice_in_dim(small, small_ring[k], at_ring[k] * cs, 1)
-    gain = jnp.concatenate([b[used - gain_rows : used].reshape(dcols) for b in small_ring]).astype(F32)
+    mine_sums = [jnp.sum(square * valid), jnp.sum(valid)]
+
     pieces, at = [], 0
     for height in heights:
         pieces.append(small[at : at + height])
@@ -487,7 +742,9 @@
     gate_grad = (gated_grad * scan_out * silu_slope(gate)).astype(BF16)
     wg_grad = tn_dot(normed, gate_grad).astype(BF16)
     wo_grad = tn_dot(gated, dy_all).astype(BF16)
-    wg_own = ring_reduce(lambda k: wg_grad[k * dcols : (k + 1) * dcols], n_f, n_f // 2, BF16)
+    wg_own = ring_reduce(
+        lambda k: lax.dynamic_slice_in_dim(wg_grad, at_ring[k] * dcols, dcols, 0), n_f, n_f // 2, BF16
+    )
     wo_own = ring_reduce(
         lambda k: lax.dynamic_slice_in_dim(wo_grad, at_ring[k] * cs, cs, 0), n_f, n_f - 1 - n_f // 2, BF16
     )
@@ -506,7 +763,9 @@
         conv_w[taps - 1 - lag][None] * shifted(conv_grad, -lag) * same_next[lag] for lag in range(taps)
     ).astype(BF16)
     wx_grad = tn_dot(normed, in_grad).astype(BF16)
-    wx_own = ring_reduce(lambda k: wx_grad[k * dcols : (k + 1) * dcols], n_f, n_f // 2, BF16)
+    wx_own = ring_reduce(
+        lambda k: lax.dynamic_slice_in_dim(wx_grad, at_ring[k] * dcols, dcols, 0), n_f, n_f // 2, BF16
+    )
     normed_grad_part = (nt_dot(in_grad, wx) + nt_dot(gate_grad, wg)).astype(BF16)
     normed_grad = group_reduce(split(normed_grad_part), n_dp, BF16)
 
@@ -535,26 +794,28 @@
         return [lax.dynamic_index_in_dim(stacked, me_d ^ i, 0, keepdims=False) for i in range(n_dp)]
 
     def interleaved(blocks):
-        parts = in_group_order(blocks)
-        return jnp.concatenate(
-            [p[:, f * cs : (f + 1) * cs] for f in range(parts[0].shape[1] // cs) for p in parts], axis=1
-        )
-
-    gx = interleaved(group_gather(wx_own.astype(BF16), n_dp))
-    gg = interleaved(group_gather(wg_own.astype(BF16), n_dp))
-    grad_in_weight = jnp.concatenate([gx, gg], axis=1).astype(F32)
+        return jnp.stack(in_group_order(blocks), axis=1)
+
+    own_in = jnp.concatenate(
+        [
+            jnp.stack(group_gather(wx_own.astype(BF16), n_dp)),
+            jnp.stack(group_gather(wg_own.astype(BF16), n_dp)),
+        ],
+        axis=2,
+    )
+    grad_in_weight, gain_sum = spread_columns(own_in, in_weight, cs)
     grad_out_weight = jnp.concatenate(in_group_order(group_gather(wo_own.astype(BF16), n_dp)), axis=0).astype(F32)
-    small_full = interleaved(group_gather(small_own, n_dp))
+    small_full = interleaved(group_gather(small_own, n_dp)).reshape(-1, n_dp * cs)
     out_small, at = [], 0
     for height, s in zip(heights, smalls):
         out_small.append(small_full[at : at + height].reshape(s.shape))
         at += height
-    grad_norm_gain = jnp.sum(grad_in_weight * in_weight.astype(F32), axis=1) / norm_gain.astype(F32)
+    grad_norm_gain = gain_sum / norm_gain.astype(F32)
 
     hat = x_all32[:tok] * rstd[:tok]
     hat_grad = normed_grad * gain[None]
     change = rstd[:tok] * (hat_grad - hat * jnp.mean(hat_grad * hat, axis=1, keepdims=True))
-    row_grad = (dy_own.astype(F32) + plain_columns(change)).astype(BF16)
+    row_grad = (dy_own.astype(F32) + change).astype(BF16)
     layer = (x_own32 + mixed).astype(BF16)
 
     def returned(value):
@@ -563,9 +824,18 @@
         back = lax.all_to_all(out, both, 0, 0, tiled=True).reshape(tok, cols)
         return flat_dot(from_send, back).astype(BF16)
 
-    ahead = returned(jnp.concatenate([layer, mixed.astype(BF16)], axis=1))
-    layer_output = ahead[:, :width]
-    mixer_output = ahead[:, width:]
+    lanes = lax.broadcasted_iota(jnp.int32, (tok, 128), 1)
+    ride = jnp.zeros((tok, 128), F32)
+    for j, value in enumerate(mine_sums):
+        high = value.astype(BF16).astype(F32)
+        ride = ride + jnp.where(lanes == 2 * j, high, 0.0) + jnp.where(lanes == 2 * j + 1, value - high, 0.0)
+    out = flat_dot(from_row, jnp.concatenate([layer, mixed.astype(BF16)], axis=1)).astype(BF16)
+    out = jnp.concatenate([out, ride.astype(BF16)], axis=1).reshape(rows, pair, 2 * width + 128)
+    back = lax.all_to_all(out, both, 0, 0, tiled=True).reshape(tok, 2 * width + 128)
+    totals = jnp.sum(back.reshape(rows, pair, -1)[:, 0, 2 * width : 2 * width + 4].astype(F32), axis=0)
+    input_rms = jnp.sqrt((totals[0] + totals[1]) / ((totals[2] + totals[3]) * width))
+    layer_output = flat_dot(from_send, back[:, :width]).astype(BF16)
+    mixer_output = flat_dot(from_send, back[:, width : 2 * width]).astype(BF16)
     input_grad = returned(row_grad)
     return (
         layer_output,

time: 976 us -> 814 us (0.83)
  Pallas kernels: 89.5 us -> 290 us
  local copies, waits for them, and re-layouts: 226 us -> 57.8 us
  waiting for transfers between devices: 229 us -> 156 us
  blocking collectives: 62.8 us -> 0 us
  starting transfers between devices: 116 us -> 65 us
    pallas_call x0 -> x3, Pallas kernels: none -> 200 us  [the longest x1 184 us: gather_all(): pl.pallas_call(functools.partial(gather_kernel, n_dp, n_f, downs), in_spe...]
    unnamed x324 -> x196, local copies, waits for them, and re-layouts: 131 us -> 15.8 us
    ppermute x56 -> x28, waiting for transfers between devices: 159 us -> 79.8 us  [ring_step(): return lax.ppermute(value, 'fsdp', pairs)]
    psum x1 -> x0, blocking collectives: 62.8 us -> none  [per_device(): lax.psum(jnp.stack([jnp.sum(square * valid), jnp.sum(valid)]), both)]
    ppermute x24 -> x20, waiting for transfers between devices: 54.6 us -> 76 us  [swap(): return lax.ppermute(value, 'dp', [(i, i ^ mask) for i in range(count)])]
    ppermute x56 -> x28, starting transfers between devices: 37.6 us -> 18.4 us  [ring_step(): return lax.ppermute(value, 'fsdp', pairs)]
    dynamic_slice x10 -> x1, local copies, waits for them, and re-layouts: 19.4 us -> 0.76 us  [in_group_order(): lax.dynamic_index_in_dim(stacked, me_d ^ i, 0, keepdims=False)]
    all_to_all x2 -> x1, waiting for transfers between devices: 15.8 us -> 0.01 us  [returned(): back = lax.all_to_all(out, both, 0, 0, tiled=True).reshape(tok, cols)]
  transfers between devices with their start and end apart: 84 -> 50, of which waited for: 31 -> 19; matrix products, arithmetic and copies ran while one was open for 34% -> 19% of each run, Pallas kernels for 0% -> 25%
where the time goes in v2:
time: 814 us; the launch traced here: 800 us
  Pallas kernels  290 us (36%)
  waiting for transfers between devices  156 us (19%)
  matrix products  106 us (13%)
  other arithmetic  89.3 us (11%)
  starting transfers between devices  65 us (8%)
  local copies, waits for them, and re-layouts  57.8 us (7%)
  between operations  36.6 us (4%)
    pallas_call x1, Pallas kernels, gather_all(): pl.pallas_call(functools.partial(gather_kernel, n_dp, n_f, downs), in_spe...  184 us
    ppermute x28, waiting for transfers between devices, ring_step(): return lax.ppermute(value, 'fsdp', pairs)  79.8 us
    ppermute x20, waiting for transfers between devices, swap(): return lax.ppermute(value, 'dp', [(i, i ^ mask) for i in range(count)])  76 us
    pallas_call x1, Pallas kernels, scan_backward(): pl.pallas_call(functools.partial(bwd_kernel, k, min(lanes, ch)), grid=(t...  62.4 us
    dot_general x12, matrix products, per_device(): flat_dot = lambda a, b: jnp.dot(a, b, preferred_element_type=F32)  46 us
    dot_general x5, matrix products, per_device(): lax.dot_general(a, b, (((1,), (1,)), ((), ())), preferred_element_type=F32)  39.5 us
    ppermute x20, starting transfers between devices, swap(): return lax.ppermute(value, 'dp', [(i, i ^ mask) for i in range(count)])  31.1 us
    pallas_call x1, Pallas kernels, scan_forward(): pl.pallas_call(functools.partial(fwd_kernel, k, min(lanes, ch)), grid=(t...  27.2 us
  transfers between devices with their start and end apart: 50, of which 19 were waited for; matrix products, arithmetic and copies ran while one was open for 19% of the time, Pallas kernels for 25%

profile of v2, /device:TPU:21, one launch (start us, length us, event | category | flops | bytes accessed | tf_op | source)
XLA Modules:
  0.0 800.3 jit_solution(16507790626062918713)
XLA Ops:
  24.5 183.6 %shard_map.267 = (bf16[4,256,2048]{2,1,0:T(8,128)(2,1)S(1)}, bf16[4,256,2048]{2,1,0:T(8,128)(2,1)S(1)}, bf16[256,2048]{1,0:T(8,128)(2,1)S(1)}, bf16[256,2048]{1,...) custom-call(bf16[32,16,2176]{2,1,0:T(8,128)(2,1)S(1)} %copy-done.6, ...), custom_call_target="tpu_custom_call" | custom-call | flops 10000000000 | bytes 200000000 | tf_op jit(solution)/shard_map/pallas_call | solution.py:491
  247.1 6.1 fusion.113
  253.2 6.0 fusion.114
  282.5 21.2 %multiply_reduce_fusion.1 = (f32[1024]{0:T(1024)}, f32[1024,1024]{1,0:T(8,128)}, bf16[1024,1024]{1,0:T(8,128)(2,1)S(1)}, f32[1024,1024]{1,0:T(8,128)}, f32[1024,1024]{1,0:T(8,128)}) fusion(f32[1024,1024]{1,0:T(8,128)} %fusion.114, f32[1024]{0:T(1024)S(1)} %fusion.60, f32[1021,1024]{1,0:T(8,128)} %bitcast.373, f32[1024]{0:T(1024)S(1)} %bitcast.420, ...), kind=kOutput, calls=%fused_computation.14 | convolution fusion | flops 4320132096 | bytes 44052480 | tf_op jit(solution)/shard_map/dot_general | solution.py:627
  313.3 6.1 collective-permute-done.3
  350.0 27.2 %shard_map.268 = (f32[1024,1024]{1,0:T(8,128)S(1)}, bf16[16384,1024]{1,0:T(8,128)(2,1)}) custom-call(f32[1024,1024]{1,0:T(8,128)S(1)} %get-tuple-element.191.delta_ref, bf16[1024,1024]{1,0:T(8,128)(2,1)S(1)} %get-tuple-element.63.act_ref, f32[1024,1]{1,0:T(8,128)S(1)} %broadcast_select_fusion.big_ref, f32[64,16,16]{2,1,0:T(8,128)S(1)} %bitcast.360, ...), custom_call_target="tpu_custom_call" | custom-call | flops 671088640 | bytes 46137344 | tf_op jit(solution)/shard_map/pallas_call | solution.py:77
  377.2 62.4 %shard_map.269 = (f32[1024,1024]{1,0:T(8,128)S(1)}, f32[1024,1024]{1,0:T(8,128)S(1)}, f32[16384,16]{1,0:T(8,128)}, f32[16384,16]{1,0:T(8,128)}, f32[16,1024]{1,0:T(8,128)S(1)}) custom-call(f32[1024,1024]{1,0:T(8,128)S(1)} %get-tuple-element.191.delta_ref, bf16[1024,1024]{1,0:T(8,128)(2,1)S(1)} %get-tuple-element.63.act_ref, ...), custom_call_target="tpu_custom_call" | custom-call | flops 1342177280 | bytes 62914560 | tf_op jit(solution)/shard_map/pallas_call | solution.py:174
  455.3 9.8 %convolution_convert_fusion.4 = bf16[1024,2048]{1,0:T(8,128)(2,1)} fusion(bf16[1024,1024]{1,0:T(8,128)(2,1)S(1)} %get-tuple-element.68, bf16[1024,2048]{1,0:T(8,128)(2,1)} %bitcast.445), kind=kOutput, calls=%fused_computation.33 | convolution fusion | flops 4297064448 | bytes 10485760 | tf_op jit(solution)/shard_map/dot_general | solution.py:626
  474.4 7.6 convolution_convert_fusion.2
  490.0 6.7 collective-permute-done.21
  506.2 6.9 fusion.97
  513.1 6.3 convolution_convert_fusion.3
  519.4 6.8 fusion.116
  527.6 9.8 %add_convert_fusion = bf16[1024,2048]{1,0:T(8,128)(2,1)S(1)} fusion(f32[1024,2048]{1,0:T(8,128)} %fusion.116, bf16[1024,1024]{1,0:T(8,128)(2,1)} %get-tuple-element.67, bf16[2048,1024]{1,0:T(8,128)(2,1)} %bitcast.442), kind=kOutput, calls=%fused_computation.9 | convolution fusion | flops 4299161600 | bytes 18874368 | tf_op jit(solution)/shard_map/dot_general | solution.py:627
  547.5 22.6 %collective-permute-done.31 = f32[320,128]{1,0:T(8,128)S(1)} collective-permute-done((f32[320,128]{1,0:T(8,128)S(1)}, f32[320,128]{1,0:T(8,128)S(1)}, u32[]{:S(2)}, u32[]{:S(2)}) %collective-permute-start.31) | collective-permute-done | bytes 163872 | tf_op jit(solution)/shard_map/ppermute | solution.py:230
  574.6 10.3 %collective-permute-done.32 = f32[320,128]{1,0:T(8,128)S(1)} collective-permute-done((f32[320,128]{1,0:T(8,128)S(1)}, f32[320,128]{1,0:T(8,128)S(1)}, u32[]{:S(2)}, u32[]{:S(2)}) %collective-permute-start.32) | collective-permute-done | bytes 163872 | tf_op jit(solution)/shard_map/ppermute | solution.py:230
  596.0 8.3 %collective-permute-done.23 = bf16[256,1024]{1,0:T(8,128)(2,1)S(1)} collective-permute-done((bf16[256,1024]{1,0:T(8,128)(2,1)S(1)}, bf16[256,1024]{1,0:T(8,128)(2,1)S(1)}, u32[]{:S(2)}, u32[]{:S(2)}) %collective-permute-start.23) | collective-permute-done | bytes 524320 | tf_op jit(solution)/shard_map/ppermute | solution.py:230
  617.6 9.2 %collective-permute-done.41 = bf16[128,2048]{1,0:T(8,128)(2,1)S(1)} collective-permute-done((bf16[128,2048]{1,0:T(8,128)(2,1)S(1)}, bf16[128,2048]{1,0:T(8,128)(2,1)S(1)}, u32[]{:S(2)}, u32[]{:S(2)}) %collective-permute-start.41) | collective-permute-done | bytes 524320 | tf_op jit(solution)/shard_map/ppermute | solution.py:230
  629.3 8.8 %collective-permute-done.24 = bf16[256,1024]{1,0:T(8,128)(2,1)S(1)} collective-permute-done((bf16[256,1024]{1,0:T(8,128)(2,1)S(1)}, bf16[256,1024]{1,0:T(8,128)(2,1)S(1)}, u32[]{:S(2)}, u32[]{:S(2)}) %collective-permute-start.24) | collective-permute-done | bytes 524320 | tf_op jit(solution)/shard_map/ppermute | solution.py:230
  653.9 30.4 %collective-permute-done.11 = bf16[1,256,2048]{2,1,0:T(8,128)(2,1)S(1)} collective-permute-done((bf16[1,256,2048]{2,1,0:T(8,128)(2,1)S(1)}, bf16[1,256,2048]{2,1,0:T(8,128)(2,1)S(1)}, u32[]{:S(2)}, u32[]{:S(2)}) %collective-permute-start.11) | collective-permute-done | bytes 1048608 | tf_op jit(solution)/shard_map/ppermute | solution.py:254
  696.7 14.5 %collective-permute-done.6 = bf16[1,256,2048]{2,1,0:T(8,128)(2,1)} collective-permute-done((bf16[1,256,2048]{2,1,0:T(8,128)(2,1)}, bf16[1,256,2048]{2,1,0:T(8,128)(2,1)}, u32[]{:S(2)}, u32[]{:S(2)}) %collective-permute-start.6) | collective-permute-done | bytes 1048608 | tf_op jit(solution)/shard_map/ppermute | solution.py:254
  721.4 11.8 %all-to-all-start = ((bf16[32,8,4224]{2,1,0:T(8,128)(2,1)}), bf16[32,8,4224]{2,1,0:T(8,128)(2,1)}, u32[]{:S(2)}, u32[]{:S(2)}) async-start(bf16[32,8,4224]{2,1,0:T(8,128)(2,1)} %maximum_bitcast_fusion), calls=%async_computation | async-start | bytes 4325376 | tf_op jit(solution)/shard_map/all_to_all | solution.py:834
  742.0 20.7 %collective-permute-done.19 = bf16[1,256,1024]{2,1,0:T(8,128)(2,1)S(1)} collective-permute-done((bf16[1,256,1024]{2,1,0:T(8,128)(2,1)S(1)}, bf16[1,256,1024]{2,1,0:T(8,128)(2,1)S(1)}, u32[]{:S(2)}, u32[]{:S(2)}) %collective-permute-start.19) | collective-permute-done | bytes 524320 | tf_op jit(solution)/shard_map/ppermute | solution.py:254
  773.4 12.5 %shard_map.270 = (f32[256,8192]{1,0:T(8,128)}, f32[256,128]{1,0:T(8,128)}) custom-call(bf16[4,256,2048]{2,1,0:T(8,128)(2,1)} %maximum_maximum_fusion.x_ref, bf16[256,8192]{1,0:T(8,128)(2,1)} %w_ref.3), custom_call_target="tpu_custom_call" | custom-call | flops 8388608 | bytes 16777216 | tf_op jit(solution)/shard_map/pallas_call | solution.py:571
  (472 shorter events, 248.3 us)
Async XLA Ops:
  1.5 265.6 %collective-permute-start = (s32[1,8,4]{1,2,0:T(4,128)S(1)}, s32[1,8,4]{1,2,0:T(4,128)S(1)}, u32[]{:S(2)}, u32[]{:S(2)}) collective-permute-start(s32[1,8,4]{1,2,0:T(4,128)S(1)} %stack_broadcast_in_dim.2), channel_id=1, source_target_pairs={{0,16},{8,24},{16,0},{24,8},{1,17},{9,25},{17,1},{25,9},{2,18},{10... | collective-permute-start | bytes 392 | tf_op jit(solution)/shard_map/ppermute | solution.py:254
  466.1 21.4 %collective-permute-start.42 = (bf16[128,2048]{1,0:T(8,128)(2,1)}, bf16[128,2048]{1,0:T(8,128)(2,1)}, u32[]{:S(2)}, u32[]{:S(2)}) collective-permute-start(bf16[128,2048]{1,0:T(8,128)(2,1)} %get-tuple-element.76), channel_id=1, source_target_pairs={{0,2},{2,4},{4,6},{6,7},{7,5},{5,3},{3,1},{1,0},{8,10},{10,12},{12... | collective-permute-start | bytes 1572872 | tf_op jit(solution)/shard_map/ppermute | solution.py:230
  466.1 78.2 %collective-permute-start.39 = (bf16[128,2048]{1,0:T(8,128)(2,1)}, bf16[128,2048]{1,0:T(8,128)(2,1)}, u32[]{:S(2)}, u32[]{:S(2)}) collective-permute-start(bf16[128,2048]{1,0:T(8,128)(2,1)} %get-tuple-element.75), channel_id=1, source_target_pairs={{0,1},{2,0},{4,2},{6,4},{7,6},{5,7},{3,5},{1,3},{8,9},{10,8},{12,1... | collective-permute-start | bytes 1572872 | tf_op jit(solution)/shard_map/ppermute | solution.py:230
  483.0 88.7 %collective-permute-start.25 = (bf16[256,1024]{1,0:T(8,128)(2,1)}, bf16[256,1024]{1,0:T(8,128)(2,1)}, u32[]{:S(2)}, u32[]{:S(2)}) collective-permute-start(bf16[256,1024]{1,0:T(8,128)(2,1)} %get-tuple-element.89), channel_id=1, source_target_pairs={{0,2},{2,4},{4,6},{6,7},{7,5},{5,3},{3,1},{1,0},{8,10},{10,12},{12... | collective-permute-start | bytes 1572872 | tf_op jit(solution)/shard_map/ppermute | solution.py:230
  489.8 54.9 %collective-permute-start.43 = (bf16[128,2048]{1,0:T(8,128)(2,1)}, bf16[128,2048]{1,0:T(8,128)(2,1)}, u32[]{:S(2)}, u32[]{:S(2)}) collective-permute-start(bf16[128,2048]{1,0:T(8,128)(2,1)} %add_convert_fusion.6), channel_id=1, source_target_pairs={{0,2},{2,4},{4,6},{6,7},{7,5},{5,3},{3,1},{1,0},{8,10},{10,12},{12... | collective-permute-start | bytes 1572872 | tf_op jit(solution)/shard_map/ppermute | solution.py:230
  543.1 29.4 %collective-permute-start.22 = (bf16[256,1024]{1,0:T(8,128)(2,1)S(1)}, bf16[256,1024]{1,0:T(8,128)(2,1)S(1)}, u32[]{:S(2)}, u32[]{:S(2)}) collective-permute-start(bf16[256,1024]{1,0:T(8,128)(2,1)S(1)} %copy-done.52), channel_id=1, source_target_pairs={{0,1},{2,0},{4,2},{6,4},{7,6},{5,7},{3,5},{1,3},{8,9},{10,8},{12,1... | collective-permute-start | bytes 1572872 | tf_op jit(solution)/shard_map/ppermute | solution.py:230
  544.3 45.2 %collective-permute-start.12 = (bf16[256,1024]{1,0:T(8,128)(2,1)S(1)}, bf16[256,1024]{1,0:T(8,128)(2,1)S(1)}, u32[]{:S(2)}, u32[]{:S(2)}) collective-permute-start(bf16[256,1024]{1,0:T(8,128)(2,1)S(1)} %get-tuple-element.82), channel_id=1, source_target_pairs={{0,1},{2,0},{4,2},{6,4},{7,6},{5,7},{3,5},{1,3},{8,9},{10,8},{12,1... | collective-permute-start | bytes 1572872 | tf_op jit(solution)/shard_map/ppermute | solution.py:230
  544.4 25.7 %collective-permute-start.31 = (f32[320,128]{1,0:T(8,128)S(1)}, f32[320,128]{1,0:T(8,128)S(1)}, u32[]{:S(2)}, u32[]{:S(2)}) collective-permute-start(f32[320,128]{1,0:T(8,128)S(1)} %get-tuple-element.100), channel_id=1, source_target_pairs={{0,1},{2,0},{4,2},{6,4},{7,6},{5,7},{3,5},{1,3},{8,9},{10,8},{12,1... | collective-permute-start | bytes 491528 | tf_op jit(solution)/shard_map/ppermute | solution.py:230
  544.7 26.2 %collective-permute-start.35 = (f32[320,128]{1,0:T(8,128)S(1)}, f32[320,128]{1,0:T(8,128)S(1)}, u32[]{:S(2)}, u32[]{:S(2)}) collective-permute-start(f32[320,128]{1,0:T(8,128)S(1)} %get-tuple-element.101), channel_id=1, source_target_pairs={{0,2},{2,4},{4,6},{6,7},{7,5},{5,3},{3,1},{1,0},{8,10},{10,12},{12... | collective-permute-start | bytes 491528 | tf_op jit(solution)/shard_map/ppermute | solution.py:230
  570.1 20.9 %collective-permute-start.40 = (bf16[128,2048]{1,0:T(8,128)(2,1)S(1)}, bf16[128,2048]{1,0:T(8,128)(2,1)S(1)}, u32[]{:S(2)}, u32[]{:S(2)}) collective-permute-start(bf16[128,2048]{1,0:T(8,128)(2,1)S(1)} %get-tuple-element.73), channel_id=1, source_target_pairs={{0,1},{2,0},{4,2},{6,4},{7,6},{5,7},{3,5},{1,3},{8,9},{10,8},{12,1... | collective-permute-start | bytes 1572872 | tf_op jit(solution)/shard_map/ppermute | solution.py:230
  584.9 26.7 %collective-permute-start.16 = (bf16[256,1024]{1,0:T(8,128)(2,1)S(1)}, bf16[256,1024]{1,0:T(8,128)(2,1)S(1)}, u32[]{:S(2)}, u32[]{:S(2)}) collective-permute-start(bf16[256,1024]{1,0:T(8,128)(2,1)S(1)} %get-tuple-element.83), channel_id=1, source_target_pairs={{0,2},{2,4},{4,6},{6,7},{7,5},{5,3},{3,1},{1,0},{8,10},{10,12},{12... | collective-permute-start | bytes 1572872 | tf_op jit(solution)/shard_map/ppermute | solution.py:230
  585.1 54.7 %collective-permute-start.10 = (bf16[2,256,2048]{2,1,0:T(8,128)(2,1)S(1)}, bf16[2,256,2048]{2,1,0:T(8,128)(2,1)S(1)}, u32[]{:S(2)}, u32[]{:S(2)}) collective-permute-start(bf16[2,256,2048]{2,1,0:T(8,128)(2,1)S(1)} %pad_maximum_fusion.1), channel_id=1, source_target_pairs={{0,8},{8,0},{16,24},{24,16},{1,9},{9,1},{17,25},{25,17},{2,10},{10... | collective-permute-start | bytes 6291464 | tf_op jit(solution)/shard_map/ppermute | solution.py:254
  604.3 37.2 %collective-permute-start.5 = (bf16[2,256,2048]{2,1,0:T(8,128)(2,1)S(1)}, bf16[2,256,2048]{2,1,0:T(8,128)(2,1)S(1)}, u32[]{:S(2)}, u32[]{:S(2)}) collective-permute-start(bf16[2,256,2048]{2,1,0:T(8,128)(2,1)S(1)} %copy-done.41), channel_id=1, source_target_pairs={{0,8},{8,0},{16,24},{24,16},{1,9},{9,1},{17,25},{25,17},{2,10},{10... | collective-permute-start | bytes 6291464 | tf_op jit(solution)/shard_map/ppermute | solution.py:254
  617.2 20.8 %collective-permute-start.24 = (bf16[256,1024]{1,0:T(8,128)(2,1)S(1)}, bf16[256,1024]{1,0:T(8,128)(2,1)S(1)}, u32[]{:S(2)}, u32[]{:S(2)}) collective-permute-start(bf16[256,1024]{1,0:T(8,128)(2,1)S(1)} %get-tuple-element.84), channel_id=1, source_target_pairs={{0,1},{2,0},{4,2},{6,4},{7,6},{5,7},{3,5},{1,3},{8,9},{10,8},{12,1... | collective-permute-start | bytes 1572872 | tf_op jit(solution)/shard_map/ppermute | solution.py:230
  639.8 96.2 %collective-permute-start.28 = (bf16[1,256,1024]{2,1,0:T(8,128)(2,1)S(1)}, bf16[1,256,1024]{2,1,0:T(8,128)(2,1)}, u32[]{:S(2)}, u32[]{:S(2)}) collective-permute-start(bf16[1,256,1024]{2,1,0:T(8,128)(2,1)S(1)} %fusion.26), channel_id=1, source_target_pairs={{0,16},{8,24},{16,0},{24,8},{1,17},{9,25},{17,1},{25,9},{2,18},{10... | collective-permute-start | bytes 1572872 | tf_op jit(solution)/shard_map/ppermute | solution.py:254
  641.6 42.8 %collective-permute-start.11 = (bf16[1,256,2048]{2,1,0:T(8,128)(2,1)S(1)}, bf16[1,256,2048]{2,1,0:T(8,128)(2,1)S(1)}, u32[]{:S(2)}, u32[]{:S(2)}) collective-permute-start(bf16[1,256,2048]{2,1,0:T(8,128)(2,1)S(1)} %fusion.19), channel_id=1, source_target_pairs={{0,16},{8,24},{16,0},{24,8},{1,17},{9,25},{17,1},{25,9},{2,18},{10... | collective-permute-start | bytes 3145736 | tf_op jit(solution)/shard_map/ppermute | solution.py:254
  649.3 61.9 %collective-permute-start.6 = (bf16[1,256,2048]{2,1,0:T(8,128)(2,1)}, bf16[1,256,2048]{2,1,0:T(8,128)(2,1)}, u32[]{:S(2)}, u32[]{:S(2)}) collective-permute-start(bf16[1,256,2048]{2,1,0:T(8,128)(2,1)} %fusion.18), channel_id=1, source_target_pairs={{0,16},{8,24},{16,0},{24,8},{1,17},{9,25},{17,1},{25,9},{2,18},{10... | collective-permute-start | bytes 3145736 | tf_op jit(solution)/shard_map/ppermute | solution.py:254
  651.1 82.1 %collective-permute-start.15 = (bf16[256,1024]{1,0:T(8,128)(2,1)}, bf16[256,1024]{1,0:T(8,128)(2,1)}, u32[]{:S(2)}, u32[]{:S(2)}) collective-permute-start(bf16[256,1024]{1,0:T(8,128)(2,1)} %get-tuple-element.78), channel_id=1, source_target_pairs={{0,1},{2,0},{4,2},{6,4},{7,6},{5,7},{3,5},{1,3},{8,9},{10,8},{12,1... | collective-permute-start | bytes 1572872 | tf_op jit(solution)/shard_map/ppermute | solution.py:230
  651.3 81.9 %collective-permute-start.18 = (bf16[256,1024]{1,0:T(8,128)(2,1)}, bf16[256,1024]{1,0:T(8,128)(2,1)}, u32[]{:S(2)}, u32[]{:S(2)}) collective-permute-start(bf16[256,1024]{1,0:T(8,128)(2,1)} %get-tuple-element.79), channel_id=1, source_target_pairs={{0,2},{2,4},{4,6},{6,7},{7,5},{5,3},{3,1},{1,0},{8,10},{10,12},{12... | collective-permute-start | bytes 1572872 | tf_op jit(solution)/shard_map/ppermute | solution.py:230
  684.3 81.1 %collective-permute-start.47 = (bf16[2,128,2048]{2,1,0:T(8,128)(2,1)}, bf16[2,128,2048]{2,1,0:T(8,128)(2,1)}, u32[]{:S(2)}, u32[]{:S(2)}) collective-permute-start(bf16[2,128,2048]{2,1,0:T(8,128)(2,1)} %pad_maximum_fusion.5), channel_id=1, source_target_pairs={{0,8},{8,0},{16,24},{24,16},{1,9},{9,1},{17,25},{25,17},{2,10},{10... | collective-permute-start | bytes 3145736 | tf_op jit(solution)/shard_map/ppermute | solution.py:254
  693.0 28.4 %all-to-all-start.1 = ((bf16[32,8,2048]{2,1,0:T(8,128)(2,1)}), bf16[32,8,2048]{2,1,0:T(8,128)(2,1)S(1)}, u32[]{:S(2)}, u32[]{:S(2)}) async-start(bf16[32,8,2048]{2,1,0:T(8,128)(2,1)} %fusion.7), calls=%async_computation.1 | async-start | bytes 2097152 | tf_op jit(solution)/shard_map/all_to_all | solution.py:824
  721.4 67.6 %all-to-all-start = ((bf16[32,8,4224]{2,1,0:T(8,128)(2,1)}), bf16[32,8,4224]{2,1,0:T(8,128)(2,1)}, u32[]{:S(2)}, u32[]{:S(2)}) async-start(bf16[32,8,4224]{2,1,0:T(8,128)(2,1)} %maximum_bitcast_fusion), calls=%async_computation | async-start | bytes 4325376 | tf_op jit(solution)/shard_map/all_to_all | solution.py:834
  734.8 27.8 %collective-permute-start.19 = (bf16[1,256,1024]{2,1,0:T(8,128)(2,1)S(1)}, bf16[1,256,1024]{2,1,0:T(8,128)(2,1)S(1)}, u32[]{:S(2)}, u32[]{:S(2)}) collective-permute-start(bf16[1,256,1024]{2,1,0:T(8,128)(2,1)S(1)} %fusion.25), channel_id=1, source_target_pairs={{0,16},{8,24},{16,0},{24,8},{1,17},{9,25},{17,1},{25,9},{2,18},{10... | collective-permute-start | bytes 1572872 | tf_op jit(solution)/shard_map/ppermute | solution.py:254
  737.2 29.4 %collective-permute-start.29 = (bf16[2,256,1024]{2,1,0:T(8,128)(2,1)S(1)}, bf16[2,256,1024]{2,1,0:T(8,128)(2,1)S(1)}, u32[]{:S(2)}, u32[]{:S(2)}) collective-permute-start(bf16[2,256,1024]{2,1,0:T(8,128)(2,1)S(1)} %pad_maximum_fusion.4), channel_id=1, source_target_pairs={{0,8},{8,0},{16,24},{24,16},{1,9},{9,1},{17,25},{25,17},{2,10},{10... | collective-permute-start | bytes 3145736 | tf_op jit(solution)/shard_map/ppermute | solution.py:254
  (121 other events, 1892.7 us)

commit v3 on v2

--- a/solution.py
+++ b/solution.py
@@ -21,110 +21,481 @@
     return sigma * (1.0 + value * (1.0 - sigma))
 
 
-def fwd_kernel(chunks, lanes, delta_ref, act_ref, big_ref, bt_ref, cw_ref, rate_ref, skip_ref,
-               y_ref, s_ref, carry, d_s, u_s, sc):
+def row_at(g, n_dp):
+    return lax.rem(2 * g + 1, n_dp + 1)
+
+
+def flip(d, mask):
+    return d + mask - 2 * mask * lax.rem(d // mask, 2)
+
+
+class GroupSum:
+    def __init__(self, part, near, far, total, send, recv):
+        self.part, self.near, self.far, self.total = part, near, far, total
+        me_d, me_f = lax.axis_index("dp"), lax.axis_index("fsdp")
+        plan = [
+            (part.at[1], near.at[0], 1),
+            (part.at[3], near.at[1], 1),
+            (part.at[0], far.at[1], 2),
+            (part.at[2], far.at[0], 2),
+            (total.at[0], total.at[1], 1),
+            (total.at[2], total.at[3], 1),
+        ]
+        self.copies = [
+            pltpu.make_async_remote_copy(
+                src_ref=src,
+                dst_ref=dst,
+                send_sem=send.at[i],
+                recv_sem=recv.at[i],
+                device_id=(flip(me_d, mask), me_f),
+                device_id_type=pl.DeviceIdType.MESH,
+            )
+            for i, (src, dst, mask) in enumerate(plan)
+        ]
+
+    def row_done(self, g):
+        for j in (0, 1):
+
+            @pl.when(g == j)
+            def _(j=j):
+                self.copies[j].start()
+
+            @pl.when(g == j + 2)
+            def _(j=j):
+                self.copies[j].wait_recv()
+                self.part[2 * j] = self.part[2 * j] + self.near[j]
+                self.copies[j + 2].start()
+
+    def first(self):
+        for j in (0, 1):
+            self.copies[j].start()
+
+    def second(self):
+        for j in (0, 1):
+            self.copies[j].wait_recv()
+            self.part[2 * j] = self.part[2 * j] + self.near[j]
+            self.copies[j + 2].start()
+
+    def finish(self):
+        for j in (0, 1):
+            self.copies[3 - j].wait_recv()
+            self.total[2 * j] = self.part[2 * j] + self.far[j]
+            self.copies[4 + j].start()
+        for j in (0, 1):
+            self.copies[4 + j].wait_recv()
+        for c in self.copies:
+            c.wait_send()
+
+    @staticmethod
+    def scratch(tok, wide):
+        return [
+            pltpu.VMEM((4, tok, wide), F32),
+            pltpu.VMEM((2, tok, wide), F32),
+            pltpu.VMEM((2, tok, wide), F32),
+            pltpu.VMEM((4, tok, wide), F32),
+            pltpu.SemaphoreType.DMA((6,)),
+            pltpu.SemaphoreType.DMA((6,)),
+        ]
+
+
+def greet_neighbours(n_f, ring):
+    me_d, me_f = lax.axis_index("dp"), lax.axis_index("fsdp")
+    barrier = pltpu.get_barrier_semaphore()
+    others = [(flip(me_d, 1), me_f), (flip(me_d, 2), me_f)]
+    if ring:
+        q = ring_place(me_f, n_f)
+        others.append((me_d, ring_index(lax.rem(q + n_f - 1, n_f), n_f)))
+        others.append((me_d, ring_index(lax.rem(q + 1, n_f), n_f)))
+    for other in others:
+        pl.semaphore_signal(barrier, inc=1, device_id=other, device_id_type=pl.DeviceIdType.MESH)
+    pl.semaphore_wait(barrier, len(others))
+
+
+def ring_copy(n_f, src, dst, send, recv, up):
+    me_d, me_f = lax.axis_index("dp"), lax.axis_index("fsdp")
+    q = ring_place(me_f, n_f)
+    to = ring_index(lax.rem(q + (1 if up else n_f - 1), n_f), n_f)
+    return pltpu.make_async_remote_copy(
+        src_ref=src,
+        dst_ref=dst,
+        send_sem=send,
+        recv_sem=recv,
+        device_id=(me_d, to),
+        device_id_type=pl.DeviceIdType.MESH,
+    )
+
+
+def segment_span(lens_ref, m, first, rows):
+    t = lax.broadcasted_iota(jnp.int32, (rows, 1), 0) + first
+    begin = jnp.zeros((rows, 1), jnp.int32)
+    end = jnp.zeros((rows, 1), jnp.int32)
+    total = jnp.int32(0)
+    for j in range(lens_ref.shape[1]):
+        after = total + lens_ref[m, j]
+        inside = t >= total
+        begin = jnp.where(inside, total, begin)
+        end = jnp.where(inside, after, end)
+        total = after
+    return t - begin, end - 1 - t
+
+
+def enter_kernel(n_f, half, lens_ref, x_ref, gain_ref, wx_ref, wg_ref, taps_ref, bias_ref, sel_ref, wo_ref,
+                 normed_ref, xin_ref, conv_ref, act_ref, gate_ref, dbl_ref, next_ref,
+                 part, near, far, total, gs_send, gs_recv, hop_send, hop_recv):
+    g = pl.program_id(0)
+    n_dp, tok = part.shape[:2]
+    rows, width = x_ref.shape
+    hops = [ring_copy(n_f, wo_ref, next_ref.at[up], hop_send.at[up], hop_recv.at[up], up) for up in (0, 1)]
+    group = GroupSum(part, near, far, total, gs_send, gs_recv)
+    piece = 256
+
+    @pl.when(g == 0)
+    def _():
+        greet_neighbours(n_f, True)
+        for c in hops:
+            c.start()
+        part[...] = jnp.zeros_like(part)
+
+        def norm(i, _):
+            at = pl.ds(pl.multiple_of(i * 32, 32), 32)
+            v = x_ref[at, :].astype(F32)
+            rstd = lax.rsqrt(jnp.mean(v * v, axis=1, keepdims=True) + EPS)
+            normed_ref[at, :] = (v * rstd * gain_ref[...]).astype(BF16)
+            return 0
+
+        lax.fori_loop(0, rows // 32, norm, 0)
+
+    @pl.when(g < half)
+    def _():
+        n_taps = taps_ref.shape[0]
+        for m in range(n_dp):
+            at = slice(m * tok, (m + 1) * tok)
+            v = jnp.dot(normed_ref[at, :], wx_ref[...], preferred_element_type=F32)
+            since, _ = segment_span(lens_ref, m, 0, tok)
+            xin_ref[at, :] = v
+            conv = bias_ref[...] + taps_ref[n_taps - 1 : n_taps, :] * v
+            for lag in range(1, n_taps):
+                keep = (since >= lag).astype(F32)
+                conv = conv + taps_ref[n_taps - 1 - lag : n_taps - lag, :] * (pltpu.roll(v, lag, 0) * keep)
+            conv_ref[at, :] = conv
+            act = jax.nn.silu(conv).astype(BF16)
+            act_ref[at, :] = act
+            part[m] += lax.dot_general(act, sel_ref[...], (((1,), (1,)), ((), ())), preferred_element_type=F32)
+
+    @pl.when(g == half - 1)
+    def _():
+        group.first()
+
+    @pl.when(g >= half)
+    def _():
+        for m in range(n_dp):
+            at = slice(m * tok, (m + 1) * tok)
+            gate_ref[at, :] = jnp.dot(normed_ref[at, :], wg_ref[...], preferred_element_type=F32)
+
+    @pl.when(g == half)
+    def _():
+        group.second()
+
+    @pl.when(g == 2 * half - 1)
+    def _():
+        group.finish()
+        dbl_ref[...] = total[...]
+        for c in hops:
+            c.wait()
+
+
+def enter(lens, x_all, gain, wx, wg, taps, bias, sel, wo_block, n_f):
+    n_dp = lens.shape[0]
+    rows, width = x_all.shape
+    tok = rows // n_dp
+    ch = wx.shape[1]
+    wide = sel.shape[0]
+    piece = 256
+    half = ch // piece
+    whole = lambda g: (0, 0)
+    early = lambda g: (0, jnp.minimum(g, half - 1))
+    late = lambda g: (0, jnp.maximum(g - half, 0))
+    once = pl.Buffered(1)
+    any_ = pl.BlockSpec(memory_space=pl.ANY)
+    shaped = lambda d, t: jax.ShapeDtypeStruct((rows, d), t)
+    return pl.pallas_call(
+        functools.partial(enter_kernel, n_f, half),
+        grid=(2 * half,),
+        in_specs=[
+            pl.BlockSpec(memory_space=pltpu.SMEM),
+            pl.BlockSpec((rows, width), whole, pipeline_mode=once),
+            pl.BlockSpec((1, width), whole),
+            pl.BlockSpec((width, piece), early),
+            pl.BlockSpec((width, piece), late),
+            pl.BlockSpec((taps.shape[0], piece), early),
+            pl.BlockSpec((1, piece), early),
+            pl.BlockSpec((wide, piece), early),
+            any_,
+        ],
+        out_specs=[
+            pl.BlockSpec((rows, width), whole),
+            pl.BlockSpec((rows, piece), early),
+            pl.BlockSpec((rows, piece), early),
+            pl.BlockSpec((rows, piece), early),
+            pl.BlockSpec((rows, piece), late),
+            pl.BlockSpec((n_dp, tok, wide), lambda g: (0, 0, 0)),
+            any_,
+        ],
+        out_shape=[
+            shaped(width, BF16),
+            shaped(ch, F32),
+            shaped(ch, F32),
+            shaped(ch, BF16),
+            shaped(ch, F32),
+            jax.ShapeDtypeStruct((n_dp, tok, wide), F32),
+            jax.ShapeDtypeStruct((2,) + wo_block.shape, BF16),
+        ],
+        scratch_shapes=GroupSum.scratch(tok, wide)
+        + [pltpu.SemaphoreType.DMA((2,)), pltpu.SemaphoreType.DMA((2,))],
+        compiler_params=pltpu.CompilerParams(
+            collective_id=1, has_side_effects=True, vmem_limit_bytes=48 * 2**20
+        ),
+        cost_estimate=pl.CostEstimate(flops=10**10, bytes_accessed=4 * 10**7, transcendentals=10**6),
+    )(lens, x_all, gain, wx, wg, taps, bias, sel, wo_block)
+
+
+def fold_matrix(n):
+    i = lax.broadcasted_iota(jnp.int32, (n, TB * n), 0)
+    j = lax.broadcasted_iota(jnp.int32, (n, TB * n), 1)
+    return jnp.where(lax.rem(j, n) == i, 1.0, 0.0)
+
+
+def own_token(n):
+    i = lax.broadcasted_iota(jnp.int32, (TB, TB * n), 0)
+    j = lax.broadcasted_iota(jnp.int32, (TB, TB * n), 1)
+    return i == j // n
+
+
+def block_rows(m, n):
+    spread = jnp.dot(m.astype(BF16), fold_matrix(n).astype(BF16), preferred_element_type=F32)
+    i = lax.broadcasted_iota(jnp.int32, spread.shape, 0)
+    j = lax.broadcasted_iota(jnp.int32, spread.shape, 1)
+    return jnp.where(lax.rem(i, TB) == j // n, spread, 0.0).astype(BF16)
+
+
+def columns_of(m):
+    n = m.shape[1]
+    i = lax.broadcasted_iota(jnp.int32, (n, n), 0)
+    j = lax.broadcasted_iota(jnp.int32, (n, n), 1)
+    eye = jnp.where(i == j, 1.0, 0.0)
+    return jnp.sum(m[:, None, :] * eye[None], axis=2, keepdims=True)
+
+
+def softplus(v):
+    return jnp.maximum(v, 0.0) + jnp.log1p(jnp.exp(-jnp.abs(v)))
+
+
+class RingGather:
+    def __init__(self, n_f, mine, near, out, local, send, recv):
+        q = ring_place(lax.axis_index("fsdp"), n_f)
+        at = lambda k: ring_index(lax.rem(q + k, n_f), n_f)
+        count = [n_f // 2, n_f - 1 - n_f // 2]
+        self.locals = [
+            pltpu.make_async_copy(mine, out.at[at(0)], local.at[0]),
+            pltpu.make_async_copy(near.at[0], out.at[at(1)], local.at[1]),
+            pltpu.make_async_copy(near.at[1], out.at[at(n_f - 1)], local.at[2]),
+        ]
+        self.hops = [[], []]
+        for up in (0, 1):
+            for h in range(1, count[up]):
+                index = at(n_f - h if up else h)
+                src = near.at[up] if h == 1 else out.at[index]
+                self.hops[up].append(
+                    ring_copy(n_f, src, out.at[index], send.at[up, h], recv.at[up, h], up)
+                )
+        self.events = max(len(h) for h in self.hops)
+
+    def start(self):
+        for c in self.locals:
+            c.start()
+        for up in (0, 1):
+            if self.hops[up]:
+                self.hops[up][0].start()
+
+    def event(self, e):
+        for up in (0, 1):
+            if e < len(self.hops[up]):
+                self.hops[up][e - 1].wait_recv()
+                self.hops[up][e].start()
+
+    def finish(self):
+        for up in (0, 1):
+            if self.hops[up]:
+                self.hops[up][-1].wait_recv()
+            for c in self.hops[up]:
+                c.wait_send()
+        for c in self.locals:
+            c.wait()
+
+
+def fwd_kernel(lanes, n_f, lens_ref, dbl_ref, act_ref, stepw_ref, stepb_ref, rate_ref, skip_ref, wo_ref, next_ref,
+               y_ref, s_ref, delta_ref, pre_ref, wo_all, carry, big_s, cw_s, d_s, u_s, sc, local, hop_send, hop_recv):
     n, ch = rate_ref.shape
+    tblk = act_ref.shape[0]
+    low_n = stepw_ref.shape[0]
+    steps = pl.num_programs(0) * pl.num_programs(1)
+    now = pl.program_id(0) * pl.num_programs(1) + pl.program_id(1)
+    ring = RingGather(n_f, wo_ref, next_ref, wo_all, local, hop_send, hop_recv)
+
+    @pl.when(now == 0)
+    def _():
+        greet_neighbours(n_f, True)
+        ring.start()
+
+    for e in range(1, ring.events):
+
+        @pl.when(now == min(7 * e, 15))
+        def _(e=e):
+            ring.event(e)
 
     @pl.when(pl.program_id(1) == 0)
     def _():
         carry[...] = jnp.zeros_like(carry)
+
+    pre = jnp.dot(dbl_ref[:, :low_n].astype(BF16), stepw_ref[...], preferred_element_type=F32) + stepb_ref[...]
+    pre_ref[...] = pre
+    delta_ref[...] = softplus(pre)
+    since, _ = segment_span(lens_ref, pl.program_id(0), pl.program_id(1) * tblk, tblk)
+    big_s[...] = jnp.where(since == 0, RESET, 0.0)
+    cw_s[...] = block_rows(dbl_ref[:, low_n + n : low_n + 2 * n], n)
 
     def chunk(i, _):
         base = pl.multiple_of(i * TB, TB)
         dl = delta_ref[pl.ds(base, TB), :]
         ac = act_ref[pl.ds(base, TB), :].astype(F32)
-        d_s[...] = dl + big_ref[pl.ds(base, TB), :]
+        d_s[...] = dl + big_s[pl.ds(base, TB), :]
         u_s[...] = dl * ac
-        bt = bt_ref[i]
+        bt = columns_of(dbl_ref[pl.ds(base, TB), low_n : low_n + n])
         for lo in range(0, ch, lanes):
             cs = pl.ds(lo, lanes)
             rate = rate_ref[:, cs]
             s = carry[:, cs]
             for t in range(TB):
                 dec = jnp.exp2(d_s[t : t + 1, cs] * rate)
-                s = dec * s + bt[:, t : t + 1] * u_s[t : t + 1, cs]
+                s = dec * s + bt[t] * u_s[t : t + 1, cs]
                 sc[t * n : (t + 1) * n, cs] = s.astype(BF16)
             carry[:, cs] = s
         states = sc[...]
-        y = jnp.dot(cw_ref[i], states, preferred_element_type=F32)
+        y = jnp.dot(cw_s[pl.ds(base, TB), :], states, preferred_element_type=F32)
         y_ref[pl.ds(base, TB), :] = y + skip_ref[...] * ac
         s_ref[pl.ds(pl.multiple_of(base * n, TB * n), TB * n), :] = states
         return 0
 
-    lax.fori_loop(0, chunks, chunk, 0)
-
-
-def block_coef(m):
-    t, n = m.shape
-    eye = jnp.eye(TB, dtype=m.dtype)
-    spread = m.reshape(t // TB, TB, 1, n) * eye[None, :, :, None]
-    return spread.reshape(t // TB, TB, TB * n).astype(BF16)
-
-
-def turned(m):
-    t, n = m.shape
-    return m.reshape(t // TB, TB, n).transpose(0, 2, 1)
-
-
-def scan_forward(delta, act, big, bmat, cmat, rate2, skip, row_len, tblk=64, lanes=512):
-    t, ch = delta.shape
-    n = bmat.shape[1]
+    lax.fori_loop(0, tblk // TB, chunk, 0)
+
+    @pl.when(now == steps - 1)
+    def _():
+        ring.finish()
+
+
+def scan_forward(lens, dbl, act, stepw, stepb, rate2, skip, wo_block, wo_next, n_f, row_len, tblk=64, lanes=512):
+    t, ch = act.shape
+    n = rate2.shape[0]
     nb = row_len // tblk
-    k = tblk // TB
     at = lambda r, j: (r * nb + j, 0)
-    at3 = lambda r, j: (r * nb + j, 0, 0)
     zero = lambda r, j: (0, 0)
+    any_ = pl.BlockSpec(memory_space=pl.ANY)
+    wide = jax.ShapeDtypeStruct((t, ch), F32)
     return pl.pallas_call(
-        functools.partial(fwd_kernel, k, min(lanes, ch)),
+        functools.partial(fwd_kernel, min(lanes, ch), n_f),
         grid=(t // row_len, nb),
         in_specs=[
+            pl.BlockSpec(memory_space=pltpu.SMEM),
+            pl.BlockSpec((tblk, dbl.shape[1]), at),
+            pl.BlockSpec((tblk, ch), at),
+            pl.BlockSpec(stepw.shape, zero),
+            pl.BlockSpec((1, ch), zero),
+            pl.BlockSpec((n, ch), zero),
+            pl.BlockSpec((1, ch), zero),
+            any_,
+            any_,
+        ],
+        out_specs=[
+            pl.BlockSpec((tblk, ch), at),
+            pl.BlockSpec((tblk * n, ch), at),
             pl.BlockSpec((tblk, ch), at),
             pl.BlockSpec((tblk, ch), at),
-            pl.BlockSpec((tblk, 1), at),
-            pl.BlockSpec((k, n, TB), at3),
-            pl.BlockSpec((k, TB, TB * n), at3),
-            pl.BlockSpec((n, ch), zero),
-            pl.BlockSpec((1, ch), zero),
-        ],
-        out_specs=[pl.BlockSpec((tblk, ch), at), pl.BlockSpec((tblk * n, ch), at)],
-        out_shape=[jax.ShapeDtypeStruct((t, ch), F32), jax.ShapeDtypeStruct((t * n, ch), BF16)],
+            any_,
+        ],
+        out_shape=[
+            wide,
+            jax.ShapeDtypeStruct((t * n, ch), BF16),
+            wide,
+            wide,
+            jax.ShapeDtypeStruct((n_f,) + wo_block.shape, BF16),
+        ],
         scratch_shapes=[
             pltpu.VMEM((n, ch), F32),
+            pltpu.VMEM((tblk, 1), F32),
+            pltpu.VMEM((tblk, TB * n), BF16),
             pltpu.VMEM((TB, ch), F32),
             pltpu.VMEM((TB, ch), F32),
             pltpu.VMEM((TB * n, ch), BF16),
-        ],
-        compiler_params=pltpu.CompilerParams(vmem_limit_bytes=24 * 2**20),
-        cost_estimate=pl.CostEstimate(flops=t * n * ch * 40, bytes_accessed=t * ch * 44, transcendentals=t * n * ch),
-    )(delta, act, big, turned(bmat), block_coef(cmat), rate2, skip)
-
-
-def bwd_kernel(chunks, lanes, delta_ref, act_ref, big_ref, gy_ref, ct_ref, bw_ref, rate_ref, s_ref, sp_ref,
-               dd_ref, da_ref, db_ref, dc_ref, dl_ref, carry, d_s, u_s, g_s, h_s):
+            pltpu.SemaphoreType.DMA((3,)),
+            pltpu.SemaphoreType.DMA((2, n_f)),
+            pltpu.SemaphoreType.DMA((2, n_f)),
+        ],
+        compiler_params=pltpu.CompilerParams(
+            collective_id=2, has_side_effects=True, vmem_limit_bytes=32 * 2**20
+        ),
+        cost_estimate=pl.CostEstimate(flops=t * n * ch * 40, bytes_accessed=t * ch * 52, transcendentals=t * n * ch),
+    )(lens, dbl, act, stepw, stepb, rate2, skip, wo_block, wo_next)
+
+
+def bwd_kernel(lanes, n_f, lens_ref, dbl_ref, delta_ref, pre_ref, act_ref, gy_ref, stepw_ref, rate_ref, skip_ref,
+               s_ref, sp_ref,
+               pg_ref, da_ref, dbl_grad_ref, dl_ref, sums_ref, stepg_ref,
+               carry, big_s, bw_s, d_s, u_s, g_s, h_s, part, near, far, total, gs_send, gs_recv):
     n, ch = rate_ref.shape
-
-    @pl.when(pl.program_id(1) == 0)
+    tblk = act_ref.shape[0]
+    low_n = stepw_ref.shape[0]
+    r, j = pl.program_id(0), pl.program_id(1)
+    n_dp, nb = pl.num_programs(0), pl.num_programs(1)
+    m = row_at(r, n_dp)
+    group = GroupSum(part, near, far, total, gs_send, gs_recv)
+
+    @pl.when(j == 0)
     def _():
         carry[...] = jnp.zeros_like(carry)
 
-    @pl.when((pl.program_id(0) == 0) & (pl.program_id(1) == 0))
-    def _():
+    @pl.when((r == 0) & (j == 0))
+    def _():
+        greet_neighbours(n_f, False)
         dl_ref[...] = jnp.zeros_like(dl_ref)
-
-    row = lax.broadcasted_iota(jnp.int32, (TB, TB * n), 0)
-    col = lax.broadcasted_iota(jnp.int32, (TB, TB * n), 1)
-    ones = jnp.where(row == col // n, 1.0, 0.0).astype(BF16)
+        sums_ref[...] = jnp.zeros_like(sums_ref)
+        stepg_ref[...] = jnp.zeros_like(stepg_ref)
+
+    ones = jnp.where(own_token(n), 1.0, 0.0).astype(BF16)
     nt = (((1,), (1,)), ((), ()))
+    row = lax.broadcasted_iota(jnp.int32, (TB * n, TB), 0)
+    col = lax.broadcasted_iota(jnp.int32, (TB * n, TB), 1)
+    mask = row // n == col
+    row = lax.broadcasted_iota(jnp.int32, (TB * n, n), 0)
+    col = lax.broadcasted_iota(jnp.int32, (TB * n, n), 1)
+    fold = jnp.where(lax.rem(row, n) == col, 1.0, 0.0)
+    since, _ = segment_span(lens_ref, m, (nb - 1 - j) * tblk, tblk)
+    big_s[...] = jnp.where(since == 0, RESET, 0.0)
+    bw_s[...] = block_rows(dbl_ref[:, low_n : low_n + n], n)
+
+    def diagonal(left, right):
+        every = lax.dot_general(left, right, nt, preferred_element_type=F32)
+        column = jnp.sum(jnp.where(mask, every, 0.0), axis=1, keepdims=True)
+        return jnp.sum((column * fold).reshape(TB, n, n), axis=1)
 
     def chunk(back, _):
-        i = chunks - 1 - back
+        i = tblk // TB - 1 - back
         base = pl.multiple_of(i * TB, TB)
         sbase = pl.multiple_of(i * TB * n, TB * n)
         dl = delta_ref[pl.ds(base, TB), :]
         ac = act_ref[pl.ds(base, TB), :].astype(F32)
-        d_s[...] = dl + big_ref[pl.ds(base, TB), :]
+        d_s[...] = dl + big_s[pl.ds(base, TB), :]
         u_s[...] = dl * ac
-        ct = ct_ref[i]
+        ct = columns_of(dbl_ref[pl.ds(base, TB), low_n + n : low_n + 2 * n])
         before = pl.multiple_of(jnp.maximum(sbase - n, 0), n)
         for lo in range(0, ch, lanes):
             cs = pl.ds(lo, lanes)
@@ -134,7 +505,7 @@
             for t in reversed(range(TB)):
                 dr = d_s[t : t + 1, cs]
                 dec = jnp.exp2(dr * rate)
-                g = ct[:, t : t + 1] * gy_ref[pl.ds(base + t, 1), cs] + flow
+                g = ct[t] * gy_ref[pl.ds(base + t, 1), cs] + flow
                 flow = dec * g
                 if t > 0:
                     prev = s_ref[pl.ds(sbase + (t - 1) * n, n), cs]
@@ -147,74 +518,95 @@
             carry[:, cs] = flow
             dl_ref[:, cs] = acc
         gb = g_s[...]
-        du = jnp.dot(bw_ref[i], gb, preferred_element_type=F32)
+        gy = gy_ref[pl.ds(base, TB), :]
+        du = jnp.dot(bw_s[pl.ds(base, TB), :], gb, preferred_element_type=F32)
         hr = jnp.dot(ones, h_s[...], preferred_element_type=F32)
-        dd_ref[pl.ds(base, TB), :] = hr * (1.0 / LOG2E) + du * ac
-        da_ref[pl.ds(base, TB), :] = du * dl
-        db_ref[pl.ds(sbase, TB * n), :] = lax.dot_general(
-            gb, u_s[...].astype(BF16), nt, preferred_element_type=F32
-        )
-        dc_ref[pl.ds(sbase, TB * n), :] = lax.dot_general(
-            s_ref[pl.ds(sbase, TB * n), :], gy_ref[pl.ds(base, TB), :].astype(BF16), nt, preferred_element_type=F32
-        )
+        dd = hr * (1.0 / LOG2E) + du * ac
+        pg_ref[pl.ds(base, TB), :] = (dd * jax.nn.sigmoid(pre_ref[pl.ds(base, TB), :])).astype(BF16)
+        da_ref[pl.ds(base, TB), :] = du * dl + skip_ref[...] * gy
+        at = pl.ds(pl.multiple_of((nb - 1 - j) * tblk + base, TB), TB)
+        part[m, at, low_n : low_n + n] = diagonal(gb, u_s[...].astype(BF16))
+        part[m, at, low_n + n : low_n + 2 * n] = diagonal(s_ref[pl.ds(sbase, TB * n), :], gy.astype(BF16))
         return 0
 
-    lax.fori_loop(0, chunks, chunk, 0)
-
-
-def scan_backward(delta, act, big, gy, bmat, cmat, rate2, states, row_len, tblk=64, lanes=512):
+    lax.fori_loop(0, tblk // TB, chunk, 0)
+    pg = pg_ref[...]
+    part[m, pl.ds(pl.multiple_of((nb - 1 - j) * tblk, tblk), tblk), :low_n] = lax.dot_general(
+        pg, stepw_ref[...], nt, preferred_element_type=F32
+    )
+    stepg_ref[...] += lax.dot_general(
+        dbl_ref[:, :low_n].astype(BF16), pg, (((0,), (0,)), ((), ())), preferred_element_type=F32
+    )
+    sums_ref[0:1, :] += jnp.sum(pg.astype(F32), axis=0, keepdims=True)
+    sums_ref[1:2, :] += jnp.sum(gy_ref[...] * act_ref[...].astype(F32), axis=0, keepdims=True)
+
+    @pl.when(j == nb - 1)
+    def _():
+        group.row_done(r)
+
+    @pl.when((j == nb - 1) & (r == n_dp - 1))
+    def _():
+        group.finish()
+        dbl_grad_ref[...] = total[...]
+
+
+def scan_backward(lens, dbl, delta, pre, act, gy, stepw, rate2, skip, states, n_f, row_len, tblk=64, lanes=512):
     t, ch = delta.shape
-    n = bmat.shape[1]
+    n = rate2.shape[0]
     nb = row_len // tblk
-    k = tblk // TB
-    at = lambda r, j: (r * nb + nb - 1 - j, 0)
-    at3 = lambda r, j: (r * nb + nb - 1 - j, 0, 0)
+    n_dp = t // row_len
+    wide = dbl.shape[1]
+    spot = lambda r, j: row_at(r, n_dp) * nb + nb - 1 - j
+    at = lambda r, j: (spot(r, j), 0)
     zero = lambda r, j: (0, 0)
-    entry = lambda r, j: (jnp.maximum((r * nb + nb - 1 - j) * tblk - 1, 0), 0)
-    dd, da, db, dc, dl = pl.pallas_call(
-        functools.partial(bwd_kernel, k, min(lanes, ch)),
-        grid=(t // row_len, nb),
+    entry = lambda r, j: (jnp.maximum(spot(r, j) * tblk - 1, 0), 0)
+    return pl.pallas_call(
+        functools.partial(bwd_kernel, min(lanes, ch), n_f),
+        grid=(n_dp, nb),
         in_specs=[
+            pl.BlockSpec(memory_space=pltpu.SMEM),
+            pl.BlockSpec((tblk, wide), at),
             pl.BlockSpec((tblk, ch), at),
             pl.BlockSpec((tblk, ch), at),
-            pl.BlockSpec((tblk, 1), at),
             pl.BlockSpec((tblk, ch), at),
-            pl.BlockSpec((k, n, TB), at3),
-            pl.BlockSpec((k, TB, TB * n), at3),
+            pl.BlockSpec((tblk, ch), at),
+            pl.BlockSpec(stepw.shape, zero),
             pl.BlockSpec((n, ch), zero),
+            pl.BlockSpec((1, ch), zero),
             pl.BlockSpec((tblk * n, ch), at),
             pl.BlockSpec((n, ch), entry),
         ],
         out_specs=[
             pl.BlockSpec((tblk, ch), at),
             pl.BlockSpec((tblk, ch), at),
-            pl.BlockSpec((tblk * n, TB), at),
-            pl.BlockSpec((tblk * n, TB), at),
+            pl.BlockSpec((n_dp, row_len, wide), lambda r, j: (0, 0, 0)),
             pl.BlockSpec((n, ch), zero),
+            pl.BlockSpec((8, ch), zero),
+            pl.BlockSpec(stepw.shape, zero),
         ],
         out_shape=[
+            jax.ShapeDtypeStruct((t, ch), BF16),
             jax.ShapeDtypeStruct((t, ch), F32),
-            jax.ShapeDtypeStruct((t, ch), F32),
-            jax.ShapeDtypeStruct((t * n, TB), F32),
-            jax.ShapeDtypeStruct((t * n, TB), F32),
+            jax.ShapeDtypeStruct((n_dp, row_len, wide), F32),
             jax.ShapeDtypeStruct((n, ch), F32),
+            jax.ShapeDtypeStruct((8, ch), F32),
+            jax.ShapeDtypeStruct(stepw.shape, F32),
         ],
         scratch_shapes=[
             pltpu.VMEM((n, ch), F32),
+            pltpu.VMEM((tblk, 1), F32),
+            pltpu.VMEM((tblk, TB * n), BF16),
             pltpu.VMEM((TB, ch), F32),
             pltpu.VMEM((TB, ch), F32),
             pltpu.VMEM((TB * n, ch), BF16),
             pltpu.VMEM((TB * n, ch), BF16),
-        ],
-        compiler_params=pltpu.CompilerParams(vmem_limit_bytes=32 * 2**20),
+        ]
+        + GroupSum.scratch(row_len, wide),
+        compiler_params=pltpu.CompilerParams(
+            collective_id=3, has_side_effects=True, vmem_limit_bytes=40 * 2**20
+        ),
         cost_estimate=pl.CostEstimate(flops=t * n * ch * 80, bytes_accessed=t * ch * 60, transcendentals=t * n * ch),
-    )(delta, act, big, gy, turned(cmat), block_coef(bmat), rate2, states, states)
-
-    def diagonal(m):
-        m = m.reshape(t // TB, TB, n, TB)
-        return jnp.sum(m * jnp.eye(TB, dtype=m.dtype)[None, :, None, :], axis=3).reshape(t, n)
-
-    return dd, da, diagonal(db), diagonal(dc), dl
+    )(lens, dbl, delta, pre, act, gy, stepw, rate2, skip, states, states)
 
 
 def ring_order(count):
@@ -277,23 +669,6 @@
     return held[0]
 
 
-def group_sum(blocks, count):
-    held = {m: b for m, b in enumerate(blocks)}
-    masks = masks_of(count)
-    keep = [m for m in sorted(held) if not m & 1]
-    got = swap(jnp.stack([held[m | 1] for m in keep]), count, 1)
-    held = {m: held[m] + got[place] for place, m in enumerate(keep)}
-    for mask in masks[1:]:
-        keys = sorted(held)
-        got = swap(jnp.stack([held[m] for m in keys]), count, mask)
-        held = {m: held[m] + got[keys.index(m ^ mask)] for m in keys}
-    keys = sorted(held)
-    got = swap(jnp.stack([held[m] for m in keys]), count, 1)
-    for place, m in enumerate(keys):
-        held[m | 1] = got[place]
-    return [held[m] for m in range(count)]
-
-
 def mesh_at(index, n_f):
     return (index // n_f, lax.rem(index, n_f))
 
@@ -310,12 +685,14 @@
     return jnp.where(lax.rem(f, 2) == 0, f // 2, n_f - 1 - f // 2)
 
 
-def gather_kernel(n_dp, n_f, downs, send_ref, *refs):
+def gather_kernel(n_dp, n_f, downs, x_ref, dy_ref, meta_ref, dest_ref, lens_ref, *refs):
     streams = len(downs)
     blocks = refs[:streams]
-    x_all, dy_all, x_own_ref, dy_own_ref, tag_ref = refs[streams : streams + 5]
-    outs = refs[streams + 5 : 2 * streams + 5]
-    got, x_own, dy_own, own_sem, deal_sem, loc_sem, pair_send, pair_recv, ring_send, ring_recv = refs[2 * streams + 5 :]
+    x_all, dy_all, lens_all, x_own_ref, dy_own_ref, tag_ref, rank_ref = refs[streams : streams + 7]
+    outs = refs[streams + 7 : 2 * streams + 7]
+    send_ref, got, x_own, dy_own, deal_sem, loc_sem, pair_send, pair_recv, ring_send, ring_recv = refs[
+        2 * streams + 7 :
+    ]
     count = n_dp * n_f
     me_d = lax.axis_index("dp")
     me_f = lax.axis_index("fsdp")
@@ -333,8 +710,6 @@
         return 0
 
     lax.fori_loop(1, count, greet, 0)
-    own = pltpu.make_async_copy(send_ref.at[0], got.at[0], own_sem)
-    own.start()
     locals_ = [
         pltpu.make_async_copy(blocks[s], outs[s].at[me_f], loc_sem.at[s]) for s in range(streams)
     ]
@@ -371,8 +746,35 @@
         for up in (0, 1):
             if hops[s][up]:
                 hop(s, 0, up).start()
-        if s == 1:
-            lax.fori_loop(1, count, deal, 0)
+    tok, width = x_own.shape
+    pair2 = got.shape[1]
+    total = count * pair2
+
+    dest_row, rel_row, abs_row, in_row = (meta_ref[i : i + 1, :] for i in range(4))
+    rank = jnp.sum((dest_ref[...] < dest_row).astype(F32), axis=0, keepdims=True)
+    rank_ref[...] = jnp.broadcast_to(rank, rank_ref.shape)
+    half = pair2 // 2
+    goal = rel_row * half + rank - abs_row * half
+    row = lax.broadcasted_iota(jnp.int32, (total, tok), 0)
+    place_in = lax.rem(row, pair2)
+    first = place_in < half
+    slot = (row // pair2) * half + jnp.where(first, place_in, place_in - half)
+    chosen = slot.astype(F32) == goal
+    spot = jnp.sum(jnp.where(chosen, in_row, 0.0), axis=1, keepdims=True)
+    send_ref[:, :, width:] = jnp.broadcast_to(spot, (total, 128)).astype(BF16).reshape(count, pair2, 128)
+    x_pick = jnp.where(chosen & first, 1.0, 0.0).astype(BF16)
+    dy_pick = jnp.where(chosen & jnp.logical_not(first), 1.0, 0.0).astype(BF16)
+
+    def sort(j, _):
+        cols = pl.ds(pl.multiple_of(j * 256, 256), 256)
+        mixed = jnp.dot(x_pick, x_ref[:, cols], preferred_element_type=F32)
+        mixed = mixed + jnp.dot(dy_pick, dy_ref[:, cols], preferred_element_type=F32)
+        send_ref[:, :, cols] = mixed.astype(BF16).reshape(count, pair2, 256)
+        return 0
+
+    lax.fori_loop(0, width // 256, sort, 0)
+    lax.fori_loop(1, count, deal, 0)
+    got[0] = send_ref[0]
 
     def advance(h):
         for s in range(streams):
@@ -381,18 +783,12 @@
                     hop(s, h - 1, up).wait_recv()
                     hop(s, h, up).start()
 
-    own.wait()
     rest = got.at[pl.ds(1, count - 1)]
     pltpu.make_async_copy(send_ref.at[pl.ds(1, count - 1)], rest, deal_sem.at[1]).wait()
-    tok, width = x_own.shape
-    pair2 = got.shape[1]
-    total = count * pair2
     tag = got[:, :, width : width + 128].astype(F32).reshape(total, 128)
     reps = tok // 128
     spots = jnp.concatenate([tag] * reps, axis=1)
     lane = lax.broadcasted_iota(jnp.int32, (total, tok), 1).astype(F32)
-    row = lax.broadcasted_iota(jnp.int32, (total, tok), 0)
-    first = lax.rem(row, pair2) < pair2 // 2
     match = spots == lane
     x_pick = jnp.where(match & first, 1.0, 0.0).astype(BF16)
     dy_pick = jnp.where(match & jnp.logical_not(first), 1.0, 0.0).astype(BF16)
@@ -414,8 +810,8 @@
         return me_d + mask - 2 * mask * lax.rem(me_d // mask, 2)
 
     def share(a, m, mask):
-        out = (x_all, dy_all)[a]
-        own_block = (x_own, dy_own)[a]
+        out = (x_all, dy_all, lens_all)[a]
+        own_block = (x_own, dy_own, lens_ref)[a]
         return pltpu.make_async_remote_copy(
             src_ref=own_block if m == 0 else out.at[m],
             dst_ref=out.at[m | mask],
@@ -428,12 +824,16 @@
     copies = []
 
     def keep(a):
-        own_block = (x_own, dy_own)[a]
-        for j, dst in enumerate(((x_all, dy_all)[a].at[0], (x_own_ref, dy_own_ref)[a])):
+        own_block = (x_own, dy_own, lens_ref)[a]
+        dsts = (x_all, dy_all, lens_all)[a].at[0], (x_own_ref, dy_own_ref, None)[a]
+        for j, dst in enumerate(dsts[: 1 if a == 2 else 2]):
             c = pltpu.make_async_copy(own_block, dst, loc_sem.at[streams + 2 * a + j])
             c.start()
             copies.append(c)
 
+    for mask in masks:
+        share(2, 0, mask).start()
+    keep(2)
     advance(1)
     place(x_pick, x_own)
     for mask in masks:
@@ -462,6 +862,7 @@
     if most <= 2:
         relay(0)
     relay(1)
+    relay(2)
     for s in range(streams):
         for up in (0, 1):
             if hops[s][up]:
@@ -470,7 +871,7 @@
         for up in (0, 1):
             for h in range(hops[s][up]):
                 hop(s, h, up).wait_send()
-    for a in (0, 1):
+    for a in (0, 1, 2):
         held = [0]
         for mask in masks:
             for m in held:
@@ -481,36 +882,47 @@
     pltpu.make_async_copy(send_ref.at[pl.ds(1, count - 1)], rest, deal_sem.at[0]).wait()
 
 
-def gather_all(send, blocks, downs, n_dp, n_f, tok, width):
+def gather_all(x, dy, meta, dest, lens, blocks, downs, n_dp, n_f):
     streams = len(blocks)
-    count, pair2, _ = send.shape
+    tok, width = x.shape
+    count = n_dp * n_f
+    sent = (count, 2 * tok // count, width + 128)
     hops = max(max(d, n_f - 1 - d) for d in downs)
     any_ = pl.BlockSpec(memory_space=pl.ANY)
+    vmem = pl.BlockSpec(memory_space=pltpu.VMEM)
     row = jax.ShapeDtypeStruct((tok, width), BF16)
     rows = jax.ShapeDtypeStruct((n_dp, tok, width), BF16)
     return pl.pallas_call(
         functools.partial(gather_kernel, n_dp, n_f, downs),
-        in_specs=[any_] * (1 + streams),
-        out_specs=[any_] * 4 + [pl.BlockSpec(memory_space=pltpu.VMEM)] + [any_] * streams,
-        out_shape=[rows, rows, row, row, jax.ShapeDtypeStruct((count * pair2, 128), F32)]
+        in_specs=[vmem] * 5 + [any_] * streams,
+        out_specs=[any_] * 5 + [vmem] * 2 + [any_] * streams,
+        out_shape=[
+            rows,
+            rows,
+            jax.ShapeDtypeStruct((n_dp,) + lens.shape, lens.dtype),
+            row,
+            row,
+            jax.ShapeDtypeStruct((2 * tok, 128), F32),
+            jax.ShapeDtypeStruct((8, tok), F32),
+        ]
         + [jax.ShapeDtypeStruct((n_f,) + b.shape, b.dtype) for b in blocks],
         scratch_shapes=[
-            pltpu.VMEM(send.shape, BF16),
+            pltpu.VMEM(sent, BF16),
+            pltpu.VMEM(sent, BF16),
             pltpu.VMEM((tok, width), BF16),
             pltpu.VMEM((tok, width), BF16),
-            pltpu.SemaphoreType.DMA,
             pltpu.SemaphoreType.DMA((2,)),
-            pltpu.SemaphoreType.DMA((streams + 4,)),
-            pltpu.SemaphoreType.DMA((2, n_dp)),
-            pltpu.SemaphoreType.DMA((2, n_dp)),
+            pltpu.SemaphoreType.DMA((streams + 5,)),
+            pltpu.SemaphoreType.DMA((3, n_dp)),
+            pltpu.SemaphoreType.DMA((3, n_dp)),
             pltpu.SemaphoreType.DMA((streams, 2, hops)),
             pltpu.SemaphoreType.DMA((streams, 2, hops)),
         ],
         compiler_params=pltpu.CompilerParams(
-            collective_id=0, has_side_effects=True, vmem_limit_bytes=32 * 2**20
+            collective_id=0, has_side_effects=True, vmem_limit_bytes=40 * 2**20
         ),
         cost_estimate=pl.CostEstimate(flops=10**10, bytes_accessed=2 * 10**8, transcendentals=0),
-    )(send, *blocks)
+    )(x, dy, meta, dest, lens, *blocks)
 
 
 def columns_kernel(starts, cs, w_ref, *outs):
@@ -629,20 +1041,12 @@
 
     me = me_d * n_f + me_f
     row_to = destination // tok
-    in_row = destination % tok
-    rank = jnp.sum((destination[None, :] < destination[:, None]).astype(jnp.int32), axis=1)
+    meta = jnp.stack(
+        [destination, (row_to - me) % rows, row_to, destination % tok] + [jnp.zeros_like(destination)] * 4
+    ).astype(F32)
+    segs = lengths.shape[1]
+    lens_tile = jnp.pad(lengths, ((0, 7), (0, 128 - segs)))
     slots = jnp.arange(tok, dtype=jnp.int32)
-    rel_rank = ((row_to - me) % rows) * pair + rank % pair
-    to_send = rel_rank[None, :] == slots[:, None]
-    from_send = (rank[:, None] == slots[None, :]).astype(BF16)
-    spot = jnp.sum(jnp.where(to_send, in_row[None, :], 0), axis=1)
-    tag = jnp.broadcast_to(spot[:, None], (tok, 128)).astype(BF16).reshape(rows, pair, 128)
-    to_send = to_send.astype(BF16)
-    sorted_x = flat_dot(to_send, tokens).astype(BF16).reshape(rows, pair, width)
-    sorted_dy = flat_dot(to_send, cotangent).astype(BF16).reshape(rows, pair, width)
-    payload = jnp.concatenate(
-        [jnp.concatenate([sorted_x, tag], axis=2), jnp.concatenate([sorted_dy, tag], axis=2)], axis=1
-    )
 
     def mine(shard):
         return lax.dynamic_slice_in_dim(shard.reshape(-1, n_dp * cs), me_d * cs, cs, 1)
@@ -657,38 +1061,23 @@
     )
     wx_block, wg_block = take_columns(in_weight, 2, n_f, n_dp, cs)
     wo_block = lax.dynamic_slice_in_dim(out_weight, me_d * cs, cs, 0)
-    x_all, dy_all, x_own, dy_own, tags, small_all, wx, wg, wo = gather_all(
-        payload, [small_block, wx_block, wg_block, wo_block], [n_f // 2, n_f // 2, n_f - 1 - n_f // 2, n_f // 2],
-        n_dp, n_f, tok, width,
+    x_all, dy_all, lens_all, x_own, dy_own, tags, ranks, small_all, wx, wg = gather_all(
+        tokens, cotangent, meta, destination[:, None].astype(F32), lens_tile,
+        [small_block, wx_block, wg_block], [n_f // 2, n_f // 2, n_f - 1 - n_f // 2], n_dp, n_f,
     )
     x_all = x_all.reshape(group, width)
+    lens = lens_all[:, 0, :segs]
+    from_send = (ranks[0].astype(jnp.int32)[:, None] == slots[None, :]).astype(BF16)
     dy_all = dy_all.reshape(group, width)
     wx = wx.reshape(width, ch)
     wg = wg.reshape(width, ch)
-    wo = wo.reshape(ch, width)
     small = small_all.transpose(1, 0, 2).reshape(used + filler, ch)
     gain = small_all[:, used - gain_rows : used].reshape(width).astype(F32)
     tags = tags.reshape(rows, 2 * pair, 128)[:, :pair, 0].astype(jnp.int32)
     tags = tags[(me - jnp.arange(rows, dtype=jnp.int32)) % rows].reshape(tok)
     from_row = (tags[:, None] == slots[None, :]).astype(BF16)
 
-    lens = group_gather(jnp.broadcast_to(lengths, (8, lengths.shape[1])), n_dp)
-    positions = jnp.arange(tok, dtype=jnp.int32)
-    starts, segments = [], []
-    for m in range(n_dp):
-        total = jnp.int32(0)
-        start = jnp.zeros((tok,), jnp.bool_)
-        segment = jnp.zeros((tok,), jnp.int32)
-        for s in range(lengths.shape[1]):
-            start = start | (positions == total)
-            total = total + lens[m][0, s]
-            segment = segment + (positions >= total).astype(jnp.int32)
-            if m == 0 and s == lengths.shape[1] - 2:
-                valid = (positions < total).astype(F32)
-        starts.append(start)
-        segments.append(segment + m * (lengths.shape[1] + 1))
-    big = jnp.where(jnp.concatenate(starts), RESET, 0.0).astype(F32)[:, None]
-    segment = jnp.concatenate(segments)
+    valid = (slots < jnp.sum(lengths[0, : segs - 1])).astype(F32)
     x_own32 = x_own.astype(F32)
     square = jnp.sum(x_own32 * x_own32, axis=1)
     mine_sums = [jnp.sum(square * valid), jnp.sum(valid)]
@@ -702,11 +1091,6 @@
     skip = skip.astype(F32)
     rate = -jnp.exp(dlog.astype(F32))
 
-    x_all32 = x_all.astype(F32)
-    rstd = lax.rsqrt(jnp.mean(x_all32 * x_all32, axis=1, keepdims=True) + EPS)
-    normed = (x_all32 * rstd * gain[None]).astype(BF16)
-    x_in = flat_dot(normed, wx)
-
     def shifted(values, lag):
         if lag == 0:
             return values
@@ -715,23 +1099,31 @@
             return jnp.concatenate([edge, values[:-lag]], axis=0)
         return jnp.concatenate([values[-lag:], edge], axis=0)
 
-    same = [(shifted(segment + 1, lag) == segment + 1).astype(F32)[:, None] for lag in range(taps)]
-    same_next = [(shifted(segment + 1, -lag) == segment + 1).astype(F32)[:, None] for lag in range(taps)]
-    conv = conv_b.astype(F32) + sum(
-        conv_w[taps - 1 - lag][None] * shifted(x_in, lag) * same[lag] for lag in range(taps)
-    )
-    act = jax.nn.silu(conv).astype(BF16)
-    dbl_part = nt_dot(act, sel)
+    within = jnp.arange(tok, dtype=jnp.int32)
+    since, left = [], []
+    for m in range(n_dp):
+        begin, end, total = 0, 0, 0
+        for j in range(segs):
+            after = total + lens[m, j]
+            begin = jnp.where(within >= total, total, begin)
+            end = jnp.where(within >= total, after, end)
+            total = after
+        since.append(within - begin)
+        left.append(end - 1 - within)
+    since = jnp.concatenate(since)[:, None]
+    left = jnp.concatenate(left)[:, None]
+    same = [(since >= lag).astype(F32) for lag in range(taps)]
+    same_next = [(left >= lag).astype(F32) for lag in range(taps)]
     split = lambda value: [value[m * tok : (m + 1) * tok] for m in range(n_dp)]
-    dbl = jnp.concatenate(group_sum(split(dbl_part), n_dp), axis=0)
-    step_low = dbl[:, :rank_of].astype(BF16)
-    bmat = dbl[:, rank_of : rank_of + n]
-    cmat = dbl[:, rank_of + n :]
-    pre = flat_dot(step_low, stepw) + step_b.astype(F32)
-    delta = jax.nn.softplus(pre)
+    normed, x_in, conv, act, gate, dbl, wo_next = enter(
+        lens, x_all, gain[None], wx, wg, conv_w, conv_b.astype(F32), sel, wo_block, n_f
+    )
+    dbl = dbl.reshape(group, -1)
     rate2 = rate * LOG2E
-    scan_out, states = scan_forward(delta, act, big, bmat, cmat, rate2, skip, tok)
-    gate = flat_dot(normed, wg)
+    scan_out, states, delta, pre, wo = scan_forward(
+        lens, dbl, act, stepw, step_b.astype(F32), rate2, skip, wo_block, wo_next, n_f, tok
+    )
+    wo = wo.reshape(ch, width)
     gate_silu = jax.nn.silu(gate)
     gated = (scan_out * gate_silu).astype(BF16)
     mixed_part = flat_dot(gated, wo).astype(BF16)
@@ -748,16 +1140,11 @@
     wo_own = ring_reduce(
         lambda k: lax.dynamic_slice_in_dim(wo_grad, at_ring[k] * cs, cs, 0), n_f, n_f - 1 - n_f // 2, BF16
     )
-    dd, da, bmat_grad, cmat_grad, decay_sum = scan_backward(
-        delta, act, big, scan_grad, bmat, cmat, rate2, states, tok
-    )
-    pre_grad = (dd * jax.nn.sigmoid(pre)).astype(BF16)
-    low_grad = nt_dot(pre_grad, stepw)
-    dbl_grad = jnp.concatenate(
-        group_sum(split(jnp.concatenate([low_grad, bmat_grad, cmat_grad], axis=1)), n_dp), axis=0
-    ).astype(BF16)
-    act32 = act.astype(F32)
-    act_grad = da + skip * scan_grad + flat_dot(dbl_grad, sel)
+    pre_grad, act_grad, dbl_grad, decay_sum, sums, step_grad = scan_backward(
+        lens, dbl, delta, pre, act, scan_grad, stepw, rate2, skip, states, n_f, tok
+    )
+    dbl_grad = dbl_grad.reshape(group, -1).astype(BF16)
+    act_grad = act_grad + flat_dot(dbl_grad, sel)
     conv_grad = act_grad * silu_slope(conv)
     in_grad = sum(
         conv_w[taps - 1 - lag][None] * shifted(conv_grad, -lag) * same_next[lag] for lag in range(taps)
@@ -776,11 +1163,10 @@
         [jnp.stack(tap_grads)]
         + [
             jnp.sum(conv_grad, axis=0, keepdims=True),
-            jnp.sum(pre_grad.astype(F32), axis=0, keepdims=True),
-            jnp.sum(scan_grad * act32, axis=0, keepdims=True),
+            sums[:2],
             decay_sum * rate,
             tn_dot(dbl_grad, act),
-            tn_dot(step_low, pre_grad),
+            step_grad,
             jnp.zeros((-sum(heights) % 16, ch), F32),
         ],
         axis=0,
@@ -812,9 +1198,10 @@
         at += height
     grad_norm_gain = gain_sum / norm_gain.astype(F32)
 
-    hat = x_all32[:tok] * rstd[:tok]
+    rstd = lax.rsqrt(jnp.mean(x_own32 * x_own32, axis=1, keepdims=True) + EPS)
+    hat = x_own32 * rstd
     hat_grad = normed_grad * gain[None]
-    change = rstd[:tok] * (hat_grad - hat * jnp.mean(hat_grad * hat, axis=1, keepdims=True))
+    change = rstd * (hat_grad - hat * jnp.mean(hat_grad * hat, axis=1, keepdims=True))
     row_grad = (dy_own.astype(F32) + change).astype(BF16)
     layer = (x_own32 + mixed).astype(BF16)
 

time: 814 us -> 764 us (0.939)
  Pallas kernels: 290 us -> 346 us
  waiting for transfers between devices: 156 us -> 113 us
  other arithmetic: 89.3 us -> 58.6 us
  matrix products: 106 us -> 86.4 us
  starting transfers between devices: 65 us -> 54.8 us
    pallas_call x2 -> x3, Pallas kernels: 89.6 us -> 188 us  [the longest x1 99.2 us: scan_backward(): pl.pallas_call(functools.partial(bwd_kernel, min(lanes, ch), n_f), grid=(...]
    ppermute x20 -> x12, waiting for transfers between devices: 76 us -> 33.5 us  [swap(): return lax.ppermute(value, 'dp', [(i, i ^ mask) for i in range(count)])]
    pallas_call x1, Pallas kernels: 184 us -> 142 us  [gather_all(): pl.pallas_call(functools.partial(gather_kernel, n_dp, n_f, downs), in_spe...]
    reduce_sum x7 -> x2, other arithmetic: 21.8 us -> 0.92 us  [the longest x1 0.63 us: per_device(): valid = (slots < jnp.sum(lengths[0, :segs - 1])).astype(F32)]
    ppermute x20 -> x12, starting transfers between devices: 31.1 us -> 15.4 us  [swap(): return lax.ppermute(value, 'dp', [(i, i ^ mask) for i in range(count)])]
    convert_element_type x13 -> x8, other arithmetic: 18.2 us -> 3.53 us  [the longest x1 2.83 us: per_device(): in_grad = sum((conv_w[taps - 1 - lag][None] * shifted(conv_grad, -lag) *...]
    mul x9 -> x0, local copies, waits for them, and re-layouts: 14.1 us -> none  [block_coef(): spread = m.reshape(t // TB, TB, 1, n) * eye[None, :, :, None]]
    dot_general x12 -> x7, matrix products: 46 us -> 33.3 us  [per_device(): flat_dot = lambda a, b: jnp.dot(a, b, preferred_element_type=F32)]
  transfers between devices with their start and end apart: 50 -> 42, of which waited for: 19 -> 14; matrix products, arithmetic and copies ran while one was open for 19% -> 16% of each run, Pallas kernels for 25% -> 2%
where the time goes in v3:
time: 764 us; the launch traced here: 750 us
  Pallas kernels  346 us (45%)
  waiting for transfers between devices  113 us (15%)
  matrix products  86.4 us (11%)
  other arithmetic  58.6 us (8%)
  local copies, waits for them, and re-layouts  55.8 us (7%)
  starting transfers between devices  54.8 us (7%)
  between operations  35.5 us (5%)
    pallas_call x1, Pallas kernels, gather_all(): pl.pallas_call(functools.partial(gather_kernel, n_dp, n_f, downs), in_spe...  142 us
    pallas_call x1, Pallas kernels, scan_backward(): pl.pallas_call(functools.partial(bwd_kernel, min(lanes, ch), n_f), grid=(...  99.2 us
    ppermute x28, waiting for transfers between devices, ring_step(): return lax.ppermute(value, 'fsdp', pairs)  69.4 us
    pallas_call x1, Pallas kernels, scan_forward(): pl.pallas_call(functools.partial(fwd_kernel, min(lanes, ch), n_f), grid=(...  45.8 us
    pallas_call x1, Pallas kernels, enter(): pl.pallas_call(functools.partial(enter_kernel, n_f, half), grid=(2 * half...  42.7 us
    ppermute x12, waiting for transfers between devices, swap(): return lax.ppermute(value, 'dp', [(i, i ^ mask) for i in range(count)])  33.5 us
    dot_general x7, matrix products, per_device(): flat_dot = lambda a, b: jnp.dot(a, b, preferred_element_type=F32)  33.3 us
    dot_general x3, matrix products, per_device(): lax.dot_general(a, b, (((1,), (1,)), ((), ())), preferred_element_type=F32)  28.6 us
  transfers between devices with their start and end apart: 42, of which 14 were waited for; matrix products, arithmetic and copies ran while one was open for 16% of the time, Pallas kernels for 2%

profile of v3, /device:TPU:21, one launch (start us, length us, event | category | flops | bytes accessed | tf_op | source)
XLA Modules:
  0.0 750.1 jit_solution(14762542759573153325)
XLA Ops:
  25.5 142.0 %shard_map.264 = (bf16[4,256,2048]{2,1,0:T(8,128)(2,1)S(1)}, bf16[4,256,2048]{2,1,0:T(8,128)(2,1)}, s32[4,8,128]{2,1,0:T(8,128)S(1)}, bf16[256,2048]{1,0:T(8,128...) custom-call(bf16[256,2048]{1,0:T(8,128)(2,1)S(1)} %copy-done.11, ...), custom_call_target="tpu_custom_call" | custom-call | flops 10000000000 | bytes 200000000 | tf_op jit(solution)/shard_map/pallas_call | solution.py:895
  191.9 42.7 %shard_map.265 = (bf16[1024,2048]{1,0:T(8,128)(2,1)}, f32[1024,1024]{1,0:T(8,128)}, f32[1024,1024]{1,0:T(8,128)}, bf16[1024,1024]{1,0:T(8,128)(2,1)S(1)}, f32[10...) custom-call(s32[4,4]{1,0:T(4,128)S(1)} %bitcast.246, bf16[1024,2048]{1,0:T(8,128)(2,1)} %bitcast.255, ...), custom_call_target="tpu_custom_call" | custom-call | flops 10000000000 | bytes 40000000 | tf_op jit(solution)/shard_map/pallas_call | solution.py:221
  234.7 45.8 %shard_map.266 = (f32[1024,1024]{1,0:T(8,128)S(1)}, bf16[16384,1024]{1,0:T(8,128)(2,1)}, f32[1024,1024]{1,0:T(8,128)S(1)}, f32[1024,1024]{1,0:T(8,128)S(1)}, bf16[8,128,2048]{2,1,0:T(8,128)(2,1)S(1)}) custom-call(s32[4,4]{1,0:T(4,128)S(1)} %bitcast.247, f32[1024,160]{1,0:T(8,128)S(1)} %bitcast.236, bf16[1024,1024]{1,0:T(8,128)(2,1)S(1)} %get-tuple-element.56.act_ref, ...), custom_call_target="tpu_custom_call" | custom-call | flops 671088640 | bytes 54525952 | tf_op jit(solution)/shard_map/pallas_call | solution.py:404
  282.5 14.2 %multiply_convert_fusion = (bf16[1024,1024]{1,0:T(8,128)(2,1)}, f32[1024,1024]{1,0:T(8,128)}, bf16[1024,1024]{1,0:T(8,128)(2,1)}) fusion(f32[1024,1024]{1,0:T(8,128)} %get-tuple-element.59, f32[1024,1024]{1,0:T(8,128)S(1)} %get-tuple-element.58, bf16[1024,2048]{1,0:T(8,128)(2,1)} %bitcast.303, bf16[1024,2048]{1,0:T(8,128)(2,1)S(1)} %bitcast.253), kind=kOutput, calls=%fused_computation.8 | convolution fusion | flops 4309647360 | bytes 25165824 | tf_op jit(solution)/shard_map/dot_general | solution.py:1039
  296.6 99.2 %shard_map.267 = (bf16[1024,1024]{1,0:T(8,128)(2,1)}, f32[1024,1024]{1,0:T(8,128)S(1)}, f32[4,256,160]{2,1,0:T(8,128)S(1)}, f32[16,1024]{1,0:T(8,128)S(1)}, f32[...) custom-call(s32[4,4]{1,0:T(4,128)S(1)} %bitcast.248, f32[1024,160]{1,0:T(8,128)S(1)} %bitcast.237, f32[1024,1024]{1,0:T(8,128)} %copy-done.2, ...), custom_call_target="tpu_custom_call" | custom-call | flops 1342177280 | bytes 62914560 | tf_op jit(solution)/shard_map/pallas_call | solution.py:563
  401.0 13.9 %fusion.51 = (f32[1024]{0:T(1024)S(1)}, f32[1024]{0:T(1024)S(1)}, f32[1024]{0:T(1024)S(1)}, f32[1024]{0:T(1024)S(1)}, f32[1024]{0:T(1024)S(1)}, /*index=5*/f32[1024,1024]{1,0:T(8,128)}) fusion(f32[1024]{0:T(1024)S(1)} %get-tuple-element.148, f32[1024,1024]{1,0:T(8,128)} %get-tuple-element.72, f32[1024]{0:T(1024)S(1)} %get-tuple-element.147, ...), kind=kOutput, calls=%fused_computation.229 | convolution fusion | flops 358607872 | bytes 30248960 | tf_op jit(solution)/shard_map/dot_general | solution.py:1038
  419.0 9.4 %convolution_convert_fusion.1 = bf16[1024,2048]{1,0:T(8,128)(2,1)} fusion(bf16[1024,1024]{1,0:T(8,128)(2,1)} %get-tuple-element.85, bf16[1024,2048]{1,0:T(8,128)(2,1)} %bitcast.304), kind=kOutput, calls=%fused_computation.14 | convolution fusion | flops 4297064448 | bytes 10485760 | tf_op jit(solution)/shard_map/dot_general | solution.py:1040
  433.4 7.4 convolution_convert_fusion.2
  451.8 9.5 %convolution_convert_fusion.4 = bf16[1024,2048]{1,0:T(8,128)(2,1)} fusion(bf16[1024,1024]{1,0:T(8,128)(2,1)} %get-tuple-element.85, bf16[1024,2048]{1,0:T(8,128)(2,1)} %bitcast.254), kind=kOutput, calls=%fused_computation.17 | convolution fusion | flops 4297064448 | bytes 10485760 | tf_op jit(solution)/shard_map/dot_general | solution.py:1038
  466.9 6.3 convolution_convert_fusion.3
  473.3 6.8 fusion.60
  483.9 7.7 %add_convert_fusion = bf16[1024,2048]{1,0:T(8,128)(2,1)S(1)} fusion(f32[1024,2048]{1,0:T(8,128)} %fusion.60, bf16[1024,1024]{1,0:T(8,128)(2,1)} %get-tuple-element.83, bf16[2048,1024]{1,0:T(8,128)(2,1)S(1)} %bitcast.300), kind=kOutput, calls=%fused_computation.1 | convolution fusion | flops 4299161600 | bytes 18874368 | tf_op jit(solution)/shard_map/dot_general | solution.py:1039
  520.8 11.0 %collective-permute-done.24 = f32[320,128]{1,0:T(8,128)S(1)} collective-permute-done((f32[320,128]{1,0:T(8,128)S(1)}, f32[320,128]{1,0:T(8,128)S(1)}, u32[]{:S(2)}, u32[]{:S(2)}) %collective-permute-start.24) | collective-permute-done | bytes 163872 | tf_op jit(solution)/shard_map/ppermute | solution.py:622
  552.9 8.6 %collective-permute-done.5 = bf16[256,1024]{1,0:T(8,128)(2,1)S(1)} collective-permute-done((bf16[256,1024]{1,0:T(8,128)(2,1)S(1)}, bf16[256,1024]{1,0:T(8,128)(2,1)S(1)}, u32[]{:S(2)}, u32[]{:S(2)}) %collective-permute-start.5) | collective-permute-done | bytes 524320 | tf_op jit(solution)/shard_map/ppermute | solution.py:622
  563.3 9.5 %collective-permute-done.31 = bf16[128,2048]{1,0:T(8,128)(2,1)S(1)} collective-permute-done((bf16[128,2048]{1,0:T(8,128)(2,1)S(1)}, bf16[128,2048]{1,0:T(8,128)(2,1)S(1)}, u32[]{:S(2)}, u32[]{:S(2)}) %collective-permute-start.31) | collective-permute-done | bytes 524320 | tf_op jit(solution)/shard_map/ppermute | solution.py:622
  588.6 8.0 %collective-permute-done.6 = bf16[256,1024]{1,0:T(8,128)(2,1)S(1)} collective-permute-done((bf16[256,1024]{1,0:T(8,128)(2,1)S(1)}, bf16[256,1024]{1,0:T(8,128)(2,1)S(1)}, u32[]{:S(2)}, u32[]{:S(2)}) %collective-permute-start.6) | collective-permute-done | bytes 524320 | tf_op jit(solution)/shard_map/ppermute | solution.py:622
  600.3 7.5 collective-permute-done.16
  610.6 18.9 %collective-permute-done.3 = bf16[1,256,2048]{2,1,0:T(8,128)(2,1)S(1)} collective-permute-done((bf16[1,256,2048]{2,1,0:T(8,128)(2,1)S(1)}, bf16[1,256,2048]{2,1,0:T(8,128)(2,1)S(1)}, u32[]{:S(2)}, u32[]{:S(2)}) %collective-permute-start.3) | collective-permute-done | bytes 1048608 | tf_op jit(solution)/shard_map/ppermute | solution.py:646
  635.5 9.8 %all-to-all-start.1 = ((bf16[32,8,2048]{2,1,0:T(8,128)(2,1)}), bf16[32,8,2048]{2,1,0:T(8,128)(2,1)S(1)}, u32[]{:S(2)}, u32[]{:S(2)}) async-start(bf16[32,8,2048]{2,1,0:T(8,128)(2,1)} %fusion.3), calls=%async_computation.1 | async-start | bytes 2097152 | tf_op jit(solution)/shard_map/all_to_all | solution.py:1211
  659.5 9.9 %all-to-all-done.1 = bf16[32,8,2048]{2,1,0:T(8,128)(2,1)S(1)} async-done(((bf16[32,8,2048]{2,1,0:T(8,128)(2,1)}), bf16[32,8,2048]{2,1,0:T(8,128)(2,1)S(1)}, u32[]{:S(2)}, u32[]{:S(2)}) %all-to-all-start.1) | async-done | bytes 1048608 | tf_op jit(solution)/shard_map/all_to_all | solution.py:1211
  669.4 7.4 all-to-all-start
  676.8 12.4 %collective-permute-done.33 = bf16[128,2048]{1,0:T(8,128)(2,1)S(1)} collective-permute-done((bf16[128,2048]{1,0:T(8,128)(2,1)}, bf16[128,2048]{1,0:T(8,128)(2,1)S(1)}, u32[]{:S(2)}, u32[]{:S(2)}) %collective-permute-start.33) | collective-permute-done | bytes 524320 | tf_op jit(solution)/shard_map/ppermute | solution.py:622
  699.0 11.7 %collective-permute-done.38 = bf16[1,128,2048]{2,1,0:T(8,128)(2,1)S(1)} collective-permute-done((bf16[1,128,2048]{2,1,0:T(8,128)(2,1)S(1)}, bf16[1,128,2048]{2,1,0:T(8,128)(2,1)S(1)}, u32[]{:S(2)}, u32[]{:S(2)}) %collective-permute-start.38) | collective-permute-done | bytes 524320 | tf_op jit(solution)/shard_map/ppermute | solution.py:646
  719.2 12.4 %shard_map.268 = (f32[256,8192]{1,0:T(8,128)}, f32[256,128]{1,0:T(8,128)}) custom-call(bf16[4,256,2048]{2,1,0:T(8,128)(2,1)} %maximum_maximum_fusion.x_ref, bf16[256,8192]{1,0:T(8,128)(2,1)} %w_ref.3), custom_call_target="tpu_custom_call" | custom-call | flops 8388608 | bytes 16777216 | tf_op jit(solution)/shard_map/pallas_call | solution.py:983
  (289 shorter events, 182.6 us)
Async XLA Ops:
  417.8 83.3 %collective-permute-start.25 = (f32[320,128]{1,0:T(8,128)S(1)}, f32[320,128]{1,0:T(8,128)S(1)}, u32[]{:S(2)}, u32[]{:S(2)}) collective-permute-start(f32[320,128]{1,0:T(8,128)S(1)} %constant_dynamic-slice_fusion.6), channel_id=1, source_target_pairs={{0,2},{2,4},{4,6},{6,7},{7,5},{5,3},{3,1},{1,0},{8,10},{10,12},{12... | collective-permute-start | bytes 491528 | tf_op jit(solution)/shard_map/ppermute | solution.py:622
  430.7 105.5 %collective-permute-start.34 = (bf16[128,2048]{1,0:T(8,128)(2,1)}, bf16[128,2048]{1,0:T(8,128)(2,1)}, u32[]{:S(2)}, u32[]{:S(2)}) collective-permute-start(bf16[128,2048]{1,0:T(8,128)(2,1)} %get-tuple-element.93), channel_id=1, source_target_pairs={{0,2},{2,4},{4,6},{6,7},{7,5},{5,3},{3,1},{1,0},{8,10},{10,12},{12... | collective-permute-start | bytes 1572872 | tf_op jit(solution)/shard_map/ppermute | solution.py:622
  443.9 75.0 %collective-permute-start.13 = (bf16[256,1024]{1,0:T(8,128)(2,1)}, bf16[256,1024]{1,0:T(8,128)(2,1)}, u32[]{:S(2)}, u32[]{:S(2)}) collective-permute-start(bf16[256,1024]{1,0:T(8,128)(2,1)} %get-tuple-element.104), channel_id=1, source_target_pairs={{0,1},{2,0},{4,2},{6,4},{7,6},{5,7},{3,5},{1,3},{8,9},{10,8},{12,1... | collective-permute-start | bytes 1572872 | tf_op jit(solution)/shard_map/ppermute | solution.py:622
  444.4 92.4 %collective-permute-start.17 = (bf16[256,1024]{1,0:T(8,128)(2,1)}, bf16[256,1024]{1,0:T(8,128)(2,1)}, u32[]{:S(2)}, u32[]{:S(2)}) collective-permute-start(bf16[256,1024]{1,0:T(8,128)(2,1)} %get-tuple-element.105), channel_id=1, source_target_pairs={{0,2},{2,4},{4,6},{6,7},{7,5},{5,3},{3,1},{1,0},{8,10},{10,12},{12... | collective-permute-start | bytes 1572872 | tf_op jit(solution)/shard_map/ppermute | solution.py:622
  531.8 45.0 %collective-permute-start = (bf16[2,256,2048]{2,1,0:T(8,128)(2,1)}, bf16[2,256,2048]{2,1,0:T(8,128)(2,1)S(1)}, u32[]{:S(2)}, u32[]{:S(2)}) collective-permute-start(bf16[2,256,2048]{2,1,0:T(8,128)(2,1)} %pad_maximum_fusion), channel_id=1, source_target_pairs={{0,8},{8,0},{16,24},{24,16},{1,9},{9,1},{17,25},{25,17},{2,10},{10... | collective-permute-start | bytes 6291464 | tf_op jit(solution)/shard_map/ppermute | solution.py:646
  536.2 42.4 %collective-permute-start.2 = (bf16[2,256,2048]{2,1,0:T(8,128)(2,1)}, bf16[2,256,2048]{2,1,0:T(8,128)(2,1)S(1)}, u32[]{:S(2)}, u32[]{:S(2)}) collective-permute-start(bf16[2,256,2048]{2,1,0:T(8,128)(2,1)} %pad_maximum_fusion.1), channel_id=1, source_target_pairs={{0,8},{8,0},{16,24},{24,16},{1,9},{9,1},{17,25},{25,17},{2,10},{10... | collective-permute-start | bytes 6291464 | tf_op jit(solution)/shard_map/ppermute | solution.py:646
  548.7 24.1 %collective-permute-start.31 = (bf16[128,2048]{1,0:T(8,128)(2,1)S(1)}, bf16[128,2048]{1,0:T(8,128)(2,1)S(1)}, u32[]{:S(2)}, u32[]{:S(2)}) collective-permute-start(bf16[128,2048]{1,0:T(8,128)(2,1)S(1)} %copy-done.38), channel_id=1, source_target_pairs={{0,1},{2,0},{4,2},{6,4},{7,6},{5,7},{3,5},{1,3},{8,9},{10,8},{12,1... | collective-permute-start | bytes 1572872 | tf_op jit(solution)/shard_map/ppermute | solution.py:622
  550.3 23.8 %collective-permute-start.35 = (bf16[128,2048]{1,0:T(8,128)(2,1)S(1)}, bf16[128,2048]{1,0:T(8,128)(2,1)S(1)}, u32[]{:S(2)}, u32[]{:S(2)}) collective-permute-start(bf16[128,2048]{1,0:T(8,128)(2,1)S(1)} %add_convert_fusion.5), channel_id=1, source_target_pairs={{0,2},{2,4},{4,6},{6,7},{7,5},{5,3},{3,1},{1,0},{8,10},{10,12},{12... | collective-permute-start | bytes 1572872 | tf_op jit(solution)/shard_map/ppermute | solution.py:622
  561.5 26.2 %collective-permute-start.30 = (f32[2,320,128]{2,1,0:T(8,128)S(1)}, f32[2,320,128]{2,1,0:T(8,128)S(1)}, u32[]{:S(2)}, u32[]{:S(2)}) collective-permute-start(f32[2,320,128]{2,1,0:T(8,128)S(1)} %pad_maximum_fusion.8), channel_id=1, source_target_pairs={{0,8},{8,0},{16,24},{24,16},{1,9},{9,1},{17,25},{25,17},{2,10},{10... | collective-permute-start | bytes 983048 | tf_op jit(solution)/shard_map/ppermute | solution.py:646
  585.4 24.2 %collective-permute-start.1 = (bf16[1,256,2048]{2,1,0:T(8,128)(2,1)S(1)}, bf16[1,256,2048]{2,1,0:T(8,128)(2,1)S(1)}, u32[]{:S(2)}, u32[]{:S(2)}) collective-permute-start(bf16[1,256,2048]{2,1,0:T(8,128)(2,1)S(1)} %fusion.18), channel_id=1, source_target_pairs={{0,16},{8,24},{16,0},{24,8},{1,17},{9,25},{17,1},{25,9},{2,18},{10... | collective-permute-start | bytes 3145736 | tf_op jit(solution)/shard_map/ppermute | solution.py:646
  586.4 43.1 %collective-permute-start.3 = (bf16[1,256,2048]{2,1,0:T(8,128)(2,1)S(1)}, bf16[1,256,2048]{2,1,0:T(8,128)(2,1)S(1)}, u32[]{:S(2)}, u32[]{:S(2)}) collective-permute-start(bf16[1,256,2048]{2,1,0:T(8,128)(2,1)S(1)} %fusion.19), channel_id=1, source_target_pairs={{0,16},{8,24},{16,0},{24,8},{1,17},{9,25},{17,1},{25,9},{2,18},{10... | collective-permute-start | bytes 3145736 | tf_op jit(solution)/shard_map/ppermute | solution.py:646
  598.5 46.9 %collective-permute-start.32 = (bf16[128,2048]{1,0:T(8,128)(2,1)}, bf16[128,2048]{1,0:T(8,128)(2,1)}, u32[]{:S(2)}, u32[]{:S(2)}) collective-permute-start(bf16[128,2048]{1,0:T(8,128)(2,1)} %get-tuple-element.90), channel_id=1, source_target_pairs={{0,1},{2,0},{4,2},{6,4},{7,6},{5,7},{3,5},{1,3},{8,9},{10,8},{12,1... | collective-permute-start | bytes 1572872 | tf_op jit(solution)/shard_map/ppermute | solution.py:622
  607.8 37.5 %collective-permute-start.36 = (bf16[128,2048]{1,0:T(8,128)(2,1)}, bf16[128,2048]{1,0:T(8,128)(2,1)}, u32[]{:S(2)}, u32[]{:S(2)}) collective-permute-start(bf16[128,2048]{1,0:T(8,128)(2,1)} %get-tuple-element.91), channel_id=1, source_target_pairs={{0,2},{2,4},{4,6},{6,7},{7,5},{5,3},{3,1},{1,0},{8,10},{10,12},{12... | collective-permute-start | bytes 1572872 | tf_op jit(solution)/shard_map/ppermute | solution.py:622
  608.8 41.1 %collective-permute-start.7 = (bf16[256,1024]{1,0:T(8,128)(2,1)}, bf16[256,1024]{1,0:T(8,128)(2,1)S(1)}, u32[]{:S(2)}, u32[]{:S(2)}) collective-permute-start(bf16[256,1024]{1,0:T(8,128)(2,1)} %get-tuple-element.94), channel_id=1, source_target_pairs={{0,1},{2,0},{4,2},{6,4},{7,6},{5,7},{3,5},{1,3},{8,9},{10,8},{12,1... | collective-permute-start | bytes 1572872 | tf_op jit(solution)/shard_map/ppermute | solution.py:622
  609.6 41.1 %collective-permute-start.10 = (bf16[256,1024]{1,0:T(8,128)(2,1)}, bf16[256,1024]{1,0:T(8,128)(2,1)}, u32[]{:S(2)}, u32[]{:S(2)}) collective-permute-start(bf16[256,1024]{1,0:T(8,128)(2,1)} %get-tuple-element.95), channel_id=1, source_target_pairs={{0,2},{2,4},{4,6},{6,7},{7,5},{5,3},{3,1},{1,0},{8,10},{10,12},{12... | collective-permute-start | bytes 1572872 | tf_op jit(solution)/shard_map/ppermute | solution.py:622
  629.5 24.1 %collective-permute-start.20 = (bf16[1,256,1024]{2,1,0:T(8,128)(2,1)S(1)}, bf16[1,256,1024]{2,1,0:T(8,128)(2,1)}, u32[]{:S(2)}, u32[]{:S(2)}) collective-permute-start(bf16[1,256,1024]{2,1,0:T(8,128)(2,1)S(1)} %fusion.31), channel_id=1, source_target_pairs={{0,16},{8,24},{16,0},{24,8},{1,17},{9,25},{17,1},{25,9},{2,18},{10... | collective-permute-start | bytes 1572872 | tf_op jit(solution)/shard_map/ppermute | solution.py:646
  635.5 33.9 %all-to-all-start.1 = ((bf16[32,8,2048]{2,1,0:T(8,128)(2,1)}), bf16[32,8,2048]{2,1,0:T(8,128)(2,1)S(1)}, u32[]{:S(2)}, u32[]{:S(2)}) async-start(bf16[32,8,2048]{2,1,0:T(8,128)(2,1)} %fusion.3), calls=%async_computation.1 | async-start | bytes 2097152 | tf_op jit(solution)/shard_map/all_to_all | solution.py:1211
  648.4 40.7 %collective-permute-start.33 = (bf16[128,2048]{1,0:T(8,128)(2,1)}, bf16[128,2048]{1,0:T(8,128)(2,1)S(1)}, u32[]{:S(2)}, u32[]{:S(2)}) collective-permute-start(bf16[128,2048]{1,0:T(8,128)(2,1)} %get-tuple-element.88), channel_id=1, source_target_pairs={{0,1},{2,0},{4,2},{6,4},{7,6},{5,7},{3,5},{1,3},{8,9},{10,8},{12,1... | collective-permute-start | bytes 1572872 | tf_op jit(solution)/shard_map/ppermute | solution.py:622
  649.7 40.3 %collective-permute-start.37 = (bf16[128,2048]{1,0:T(8,128)(2,1)}, bf16[128,2048]{1,0:T(8,128)(2,1)}, u32[]{:S(2)}, u32[]{:S(2)}) collective-permute-start(bf16[128,2048]{1,0:T(8,128)(2,1)} %get-tuple-element.89), channel_id=1, source_target_pairs={{0,2},{2,4},{4,6},{6,7},{7,5},{5,3},{3,1},{1,0},{8,10},{10,12},{12... | collective-permute-start | bytes 1572872 | tf_op jit(solution)/shard_map/ppermute | solution.py:622
  652.3 40.7 %collective-permute-start.11 = (bf16[1,256,1024]{2,1,0:T(8,128)(2,1)S(1)}, bf16[1,256,1024]{2,1,0:T(8,128)(2,1)}, u32[]{:S(2)}, u32[]{:S(2)}) collective-permute-start(bf16[1,256,1024]{2,1,0:T(8,128)(2,1)S(1)} %fusion.30), channel_id=1, source_target_pairs={{0,16},{8,24},{16,0},{24,8},{1,17},{9,25},{17,1},{25,9},{2,18},{10... | collective-permute-start | bytes 1572872 | tf_op jit(solution)/shard_map/ppermute | solution.py:646
  655.7 58.3 %collective-permute-start.21 = (bf16[2,256,1024]{2,1,0:T(8,128)(2,1)}, bf16[2,256,1024]{2,1,0:T(8,128)(2,1)}, u32[]{:S(2)}, u32[]{:S(2)}) collective-permute-start(bf16[2,256,1024]{2,1,0:T(8,128)(2,1)} %pad_maximum_fusion.4), channel_id=1, source_target_pairs={{0,8},{8,0},{16,24},{24,16},{1,9},{9,1},{17,25},{25,17},{2,10},{10... | collective-permute-start | bytes 3145736 | tf_op jit(solution)/shard_map/ppermute | solution.py:646
  669.4 69.7 %all-to-all-start = ((bf16[32,8,4224]{2,1,0:T(8,128)(2,1)}), bf16[32,8,4224]{2,1,0:T(8,128)(2,1)}, u32[]{:S(2)}, u32[]{:S(2)}) async-start(bf16[32,8,4224]{2,1,0:T(8,128)(2,1)} %maximum_bitcast_fusion), calls=%async_computation | async-start | bytes 4325376 | tf_op jit(solution)/shard_map/all_to_all | solution.py:1221
  694.2 21.1 %collective-permute-start.12 = (bf16[2,256,1024]{2,1,0:T(8,128)(2,1)S(1)}, bf16[2,256,1024]{2,1,0:T(8,128)(2,1)S(1)}, u32[]{:S(2)}, u32[]{:S(2)}) collective-permute-start(bf16[2,256,1024]{2,1,0:T(8,128)(2,1)S(1)} %pad_maximum_fusion.3), channel_id=1, source_target_pairs={{0,8},{8,0},{16,24},{24,16},{1,9},{9,1},{17,25},{25,17},{2,10},{10... | collective-permute-start | bytes 3145736 | tf_op jit(solution)/shard_map/ppermute | solution.py:646
  711.9 21.3 %collective-permute-start.39 = (bf16[2,128,2048]{2,1,0:T(8,128)(2,1)}, bf16[2,128,2048]{2,1,0:T(8,128)(2,1)}, u32[]{:S(2)}, u32[]{:S(2)}) collective-permute-start(bf16[2,128,2048]{2,1,0:T(8,128)(2,1)} %pad_maximum_fusion.5), channel_id=1, source_target_pairs={{0,8},{8,0},{16,24},{24,16},{1,9},{9,1},{17,25},{25,17},{2,10},{10... | collective-permute-start | bytes 3145736 | tf_op jit(solution)/shard_map/ppermute | solution.py:646
  (65 other events, 1017.0 us)

commit v4 on v3

--- a/solution.py
+++ b/solution.py
@@ -98,6 +98,138 @@
         ]
 
 
+class RingReduce:
+    def __init__(self, n_f, part, got, send, recv, down):
+        self.part, self.got = part, got
+        q = ring_place(lax.axis_index("fsdp"), n_f)
+        self.at = lambda k: ring_index(lax.rem(q + k, n_f), n_f)
+        self.n_f = n_f
+        self.counts = [down, n_f - 1 - down]
+        self.copies = [[], []]
+        for up in (0, 1):
+            for h in range(self.counts[up]):
+                src = part.at[self.at(self.goal(up, 0))] if h == 0 else got.at[up, h - 1]
+                self.copies[up].append(ring_copy(n_f, src, got.at[up, h], send.at[up, h], recv.at[up, h], up))
+        self.events = max(self.counts)
+
+    def goal(self, up, h):
+        left = self.counts[up] - h
+        return left if up else self.n_f - left
+
+    def add(self, slot, addend):
+        rows = slot.shape[0]
+        step = min(rows, 64)
+
+        def piece(i, _):
+            at = pl.ds(pl.multiple_of(i * step, step), step)
+            slot[at, :] = (slot[at, :].astype(F32) + addend[at, :].astype(F32)).astype(slot.dtype)
+            return 0
+
+        lax.fori_loop(0, rows // step, piece, 0)
+
+    def start(self):
+        for up in (0, 1):
+            if self.copies[up]:
+                self.copies[up][0].start()
+
+    def event(self, e):
+        for up in (0, 1):
+            if e < self.counts[up]:
+                self.copies[up][e - 1].wait_recv()
+                self.add(self.got.at[up, e - 1], self.part.at[self.at(self.goal(up, e))])
+                self.copies[up][e].start()
+
+    def finish(self, out):
+        last = []
+        for up in (0, 1):
+            if self.copies[up]:
+                self.copies[up][-1].wait_recv()
+                last.append(self.got.at[up, self.counts[up] - 1])
+        mine = self.part.at[self.at(0)]
+        rows = mine.shape[0]
+        step = min(rows, 64)
+
+        def piece(i, _):
+            at = pl.ds(pl.multiple_of(i * step, step), step)
+            total_ = mine[at, :].astype(F32)
+            for slot in last:
+                total_ = total_ + slot[at, :].astype(F32)
+            out[at, :] = total_.astype(out.dtype)
+            return 0
+
+        lax.fori_loop(0, rows // step, piece, 0)
+        for up in (0, 1):
+            for c in self.copies[up]:
+                c.wait_send()
+
+    @staticmethod
+    def scratch(n_f, block, dtype=BF16):
+        return [
+            pltpu.VMEM((2, n_f // 2) + block, dtype),
+            pltpu.SemaphoreType.DMA((2, n_f // 2)),
+            pltpu.SemaphoreType.DMA((2, n_f // 2)),
+        ]
+
+
+class PairReduce:
+    def __init__(self, part, near, far, send, recv):
+        self.part, self.near, self.far = part, near, far
+        me_d, me_f = lax.axis_index("dp"), lax.axis_index("fsdp")
+        plan = [
+            (part.at[1], near.at[0], 1),
+            (part.at[3], near.at[1], 1),
+            (part.at[2], far, 2),
+        ]
+        self.copies = [
+            pltpu.make_async_remote_copy(
+                src_ref=src,
+                dst_ref=dst,
+                send_sem=send.at[i],
+                recv_sem=recv.at[i],
+                device_id=(flip(me_d, mask), me_f),
+                device_id_type=pl.DeviceIdType.MESH,
+            )
+            for i, (src, dst, mask) in enumerate(plan)
+        ]
+
+    def start(self):
+        for c in self.copies[:2]:
+            c.start()
+
+    def middle(self):
+        self.copies[1].wait_recv()
+        rows_add(self.part.at[2], [self.part.at[2], self.near.at[1]])
+        self.copies[2].start()
+        self.copies[0].wait_recv()
+
+    def finish(self, out):
+        self.copies[2].wait_recv()
+        rows_add(out, [self.part.at[0], self.near.at[0], self.far])
+        for c in self.copies:
+            c.wait_send()
+
+    @staticmethod
+    def scratch(block, dtype=BF16):
+        return [
+            pltpu.VMEM((2,) + block, dtype),
+            pltpu.VMEM(block, dtype),
+            pltpu.SemaphoreType.DMA((3,)),
+            pltpu.SemaphoreType.DMA((3,)),
+        ]
+
+
+def rows_add(out, terms, step=32):
+    def piece(i, _):
+        at = pl.ds(pl.multiple_of(i * step, step), step)
+        total_ = terms[0][at, :].astype(F32)
+        for t in terms[1:]:
+            total_ = total_ + t[at, :].astype(F32)
+        out[at, :] = total_.astype(out.dtype)
+        return 0
+
+    lax.fori_loop(0, out.shape[0] // step, piece, 0)
+
+
 def greet_neighbours(n_f, ring):
     me_d, me_f = lax.axis_index("dp"), lax.axis_index("fsdp")
     barrier = pltpu.get_barrier_semaphore()
@@ -145,9 +277,12 @@
     g = pl.program_id(0)
     n_dp, tok = part.shape[:2]
     rows, width = x_ref.shape
-    hops = [ring_copy(n_f, wo_ref, next_ref.at[up], hop_send.at[up], hop_recv.at[up], up) for up in (0, 1)]
+    hops = [ring_copy(n_f, wo_ref, next_ref.at[up, 0], hop_send.at[up, 0], hop_recv.at[up, 0], up) for up in (0, 1)]
+    hops2 = [
+        ring_copy(n_f, next_ref.at[up, 0], next_ref.at[up, 1], hop_send.at[up, 1], hop_recv.at[up, 1], up)
+        for up in (0, 1)
+    ]
     group = GroupSum(part, near, far, total, gs_send, gs_recv)
-    piece = 256
 
     @pl.when(g == 0)
     def _():
@@ -164,6 +299,12 @@
             return 0
 
         lax.fori_loop(0, rows // 32, norm, 0)
+
+    @pl.when(g == half)
+    def _():
+        for a, b in zip(hops, hops2):
+            a.wait_recv()
+            b.start()
 
     @pl.when(g < half)
     def _():
@@ -200,8 +341,9 @@
     def _():
         group.finish()
         dbl_ref[...] = total[...]
-        for c in hops:
-            c.wait()
+        for a, b in zip(hops, hops2):
+            a.wait_send()
+            b.wait()
 
 
 def enter(lens, x_all, gain, wx, wg, taps, bias, sel, wo_block, n_f):
@@ -248,10 +390,10 @@
             shaped(ch, BF16),
             shaped(ch, F32),
             jax.ShapeDtypeStruct((n_dp, tok, wide), F32),
-            jax.ShapeDtypeStruct((2,) + wo_block.shape, BF16),
+            jax.ShapeDtypeStruct((2, 2) + wo_block.shape, BF16),
         ],
         scratch_shapes=GroupSum.scratch(tok, wide)
-        + [pltpu.SemaphoreType.DMA((2,)), pltpu.SemaphoreType.DMA((2,))],
+        + [pltpu.SemaphoreType.DMA((2, 2)), pltpu.SemaphoreType.DMA((2, 2))],
         compiler_params=pltpu.CompilerParams(
             collective_id=1, has_side_effects=True, vmem_limit_bytes=48 * 2**20
         ),
@@ -278,12 +420,14 @@
     return jnp.where(lax.rem(i, TB) == j // n, spread, 0.0).astype(BF16)
 
 
-def columns_of(m):
+def turned(m):
     n = m.shape[1]
     i = lax.broadcasted_iota(jnp.int32, (n, n), 0)
     j = lax.broadcasted_iota(jnp.int32, (n, n), 1)
     eye = jnp.where(i == j, 1.0, 0.0)
-    return jnp.sum(m[:, None, :] * eye[None], axis=2, keepdims=True)
+    return lax.dot_general(
+        eye, m, (((1,), (1,)), ((), ())), preferred_element_type=F32, precision=lax.Precision.HIGHEST
+    )
 
 
 def softplus(v):
@@ -295,16 +439,16 @@
         q = ring_place(lax.axis_index("fsdp"), n_f)
         at = lambda k: ring_index(lax.rem(q + k, n_f), n_f)
         count = [n_f // 2, n_f - 1 - n_f // 2]
-        self.locals = [
-            pltpu.make_async_copy(mine, out.at[at(0)], local.at[0]),
-            pltpu.make_async_copy(near.at[0], out.at[at(1)], local.at[1]),
-            pltpu.make_async_copy(near.at[1], out.at[at(n_f - 1)], local.at[2]),
-        ]
+        known = near.shape[1]
+        self.locals = [pltpu.make_async_copy(mine, out.at[at(0)], local.at[0])]
         self.hops = [[], []]
         for up in (0, 1):
-            for h in range(1, count[up]):
+            for j in range(known):
+                index = at(n_f - 1 - j if up else 1 + j)
+                self.locals.append(pltpu.make_async_copy(near.at[up, j], out.at[index], local.at[1 + known * up + j]))
+            for h in range(known, count[up]):
                 index = at(n_f - h if up else h)
-                src = near.at[up] if h == 1 else out.at[index]
+                src = near.at[up, known - 1] if h == known else out.at[index]
                 self.hops[up].append(
                     ring_copy(n_f, src, out.at[index], send.at[up, h], recv.at[up, h], up)
                 )
@@ -334,7 +478,7 @@
 
 
 def fwd_kernel(lanes, n_f, lens_ref, dbl_ref, act_ref, stepw_ref, stepb_ref, rate_ref, skip_ref, wo_ref, next_ref,
-               y_ref, s_ref, delta_ref, pre_ref, wo_all, carry, big_s, cw_s, d_s, u_s, sc, local, hop_send, hop_recv):
+               y_ref, s_ref, delta_ref, pre_ref, wo_all, carry, big_s, cw_s, bt_s, d_s, u_s, sc, local, hop_send, hop_recv):
     n, ch = rate_ref.shape
     tblk = act_ref.shape[0]
     low_n = stepw_ref.shape[0]
@@ -363,6 +507,9 @@
     since, _ = segment_span(lens_ref, pl.program_id(0), pl.program_id(1) * tblk, tblk)
     big_s[...] = jnp.where(since == 0, RESET, 0.0)
     cw_s[...] = block_rows(dbl_ref[:, low_n + n : low_n + 2 * n], n)
+    flat = turned(dbl_ref[:, low_n : low_n + n])
+    for i in range(tblk // TB):
+        bt_s[i] = flat[:, i * TB : (i + 1) * TB]
 
     def chunk(i, _):
         base = pl.multiple_of(i * TB, TB)
@@ -370,14 +517,14 @@
         ac = act_ref[pl.ds(base, TB), :].astype(F32)
         d_s[...] = dl + big_s[pl.ds(base, TB), :]
         u_s[...] = dl * ac
-        bt = columns_of(dbl_ref[pl.ds(base, TB), low_n : low_n + n])
+        bt = bt_s[i]
         for lo in range(0, ch, lanes):
             cs = pl.ds(lo, lanes)
             rate = rate_ref[:, cs]
             s = carry[:, cs]
             for t in range(TB):
                 dec = jnp.exp2(d_s[t : t + 1, cs] * rate)
-                s = dec * s + bt[t] * u_s[t : t + 1, cs]
+                s = dec * s + bt[:, t : t + 1] * u_s[t : t + 1, cs]
                 sc[t * n : (t + 1) * n, cs] = s.astype(BF16)
             carry[:, cs] = s
         states = sc[...]
@@ -433,10 +580,11 @@
             pltpu.VMEM((n, ch), F32),
             pltpu.VMEM((tblk, 1), F32),
             pltpu.VMEM((tblk, TB * n), BF16),
+            pltpu.VMEM((tblk // TB, n, TB), F32),
             pltpu.VMEM((TB, ch), F32),
             pltpu.VMEM((TB, ch), F32),
             pltpu.VMEM((TB * n, ch), BF16),
-            pltpu.SemaphoreType.DMA((3,)),
+            pltpu.SemaphoreType.DMA((5,)),
             pltpu.SemaphoreType.DMA((2, n_f)),
             pltpu.SemaphoreType.DMA((2, n_f)),
         ],
@@ -448,9 +596,10 @@
 
 
 def bwd_kernel(lanes, n_f, lens_ref, dbl_ref, delta_ref, pre_ref, act_ref, gy_ref, stepw_ref, rate_ref, skip_ref,
-               s_ref, sp_ref,
-               pg_ref, da_ref, dbl_grad_ref, dl_ref, sums_ref, stepg_ref,
-               carry, big_s, bw_s, d_s, u_s, g_s, h_s, part, near, far, total, gs_send, gs_recv):
+               s_ref, sp_ref, wg_part, mixed_part,
+               pg_ref, da_ref, dbl_grad_ref, dl_ref, sums_ref, stepg_ref, wg_own, mixed_own,
+               carry, big_s, bw_s, ct_s, d_all, u_all, g_all, h_all, b_all, c_all, part, near, far, total, gs_send, gs_recv,
+               ring_got, ring_send, ring_recv, mix, mix_near, mix_far, mix_send, mix_recv, mix_load):
     n, ch = rate_ref.shape
     tblk = act_ref.shape[0]
     low_n = stepw_ref.shape[0]
@@ -458,23 +607,42 @@
     n_dp, nb = pl.num_programs(0), pl.num_programs(1)
     m = row_at(r, n_dp)
     group = GroupSum(part, near, far, total, gs_send, gs_recv)
-
+    ring = RingReduce(n_f, wg_part, ring_got, ring_send, ring_recv, n_f // 2)
+    pairs = PairReduce(mix, mix_near, mix_far, mix_send, mix_recv)
+    now = r * nb + j
+    last_step = n_dp * nb - 1
     @pl.when(j == 0)
     def _():
         carry[...] = jnp.zeros_like(carry)
 
     @pl.when((r == 0) & (j == 0))
     def _():
-        greet_neighbours(n_f, False)
+        load = pltpu.make_async_copy(mixed_part, mix, mix_load)
+        load.start()
+        greet_neighbours(n_f, True)
+        ring.start()
+        load.wait()
+        pairs.start()
         dl_ref[...] = jnp.zeros_like(dl_ref)
         sums_ref[...] = jnp.zeros_like(sums_ref)
         stepg_ref[...] = jnp.zeros_like(stepg_ref)
 
+    for e in range(1, ring.events):
+
+        @pl.when(now == min(4 * e, 15))
+        def _(e=e):
+            ring.event(e)
+
+    @pl.when(now == 2)
+    def _():
+        pairs.middle()
+
+    @pl.when(now == 12)
+    def _():
+        pairs.finish(mixed_own)
+
     ones = jnp.where(own_token(n), 1.0, 0.0).astype(BF16)
     nt = (((1,), (1,)), ((), ()))
-    row = lax.broadcasted_iota(jnp.int32, (TB * n, TB), 0)
-    col = lax.broadcasted_iota(jnp.int32, (TB * n, TB), 1)
-    mask = row // n == col
     row = lax.broadcasted_iota(jnp.int32, (TB * n, n), 0)
     col = lax.broadcasted_iota(jnp.int32, (TB * n, n), 1)
     fold = jnp.where(lax.rem(row, n) == col, 1.0, 0.0)
@@ -482,54 +650,72 @@
     big_s[...] = jnp.where(since == 0, RESET, 0.0)
     bw_s[...] = block_rows(dbl_ref[:, low_n : low_n + n], n)
 
-    def diagonal(left, right):
-        every = lax.dot_general(left, right, nt, preferred_element_type=F32)
-        column = jnp.sum(jnp.where(mask, every, 0.0), axis=1, keepdims=True)
-        return jnp.sum((column * fold).reshape(TB, n, n), axis=1)
-
-    def chunk(back, _):
-        i = tblk // TB - 1 - back
-        base = pl.multiple_of(i * TB, TB)
-        sbase = pl.multiple_of(i * TB * n, TB * n)
-        dl = delta_ref[pl.ds(base, TB), :]
-        ac = act_ref[pl.ds(base, TB), :].astype(F32)
-        d_s[...] = dl + big_s[pl.ds(base, TB), :]
+    flat = turned(dbl_ref[:, low_n + n : low_n + 2 * n])
+    for i in range(tblk // TB):
+        ct_s[i] = flat[:, i * TB : (i + 1) * TB]
+
+    def lane_sum(value):
+        total_ = value[:, :128]
+        for at in range(128, value.shape[1], 128):
+            total_ = total_ + value[:, at : at + 128]
+        return total_
+
+    def gathered(sums):
+        spread = jnp.sum(sums, axis=1, keepdims=True) * fold
+        high = spread.astype(BF16)
+        rest = (spread - high.astype(F32)).astype(BF16)
+        return jnp.dot(ones, high, preferred_element_type=F32) + jnp.dot(ones, rest, preferred_element_type=F32)
+
+    for i in reversed(range(tblk // TB)):
+        base = i * TB
+        d_s, u_s, g_s, h_s, b_s, c_s = (v.at[i % 2] for v in (d_all, u_all, g_all, h_all, b_all, c_all))
+        dl = delta_ref[base : base + TB, :]
+        ac = act_ref[base : base + TB, :].astype(F32)
+        d_s[...] = dl + big_s[base : base + TB, :]
         u_s[...] = dl * ac
-        ct = columns_of(dbl_ref[pl.ds(base, TB), low_n + n : low_n + 2 * n])
-        before = pl.multiple_of(jnp.maximum(sbase - n, 0), n)
+        ct = ct_s[i]
         for lo in range(0, ch, lanes):
             cs = pl.ds(lo, lanes)
             rate = rate_ref[:, cs]
             flow = carry[:, cs]
             acc = dl_ref[:, cs]
+            here = s_ref[(base + TB - 1) * n : (base + TB) * n, cs].astype(F32)
             for t in reversed(range(TB)):
                 dr = d_s[t : t + 1, cs]
                 dec = jnp.exp2(dr * rate)
-                g = ct[t] * gy_ref[pl.ds(base + t, 1), cs] + flow
+                gy = gy_ref[base + t : base + t + 1, cs]
+                g = ct[:, t : t + 1] * gy + flow
                 flow = dec * g
-                if t > 0:
-                    prev = s_ref[pl.ds(sbase + (t - 1) * n, n), cs]
+                if base + t > 0:
+                    prev = s_ref[(base + t - 1) * n : (base + t) * n, cs].astype(F32)
                 else:
-                    prev = jnp.where(i > 0, s_ref[pl.ds(before, n), cs], sp_ref[:, cs])
-                h = flow * prev.astype(F32)
+                    prev = sp_ref[:, cs].astype(F32)
+                h = flow * prev
                 acc = acc + h * dr
+                at = slice(t * n, (t + 1) * n)
+                b_now = lane_sum(g * u_s[t : t + 1, cs])
+                c_now = lane_sum(here * gy)
+                if lo:
+                    b_now = b_now + b_s[at, :]
+                    c_now = c_now + c_s[at, :]
+                b_s[at, :] = b_now
+                c_s[at, :] = c_now
+                here = prev
                 g_s[t * n : (t + 1) * n, cs] = g.astype(BF16)
                 h_s[t * n : (t + 1) * n, cs] = (h * rate).astype(BF16)
             carry[:, cs] = flow
             dl_ref[:, cs] = acc
         gb = g_s[...]
-        gy = gy_ref[pl.ds(base, TB), :]
-        du = jnp.dot(bw_s[pl.ds(base, TB), :], gb, preferred_element_type=F32)
+        gy = gy_ref[base : base + TB, :]
+        du = jnp.dot(bw_s[base : base + TB, :], gb, preferred_element_type=F32)
         hr = jnp.dot(ones, h_s[...], preferred_element_type=F32)
         dd = hr * (1.0 / LOG2E) + du * ac
-        pg_ref[pl.ds(base, TB), :] = (dd * jax.nn.sigmoid(pre_ref[pl.ds(base, TB), :])).astype(BF16)
-        da_ref[pl.ds(base, TB), :] = du * dl + skip_ref[...] * gy
+        pg_ref[base : base + TB, :] = (dd * jax.nn.sigmoid(pre_ref[base : base + TB, :])).astype(BF16)
+        da_ref[base : base + TB, :] = du * dl + skip_ref[...] * gy
         at = pl.ds(pl.multiple_of((nb - 1 - j) * tblk + base, TB), TB)
-        part[m, at, low_n : low_n + n] = diagonal(gb, u_s[...].astype(BF16))
-        part[m, at, low_n + n : low_n + 2 * n] = diagonal(s_ref[pl.ds(sbase, TB * n), :], gy.astype(BF16))
-        return 0
-
-    lax.fori_loop(0, tblk // TB, chunk, 0)
+        part[m, at, low_n : low_n + n] = gathered(b_s[...])
+        part[m, at, low_n + n : low_n + 2 * n] = gathered(c_s[...])
+
     pg = pg_ref[...]
     part[m, pl.ds(pl.multiple_of((nb - 1 - j) * tblk, tblk), tblk), :low_n] = lax.dot_general(
         pg, stepw_ref[...], nt, preferred_element_type=F32
@@ -546,11 +732,13 @@
 
     @pl.when((j == nb - 1) & (r == n_dp - 1))
     def _():
+        ring.finish(wg_own)
         group.finish()
         dbl_grad_ref[...] = total[...]
 
 
-def scan_backward(lens, dbl, delta, pre, act, gy, stepw, rate2, skip, states, n_f, row_len, tblk=64, lanes=512):
+def scan_backward(lens, dbl, delta, pre, act, gy, stepw, rate2, skip, states, wg_part, mixed_part, n_f, row_len,
+                  tblk=64, lanes=512):
     t, ch = delta.shape
     n = rate2.shape[0]
     nb = row_len // tblk
@@ -575,6 +763,8 @@
             pl.BlockSpec((1, ch), zero),
             pl.BlockSpec((tblk * n, ch), at),
             pl.BlockSpec((n, ch), entry),
+            pl.BlockSpec(memory_space=pltpu.VMEM),
+            pl.BlockSpec(memory_space=pl.ANY),
         ],
         out_specs=[
             pl.BlockSpec((tblk, ch), at),
@@ -583,6 +773,8 @@
             pl.BlockSpec((n, ch), zero),
             pl.BlockSpec((8, ch), zero),
             pl.BlockSpec(stepw.shape, zero),
+            pl.BlockSpec(wg_part.shape[1:], zero),
+            pl.BlockSpec(mixed_part.shape[1:], zero),
         ],
         out_shape=[
             jax.ShapeDtypeStruct((t, ch), BF16),
@@ -591,22 +783,31 @@
             jax.ShapeDtypeStruct((n, ch), F32),
             jax.ShapeDtypeStruct((8, ch), F32),
             jax.ShapeDtypeStruct(stepw.shape, F32),
+            jax.ShapeDtypeStruct(wg_part.shape[1:], BF16),
+            jax.ShapeDtypeStruct(mixed_part.shape[1:], F32),
         ],
         scratch_shapes=[
             pltpu.VMEM((n, ch), F32),
             pltpu.VMEM((tblk, 1), F32),
             pltpu.VMEM((tblk, TB * n), BF16),
-            pltpu.VMEM((TB, ch), F32),
-            pltpu.VMEM((TB, ch), F32),
-            pltpu.VMEM((TB * n, ch), BF16),
-            pltpu.VMEM((TB * n, ch), BF16),
+            pltpu.VMEM((tblk // TB, n, TB), F32),
+            pltpu.VMEM((2, TB, ch), F32),
+            pltpu.VMEM((2, TB, ch), F32),
+            pltpu.VMEM((2, TB * n, ch), BF16),
+            pltpu.VMEM((2, TB * n, ch), BF16),
+            pltpu.VMEM((2, TB * n, 128), F32),
+            pltpu.VMEM((2, TB * n, 128), F32),
         ]
-        + GroupSum.scratch(row_len, wide),
+        + GroupSum.scratch(row_len, wide)
+        + RingReduce.scratch(n_f, wg_part.shape[1:])
+        + [pltpu.VMEM(mixed_part.shape, BF16)]
+        + PairReduce.scratch(mixed_part.shape[1:])
+        + [pltpu.SemaphoreType.DMA],
         compiler_params=pltpu.CompilerParams(
-            collective_id=3, has_side_effects=True, vmem_limit_bytes=40 * 2**20
+            collective_id=3, has_side_effects=True, vmem_limit_bytes=56 * 2**20
         ),
         cost_estimate=pl.CostEstimate(flops=t * n * ch * 80, bytes_accessed=t * ch * 60, transcendentals=t * n * ch),
-    )(lens, dbl, delta, pre, act, gy, stepw, rate2, skip, states, states)
+    )(lens, dbl, delta, pre, act, gy, stepw, rate2, skip, states, states, wg_part, mixed_part)
 
 
 def ring_order(count):
@@ -1126,22 +1327,19 @@
     wo = wo.reshape(ch, width)
     gate_silu = jax.nn.silu(gate)
     gated = (scan_out * gate_silu).astype(BF16)
-    mixed_part = flat_dot(gated, wo).astype(BF16)
-    mixed = group_reduce(split(mixed_part), n_dp, BF16)
+    mixed_part = flat_dot(gated, wo).astype(BF16).reshape(n_dp, tok, width)
 
     gated_grad = nt_dot(dy_all, wo)
     scan_grad = gated_grad * gate_silu
     gate_grad = (gated_grad * scan_out * silu_slope(gate)).astype(BF16)
     wg_grad = tn_dot(normed, gate_grad).astype(BF16)
     wo_grad = tn_dot(gated, dy_all).astype(BF16)
-    wg_own = ring_reduce(
-        lambda k: lax.dynamic_slice_in_dim(wg_grad, at_ring[k] * dcols, dcols, 0), n_f, n_f // 2, BF16
-    )
     wo_own = ring_reduce(
         lambda k: lax.dynamic_slice_in_dim(wo_grad, at_ring[k] * cs, cs, 0), n_f, n_f - 1 - n_f // 2, BF16
     )
-    pre_grad, act_grad, dbl_grad, decay_sum, sums, step_grad = scan_backward(
-        lens, dbl, delta, pre, act, scan_grad, stepw, rate2, skip, states, n_f, tok
+    pre_grad, act_grad, dbl_grad, decay_sum, sums, step_grad, wg_own, mixed = scan_backward(
+        lens, dbl, delta, pre, act, scan_grad, stepw, rate2, skip, states,
+        wg_grad.reshape(n_f, dcols, ch), mixed_part, n_f, tok,
     )
     dbl_grad = dbl_grad.reshape(group, -1).astype(BF16)
     act_grad = act_grad + flat_dot(dbl_grad, sel)
@@ -1203,7 +1401,6 @@
     hat_grad = normed_grad * gain[None]
     change = rstd * (hat_grad - hat * jnp.mean(hat_grad * hat, axis=1, keepdims=True))
     row_grad = (dy_own.astype(F32) + change).astype(BF16)
-    layer = (x_own32 + mixed).astype(BF16)
 
     def returned(value):
         cols = value.shape[1]
@@ -1216,13 +1413,14 @@
     for j, value in enumerate(mine_sums):
         high = value.astype(BF16).astype(F32)
         ride = ride + jnp.where(lanes == 2 * j, high, 0.0) + jnp.where(lanes == 2 * j + 1, value - high, 0.0)
-    out = flat_dot(from_row, jnp.concatenate([layer, mixed.astype(BF16)], axis=1)).astype(BF16)
-    out = jnp.concatenate([out, ride.astype(BF16)], axis=1).reshape(rows, pair, 2 * width + 128)
-    back = lax.all_to_all(out, both, 0, 0, tiled=True).reshape(tok, 2 * width + 128)
-    totals = jnp.sum(back.reshape(rows, pair, -1)[:, 0, 2 * width : 2 * width + 4].astype(F32), axis=0)
+    out = flat_dot(from_row, mixed.astype(BF16)).astype(BF16)
+    out = jnp.concatenate([out, ride.astype(BF16)], axis=1).reshape(rows, pair, width + 128)
+    back = lax.all_to_all(out, both, 0, 0, tiled=True).reshape(tok, width + 128)
+    totals = jnp.sum(back.reshape(rows, pair, -1)[:, 0, width : width + 4].astype(F32), axis=0)
     input_rms = jnp.sqrt((totals[0] + totals[1]) / ((totals[2] + totals[3]) * width))
-    layer_output = flat_dot(from_send, back[:, :width]).astype(BF16)
-    mixer_output = flat_dot(from_send, back[:, width : 2 * width]).astype(BF16)
+    mixer_output = flat_dot(from_send, back[:, :width])
+    layer_output = (tokens.astype(F32) + mixer_output).astype(BF16)
+    mixer_output = mixer_output.astype(BF16)
     input_grad = returned(row_grad)
     return (
         layer_output,

time: 764 us -> 676 us (0.88)
  the two profiles are of different devices: /device:TPU:21 before, /device:TPU:0 now
where the time goes in v4:
time: 676 us; the launch traced here: 665 us
  Pallas kernels  319 us (47%)
  matrix products  87.5 us (13%)
  waiting for transfers between devices  86.9 us (13%)
  local copies, waits for them, and re-layouts  50.9 us (8%)
  other arithmetic  46.8 us (7%)
  starting transfers between devices  38.1 us (6%)
  between operations  35.3 us (5%)
    pallas_call x1, Pallas kernels, gather_all(): pl.pallas_call(functools.partial(gather_kernel, n_dp, n_f, downs), in_spe...  144 us
    pallas_call x1, Pallas kernels, scan_backward(): pl.pallas_call(functools.partial(bwd_kernel, min(lanes, ch), n_f), grid=(...  79.9 us
    ppermute x21, waiting for transfers between devices, ring_step(): return lax.ppermute(value, 'fsdp', pairs)  53.3 us
    pallas_call x1, Pallas kernels, enter(): pl.pallas_call(functools.partial(enter_kernel, n_f, half), grid=(2 * half...  42 us
    pallas_call x1, Pallas kernels, scan_forward(): pl.pallas_call(functools.partial(fwd_kernel, min(lanes, ch), n_f), grid=(...  36.6 us
    dot_general x6, matrix products, per_device(): flat_dot = lambda a, b: jnp.dot(a, b, preferred_element_type=F32)  35.1 us
    ppermute x10, waiting for transfers between devices, swap(): return lax.ppermute(value, 'dp', [(i, i ^ mask) for i in range(count)])  30.4 us
    dot_general x3, matrix products, per_device(): lax.dot_general(a, b, (((1,), (1,)), ((), ())), preferred_element_type=F32)  28.7 us
  transfers between devices with their start and end apart: 33, of which 14 were waited for; matrix products, arithmetic and copies ran while one was open for 19% of the time, Pallas kernels for 14%

profile of v4, /device:TPU:0, one launch (start us, length us, event | category | flops | bytes accessed | tf_op | source)
XLA Modules:
  0.0 664.6 jit_solution(13763253331618901945)
XLA Ops:
  19.0 4.1 shard_map.263
  28.3 143.9 %shard_map.264 = (bf16[4,256,2048]{2,1,0:T(8,128)(2,1)S(1)}, bf16[4,256,2048]{2,1,0:T(8,128)(2,1)}, s32[4,8,128]{2,1,0:T(8,128)S(1)}, bf16[256,2048]{1,0:T(8,128...) custom-call(bf16[256,2048]{1,0:T(8,128)(2,1)S(1)} %copy-done.8, ...), custom_call_target="tpu_custom_call" | custom-call | flops 10000000000 | bytes 200000000 | tf_op jit(solution)/shard_map/pallas_call | solution.py:1096
  175.6 42.0 %shard_map.265 = (bf16[1024,2048]{1,0:T(8,128)(2,1)}, f32[1024,1024]{1,0:T(8,128)}, f32[1024,1024]{1,0:T(8,128)}, bf16[1024,1024]{1,0:T(8,128)(2,1)S(1)}, f32[10...) custom-call(s32[4,4]{1,0:T(4,128)S(1)} %bitcast.224, ...), custom_call_target="tpu_custom_call" | custom-call | flops 10000000000 | bytes 40000000 | tf_op jit(solution)/shard_map/pallas_call | solution.py:363
  221.7 36.6 %shard_map.266 = (f32[1024,1024]{1,0:T(8,128)S(1)}, bf16[16384,1024]{1,0:T(8,128)(2,1)}, f32[1024,1024]{1,0:T(8,128)S(1)}, f32[1024,1024]{1,0:T(8,128)S(1)}, bf16[8,128,2048]{2,1,0:T(8,128)(2,1)S(1)}) custom-call(s32[4,4]{1,0:T(4,128)S(1)} %bitcast.225, f32[1024,160]{1,0:T(8,128)S(1)} %bitcast.215, bf16[1024,1024]{1,0:T(8,128)(2,1)S(1)} %get-tuple-element.57.act_ref, ...), custom_call_target="tpu_custom_call" | custom-call | flops 671088640 | bytes 54525952 | tf_op jit(solution)/shard_map/pallas_call | solution.py:551
  262.4 14.9 %multiply_convert_fusion = (bf16[1024,1024]{1,0:T(8,128)(2,1)S(1)}, bf16[1024,1024]{1,0:T(8,128)(2,1)}, f32[1024,1024]{1,0:T(8,128)}) fusion(f32[1024,1024]{1,0:T(8,128)S(1)} %get-tuple-element.66, f32[1024,1024]{1,0:T(8,128)} %get-tuple-element.63, bf16[1024,2048]{1,0:T(8,128)(2,1)} %bitcast.289, bf16[1024,2048]{1,0:T(8,128)(2,1)} %bitcast.232), kind=kOutput, calls=%fused_computation.9 | convolution fusion | flops 4309647360 | bytes 25165824 | tf_op jit(solution)/shard_map/dot_general | solution.py:1240
  277.3 6.7 %convolution_convert_fusion = bf16[1024,2048]{1,0:T(8,128)(2,1)} fusion(bf16[1024,1024]{1,0:T(8,128)(2,1)S(1)} %get-tuple-element.87, bf16[1024,2048]{1,0:T(8,128)(2,1)S(1)} %bitcast.290), kind=kOutput, calls=%fused_computation.13 | convolution fusion | flops 4297064448 | bytes 10485760 | tf_op jit(solution)/shard_map/dot_general | solution.py:1241
  294.7 9.4 %convolution_convert_fusion.2 = bf16[1024,2048]{1,0:T(8,128)(2,1)} fusion(bf16[1024,1024]{1,0:T(8,128)(2,1)} %copy-done.49, bf16[1024,2048]{1,0:T(8,128)(2,1)} %bitcast.233), kind=kOutput, calls=%fused_computation.15 | convolution fusion | flops 4297064448 | bytes 10485760 | tf_op jit(solution)/shard_map/dot_general | solution.py:1239
  305.1 9.4 %convolution_convert_fusion.3 = bf16[2048,1024]{1,0:T(8,128)(2,1)} fusion(bf16[1024,2048]{1,0:T(8,128)(2,1)} %get-tuple-element.65, bf16[1024,1024]{1,0:T(8,128)(2,1)} %get-tuple-element.88), kind=kOutput, calls=%fused_computation.16 | convolution fusion | flops 4297064448 | bytes 10485760 | tf_op jit(solution)/shard_map/dot_general | solution.py:1241
  314.6 79.9 %shard_map.267 = (bf16[1024,1024]{1,0:T(8,128)(2,1)}, f32[1024,1024]{1,0:T(8,128)}, f32[4,256,160]{2,1,0:T(8,128)}, f32[16,1024]{1,0:T(8,128)}, f32[8,1024]{1,0:...) custom-call(s32[4,4]{1,0:T(4,128)} %bitcast.226, f32[1024,160]{1,0:T(8,128)} %bitcast.216, ...), custom_call_target="tpu_custom_call" | custom-call | flops 1342177280 | bytes 62914560 | tf_op jit(solution)/shard_map/pallas_call | solution.py:751
  417.3 14.2 %fusion.42 = (f32[1024]{0:T(1024)S(1)}, f32[1024]{0:T(1024)S(1)}, f32[1024]{0:T(1024)S(1)}, f32[1024]{0:T(1024)S(1)}, f32[1024]{0:T(1024)S(1)}, /*index=5*/f32[1024,1024]{1,0:T(8,128)}) fusion(f32[1024]{0:T(1024)S(1)} %get-tuple-element.143, f32[1024,1024]{1,0:T(8,128)} %get-tuple-element.76, f32[1024]{0:T(1024)S(1)} %get-tuple-element.142, ...), kind=kOutput, calls=%fused_computation.202 | convolution fusion | flops 358607872 | bytes 30224384 | tf_op jit(solution)/shard_map/dot_general | solution.py:1239
  450.7 6.2 convolution_convert_fusion.1
  456.9 6.8 %fusion.52 = f32[1024,2048]{1,0:T(8,128)} fusion(bf16[1024,1024]{1,0:T(8,128)(2,1)S(1)} %add_convert_fusion.1, bf16[2048,1024]{1,0:T(8,128)(2,1)S(1)} %bitcast.285), kind=kOutput, calls=%fused_computation.212 | convolution fusion | flops 4294967296 | bytes 14680064 | tf_op jit(solution)/shard_map/dot_general | solution.py:1240
  463.7 7.0 %add_convert_fusion = bf16[1024,2048]{1,0:T(8,128)(2,1)S(1)} fusion(f32[1024,2048]{1,0:T(8,128)} %fusion.52, bf16[1024,1024]{1,0:T(8,128)(2,1)S(1)} %copy-done.51, bf16[2048,1024]{1,0:T(8,128)(2,1)S(1)} %bitcast.283), kind=kOutput, calls=%fused_computation.1 | convolution fusion | flops 4299161600 | bytes 18874368 | tf_op jit(solution)/shard_map/dot_general | solution.py:1240
  498.1 10.3 %collective-permute-done.15 = f32[320,128]{1,0:T(8,128)S(1)} collective-permute-done((f32[320,128]{1,0:T(8,128)S(1)}, f32[320,128]{1,0:T(8,128)S(1)}, u32[]{:S(2)}, u32[]{:S(2)}) %collective-permute-start.15) | collective-permute-done | bytes 163872 | tf_op jit(solution)/shard_map/ppermute | solution.py:823
  517.5 13.0 %collective-permute-done.26 = bf16[128,2048]{1,0:T(8,128)(2,1)S(1)} collective-permute-done((bf16[128,2048]{1,0:T(8,128)(2,1)S(1)}, bf16[128,2048]{1,0:T(8,128)(2,1)S(1)}, u32[]{:S(2)}, u32[]{:S(2)}) %collective-permute-start.26) | collective-permute-done | bytes 524320 | tf_op jit(solution)/shard_map/ppermute | solution.py:823
  536.5 10.0 %collective-permute-done.23 = bf16[128,2048]{1,0:T(8,128)(2,1)S(1)} collective-permute-done((bf16[128,2048]{1,0:T(8,128)(2,1)S(1)}, bf16[128,2048]{1,0:T(8,128)(2,1)S(1)}, u32[]{:S(2)}, u32[]{:S(2)}) %collective-permute-start.23) | collective-permute-done | bytes 524320 | tf_op jit(solution)/shard_map/ppermute | solution.py:823
  552.6 5.2 collective-permute-done.4
  563.7 5.4 collective-permute-done.24
  569.0 3.6 collective-permute-done.28
  590.7 27.1 %collective-permute-done.9 = bf16[1,256,1024]{2,1,0:T(8,128)(2,1)} collective-permute-done((bf16[1,256,1024]{2,1,0:T(8,128)(2,1)S(1)}, bf16[1,256,1024]{2,1,0:T(8,128)(2,1)}, u32[]{:S(2)}, u32[]{:S(2)}) %collective-permute-start.9) | collective-permute-done | bytes 524320 | tf_op jit(solution)/shard_map/ppermute | solution.py:847
  624.6 3.5 fusion.3
  628.1 4.7 all-to-all-start.1
  634.1 3.8 maximum_maximum_fusion.x_ref
  637.9 12.4 %shard_map.268 = (f32[256,8192]{1,0:T(8,128)}, f32[256,128]{1,0:T(8,128)}) custom-call(bf16[4,256,2048]{2,1,0:T(8,128)(2,1)} %maximum_maximum_fusion.x_ref, bf16[256,8192]{1,0:T(8,128)(2,1)} %w_ref.3), custom_call_target="tpu_custom_call" | custom-call | flops 8388608 | bytes 16777216 | tf_op jit(solution)/shard_map/pallas_call | solution.py:1184
  (272 shorter events, 149.2 us)
Async XLA Ops:
  286.3 231.1 %collective-permute-start.22 = (bf16[128,2048]{1,0:T(8,128)(2,1)}, bf16[128,2048]{1,0:T(8,128)(2,1)}, u32[]{:S(2)}, u32[]{:S(2)}) collective-permute-start(bf16[128,2048]{1,0:T(8,128)(2,1)} %get-tuple-element.94), channel_id=1, source_target_pairs={{0,1},{2,0},{4,2},{6,4},{7,6},{5,7},{3,5},{1,3},{8,9},{10,8},{12,1... | collective-permute-start | bytes 1572872 | tf_op jit(solution)/shard_map/ppermute | solution.py:823
  288.7 207.5 %collective-permute-start.25 = (bf16[128,2048]{1,0:T(8,128)(2,1)}, bf16[128,2048]{1,0:T(8,128)(2,1)}, u32[]{:S(2)}, u32[]{:S(2)}) collective-permute-start(bf16[128,2048]{1,0:T(8,128)(2,1)} %get-tuple-element.95), channel_id=1, source_target_pairs={{0,2},{2,4},{4,6},{6,7},{7,5},{5,3},{3,1},{1,0},{8,10},{10,12},{12... | collective-permute-start | bytes 1572872 | tf_op jit(solution)/shard_map/ppermute | solution.py:823
  397.9 185.4 %all-to-all-start = ((bf16[32,8,2176]{2,1,0:T(8,128)(2,1)}), bf16[32,8,2176]{2,1,0:T(8,128)(2,1)}, u32[]{:S(2)}, u32[]{:S(2)}) async-start(bf16[32,8,2176]{2,1,0:T(8,128)(2,1)} %maximum_bitcast_fusion), calls=%async_computation | async-start | bytes 2228224 | tf_op jit(solution)/shard_map/all_to_all | solution.py:1418
  434.2 41.8 %collective-permute-start.16 = (f32[320,128]{1,0:T(8,128)S(1)}, f32[320,128]{1,0:T(8,128)S(1)}, u32[]{:S(2)}, u32[]{:S(2)}) collective-permute-start(f32[320,128]{1,0:T(8,128)S(1)} %constant_dynamic-slice_fusion.6), channel_id=1, source_target_pairs={{0,2},{2,4},{4,6},{6,7},{7,5},{5,3},{3,1},{1,0},{8,10},{10,12},{12... | collective-permute-start | bytes 491528 | tf_op jit(solution)/shard_map/ppermute | solution.py:823
  435.8 76.5 %collective-permute-start.11 = (bf16[1,256,1024]{2,1,0:T(8,128)(2,1)}, bf16[1,256,1024]{2,1,0:T(8,128)(2,1)}, u32[]{:S(2)}, u32[]{:S(2)}) collective-permute-start(bf16[1,256,1024]{2,1,0:T(8,128)(2,1)} %bitcast.255), channel_id=1, source_target_pairs={{0,16},{8,24},{16,0},{24,8},{1,17},{9,25},{17,1},{25,9},{2,18},{10... | collective-permute-start | bytes 1572872 | tf_op jit(solution)/shard_map/ppermute | solution.py:847
  493.1 18.4 %collective-permute-start.2 = (bf16[256,1024]{1,0:T(8,128)(2,1)S(1)}, bf16[256,1024]{1,0:T(8,128)(2,1)S(1)}, u32[]{:S(2)}, u32[]{:S(2)}) collective-permute-start(bf16[256,1024]{1,0:T(8,128)(2,1)S(1)} %get-tuple-element.100), channel_id=1, source_target_pairs={{0,1},{2,0},{4,2},{6,4},{7,6},{5,7},{3,5},{1,3},{8,9},{10,8},{12,1... | collective-permute-start | bytes 1572872 | tf_op jit(solution)/shard_map/ppermute | solution.py:823
  494.7 13.7 %collective-permute-start.15 = (f32[320,128]{1,0:T(8,128)S(1)}, f32[320,128]{1,0:T(8,128)S(1)}, u32[]{:S(2)}, u32[]{:S(2)}) collective-permute-start(f32[320,128]{1,0:T(8,128)S(1)} %get-tuple-element.110), channel_id=1, source_target_pairs={{0,1},{2,0},{4,2},{6,4},{7,6},{5,7},{3,5},{1,3},{8,9},{10,8},{12,1... | collective-permute-start | bytes 491528 | tf_op jit(solution)/shard_map/ppermute | solution.py:823
  508.4 23.4 %collective-permute-start.6 = (bf16[256,1024]{1,0:T(8,128)(2,1)S(1)}, bf16[256,1024]{1,0:T(8,128)(2,1)S(1)}, u32[]{:S(2)}, u32[]{:S(2)}) collective-permute-start(bf16[256,1024]{1,0:T(8,128)(2,1)S(1)} %get-tuple-element.101), channel_id=1, source_target_pairs={{0,2},{2,4},{4,6},{6,7},{7,5},{5,3},{3,1},{1,0},{8,10},{10,12},{12... | collective-permute-start | bytes 1572872 | tf_op jit(solution)/shard_map/ppermute | solution.py:823
  509.9 20.6 %collective-permute-start.26 = (bf16[128,2048]{1,0:T(8,128)(2,1)S(1)}, bf16[128,2048]{1,0:T(8,128)(2,1)S(1)}, u32[]{:S(2)}, u32[]{:S(2)}) collective-permute-start(bf16[128,2048]{1,0:T(8,128)(2,1)S(1)} %add_convert_fusion.6), channel_id=1, source_target_pairs={{0,2},{2,4},{4,6},{6,7},{7,5},{5,3},{3,1},{1,0},{8,10},{10,12},{12... | collective-permute-start | bytes 1572872 | tf_op jit(solution)/shard_map/ppermute | solution.py:823
  512.3 61.3 %collective-permute-start = (bf16[2,256,2048]{2,1,0:T(8,128)(2,1)}, bf16[2,256,2048]{2,1,0:T(8,128)(2,1)S(1)}, u32[]{:S(2)}, u32[]{:S(2)}) collective-permute-start(bf16[2,256,2048]{2,1,0:T(8,128)(2,1)} %pad_maximum_fusion), channel_id=1, source_target_pairs={{0,8},{8,0},{16,24},{24,16},{1,9},{9,1},{17,25},{25,17},{2,10},{10... | collective-permute-start | bytes 6291464 | tf_op jit(solution)/shard_map/ppermute | solution.py:847
  516.9 16.3 %collective-permute-start.3 = (bf16[256,1024]{1,0:T(8,128)(2,1)S(1)}, bf16[256,1024]{1,0:T(8,128)(2,1)S(1)}, u32[]{:S(2)}, u32[]{:S(2)}) collective-permute-start(bf16[256,1024]{1,0:T(8,128)(2,1)S(1)} %add_convert_fusion.14), channel_id=1, source_target_pairs={{0,1},{2,0},{4,2},{6,4},{7,6},{5,7},{3,5},{1,3},{8,9},{10,8},{12,1... | collective-permute-start | bytes 1572872 | tf_op jit(solution)/shard_map/ppermute | solution.py:823
  517.4 44.5 %collective-permute-start.12 = (bf16[2,256,1024]{2,1,0:T(8,128)(2,1)S(1)}, bf16[2,256,1024]{2,1,0:T(8,128)(2,1)S(1)}, u32[]{:S(2)}, u32[]{:S(2)}) collective-permute-start(bf16[2,256,1024]{2,1,0:T(8,128)(2,1)S(1)} %pad_maximum_fusion.3), channel_id=1, source_target_pairs={{0,8},{8,0},{16,24},{24,16},{1,9},{9,1},{17,25},{25,17},{2,10},{10... | collective-permute-start | bytes 3145736 | tf_op jit(solution)/shard_map/ppermute | solution.py:847
  531.8 14.8 %collective-permute-start.23 = (bf16[128,2048]{1,0:T(8,128)(2,1)S(1)}, bf16[128,2048]{1,0:T(8,128)(2,1)S(1)}, u32[]{:S(2)}, u32[]{:S(2)}) collective-permute-start(bf16[128,2048]{1,0:T(8,128)(2,1)S(1)} %get-tuple-element.92), channel_id=1, source_target_pairs={{0,1},{2,0},{4,2},{6,4},{7,6},{5,7},{3,5},{1,3},{8,9},{10,8},{12,1... | collective-permute-start | bytes 1572872 | tf_op jit(solution)/shard_map/ppermute | solution.py:823
  533.2 18.4 %collective-permute-start.27 = (bf16[128,2048]{1,0:T(8,128)(2,1)S(1)}, bf16[128,2048]{1,0:T(8,128)(2,1)S(1)}, u32[]{:S(2)}, u32[]{:S(2)}) collective-permute-start(bf16[128,2048]{1,0:T(8,128)(2,1)S(1)} %get-tuple-element.93), channel_id=1, source_target_pairs={{0,2},{2,4},{4,6},{6,7},{7,5},{5,3},{3,1},{1,0},{8,10},{10,12},{12... | collective-permute-start | bytes 1572872 | tf_op jit(solution)/shard_map/ppermute | solution.py:823
  534.3 23.5 %collective-permute-start.4 = (bf16[256,1024]{1,0:T(8,128)(2,1)S(1)}, bf16[256,1024]{1,0:T(8,128)(2,1)S(1)}, u32[]{:S(2)}, u32[]{:S(2)}) collective-permute-start(bf16[256,1024]{1,0:T(8,128)(2,1)S(1)} %get-tuple-element.98), channel_id=1, source_target_pairs={{0,1},{2,0},{4,2},{6,4},{7,6},{5,7},{3,5},{1,3},{8,9},{10,8},{12,1... | collective-permute-start | bytes 1572872 | tf_op jit(solution)/shard_map/ppermute | solution.py:823
  552.0 17.0 %collective-permute-start.24 = (bf16[128,2048]{1,0:T(8,128)(2,1)S(1)}, bf16[128,2048]{1,0:T(8,128)(2,1)S(1)}, u32[]{:S(2)}, u32[]{:S(2)}) collective-permute-start(bf16[128,2048]{1,0:T(8,128)(2,1)S(1)} %get-tuple-element.90), channel_id=1, source_target_pairs={{0,1},{2,0},{4,2},{6,4},{7,6},{5,7},{3,5},{1,3},{8,9},{10,8},{12,1... | collective-permute-start | bytes 1572872 | tf_op jit(solution)/shard_map/ppermute | solution.py:823
  557.8 14.9 %collective-permute-start.28 = (bf16[128,2048]{1,0:T(8,128)(2,1)S(1)}, bf16[128,2048]{1,0:T(8,128)(2,1)S(1)}, u32[]{:S(2)}, u32[]{:S(2)}) collective-permute-start(bf16[128,2048]{1,0:T(8,128)(2,1)S(1)} %get-tuple-element.91), channel_id=1, source_target_pairs={{0,2},{2,4},{4,6},{6,7},{7,5},{5,3},{3,1},{1,0},{8,10},{10,12},{12... | collective-permute-start | bytes 1572872 | tf_op jit(solution)/shard_map/ppermute | solution.py:823
  560.5 19.3 %collective-permute-start.5 = (bf16[256,1024]{1,0:T(8,128)(2,1)S(1)}, bf16[256,1024]{1,0:T(8,128)(2,1)S(1)}, u32[]{:S(2)}, u32[]{:S(2)}) collective-permute-start(bf16[256,1024]{1,0:T(8,128)(2,1)S(1)} %get-tuple-element.96), channel_id=1, source_target_pairs={{0,1},{2,0},{4,2},{6,4},{7,6},{5,7},{3,5},{1,3},{8,9},{10,8},{12,1... | collective-permute-start | bytes 1572872 | tf_op jit(solution)/shard_map/ppermute | solution.py:823
  561.9 20.5 %collective-permute-start.8 = (bf16[256,1024]{1,0:T(8,128)(2,1)S(1)}, bf16[256,1024]{1,0:T(8,128)(2,1)S(1)}, u32[]{:S(2)}, u32[]{:S(2)}) collective-permute-start(bf16[256,1024]{1,0:T(8,128)(2,1)S(1)} %get-tuple-element.97), channel_id=1, source_target_pairs={{0,2},{2,4},{4,6},{6,7},{7,5},{5,3},{3,1},{1,0},{8,10},{10,12},{12... | collective-permute-start | bytes 1572872 | tf_op jit(solution)/shard_map/ppermute | solution.py:823
  572.9 47.1 %collective-permute-start.29 = (bf16[1,128,2048]{2,1,0:T(8,128)(2,1)S(1)}, bf16[1,128,2048]{2,1,0:T(8,128)(2,1)}, u32[]{:S(2)}, u32[]{:S(2)}) collective-permute-start(bf16[1,128,2048]{2,1,0:T(8,128)(2,1)S(1)} %fusion.25), channel_id=1, source_target_pairs={{0,16},{8,24},{16,0},{24,8},{1,17},{9,25},{17,1},{25,9},{2,18},{10... | collective-permute-start | bytes 1572872 | tf_op jit(solution)/shard_map/ppermute | solution.py:847
  576.9 45.7 %collective-permute-start.1 = (bf16[1,256,2048]{2,1,0:T(8,128)(2,1)}, bf16[1,256,2048]{2,1,0:T(8,128)(2,1)}, u32[]{:S(2)}, u32[]{:S(2)}) collective-permute-start(bf16[1,256,2048]{2,1,0:T(8,128)(2,1)} %fusion.12), channel_id=1, source_target_pairs={{0,16},{8,24},{16,0},{24,8},{1,17},{9,25},{17,1},{25,9},{2,18},{10... | collective-permute-start | bytes 3145736 | tf_op jit(solution)/shard_map/ppermute | solution.py:847
  582.7 35.1 %collective-permute-start.9 = (bf16[1,256,1024]{2,1,0:T(8,128)(2,1)S(1)}, bf16[1,256,1024]{2,1,0:T(8,128)(2,1)}, u32[]{:S(2)}, u32[]{:S(2)}) collective-permute-start(bf16[1,256,1024]{2,1,0:T(8,128)(2,1)S(1)} %fusion.24), channel_id=1, source_target_pairs={{0,16},{8,24},{16,0},{24,8},{1,17},{9,25},{17,1},{25,9},{2,18},{10... | collective-permute-start | bytes 1572872 | tf_op jit(solution)/shard_map/ppermute | solution.py:847
  622.1 29.8 %collective-permute-start.30 = (bf16[2,128,2048]{2,1,0:T(8,128)(2,1)}, bf16[2,128,2048]{2,1,0:T(8,128)(2,1)}, u32[]{:S(2)}, u32[]{:S(2)}) collective-permute-start(bf16[2,128,2048]{2,1,0:T(8,128)(2,1)} %pad_maximum_fusion.4), channel_id=1, source_target_pairs={{0,8},{8,0},{16,24},{24,16},{1,9},{9,1},{17,25},{25,17},{2,10},{10... | collective-permute-start | bytes 3145736 | tf_op jit(solution)/shard_map/ppermute | solution.py:847
  628.1 32.3 %all-to-all-start.1 = ((bf16[32,8,2048]{2,1,0:T(8,128)(2,1)}), bf16[32,8,2048]{2,1,0:T(8,128)(2,1)}, u32[]{:S(2)}, u32[]{:S(2)}) async-start(bf16[32,8,2048]{2,1,0:T(8,128)(2,1)} %fusion.3), calls=%async_computation.1 | async-start | bytes 2097152 | tf_op jit(solution)/shard_map/all_to_all | solution.py:1408
  (61 other events, 1045.6 us)

commit v5 on v4

--- a/solution.py
+++ b/solution.py
@@ -810,64 +810,327 @@
     )(lens, dbl, delta, pre, act, gy, stepw, rate2, skip, states, states, wg_part, mixed_part)
 
 
-def ring_order(count):
-    half = count // 2
-    if count % 2:
-        return list(range(count))
-    return [2 * p if p < half else 2 * (count - 1 - p) + 1 for p in range(count)]
-
-
-def ring_step(value, count, by):
-    order = ring_order(count)
-    pairs = [(order[p], order[(p + by) % count]) for p in range(count)]
-    return lax.ppermute(value, "fsdp", pairs)
-
-
-def ring_reduce(part, count, down, dtype):
-    total = part(0).astype(F32)
-    if down:
-        moving = part(count - down).astype(dtype)
-        for hop in range(down):
-            moving = ring_step(moving, count, -1)
-            if hop < down - 1:
-                moving = (moving.astype(F32) + part(count - down + hop + 1).astype(F32)).astype(dtype)
-        total = total + moving.astype(F32)
-    up = count - 1 - down
-    if up:
-        moving = part(up).astype(dtype)
-        for hop in range(up):
-            moving = ring_step(moving, count, 1)
-            if hop < up - 1:
-                moving = (moving.astype(F32) + part(up - hop - 1).astype(F32)).astype(dtype)
-        total = total + moving.astype(F32)
-    return total
-
-
-def swap(value, count, mask):
-    return lax.ppermute(value, "dp", [(i, i ^ mask) for i in range(count)])
+class PairShare:
+    def __init__(self, mine, out, local, send, recv):
+        me_d, me_f = lax.axis_index("dp"), lax.axis_index("fsdp")
+        self.local = pltpu.make_async_copy(mine, out.at[0], local)
+        self.copies = [
+            pltpu.make_async_remote_copy(
+                src_ref=src,
+                dst_ref=out.at[i + 1],
+                send_sem=send.at[i],
+                recv_sem=recv.at[i],
+                device_id=(flip(me_d, mask), me_f),
+                device_id_type=pl.DeviceIdType.MESH,
+            )
+            for i, (src, mask) in enumerate([(mine, 1), (mine, 2), (out.at[2], 1)])
+        ]
+
+    def start(self):
+        self.copies[1].start()
+        self.copies[0].start()
+        self.local.start()
+
+    def relay(self):
+        self.copies[1].wait_recv()
+        self.copies[2].start()
+
+    def finish(self):
+        self.copies[0].wait_recv()
+        self.copies[2].wait_recv()
+        for c in self.copies:
+            c.wait_send()
+        self.local.wait()
+
+
+class Return:
+    def __init__(self, count, n_f, buf, out, local, send, recv):
+        self.count, self.n_f, self.buf, self.out = count, n_f, buf, out
+        self.local, self.send, self.recv = local, send, recv
+        self.me = lax.axis_index("dp") * n_f + lax.axis_index("fsdp")
+
+    def fill(self, pick, values):
+        count, pair = self.buf.shape[:2]
+
+        def piece(j, _):
+            cols = pl.ds(pl.multiple_of(j * 256, 256), 256)
+            moved = jnp.dot(pick, values[:, cols].astype(BF16), preferred_element_type=F32)
+            self.buf[:, :, cols] = moved.astype(BF16).reshape(count, pair, 256)
+            return 0
+
+        lax.fori_loop(0, values.shape[1] // 256, piece, 0)
+
+    def start(self):
+        def one(p, _):
+            pltpu.make_async_remote_copy(
+                src_ref=self.buf.at[p],
+                dst_ref=self.out.at[p],
+                send_sem=self.send,
+                recv_sem=self.recv,
+                device_id=mesh_at(lax.rem(self.me + self.count - p, self.count), self.n_f),
+                device_id_type=pl.DeviceIdType.MESH,
+            ).start()
+            return 0
+
+        pltpu.make_async_copy(self.buf.at[0], self.out.at[0], self.local).start()
+        lax.fori_loop(1, self.count, one, 0)
+
+    def finish(self):
+        pltpu.make_async_copy(self.buf.at[0], self.out.at[0], self.local).wait()
+        rest = pl.ds(1, self.count - 1)
+        for sem in (self.recv, self.send):
+            pltpu.make_async_copy(self.buf.at[rest], self.out.at[rest], sem).wait()
+
+
+def leave_kernel(n_f, half, lens_ref, da_ref, conv_ref, xin_ref, act_ref, dblg_ref, sel_ref, taps_ref,
+                 sums_ref, dsum_ref, rate_ref, stepg_ref, normed_ref, wx_ref, wg_ref, gg_ref,
+                 wo_part, wg_own, x_own, dy_own, mixed_own, gain_ref, tags_ref, ride_ref,
+                 mix_back, dx_back, gx_all, gg_all, go_all, small_all,
+                 ig_s, wx_s, ng_s, small_s, pick_s, ret_mix, ret_dx, change_s,
+                 wo_got, wo_send, wo_recv, wx_got, wx_send, wx_recv, sm_got, sm_send, sm_recv,
+                 ng_near, ng_far, ng_send, ng_recv, wo_own, wx_own, sm_own, local, sh_send, sh_recv, ret_sem):
+    g = pl.program_id(0)
+    steps = pl.num_programs(0)
+    n_dp, tok, wide = dblg_ref.shape
+    count = n_dp * n_f
+    width = x_own.shape[1]
+    ch = ig_s.shape[1]
+    piece = 256
+    n_taps = taps_ref.shape[0]
+    down = n_f // 2
+    ring_o = RingReduce(n_f, wo_part, wo_got, wo_send, wo_recv, n_f - 1 - down)
+    ring_x = RingReduce(n_f, wx_s, wx_got, wx_send, wx_recv, down)
+    ring_s = RingReduce(n_f, small_s, sm_got, sm_send, sm_recv, down)
+    pairs = PairReduce(ng_s, ng_near, ng_far, ng_send, ng_recv)
+    shares = [
+        PairShare(mine, out, local.at[i], sh_send.at[i], sh_recv.at[i])
+        for i, (mine, out) in enumerate(
+            [(wg_own, gg_all), (wo_own, go_all), (wx_own, gx_all), (sm_own, small_all)]
+        )
+    ]
+    ret_m = Return(count, n_f, ret_mix, mix_back, local.at[4], ret_sem.at[0], ret_sem.at[1])
+    ret_x = Return(count, n_f, ret_dx, dx_back, local.at[5], ret_sem.at[2], ret_sem.at[3])
+    tn = (((0,), (0,)), ((), ()))
+    nt = (((1,), (1,)), ((), ()))
+
+    @pl.when(g == 0)
+    def _():
+        me = lax.axis_index("dp") * n_f + lax.axis_index("fsdp")
+        barrier = pltpu.get_barrier_semaphore()
+
+        def greet(p, _):
+            pl.semaphore_signal(
+                barrier, inc=1, device_id=mesh_at(lax.rem(me + p, count), n_f), device_id_type=pl.DeviceIdType.MESH
+            )
+            return 0
+
+        lax.fori_loop(1, count, greet, 0)
+        pl.semaphore_wait(barrier, count - 1)
+        ring_o.start()
+        shares[0].start()
+        spots = jnp.concatenate([tags_ref[...]] * (tok // 128), axis=1)
+        lane = lax.broadcasted_iota(jnp.int32, (tok, tok), 1).astype(F32)
+        pick_s[...] = jnp.where(spots == lane, 1.0, 0.0).astype(BF16)
+        ret_m.fill(pick_s[...], mixed_own)
+        ret_mix[:, :, width:] = jnp.broadcast_to(ride_ref[...], (tok, 128)).astype(BF16).reshape(
+            count, tok // count, 128
+        )
+        ret_m.start()
+
+    for e in range(1, ring_o.events - 1):
+
+        @pl.when(g == min(5 * e, 2 * half + 2))
+        def _(e=e):
+            ring_o.event(e)
+
+    @pl.when(g < half)
+    def _():
+        cols = pl.ds(pl.multiple_of(g * piece, piece), piece)
+        zero = jnp.zeros((1, piece), F32)
+        misc = [zero] * (n_taps + 1)
+        sel_grad = jnp.zeros((wide, piece), F32)
+        for m in range(n_dp):
+            at = slice(m * tok, (m + 1) * tok)
+            low = dblg_ref[m].astype(BF16)
+            since, left = segment_span(lens_ref, m, 0, tok)
+            act_grad = da_ref[at, :] + jnp.dot(low, sel_ref[...], preferred_element_type=F32)
+            conv_grad = act_grad * silu_slope(conv_ref[at, :])
+            back = taps_ref[n_taps - 1 : n_taps, :] * conv_grad
+            x_in = xin_ref[at, :]
+            misc[n_taps - 1] = misc[n_taps - 1] + jnp.sum(conv_grad * x_in, axis=0, keepdims=True)
+            for lag in range(1, n_taps):
+                tap = n_taps - 1 - lag
+                later = pltpu.roll(conv_grad, tok - lag, 0) * (left >= lag).astype(F32)
+                back = back + taps_ref[tap : tap + 1, :] * later
+                misc[tap] = misc[tap] + jnp.sum(later * x_in, axis=0, keepdims=True)
+            ig_s[at, cols] = back.astype(BF16)
+            misc[n_taps] = misc[n_taps] + jnp.sum(conv_grad, axis=0, keepdims=True)
+            sel_grad = sel_grad + lax.dot_general(low, act_ref[at, :], tn, preferred_element_type=F32)
+        rows = jnp.concatenate(
+            [
+                sel_grad,
+                stepg_ref[...],
+                dsum_ref[...] * rate_ref[...],
+                jnp.concatenate(misc + [sums_ref[0:2, :], zero], axis=0),
+                jnp.zeros((small_s.shape[1] - wide - stepg_ref.shape[0] - rate_ref.shape[0] - 8, piece), F32),
+            ],
+            axis=0,
+        )
+        cs = small_s.shape[2]
+        for i in range(piece // cs):
+            small_s[g * (piece // cs) + i] = rows[:, i * cs : (i + 1) * cs]
+
+    @pl.when(g >= half)
+    def _():
+        block = g - half
+        dcols = wx_s.shape[1]
+
+        def weights(j, _):
+            cols = pl.ds(pl.multiple_of(j * piece, piece), piece)
+            grad = lax.dot_general(normed_ref[...], ig_s[:, cols], tn, preferred_element_type=F32).astype(BF16)
+            for i in range(piece // dcols):
+                wx_s[block * (piece // dcols) + i, :, cols] = grad[i * dcols : (i + 1) * dcols]
+            return 0
+
+        lax.fori_loop(0, ch // piece, weights, 0)
+
+        def tokens_(m, _):
+            at = pl.ds(pl.multiple_of(m * tok, tok), tok)
+            grad = lax.dot_general(ig_s[at, :], wx_ref[...], nt, preferred_element_type=F32)
+            grad = grad + lax.dot_general(gg_ref[at, :], wg_ref[...], nt, preferred_element_type=F32)
+            ng_s[m, :, pl.ds(pl.multiple_of(block * piece, piece), piece)] = grad.astype(BF16)
+            return 0
+
+        lax.fori_loop(0, n_dp, tokens_, 0)
+
+    @pl.when(g == steps - 1)
+    def _():
+        ring_x.start()
+        ring_s.start()
+        pairs.start()
+        shares[0].relay()
+        pairs.middle()
+        if ring_o.events > 1:
+            ring_o.event(ring_o.events - 1)
+        if ring_x.events > 1:
+            ring_s.event(1)
+            ring_x.event(1)
+        ring_o.finish(wo_own)
+        shares[1].start()
+        pairs.finish(change_s)
+
+        def rows(i, _):
+            at = pl.ds(pl.multiple_of(i * 16, 16), 16)
+            v = x_own[at, :].astype(F32)
+            rstd = lax.rsqrt(jnp.mean(v * v, axis=1, keepdims=True) + EPS)
+            hat = v * rstd
+            grad = change_s[at, :] * gain_ref[...]
+            grad = rstd * (grad - hat * jnp.mean(grad * hat, axis=1, keepdims=True))
+            change_s[at, :] = dy_own[at, :].astype(F32) + grad
+            return 0
+
+        lax.fori_loop(0, tok // 16, rows, 0)
+        ret_x.fill(pick_s[...], change_s)
+        ret_x.start()
+        for e in range(2, ring_x.events):
+            ring_s.event(e)
+            ring_x.event(e)
+        shares[1].relay()
+        ring_s.finish(sm_own)
+        shares[3].start()
+        ring_x.finish(wx_own)
+        shares[2].start()
+        shares[3].relay()
+        shares[2].relay()
+        for share in shares:
+            share.finish()
+        ret_m.finish()
+        ret_x.finish()
+
+
+def leave(lens, da, conv, x_in, act, dbl_grad, sel, taps, sums, decay_sum, rate, stepg, normed, wx, wg, gate_grad,
+          wo_part, wg_own, x_own, dy_own, mixed_own, gain, tags, ride, n_f):
+    n_dp, tok, wide = dbl_grad.shape
+    group, ch = act.shape
+    width = x_own.shape[1]
+    count = n_dp * n_f
+    pair = tok // count
+    piece = 256
+    half = ch // piece
+    dcols = width // n_f
+    cs = ch // n_f
+    n = rate.shape[0]
+    tall = -(-(wide + stepg.shape[0] + n + 8) // 64) * 64
+    early = lambda g: (0, jnp.minimum(g, half - 1))
+    late = lambda g: (0, jnp.maximum(g - half, 0))
+    late_rows = lambda g: (jnp.maximum(g - half, 0), 0)
+    any_ = pl.BlockSpec(memory_space=pl.ANY)
+    vmem = pl.BlockSpec(memory_space=pltpu.VMEM)
+    block = lambda rows: pl.BlockSpec((rows, piece), early)
+    shaped = jax.ShapeDtypeStruct
+    return pl.pallas_call(
+        functools.partial(leave_kernel, n_f, half),
+        grid=(half + width // piece,),
+        in_specs=[
+            pl.BlockSpec(memory_space=pltpu.SMEM),
+            block(group),
+            block(group),
+            block(group),
+            block(group),
+            vmem,
+            block(wide),
+            block(taps.shape[0]),
+            block(8),
+            block(n),
+            block(n),
+            block(stepg.shape[0]),
+            pl.BlockSpec((group, piece), late),
+            pl.BlockSpec((piece, ch), late_rows),
+            pl.BlockSpec((piece, ch), late_rows),
+        ]
+        + [vmem] * 9,
+        out_specs=[any_] * 6,
+        out_shape=[
+            shaped((count, pair, width + 128), BF16),
+            shaped((count, pair, width), BF16),
+            shaped((n_dp, dcols, ch), BF16),
+            shaped((n_dp, dcols, ch), BF16),
+            shaped((n_dp, cs, width), BF16),
+            shaped((n_dp, tall, cs), F32),
+        ],
+        scratch_shapes=[
+            pltpu.VMEM((group, ch), BF16),
+            pltpu.VMEM((n_f, dcols, ch), BF16),
+            pltpu.VMEM((n_dp, tok, width), BF16),
+            pltpu.VMEM((n_f, tall, cs), F32),
+            pltpu.VMEM((tok, tok), BF16),
+            pltpu.VMEM((count, pair, width + 128), BF16),
+            pltpu.VMEM((count, pair, width), BF16),
+            pltpu.VMEM((tok, width), F32),
+        ]
+        + RingReduce.scratch(n_f, (cs, width))
+        + RingReduce.scratch(n_f, (dcols, ch))
+        + RingReduce.scratch(n_f, (tall, cs), F32)
+        + PairReduce.scratch((tok, width))
+        + [
+            pltpu.VMEM((cs, width), BF16),
+            pltpu.VMEM((dcols, ch), BF16),
+            pltpu.VMEM((tall, cs), F32),
+            pltpu.SemaphoreType.DMA((6,)),
+            pltpu.SemaphoreType.DMA((4, 3)),
+            pltpu.SemaphoreType.DMA((4, 3)),
+            pltpu.SemaphoreType.DMA((4,)),
+        ],
+        compiler_params=pltpu.CompilerParams(
+            collective_id=4, has_side_effects=True, vmem_limit_bytes=62 * 2**20
+        ),
+        cost_estimate=pl.CostEstimate(flops=2 * 10**10, bytes_accessed=6 * 10**7, transcendentals=10**6),
+    )(lens, da, conv, x_in, act, dbl_grad, sel, taps, sums, decay_sum, rate, stepg, normed, wx, wg, gate_grad,
+      wo_part, wg_own, x_own, dy_own, mixed_own, gain, tags, ride)
 
 
 def masks_of(count):
     return [1 << b for b in range(count.bit_length() - 1)]
-
-
-def group_gather(block, count):
-    blocks = {0: block}
-    for mask in reversed(masks_of(count)):
-        keys = sorted(blocks)
-        got = swap(jnp.stack([blocks[m] for m in keys]), count, mask)
-        for place, m in enumerate(keys):
-            blocks[m | mask] = got[place]
-    return [blocks[m] for m in range(count)]
-
-
-def group_reduce(blocks, count, dtype):
-    held = {m: b for m, b in enumerate(blocks)}
-    for mask in masks_of(count):
-        keep = [m for m in sorted(held) if not m & mask]
-        got = swap(jnp.stack([held[m | mask].astype(dtype) for m in keep]), count, mask)
-        held = {m: held[m].astype(F32) + got[place].astype(F32) for place, m in enumerate(keep)}
-    return held[0]
 
 
 def mesh_at(index, n_f):
@@ -953,9 +1216,9 @@
 
     dest_row, rel_row, abs_row, in_row = (meta_ref[i : i + 1, :] for i in range(4))
     rank = jnp.sum((dest_ref[...] < dest_row).astype(F32), axis=0, keepdims=True)
-    rank_ref[...] = jnp.broadcast_to(rank, rank_ref.shape)
     half = pair2 // 2
     goal = rel_row * half + rank - abs_row * half
+    rank_ref[...] = jnp.broadcast_to(goal, rank_ref.shape)
     row = lax.broadcasted_iota(jnp.int32, (total, tok), 0)
     place_in = lax.rem(row, pair2)
     first = place_in < half
@@ -1231,11 +1494,6 @@
     both = ("dp", "fsdp")
     me_d = lax.axis_index("dp")
     me_f = lax.axis_index("fsdp")
-    order = ring_order(n_f)
-    place_of = jnp.asarray([order.index(f) for f in range(n_f)], jnp.int32)
-    order_arr = jnp.asarray(order, jnp.int32)
-    q = place_of[me_f]
-    at_ring = [order_arr[(q + k) % n_f] for k in range(n_f)]
     flat_dot = lambda a, b: jnp.dot(a, b, preferred_element_type=F32)
     nt_dot = lambda a, b: lax.dot_general(a, b, (((1,), (1,)), ((), ())), preferred_element_type=F32)
     tn_dot = lambda a, b: lax.dot_general(a, b, (((0,), (0,)), ((), ())), preferred_element_type=F32)
@@ -1269,15 +1527,12 @@
     x_all = x_all.reshape(group, width)
     lens = lens_all[:, 0, :segs]
     from_send = (ranks[0].astype(jnp.int32)[:, None] == slots[None, :]).astype(BF16)
+    x_tags = tags.reshape(rows, 2 * pair, 128)[:, :pair].reshape(tok, 128)
     dy_all = dy_all.reshape(group, width)
     wx = wx.reshape(width, ch)
     wg = wg.reshape(width, ch)
     small = small_all.transpose(1, 0, 2).reshape(used + filler, ch)
     gain = small_all[:, used - gain_rows : used].reshape(width).astype(F32)
-    tags = tags.reshape(rows, 2 * pair, 128)[:, :pair, 0].astype(jnp.int32)
-    tags = tags[(me - jnp.arange(rows, dtype=jnp.int32)) % rows].reshape(tok)
-    from_row = (tags[:, None] == slots[None, :]).astype(BF16)
-
     valid = (slots < jnp.sum(lengths[0, : segs - 1])).astype(F32)
     x_own32 = x_own.astype(F32)
     square = jnp.sum(x_own32 * x_own32, axis=1)
@@ -1292,30 +1547,6 @@
     skip = skip.astype(F32)
     rate = -jnp.exp(dlog.astype(F32))
 
-    def shifted(values, lag):
-        if lag == 0:
-            return values
-        edge = jnp.zeros((abs(lag),) + values.shape[1:], values.dtype)
-        if lag > 0:
-            return jnp.concatenate([edge, values[:-lag]], axis=0)
-        return jnp.concatenate([values[-lag:], edge], axis=0)
-
-    within = jnp.arange(tok, dtype=jnp.int32)
-    since, left = [], []
-    for m in range(n_dp):
-        begin, end, total = 0, 0, 0
-        for j in range(segs):
-            after = total + lens[m, j]
-            begin = jnp.where(within >= total, total, begin)
-            end = jnp.where(within >= total, after, end)
-            total = after
-        since.append(within - begin)
-        left.append(end - 1 - within)
-    since = jnp.concatenate(since)[:, None]
-    left = jnp.concatenate(left)[:, None]
-    same = [(since >= lag).astype(F32) for lag in range(taps)]
-    same_next = [(left >= lag).astype(F32) for lag in range(taps)]
-    split = lambda value: [value[m * tok : (m + 1) * tok] for m in range(n_dp)]
     normed, x_in, conv, act, gate, dbl, wo_next = enter(
         lens, x_all, gain[None], wx, wg, conv_w, conv_b.astype(F32), sel, wo_block, n_f
     )
@@ -1334,94 +1565,44 @@
     gate_grad = (gated_grad * scan_out * silu_slope(gate)).astype(BF16)
     wg_grad = tn_dot(normed, gate_grad).astype(BF16)
     wo_grad = tn_dot(gated, dy_all).astype(BF16)
-    wo_own = ring_reduce(
-        lambda k: lax.dynamic_slice_in_dim(wo_grad, at_ring[k] * cs, cs, 0), n_f, n_f - 1 - n_f // 2, BF16
-    )
     pre_grad, act_grad, dbl_grad, decay_sum, sums, step_grad, wg_own, mixed = scan_backward(
         lens, dbl, delta, pre, act, scan_grad, stepw, rate2, skip, states,
         wg_grad.reshape(n_f, dcols, ch), mixed_part, n_f, tok,
     )
-    dbl_grad = dbl_grad.reshape(group, -1).astype(BF16)
-    act_grad = act_grad + flat_dot(dbl_grad, sel)
-    conv_grad = act_grad * silu_slope(conv)
-    in_grad = sum(
-        conv_w[taps - 1 - lag][None] * shifted(conv_grad, -lag) * same_next[lag] for lag in range(taps)
-    ).astype(BF16)
-    wx_grad = tn_dot(normed, in_grad).astype(BF16)
-    wx_own = ring_reduce(
-        lambda k: lax.dynamic_slice_in_dim(wx_grad, at_ring[k] * dcols, dcols, 0), n_f, n_f // 2, BF16
-    )
-    normed_grad_part = (nt_dot(in_grad, wx) + nt_dot(gate_grad, wg)).astype(BF16)
-    normed_grad = group_reduce(split(normed_grad_part), n_dp, BF16)
-
-    tap_grads = [
-        jnp.sum(conv_grad * shifted(x_in, taps - 1 - tap) * same[taps - 1 - tap], axis=0) for tap in range(taps)
-    ]
-    small_grads = jnp.concatenate(
-        [jnp.stack(tap_grads)]
-        + [
-            jnp.sum(conv_grad, axis=0, keepdims=True),
-            sums[:2],
-            decay_sum * rate,
-            tn_dot(dbl_grad, act),
-            step_grad,
-            jnp.zeros((-sum(heights) % 16, ch), F32),
-        ],
-        axis=0,
-    )
-    small_own = ring_reduce(
-        lambda k: lax.dynamic_slice_in_dim(small_grads, at_ring[k] * cs, cs, 1), n_f, n_f - 1 - n_f // 2, F32
-    )
-
-    def in_group_order(blocks):
-        stacked = jnp.stack(blocks)
-        return [lax.dynamic_index_in_dim(stacked, me_d ^ i, 0, keepdims=False) for i in range(n_dp)]
-
-    def interleaved(blocks):
-        return jnp.stack(in_group_order(blocks), axis=1)
-
-    own_in = jnp.concatenate(
-        [
-            jnp.stack(group_gather(wx_own.astype(BF16), n_dp)),
-            jnp.stack(group_gather(wg_own.astype(BF16), n_dp)),
-        ],
-        axis=2,
-    )
-    grad_in_weight, gain_sum = spread_columns(own_in, in_weight, cs)
-    grad_out_weight = jnp.concatenate(in_group_order(group_gather(wo_own.astype(BF16), n_dp)), axis=0).astype(F32)
-    small_full = interleaved(group_gather(small_own, n_dp)).reshape(-1, n_dp * cs)
-    out_small, at = [], 0
-    for height, s in zip(heights, smalls):
-        out_small.append(small_full[at : at + height].reshape(s.shape))
-        at += height
-    grad_norm_gain = gain_sum / norm_gain.astype(F32)
-
-    rstd = lax.rsqrt(jnp.mean(x_own32 * x_own32, axis=1, keepdims=True) + EPS)
-    hat = x_own32 * rstd
-    hat_grad = normed_grad * gain[None]
-    change = rstd * (hat_grad - hat * jnp.mean(hat_grad * hat, axis=1, keepdims=True))
-    row_grad = (dy_own.astype(F32) + change).astype(BF16)
-
-    def returned(value):
-        cols = value.shape[1]
-        out = flat_dot(from_row, value).astype(BF16).reshape(rows, pair, cols)
-        back = lax.all_to_all(out, both, 0, 0, tiled=True).reshape(tok, cols)
-        return flat_dot(from_send, back).astype(BF16)
-
-    lanes = lax.broadcasted_iota(jnp.int32, (tok, 128), 1)
-    ride = jnp.zeros((tok, 128), F32)
+    lanes = lax.broadcasted_iota(jnp.int32, (1, 128), 1)
+    ride = jnp.zeros((1, 128), F32)
     for j, value in enumerate(mine_sums):
         high = value.astype(BF16).astype(F32)
         ride = ride + jnp.where(lanes == 2 * j, high, 0.0) + jnp.where(lanes == 2 * j + 1, value - high, 0.0)
-    out = flat_dot(from_row, mixed.astype(BF16)).astype(BF16)
-    out = jnp.concatenate([out, ride.astype(BF16)], axis=1).reshape(rows, pair, width + 128)
-    back = lax.all_to_all(out, both, 0, 0, tiled=True).reshape(tok, width + 128)
-    totals = jnp.sum(back.reshape(rows, pair, -1)[:, 0, width : width + 4].astype(F32), axis=0)
+    mix_back, dx_back, gx_all, gg_all, go_all, small_full = leave(
+        lens, act_grad, conv, x_in, act, dbl_grad, sel, conv_w, sums, decay_sum, rate, step_grad, normed, wx, wg,
+        gate_grad, wo_grad.reshape(n_f, cs, width), wg_own, x_own, dy_own, mixed, gain[None], x_tags, ride, n_f,
+    )
+
+    def in_group_order(stacked):
+        return jnp.concatenate(
+            [lax.dynamic_index_in_dim(stacked, me_d ^ i, 0, keepdims=True) for i in range(n_dp)], axis=0
+        )
+
+    grad_in_weight, gain_sum = spread_columns(jnp.concatenate([gx_all, gg_all], axis=2), in_weight, cs)
+    grad_out_weight = in_group_order(go_all).reshape(n_dp * cs, width).astype(F32)
+    small_full = in_group_order(small_full).transpose(1, 0, 2).reshape(-1, n_dp * cs)
+    grad_norm_gain = gain_sum / norm_gain.astype(F32)
+    wide = select_weight.shape[0]
+    at_decay = wide + rank_of
+    at_misc = at_decay + n
+    grad_select = small_full[:wide]
+    grad_step = small_full[wide:at_decay]
+    grad_decay = small_full[at_decay:at_misc]
+    misc = small_full[at_misc : at_misc + 8]
+
+    back = mix_back.reshape(tok, width + 128)
+    totals = jnp.sum(mix_back[:, 0, width : width + 4].astype(F32), axis=0)
     input_rms = jnp.sqrt((totals[0] + totals[1]) / ((totals[2] + totals[3]) * width))
     mixer_output = flat_dot(from_send, back[:, :width])
     layer_output = (tokens.astype(F32) + mixer_output).astype(BF16)
     mixer_output = mixer_output.astype(BF16)
-    input_grad = returned(row_grad)
+    input_grad = flat_dot(from_send, dx_back.reshape(tok, width)).astype(BF16)
     return (
         layer_output,
         mixer_output,
@@ -1429,13 +1610,13 @@
         input_rms,
         grad_norm_gain,
         grad_in_weight,
-        out_small[0],
-        out_small[1],
-        out_small[5],
-        out_small[6],
-        out_small[2],
-        out_small[4],
-        out_small[3],
+        misc[:taps],
+        misc[taps],
+        grad_select,
+        grad_step,
+        misc[taps + 1],
+        grad_decay,
+        misc[taps + 2],
         grad_out_weight,
     )
 

time: 676 us -> 579 us (0.86)
  the two profiles are of different devices: /device:TPU:0 before, /device:TPU:21 now
where the time goes in v5:
time: 579 us; the launch traced here: 576 us
  Pallas kernels  484 us (84%)
  matrix products  37.8 us (7%)
  local copies, waits for them, and re-layouts  32.7 us (6%)
  other arithmetic  14.1 us (2%)
  between operations  7.44 us (1%)
    pallas_call x1, Pallas kernels, leave(): pl.pallas_call(functools.partial(leave_kernel, n_f, half), grid=(half + w...  170 us
    pallas_call x1, Pallas kernels, gather_all(): pl.pallas_call(functools.partial(gather_kernel, n_dp, n_f, downs), in_spe...  142 us
    pallas_call x1, Pallas kernels, scan_backward(): pl.pallas_call(functools.partial(bwd_kernel, min(lanes, ch), n_f), grid=(...  76.2 us
    pallas_call x1, Pallas kernels, enter(): pl.pallas_call(functools.partial(enter_kernel, n_f, half), grid=(2 * half...  42.9 us
    pallas_call x1, Pallas kernels, scan_forward(): pl.pallas_call(functools.partial(fwd_kernel, min(lanes, ch), n_f), grid=(...  36.8 us
    unnamed x61, local copies, waits for them, and re-layouts  17.1 us
    dot_general x1, matrix products, per_device(): lax.dot_general(a, b, (((1,), (1,)), ((), ())), preferred_element_type=F32)  13.1 us
    dot_general x2, matrix products, per_device(): lax.dot_general(a, b, (((0,), (0,)), ((), ())), preferred_element_type=F32)  12.7 us

profile of v5, /device:TPU:21, one launch (start us, length us, event | category | flops | bytes accessed | tf_op | source)
XLA Modules:
  0.0 576.3 jit_solution(10796021298798170688)
XLA Ops:
  0.7 1.4 slice_reduce_fusion
  10.5 1.4 concatenate.12.refs_0_
  13.1 4.1 shard_map.245
  20.5 141.9 %shard_map.246 = (bf16[4,256,2048]{2,1,0:T(8,128)(2,1)S(1)}, bf16[4,256,2048]{2,1,0:T(8,128)(2,1)}, s32[4,8,128]{2,1,0:T(8,128)S(1)}, bf16[256,2048]{1,0:T(8,128...) custom-call(bf16[256,2048]{1,0:T(8,128)(2,1)S(1)} %copy-done.7, ...), custom_call_target="tpu_custom_call" | custom-call | flops 10000000000 | bytes 200000000 | tf_op jit(solution)/shard_map/pallas_call | solution.py:1359
  162.4 2.0 copy-done.18
  170.4 42.9 %shard_map.247 = (bf16[1024,2048]{1,0:T(8,128)(2,1)}, f32[1024,1024]{1,0:T(8,128)}, f32[1024,1024]{1,0:T(8,128)}, bf16[1024,1024]{1,0:T(8,128)(2,1)S(1)}, f32[10...) custom-call(s32[4,4]{1,0:T(4,128)S(1)} %bitcast.109, ...), custom_call_target="tpu_custom_call" | custom-call | flops 10000000000 | bytes 40000000 | tf_op jit(solution)/shard_map/pallas_call | solution.py:363
  213.4 1.3 copy-done.20
  214.7 2.7 copy-done.21
  217.4 36.8 %shard_map.248 = (f32[1024,1024]{1,0:T(8,128)S(1)}, bf16[16384,1024]{1,0:T(8,128)(2,1)}, f32[1024,1024]{1,0:T(8,128)S(1)}, f32[1024,1024]{1,0:T(8,128)S(1)}, bf16[8,128,2048]{2,1,0:T(8,128)(2,1)S(1)}) custom-call(s32[4,4]{1,0:T(4,128)S(1)} %bitcast.110, f32[1024,160]{1,0:T(8,128)S(1)} %bitcast.100, bf16[1024,1024]{1,0:T(8,128)(2,1)S(1)} %get-tuple-element.62.act_ref, ...), custom_call_target="tpu_custom_call" | custom-call | flops 671088640 | bytes 54525952 | tf_op jit(solution)/shard_map/pallas_call | solution.py:551
  254.3 2.0 copy-done.2
  256.3 2.0 copy-done.19
  258.3 13.1 %multiply_convert_fusion = (bf16[1024,1024]{1,0:T(8,128)(2,1)S(1)}, bf16[1024,1024]{1,0:T(8,128)(2,1)}, f32[1024,1024]{1,0:T(8,128)}) fusion(f32[1024,1024]{1,0:T(8,128)} %copy-done.19, f32[1024,1024]{1,0:T(8,128)} %get-tuple-element.68, bf16[1024,2048]{1,0:T(8,128)(2,1)} %bitcast.137, bf16[1024,2048]{1,0:T(8,128)(2,1)S(1)} %bitcast.116), kind=kOutput, calls=%fused_computation.1 | convolution fusion | flops 4309647360 | bytes 25165824 | tf_op jit(solution)/shard_map/dot_general | solution.py:1498
  271.4 6.5 %convolution_convert_fusion = bf16[1024,2048]{1,0:T(8,128)(2,1)} fusion(bf16[1024,1024]{1,0:T(8,128)(2,1)S(1)} %get-tuple-element.108, bf16[1024,2048]{1,0:T(8,128)(2,1)S(1)} %bitcast.138), kind=kOutput, calls=%fused_computation.5 | convolution fusion | flops 4297064448 | bytes 10485760 | tf_op jit(solution)/shard_map/dot_general | solution.py:1499
  277.9 6.1 %convolution_convert_fusion.1 = bf16[1024,2048]{1,0:T(8,128)(2,1)} fusion(bf16[1024,1024]{1,0:T(8,128)(2,1)S(1)} %get-tuple-element.108, bf16[1024,2048]{1,0:T(8,128)(2,1)S(1)} %bitcast.117), kind=kOutput, calls=%fused_computation.6 | convolution fusion | flops 4297064448 | bytes 10485760 | tf_op jit(solution)/shard_map/dot_general | solution.py:1497
  284.0 6.2 %convolution_convert_fusion.2 = bf16[2048,1024]{1,0:T(8,128)(2,1)} fusion(bf16[1024,2048]{1,0:T(8,128)(2,1)S(1)} %copy-done.28, bf16[1024,1024]{1,0:T(8,128)(2,1)S(1)} %copy-done.29), kind=kOutput, calls=%fused_computation.7 | convolution fusion | flops 4297064448 | bytes 10485760 | tf_op jit(solution)/shard_map/dot_general | solution.py:1499
  290.2 76.2 %shard_map.249 = (bf16[1024,1024]{1,0:T(8,128)(2,1)}, f32[1024,1024]{1,0:T(8,128)}, f32[4,256,160]{2,1,0:T(8,128)}, f32[16,1024]{1,0:T(8,128)}, f32[8,1024]{1,0:...) custom-call(s32[4,4]{1,0:T(4,128)} %bitcast.111, f32[1024,160]{1,0:T(8,128)} %bitcast.101, ...), custom_call_target="tpu_custom_call" | custom-call | flops 1342177280 | bytes 62914560 | tf_op jit(solution)/shard_map/pallas_call | solution.py:751
  366.4 170.1 %shard_map.250 = (bf16[32,8,2176]{2,1,0:T(8,128)(2,1)}, bf16[32,8,2048]{2,1,0:T(8,128)(2,1)}, bf16[4,256,1024]{2,1,0:T(8,128)(2,1)}, bf16[4,256,1024]{2,1,0:T(8,...) custom-call(s32[4,4]{1,0:T(4,128)} %bitcast.112, f32[1024,1024]{1,0:T(8,128)} %get-tuple-element.72.da_ref, ...), custom_call_target="tpu_custom_call" | custom-call | flops 20000000000 | bytes 60000000 | tf_op jit(solution)/shard_map/pallas_call | solution.py:1071
  536.5 2.8 convolution_convert_fusion.3
  548.5 1.8 copy.36
  550.3 1.8 copy.38
  552.1 3.0 fusion.15
  555.1 2.8 bitcast_convert_fusion
  558.8 2.4 pad_maximum_fusion.x_ref
  561.2 12.3 %shard_map.251 = (f32[256,8192]{1,0:T(8,128)}, f32[256,128]{1,0:T(8,128)}) custom-call(bf16[4,256,2048]{2,1,0:T(8,128)(2,1)} %pad_maximum_fusion.x_ref, bf16[256,8192]{1,0:T(8,128)(2,1)} %w_ref.3), custom_call_target="tpu_custom_call" | custom-call | flops 8388608 | bytes 16777216 | tf_op jit(solution)/shard_map/pallas_call | solution.py:1447
  (96 shorter events, 25.3 us)
Async XLA Ops:
  0.6 9.8 %copy-start = (bf16[160,512]{1,0:T(8,128)(2,1)S(1)}, bf16[160,512]{1,0:T(8,128)(2,1)}, u32[]{:S(2)}) copy-start(bf16[160,512]{1,0:T(8,128)(2,1)} %param.22) | copy-start | bytes 491524
  0.7 16.5 %copy-start.7 = (bf16[256,2048]{1,0:T(8,128)(2,1)S(1)}, bf16[256,2048]{1,0:T(8,128)(2,1)}, u32[]{:S(2)}) copy-start(bf16[256,2048]{1,0:T(8,128)(2,1)} %x_ref.1) | copy-start | bytes 3145732
  162.4 2.0 copy-start.18
  168.8 45.9 %copy-start.13 = (s32[4,1,4]{2,1,0:T(1,128)}, s32[4,1,4]{2,1,0:T(1,128)S(1)}, u32[]{:S(2)}) copy-start(s32[4,1,4]{2,1,0:T(1,128)S(1)} %slice.108) | copy-start | bytes 196
  168.8 44.5 %copy-start.14 = (f32[8,2,128]{2,1,0:T(2,128)}, f32[8,2,128]{2,1,0:T(2,128)S(1)}, u32[]{:S(2)}) copy-start(f32[8,2,128]{2,1,0:T(2,128)S(1)} %slice_convert_fusion) | copy-start | bytes 24580
  168.8 45.9 %copy-start.11 = (f32[1,1024]{1,0:T(1,128)}, f32[1,1024]{1,0:T(1,128)S(1)}, u32[]{:S(2)}) copy-start(f32[1,1024]{1,0:T(1,128)S(1)} %get-tuple-element.124.skip_ref) | copy-start | bytes 12292
  168.9 44.5 %copy-start.12 = (f32[4,1024]{1,0:T(4,128)}, f32[4,1024]{1,0:T(4,128)S(1)}, u32[]{:S(2)}) copy-start(f32[4,1024]{1,0:T(4,128)S(1)} %fusion.7.taps_ref) | copy-start | bytes 49156
  168.9 45.8 %copy-start.10 = (f32[16,1024]{1,0:T(8,128)}, f32[16,1024]{1,0:T(8,128)S(1)}, u32[]{:S(2)}) copy-start(f32[16,1024]{1,0:T(8,128)S(1)} %broadcast_multiply_fusion.rate_ref) | copy-start | bytes 196612
  170.3 44.4 %copy-start.6 = (bf16[128,1024]{1,0:T(8,128)(2,1)}, bf16[128,1024]{1,0:T(8,128)(2,1)S(1)}, u32[]{:S(2)}) copy-start(bf16[128,1024]{1,0:T(8,128)(2,1)S(1)} %copy_bitcast_fusion.2.stepw_ref) | copy-start | bytes 786436
  170.4 42.9 %copy-start.9 = (bf16[160,1024]{1,0:T(8,128)(2,1)}, bf16[160,1024]{1,0:T(8,128)(2,1)S(1)}, u32[]{:S(2)}) copy-start(bf16[160,1024]{1,0:T(8,128)(2,1)S(1)} %copy_bitcast_fusion.1.sel_ref) | copy-start | bytes 983044
  214.7 39.6 %copy-start.4 = (bf16[1024,1024]{1,0:T(8,128)(2,1)}, bf16[1024,1024]{1,0:T(8,128)(2,1)S(1)}, u32[]{:S(2)}) copy-start(bf16[1024,1024]{1,0:T(8,128)(2,1)S(1)} %get-tuple-element.62.act_ref) | copy-start | bytes 6291460
  214.7 39.6 %copy-start.5 = (f32[4,256,160]{2,1,0:T(8,128)}, f32[4,256,160]{2,1,0:T(8,128)S(1)}, u32[]{:S(2)}) copy-start(f32[4,256,160]{2,1,0:T(8,128)S(1)} %get-tuple-element.61) | copy-start | bytes 1966084
  214.7 2.7 copy-start.21
  254.3 2.0 copy-start.2
  256.3 2.0 copy-start.19
  258.3 13.1 %copy-start.3 = (f32[1024,1024]{1,0:T(8,128)}, f32[1024,1024]{1,0:T(8,128)S(1)}, u32[]{:S(2)}) copy-start(f32[1024,1024]{1,0:T(8,128)S(1)} %get-tuple-element.65.pre_ref) | copy-start | bytes 12582916
  258.3 13.1 %copy-start.27 = (bf16[4,256,2048]{2,1,0:T(8,128)(2,1)S(1)}, bf16[4,256,2048]{2,1,0:T(8,128)(2,1)}, u32[]{:S(2)}) copy-start(bf16[4,256,2048]{2,1,0:T(8,128)(2,1)} %get-tuple-element.66) | copy-start | bytes 12582916
  277.9 6.1 %copy-start.28 = (bf16[1024,2048]{1,0:T(8,128)(2,1)S(1)}, bf16[1024,2048]{1,0:T(8,128)(2,1)}, u32[]{:S(2)}) copy-start(bf16[1024,2048]{1,0:T(8,128)(2,1)} %get-tuple-element.70.normed_ref) | copy-start | bytes 12582916
  277.9 6.1 %copy-start.29 = (bf16[1024,1024]{1,0:T(8,128)(2,1)S(1)}, bf16[1024,1024]{1,0:T(8,128)(2,1)}, u32[]{:S(2)}) copy-start(bf16[1024,1024]{1,0:T(8,128)(2,1)} %get-tuple-element.109.gg_ref) | copy-start | bytes 6291460
  536.5 8.2 %copy-start.23 = (bf16[4,128,2048]{2,1,0:T(8,128)(2,1)S(1)}, bf16[4,128,2048]{2,1,0:T(8,128)(2,1)}, u32[]{:S(2)}) copy-start(bf16[4,128,2048]{2,1,0:T(8,128)(2,1)} %get-tuple-element.91) | copy-start | bytes 6291460
  555.1 2.8 copy-start.24
  555.1 3.7 copy-start.25
  558.8 16.3 %copy-start.1 = (bf16[160,512]{1,0:T(8,128)(2,1)S(1)}, bf16[160,512]{1,0:T(8,128)(2,1)}, u32[]{:S(2)}) copy-start(bf16[160,512]{1,0:T(8,128)(2,1)} %param.22) | copy-start | bytes 491524
  561.2 13.4 %copy-start.26 = (bf16[256]{0:T(256)(128)(2,1)S(1)}, bf16[256]{0:T(256)(128)(2,1)}, u32[]{:S(2)}) copy-start(bf16[256]{0:T(256)(128)(2,1)} %param.18) | copy-start | bytes 1540
  (6 other events, 6.9 us)

commit v6 on v5

--- a/solution.py
+++ b/solution.py
@@ -107,7 +107,7 @@
         self.counts = [down, n_f - 1 - down]
         self.copies = [[], []]
         for up in (0, 1):
-            for h in range(self.counts[up]):
+            for h in range(min(self.counts[up], got.shape[1])):
                 src = part.at[self.at(self.goal(up, 0))] if h == 0 else got.at[up, h - 1]
                 self.copies[up].append(ring_copy(n_f, src, got.at[up, h], send.at[up, h], recv.at[up, h], up))
         self.events = max(self.counts)
@@ -131,6 +131,19 @@
         for up in (0, 1):
             if self.copies[up]:
                 self.copies[up][0].start()
+
+    def stop(self, hops, out):
+        for up in (0, 1):
+            self.copies[up][hops - 1].wait_recv()
+            rows_add(out.at[up], [self.got.at[up, hops - 1]])
+            for c in self.copies[up][:hops]:
+                c.wait_send()
+
+    def resume(self, hops, arrived):
+        for up in (0, 1):
+            slot = self.got.at[up, hops - 1]
+            rows_add(slot, [arrived.at[up], self.part.at[self.at(self.goal(up, hops))]])
+            self.copies[up][hops].start()
 
     def event(self, e):
         for up in (0, 1):
@@ -139,7 +152,7 @@
                 self.add(self.got.at[up, e - 1], self.part.at[self.at(self.goal(up, e))])
                 self.copies[up][e].start()
 
-    def finish(self, out):
+    def finish(self, out, since=0):
         last = []
         for up in (0, 1):
             if self.copies[up]:
@@ -159,13 +172,13 @@
 
         lax.fori_loop(0, rows // step, piece, 0)
         for up in (0, 1):
-            for c in self.copies[up]:
+            for c in self.copies[up][since:]:
                 c.wait_send()
 
     @staticmethod
-    def scratch(n_f, block, dtype=BF16):
+    def scratch(n_f, block, dtype=BF16, slots=0):
         return [
-            pltpu.VMEM((2, n_f // 2) + block, dtype),
+            pltpu.VMEM((2, slots or n_f // 2) + block, dtype),
             pltpu.SemaphoreType.DMA((2, n_f // 2)),
             pltpu.SemaphoreType.DMA((2, n_f // 2)),
         ]
@@ -230,6 +243,59 @@
     lax.fori_loop(0, out.shape[0] // step, piece, 0)
 
 
+class PairShare:
+    def __init__(self, mine, out, local, send, recv, relative=False):
+        me_d, me_f = lax.axis_index("dp"), lax.axis_index("fsdp")
+        far = 2 if relative else flip(me_d, 2)
+        here, at_near, at_far, relayed = (0, 1, 2, 3) if relative else (me_d, me_d, me_d, far)
+        self.local = pltpu.make_async_copy(mine, out(here), local)
+        self.copies = [
+            pltpu.make_async_remote_copy(
+                src_ref=src,
+                dst_ref=dst,
+                send_sem=send.at[i],
+                recv_sem=recv.at[i],
+                device_id=(flip(me_d, mask), me_f),
+                device_id_type=pl.DeviceIdType.MESH,
+            )
+            for i, (src, dst, mask) in enumerate(
+                [(mine, out(at_near), 1), (mine, out(at_far), 2), (out(far), out(relayed), 1)]
+            )
+        ]
+
+    def start(self):
+        self.copies[1].start()
+        self.copies[0].start()
+        self.local.start()
+
+    def relay(self):
+        self.copies[1].wait_recv()
+        self.copies[2].start()
+
+    def finish(self):
+        self.copies[0].wait_recv()
+        self.copies[2].wait_recv()
+        for c in self.copies:
+            c.wait_send()
+        self.local.wait()
+
+
+def side_by_side(count, height, wide):
+    return (count, height, wide) if wide % 128 else (height, count * wide)
+
+
+def lane_block(ref, index, wide):
+    if wide % 128:
+        return ref.at[index]
+    return ref.at[:, pl.ds(pl.multiple_of(index * wide, 128), wide)]
+
+
+def joined(value):
+    if value.ndim == 2:
+        return value
+    return value.transpose(1, 0, 2).reshape(value.shape[1], -1)
+
+
 def greet_neighbours(n_f, ring):
     me_d, me_f = lax.axis_index("dp"), lax.axis_index("fsdp")
     barrier = pltpu.get_barrier_semaphore()
@@ -292,13 +358,14 @@
         part[...] = jnp.zeros_like(part)
 
         def norm(i, _):
-            at = pl.ds(pl.multiple_of(i * 32, 32), 32)
-            v = x_ref[at, :].astype(F32)
-            rstd = lax.rsqrt(jnp.mean(v * v, axis=1, keepdims=True) + EPS)
-            normed_ref[at, :] = (v * rstd * gain_ref[...]).astype(BF16)
+            for j in range(4):
+                at = pl.ds(pl.multiple_of(i * 128 + j * 32, 32), 32)
+                v = x_ref[at, :].astype(F32)
+                rstd = lax.rsqrt(jnp.mean(v * v, axis=1, keepdims=True) + EPS)
+                normed_ref[at, :] = (v * rstd * gain_ref[...]).astype(BF16)
             return 0
 
-        lax.fori_loop(0, rows // 32, norm, 0)
+        lax.fori_loop(0, rows // 128, norm, 0)
 
     @pl.when(g == half)
     def _():
@@ -309,11 +376,11 @@
     @pl.when(g < half)
     def _():
         n_taps = taps_ref.shape[0]
+        xin_ref[...] = jnp.dot(normed_ref[...], wx_ref[...], preferred_element_type=F32)
         for m in range(n_dp):
             at = slice(m * tok, (m + 1) * tok)
-            v = jnp.dot(normed_ref[at, :], wx_ref[...], preferred_element_type=F32)
+            v = xin_ref[at, :]
             since, _ = segment_span(lens_ref, m, 0, tok)
-            xin_ref[at, :] = v
             conv = bias_ref[...] + taps_ref[n_taps - 1 : n_taps, :] * v
             for lag in range(1, n_taps):
                 keep = (since >= lag).astype(F32)
@@ -329,9 +396,7 @@
 
     @pl.when(g >= half)
     def _():
-        for m in range(n_dp):
-            at = slice(m * tok, (m + 1) * tok)
-            gate_ref[at, :] = jnp.dot(normed_ref[at, :], wg_ref[...], preferred_element_type=F32)
+        gate_ref[...] = jnp.dot(normed_ref[...], wg_ref[...], preferred_element_type=F32)
 
     @pl.when(g == half)
     def _():
@@ -477,19 +542,25 @@
             c.wait()
 
 
-def fwd_kernel(lanes, n_f, lens_ref, dbl_ref, act_ref, stepw_ref, stepb_ref, rate_ref, skip_ref, wo_ref, next_ref,
-               y_ref, s_ref, delta_ref, pre_ref, wo_all, carry, big_s, cw_s, bt_s, d_s, u_s, sc, local, hop_send, hop_recv):
+def fwd_kernel(lanes, n_f, lens_ref, dbl_ref, act_ref, stepw_ref, stepb_ref, rate_ref, skip_ref, wo_ref, next_ref, dy_ref,
+               y_ref, s_ref, delta_ref, pre_ref, wo_all, dy_all, carry, big_s, cw_s, bt_s, d_s, u_s, sc, local, hop_send, hop_recv, sh_send, sh_recv):
     n, ch = rate_ref.shape
     tblk = act_ref.shape[0]
     low_n = stepw_ref.shape[0]
     steps = pl.num_programs(0) * pl.num_programs(1)
     now = pl.program_id(0) * pl.num_programs(1) + pl.program_id(1)
     ring = RingGather(n_f, wo_ref, next_ref, wo_all, local, hop_send, hop_recv)
+    share = PairShare(dy_ref, lambda m: dy_all.at[m], local.at[5], sh_send, sh_recv, True)
 
     @pl.when(now == 0)
     def _():
         greet_neighbours(n_f, True)
         ring.start()
+        share.start()
+
+    @pl.when(now == 13)
+    def _():
+        share.relay()
 
     for e in range(1, ring.events):
 
@@ -538,9 +609,10 @@
     @pl.when(now == steps - 1)
     def _():
         ring.finish()
-
-
-def scan_forward(lens, dbl, act, stepw, stepb, rate2, skip, wo_block, wo_next, n_f, row_len, tblk=64, lanes=512):
+        share.finish()
+
+
+def scan_forward(lens, dbl, act, stepw, stepb, rate2, skip, wo_block, wo_next, dy_own, n_f, row_len, tblk=64, lanes=512):
     t, ch = act.shape
     n = rate2.shape[0]
     nb = row_len // tblk
@@ -561,12 +633,14 @@
             pl.BlockSpec((1, ch), zero),
             any_,
             any_,
+            any_,
         ],
         out_specs=[
             pl.BlockSpec((tblk, ch), at),
             pl.BlockSpec((tblk * n, ch), at),
             pl.BlockSpec((tblk, ch), at),
             pl.BlockSpec((tblk, ch), at),
+            any_,
             any_,
         ],
         out_shape=[
@@ -575,6 +649,7 @@
             wide,
             wide,
             jax.ShapeDtypeStruct((n_f,) + wo_block.shape, BF16),
+            jax.ShapeDtypeStruct((t // row_len,) + dy_own.shape, BF16),
         ],
         scratch_shapes=[
             pltpu.VMEM((n, ch), F32),
@@ -584,22 +659,24 @@
             pltpu.VMEM((TB, ch), F32),
             pltpu.VMEM((TB, ch), F32),
             pltpu.VMEM((TB * n, ch), BF16),
-            pltpu.SemaphoreType.DMA((5,)),
+            pltpu.SemaphoreType.DMA((6,)),
             pltpu.SemaphoreType.DMA((2, n_f)),
             pltpu.SemaphoreType.DMA((2, n_f)),
+            pltpu.SemaphoreType.DMA((3,)),
+            pltpu.SemaphoreType.DMA((3,)),
         ],
         compiler_params=pltpu.CompilerParams(
             collective_id=2, has_side_effects=True, vmem_limit_bytes=32 * 2**20
         ),
         cost_estimate=pl.CostEstimate(flops=t * n * ch * 40, bytes_accessed=t * ch * 52, transcendentals=t * n * ch),
-    )(lens, dbl, act, stepw, stepb, rate2, skip, wo_block, wo_next)
+    )(lens, dbl, act, stepw, stepb, rate2, skip, wo_block, wo_next, dy_own)
 
 
 def bwd_kernel(lanes, n_f, lens_ref, dbl_ref, delta_ref, pre_ref, act_ref, gy_ref, stepw_ref, rate_ref, skip_ref,
-               s_ref, sp_ref, wg_part, mixed_part,
-               pg_ref, da_ref, dbl_grad_ref, dl_ref, sums_ref, stepg_ref, wg_own, mixed_own,
+               s_ref, sp_ref, wg_part, gated_ref, dy_ref, wo_ref,
+               pg_ref, da_ref, dbl_grad_ref, dl_ref, sums_ref, stepg_ref, wg_own, wo_out, wo_half, mixed_own,
                carry, big_s, bw_s, ct_s, d_all, u_all, g_all, h_all, b_all, c_all, part, near, far, total, gs_send, gs_recv,
-               ring_got, ring_send, ring_recv, mix, mix_near, mix_far, mix_send, mix_recv, mix_load):
+               ring_got, ring_send, ring_recv, wo_got, wo_send, wo_recv, wo_part, mix, mix_near, mix_far, mix_send, mix_recv, wo_save):
     n, ch = rate_ref.shape
     tblk = act_ref.shape[0]
     low_n = stepw_ref.shape[0]
@@ -608,6 +685,7 @@
     m = row_at(r, n_dp)
     group = GroupSum(part, near, far, total, gs_send, gs_recv)
     ring = RingReduce(n_f, wg_part, ring_got, ring_send, ring_recv, n_f // 2)
+    ring_o = RingReduce(n_f, wo_part, wo_got, wo_send, wo_recv, n_f - 1 - n_f // 2)
     pairs = PairReduce(mix, mix_near, mix_far, mix_send, mix_recv)
     now = r * nb + j
     last_step = n_dp * nb - 1
@@ -617,12 +695,8 @@
 
     @pl.when((r == 0) & (j == 0))
     def _():
-        load = pltpu.make_async_copy(mixed_part, mix, mix_load)
-        load.start()
         greet_neighbours(n_f, True)
         ring.start()
-        load.wait()
-        pairs.start()
         dl_ref[...] = jnp.zeros_like(dl_ref)
         sums_ref[...] = jnp.zeros_like(sums_ref)
         stepg_ref[...] = jnp.zeros_like(stepg_ref)
@@ -632,14 +706,40 @@
         @pl.when(now == min(4 * e, 15))
         def _(e=e):
             ring.event(e)
-
-    @pl.when(now == 2)
+            if e == 2:
+                ring_o.start()
+
+    tile = 256
+    parts = ch // tile
+    save = pltpu.make_async_copy(wo_part, wo_out, wo_save)
+
+    @pl.when(now < parts)
+    def _():
+        cs = wo_part.shape[1]
+        cols = pl.ds(pl.multiple_of(now * tile, tile), tile)
+        grad = lax.dot_general(
+            gated_ref[:, cols], dy_ref[...], (((0,), (0,)), ((), ())), preferred_element_type=F32
+        ).astype(BF16)
+        for i in range(tile // cs):
+            wo_part[now * (tile // cs) + i] = grad[i * cs : (i + 1) * cs]
+
+    @pl.when(now == parts - 1)
+    def _():
+        save.start()
+
+    @pl.when((now >= parts) & (now < parts + n_dp))
+    def _():
+        row_len = mix.shape[1]
+        at = pl.ds(pl.multiple_of((now - parts) * row_len, row_len), row_len)
+        mix[now - parts] = jnp.dot(gated_ref[at, :], wo_ref[...], preferred_element_type=F32).astype(BF16)
+
+    @pl.when(now == 8)
+    def _():
+        pairs.start()
+
+    @pl.when(now == 10)
     def _():
         pairs.middle()
-
-    @pl.when(now == 12)
-    def _():
-        pairs.finish(mixed_own)
 
     ones = jnp.where(own_token(n), 1.0, 0.0).astype(BF16)
     nt = (((1,), (1,)), ((), ()))
@@ -732,18 +832,24 @@
 
     @pl.when((j == nb - 1) & (r == n_dp - 1))
     def _():
+        ring_o.event(1)
         ring.finish(wg_own)
         group.finish()
         dbl_grad_ref[...] = total[...]
-
-
-def scan_backward(lens, dbl, delta, pre, act, gy, stepw, rate2, skip, states, wg_part, mixed_part, n_f, row_len,
+        pairs.finish(mixed_own)
+        ring_o.stop(2, wo_half)
+        save.wait()
+
+
+def scan_backward(lens, dbl, delta, pre, act, gy, stepw, rate2, skip, states, wg_part, gated, dy_all, wo, n_f, row_len,
                   tblk=64, lanes=512):
     t, ch = delta.shape
     n = rate2.shape[0]
     nb = row_len // tblk
     n_dp = t // row_len
     wide = dbl.shape[1]
+    width = wo.shape[1]
+    cs = ch // n_f
     spot = lambda r, j: row_at(r, n_dp) * nb + nb - 1 - j
     at = lambda r, j: (spot(r, j), 0)
     zero = lambda r, j: (0, 0)
@@ -764,7 +870,9 @@
             pl.BlockSpec((tblk * n, ch), at),
             pl.BlockSpec((n, ch), entry),
             pl.BlockSpec(memory_space=pltpu.VMEM),
-            pl.BlockSpec(memory_space=pl.ANY),
+            pl.BlockSpec(memory_space=pltpu.VMEM),
+            pl.BlockSpec(memory_space=pltpu.VMEM),
+            pl.BlockSpec(memory_space=pltpu.VMEM),
         ],
         out_specs=[
             pl.BlockSpec((tblk, ch), at),
@@ -774,7 +882,9 @@
             pl.BlockSpec((8, ch), zero),
             pl.BlockSpec(stepw.shape, zero),
             pl.BlockSpec(wg_part.shape[1:], zero),
-            pl.BlockSpec(mixed_part.shape[1:], zero),
+            pl.BlockSpec(memory_space=pl.ANY),
+            pl.BlockSpec((2, cs, width), lambda r, j: (0, 0, 0)),
+            pl.BlockSpec((row_len, width), zero),
         ],
         out_shape=[
             jax.ShapeDtypeStruct((t, ch), BF16),
@@ -784,7 +894,9 @@
             jax.ShapeDtypeStruct((8, ch), F32),
             jax.ShapeDtypeStruct(stepw.shape, F32),
             jax.ShapeDtypeStruct(wg_part.shape[1:], BF16),
-            jax.ShapeDtypeStruct(mixed_part.shape[1:], F32),
+            jax.ShapeDtypeStruct((n_f, cs, width), BF16),
+            jax.ShapeDtypeStruct((2, cs, width), BF16),
+            jax.ShapeDtypeStruct((row_len, width), BF16),
         ],
         scratch_shapes=[
             pltpu.VMEM((n, ch), F32),
@@ -800,47 +912,15 @@
         ]
         + GroupSum.scratch(row_len, wide)
         + RingReduce.scratch(n_f, wg_part.shape[1:])
-        + [pltpu.VMEM(mixed_part.shape, BF16)]
-        + PairReduce.scratch(mixed_part.shape[1:])
+        + RingReduce.scratch(n_f, (cs, width), BF16, 2)
+        + [pltpu.VMEM((n_f, cs, width), BF16), pltpu.VMEM((n_dp, row_len, width), BF16)]
+        + PairReduce.scratch((row_len, width))
         + [pltpu.SemaphoreType.DMA],
         compiler_params=pltpu.CompilerParams(
-            collective_id=3, has_side_effects=True, vmem_limit_bytes=56 * 2**20
+            collective_id=3, has_side_effects=True, vmem_limit_bytes=60 * 2**20
         ),
         cost_estimate=pl.CostEstimate(flops=t * n * ch * 80, bytes_accessed=t * ch * 60, transcendentals=t * n * ch),
-    )(lens, dbl, delta, pre, act, gy, stepw, rate2, skip, states, states, wg_part, mixed_part)
-
-
-class PairShare:
-    def __init__(self, mine, out, local, send, recv):
-        me_d, me_f = lax.axis_index("dp"), lax.axis_index("fsdp")
-        self.local = pltpu.make_async_copy(mine, out.at[0], local)
-        self.copies = [
-            pltpu.make_async_remote_copy(
-                src_ref=src,
-                dst_ref=out.at[i + 1],
-                send_sem=send.at[i],
-                recv_sem=recv.at[i],
-                device_id=(flip(me_d, mask), me_f),
-                device_id_type=pl.DeviceIdType.MESH,
-            )
-            for i, (src, mask) in enumerate([(mine, 1), (mine, 2), (out.at[2], 1)])
-        ]
-
-    def start(self):
-        self.copies[1].start()
-        self.copies[0].start()
-        self.local.start()
-
-    def relay(self):
-        self.copies[1].wait_recv()
-        self.copies[2].start()
-
-    def finish(self):
-        self.copies[0].wait_recv()
-        self.copies[2].wait_recv()
-        for c in self.copies:
-            c.wait_send()
-        self.local.wait()
+    )(lens, dbl, delta, pre, act, gy, stepw, rate2, skip, states, states, wg_part, gated, dy_all, wo)
 
 
 class Return:
@@ -884,8 +964,8 @@
 
 def leave_kernel(n_f, half, lens_ref, da_ref, conv_ref, xin_ref, act_ref, dblg_ref, sel_ref, taps_ref,
                  sums_ref, dsum_ref, rate_ref, stepg_ref, normed_ref, wx_ref, wg_ref, gg_ref,
-                 wo_part, wg_own, x_own, dy_own, mixed_own, gain_ref, tags_ref, ride_ref,
-                 mix_back, dx_back, gx_all, gg_all, go_all, small_all,
+                 wo_part, wo_half, wg_own, x_own, dy_own, mixed_own, gain_ref, tags_ref, ride_ref,
+                 mix_back, dx_back, gin_all, go_all, small_all,
                  ig_s, wx_s, ng_s, small_s, pick_s, ret_mix, ret_dx, change_s,
                  wo_got, wo_send, wo_recv, wx_got, wx_send, wx_recv, sm_got, sm_send, sm_recv,
                  ng_near, ng_far, ng_send, ng_recv, wo_own, wx_own, sm_own, local, sh_send, sh_recv, ret_sem):
@@ -901,11 +981,20 @@
     ring_o = RingReduce(n_f, wo_part, wo_got, wo_send, wo_recv, n_f - 1 - down)
     ring_x = RingReduce(n_f, wx_s, wx_got, wx_send, wx_recv, down)
     ring_s = RingReduce(n_f, small_s, sm_got, sm_send, sm_recv, down)
-    pairs = PairReduce(ng_s, ng_near, ng_far, ng_send, ng_recv)
+    pairs = [
+        PairReduce(ng_s.at[h], ng_near.at[h], ng_far.at[h], ng_send.at[h], ng_recv.at[h]) for h in (0, 1)
+    ]
+    blocks = width // piece
+    turn = half + blocks
     shares = [
         PairShare(mine, out, local.at[i], sh_send.at[i], sh_recv.at[i])
         for i, (mine, out) in enumerate(
-            [(wg_own, gg_all), (wo_own, go_all), (wx_own, gx_all), (sm_own, small_all)]
+            [
+                (wg_own, lambda d: gin_all.at[d, :, pl.ds(ch, ch)]),
+                (wo_own, lambda d: go_all.at[d]),
+                (wx_own, lambda d: gin_all.at[d, :, pl.ds(0, ch)]),
+                (sm_own, lambda d: lane_block(small_all, d, sm_own.shape[1])),
+            ]
         )
     ]
     ret_m = Return(count, n_f, ret_mix, mix_back, local.at[4], ret_sem.at[0], ret_sem.at[1])
@@ -926,7 +1015,7 @@
 
         lax.fori_loop(1, count, greet, 0)
         pl.semaphore_wait(barrier, count - 1)
-        ring_o.start()
+        ring_o.resume(2, wo_half)
         shares[0].start()
         spots = jnp.concatenate([tags_ref[...]] * (tok // 128), axis=1)
         lane = lax.broadcasted_iota(jnp.int32, (tok, tok), 1).astype(F32)
@@ -937,11 +1026,24 @@
         )
         ret_m.start()
 
-    for e in range(1, ring_o.events - 1):
-
-        @pl.when(g == min(5 * e, 2 * half + 2))
+    for e in range(3, ring_o.events):
+
+        @pl.when(g == min(turn + e - 2, steps - 2))
         def _(e=e):
             ring_o.event(e)
+
+    @pl.when(g == turn)
+    def _():
+        ring_x.start()
+        ring_s.start()
+
+    @pl.when(g == turn + blocks // 2)
+    def _():
+        pairs[0].start()
+
+    @pl.when(g == steps - 2)
+    def _():
+        pairs[0].middle()
 
     @pl.when(g < half)
     def _():
@@ -980,44 +1082,38 @@
         for i in range(piece // cs):
             small_s[g * (piece // cs) + i] = rows[:, i * cs : (i + 1) * cs]
 
-    @pl.when(g >= half)
+    @pl.when((g >= half) & (g < turn))
     def _():
         block = g - half
         dcols = wx_s.shape[1]
-
-        def weights(j, _):
-            cols = pl.ds(pl.multiple_of(j * piece, piece), piece)
-            grad = lax.dot_general(normed_ref[...], ig_s[:, cols], tn, preferred_element_type=F32).astype(BF16)
-            for i in range(piece // dcols):
-                wx_s[block * (piece // dcols) + i, :, cols] = grad[i * dcols : (i + 1) * dcols]
-            return 0
-
-        lax.fori_loop(0, ch // piece, weights, 0)
-
-        def tokens_(m, _):
-            at = pl.ds(pl.multiple_of(m * tok, tok), tok)
-            grad = lax.dot_general(ig_s[at, :], wx_ref[...], nt, preferred_element_type=F32)
-            grad = grad + lax.dot_general(gg_ref[at, :], wg_ref[...], nt, preferred_element_type=F32)
-            ng_s[m, :, pl.ds(pl.multiple_of(block * piece, piece), piece)] = grad.astype(BF16)
-            return 0
-
-        lax.fori_loop(0, n_dp, tokens_, 0)
+        grad = lax.dot_general(normed_ref[...], ig_s[...], tn, preferred_element_type=F32).astype(BF16)
+        for i in range(piece // dcols):
+            wx_s[block * (piece // dcols) + i] = grad[i * dcols : (i + 1) * dcols]
+
+    @pl.when(g >= turn)
+    def _():
+        grad = lax.dot_general(ig_s[...], wx_ref[...], nt, preferred_element_type=F32)
+        grad = grad + lax.dot_general(gg_ref[...], wg_ref[...], nt, preferred_element_type=F32)
+        grad = grad.astype(BF16).reshape(n_dp, tok, piece)
+        for h in (0, 1):
+
+            @pl.when((g - turn) // (blocks // 2) == h)
+            def _(h=h):
+                at = (g - turn - h * (blocks // 2)) * piece
+                ng_s[h, :, :, pl.ds(pl.multiple_of(at, piece), piece)] = grad
 
     @pl.when(g == steps - 1)
     def _():
-        ring_x.start()
-        ring_s.start()
-        pairs.start()
+        pairs[1].start()
         shares[0].relay()
-        pairs.middle()
-        if ring_o.events > 1:
-            ring_o.event(ring_o.events - 1)
+        pairs[1].middle()
         if ring_x.events > 1:
             ring_s.event(1)
             ring_x.event(1)
-        ring_o.finish(wo_own)
+        ring_o.finish(wo_own, 2)
         shares[1].start()
-        pairs.finish(change_s)
+        for h in (0, 1):
+            pairs[h].finish(change_s.at[:, pl.ds(h * (width // 2), width // 2)])
 
         def rows(i, _):
             at = pl.ds(pl.multiple_of(i * 16, 16), 16)
@@ -1049,7 +1145,7 @@
 
 
 def leave(lens, da, conv, x_in, act, dbl_grad, sel, taps, sums, decay_sum, rate, stepg, normed, wx, wg, gate_grad,
-          wo_part, wg_own, x_own, dy_own, mixed_own, gain, tags, ride, n_f):
+          wo_part, wo_half, wg_own, x_own, dy_own, mixed_own, gain, tags, ride, n_f):
     n_dp, tok, wide = dbl_grad.shape
     group, ch = act.shape
     width = x_own.shape[1]
@@ -1061,16 +1157,17 @@
     cs = ch // n_f
     n = rate.shape[0]
     tall = -(-(wide + stepg.shape[0] + n + 8) // 64) * 64
+    blocks = width // piece
     early = lambda g: (0, jnp.minimum(g, half - 1))
-    late = lambda g: (0, jnp.maximum(g - half, 0))
-    late_rows = lambda g: (jnp.maximum(g - half, 0), 0)
+    late = lambda g: (0, jnp.clip(g - half, 0, blocks - 1))
+    late_rows = lambda g: (jnp.maximum(g - half - blocks, 0), 0)
     any_ = pl.BlockSpec(memory_space=pl.ANY)
     vmem = pl.BlockSpec(memory_space=pltpu.VMEM)
     block = lambda rows: pl.BlockSpec((rows, piece), early)
     shaped = jax.ShapeDtypeStruct
     return pl.pallas_call(
         functools.partial(leave_kernel, n_f, half),
-        grid=(half + width // piece,),
+        grid=(half + 2 * blocks,),
         in_specs=[
             pl.BlockSpec(memory_space=pltpu.SMEM),
             block(group),
@@ -1088,20 +1185,19 @@
             pl.BlockSpec((piece, ch), late_rows),
             pl.BlockSpec((piece, ch), late_rows),
         ]
-        + [vmem] * 9,
-        out_specs=[any_] * 6,
+        + [vmem] * 10,
+        out_specs=[any_] * 5,
         out_shape=[
             shaped((count, pair, width + 128), BF16),
             shaped((count, pair, width), BF16),
-            shaped((n_dp, dcols, ch), BF16),
-            shaped((n_dp, dcols, ch), BF16),
+            shaped((n_dp, dcols, 2 * ch), BF16),
             shaped((n_dp, cs, width), BF16),
-            shaped((n_dp, tall, cs), F32),
+            shaped(side_by_side(n_dp, tall, cs), F32),
         ],
         scratch_shapes=[
             pltpu.VMEM((group, ch), BF16),
             pltpu.VMEM((n_f, dcols, ch), BF16),
-            pltpu.VMEM((n_dp, tok, width), BF16),
+            pltpu.VMEM((2, n_dp, tok, width // 2), BF16),
             pltpu.VMEM((n_f, tall, cs), F32),
             pltpu.VMEM((tok, tok), BF16),
             pltpu.VMEM((count, pair, width + 128), BF16),
@@ -1111,8 +1207,11 @@
         + RingReduce.scratch(n_f, (cs, width))
         + RingReduce.scratch(n_f, (dcols, ch))
         + RingReduce.scratch(n_f, (tall, cs), F32)
-        + PairReduce.scratch((tok, width))
         + [
+            pltpu.VMEM((2, 2, tok, width // 2), BF16),
+            pltpu.VMEM((2, tok, width // 2), BF16),
+            pltpu.SemaphoreType.DMA((2, 3)),
+            pltpu.SemaphoreType.DMA((2, 3)),
             pltpu.VMEM((cs, width), BF16),
             pltpu.VMEM((dcols, ch), BF16),
             pltpu.VMEM((tall, cs), F32),
@@ -1126,7 +1225,7 @@
         ),
         cost_estimate=pl.CostEstimate(flops=2 * 10**10, bytes_accessed=6 * 10**7, transcendentals=10**6),
     )(lens, da, conv, x_in, act, dbl_grad, sel, taps, sums, decay_sum, rate, stepg, normed, wx, wg, gate_grad,
-      wo_part, wg_own, x_own, dy_own, mixed_own, gain, tags, ride)
+      wo_part, wo_half, wg_own, x_own, dy_own, mixed_own, gain, tags, ride)
 
 
 def masks_of(count):
@@ -1152,11 +1251,11 @@
 def gather_kernel(n_dp, n_f, downs, x_ref, dy_ref, meta_ref, dest_ref, lens_ref, *refs):
     streams = len(downs)
     blocks = refs[:streams]
-    x_all, dy_all, lens_all, x_own_ref, dy_own_ref, tag_ref, rank_ref = refs[streams : streams + 7]
-    outs = refs[streams + 7 : 2 * streams + 7]
-    send_ref, got, x_own, dy_own, deal_sem, loc_sem, pair_send, pair_recv, ring_send, ring_recv = refs[
-        2 * streams + 7 :
-    ]
+    x_all, lens_all, x_own_ref, dy_own_ref, tag_ref, rank_ref = refs[streams : streams + 6]
+    outs = refs[streams + 6 : 2 * streams + 6]
+    (send_x, send_dy, got_x, got_dy, x_own, dy_own, deal_sem, loc_sem, pair_send, pair_recv, ring_send, ring_recv) = (
+        refs[2 * streams + 6 :]
+    )
     count = n_dp * n_f
     me_d = lax.axis_index("dp")
     me_f = lax.axis_index("fsdp")
@@ -1174,31 +1273,45 @@
         return 0
 
     lax.fori_loop(1, count, greet, 0)
+    def place_of(s, index):
+        return lane_block(outs[s], index, blocks[s].shape[1]) if s == 0 else outs[s].at[index]
+
     locals_ = [
-        pltpu.make_async_copy(blocks[s], outs[s].at[me_f], loc_sem.at[s]) for s in range(streams)
+        pltpu.make_async_copy(blocks[s], place_of(s, me_f), loc_sem.at[s]) for s in range(streams)
     ]
     for c in locals_:
         c.start()
     pl.semaphore_wait(barrier, count - 1)
 
-    def deal(p, _):
-        pltpu.make_async_remote_copy(
-            src_ref=send_ref.at[p],
-            dst_ref=got.at[p],
-            send_sem=deal_sem.at[0],
-            recv_sem=deal_sem.at[1],
-            device_id=mesh_at(lax.rem(me + p, count), n_f),
-            device_id_type=pl.DeviceIdType.MESH,
-        ).start()
-        return 0
+    def deal(a):
+        src, dst = ((send_x, got_x), (send_dy, got_dy))[a]
+
+        def one(p, _):
+            pltpu.make_async_remote_copy(
+                src_ref=src.at[p],
+                dst_ref=dst.at[p],
+                send_sem=deal_sem.at[a, 0],
+                recv_sem=deal_sem.at[a, 1],
+                device_id=mesh_at(lax.rem(me + p, count), n_f),
+                device_id_type=pl.DeviceIdType.MESH,
+            ).start()
+            return 0
+
+        lax.fori_loop(1, count, one, 0)
+        dst[0] = src[0]
+
+    def dealt(a, way):
+        src, dst = ((send_x, got_x), (send_dy, got_dy))[a]
+        rest = pl.ds(1, count - 1)
+        pltpu.make_async_copy(src.at[rest], dst.at[rest], deal_sem.at[a, way]).wait()
 
     def hop(s, h, up):
         k = lax.rem(q + (n_f - h if up else h), n_f)
         index = ring_index(k, n_f)
-        src = blocks[s] if h == 0 else outs[s].at[index]
+        src = blocks[s] if h == 0 else place_of(s, index)
         return pltpu.make_async_remote_copy(
             src_ref=src,
-            dst_ref=outs[s].at[index],
+            dst_ref=place_of(s, index),
             send_sem=ring_send.at[s, int(up), h],
             recv_sem=ring_recv.at[s, int(up), h],
             device_id=(me_d, above if up else below),
@@ -1211,34 +1324,30 @@
             if hops[s][up]:
                 hop(s, 0, up).start()
     tok, width = x_own.shape
-    pair2 = got.shape[1]
-    total = count * pair2
+    pair = got_x.shape[1]
 
     dest_row, rel_row, abs_row, in_row = (meta_ref[i : i + 1, :] for i in range(4))
     rank = jnp.sum((dest_ref[...] < dest_row).astype(F32), axis=0, keepdims=True)
-    half = pair2 // 2
-    goal = rel_row * half + rank - abs_row * half
+    goal = rel_row * pair + rank - abs_row * pair
     rank_ref[...] = jnp.broadcast_to(goal, rank_ref.shape)
-    row = lax.broadcasted_iota(jnp.int32, (total, tok), 0)
-    place_in = lax.rem(row, pair2)
-    first = place_in < half
-    slot = (row // pair2) * half + jnp.where(first, place_in, place_in - half)
-    chosen = slot.astype(F32) == goal
+    chosen = lax.broadcasted_iota(jnp.int32, (tok, tok), 0).astype(F32) == goal
     spot = jnp.sum(jnp.where(chosen, in_row, 0.0), axis=1, keepdims=True)
-    send_ref[:, :, width:] = jnp.broadcast_to(spot, (total, 128)).astype(BF16).reshape(count, pair2, 128)
-    x_pick = jnp.where(chosen & first, 1.0, 0.0).astype(BF16)
-    dy_pick = jnp.where(chosen & jnp.logical_not(first), 1.0, 0.0).astype(BF16)
-
-    def sort(j, _):
-        cols = pl.ds(pl.multiple_of(j * 256, 256), 256)
-        mixed = jnp.dot(x_pick, x_ref[:, cols], preferred_element_type=F32)
-        mixed = mixed + jnp.dot(dy_pick, dy_ref[:, cols], preferred_element_type=F32)
-        send_ref[:, :, cols] = mixed.astype(BF16).reshape(count, pair2, 256)
-        return 0
-
-    lax.fori_loop(0, width // 256, sort, 0)
-    lax.fori_loop(1, count, deal, 0)
-    got[0] = send_ref[0]
+    send_x[:, :, width:] = jnp.broadcast_to(spot, (tok, 128)).astype(BF16).reshape(count, pair, 128)
+    pick = jnp.where(chosen, 1.0, 0.0).astype(BF16)
+
+    def sort(values, out):
+        def part(j, _):
+            cols = pl.ds(pl.multiple_of(j * 256, 256), 256)
+            moved = jnp.dot(pick, values[:, cols], preferred_element_type=F32)
+            out[:, :, cols] = moved.astype(BF16).reshape(count, pair, 256)
+            return 0
+
+        lax.fori_loop(0, width // 256, part, 0)
+
+    sort(x_ref, send_x)
+    deal(0)
+    sort(dy_ref, send_dy)
+    deal(1)
 
     def advance(h):
         for s in range(streams):
@@ -1247,23 +1356,19 @@
                     hop(s, h - 1, up).wait_recv()
                     hop(s, h, up).start()
 
-    rest = got.at[pl.ds(1, count - 1)]
-    pltpu.make_async_copy(send_ref.at[pl.ds(1, count - 1)], rest, deal_sem.at[1]).wait()
-    tag = got[:, :, width : width + 128].astype(F32).reshape(total, 128)
-    reps = tok // 128
-    spots = jnp.concatenate([tag] * reps, axis=1)
-    lane = lax.broadcasted_iota(jnp.int32, (total, tok), 1).astype(F32)
-    match = spots == lane
-    x_pick = jnp.where(match & first, 1.0, 0.0).astype(BF16)
-    dy_pick = jnp.where(match & jnp.logical_not(first), 1.0, 0.0).astype(BF16)
+    dealt(0, 1)
+    tag = got_x[:, :, width : width + 128].astype(F32).reshape(tok, 128)
+    spots = jnp.concatenate([tag] * (tok // 128), axis=1)
+    lane = lax.broadcasted_iota(jnp.int32, (tok, tok), 1).astype(F32)
+    settle = jnp.where(spots == lane, 1.0, 0.0).astype(BF16)
     tn = (((0,), (0,)), ((), ()))
     tag_ref[...] = tag
 
-    def place(pick, out):
+    def place(values, out):
         def part(j, _):
             cols = pl.ds(pl.multiple_of(j * 256, 256), 256)
-            values = got[:, :, cols].reshape(total, 256)
-            out[:, cols] = lax.dot_general(pick, values, tn, preferred_element_type=F32).astype(BF16)
+            block = values[:, :, cols].reshape(tok, 256)
+            out[:, cols] = lax.dot_general(settle, block, tn, preferred_element_type=F32).astype(BF16)
             return 0
 
         lax.fori_loop(0, width // 256, part, 0)
@@ -1274,8 +1379,8 @@
         return me_d + mask - 2 * mask * lax.rem(me_d // mask, 2)
 
     def share(a, m, mask):
-        out = (x_all, dy_all, lens_all)[a]
-        own_block = (x_own, dy_own, lens_ref)[a]
+        out = (x_all, lens_all)[a]
+        own_block = (x_own, lens_ref)[a]
         return pltpu.make_async_remote_copy(
             src_ref=own_block if m == 0 else out.at[m],
             dst_ref=out.at[m | mask],
@@ -1287,26 +1392,19 @@
 
     copies = []
 
-    def keep(a):
-        own_block = (x_own, dy_own, lens_ref)[a]
-        dsts = (x_all, dy_all, lens_all)[a].at[0], (x_own_ref, dy_own_ref, None)[a]
-        for j, dst in enumerate(dsts[: 1 if a == 2 else 2]):
-            c = pltpu.make_async_copy(own_block, dst, loc_sem.at[streams + 2 * a + j])
-            c.start()
-            copies.append(c)
-
-    for mask in masks:
-        share(2, 0, mask).start()
-    keep(2)
+    def keep(src, dst):
+        c = pltpu.make_async_copy(src, dst, loc_sem.at[streams + len(copies)])
+        c.start()
+        copies.append(c)
+
+    place(got_x, x_own)
+    for a in (0, 1):
+        for mask in masks:
+            share(a, 0, mask).start()
+    keep(lens_ref, lens_all.at[0])
+    keep(x_own, x_all.at[0])
+    keep(x_own, x_own_ref)
     advance(1)
-    place(x_pick, x_own)
-    for mask in masks:
-        share(0, 0, mask).start()
-    keep(0)
-    place(dy_pick, dy_own)
-    for mask in masks:
-        share(1, 0, mask).start()
-    keep(1)
 
     def relay(a):
         held = [0]
@@ -1322,11 +1420,16 @@
     for h in range(2, most):
         advance(h)
         if h == 2:
+            dealt(1, 1)
+            place(got_dy, dy_own)
+            keep(dy_own, dy_own_ref)
             relay(0)
     if most <= 2:
+        dealt(1, 1)
+        place(got_dy, dy_own)
+        keep(dy_own, dy_own_ref)
         relay(0)
     relay(1)
-    relay(2)
     for s in range(streams):
         for up in (0, 1):
             if hops[s][up]:
@@ -1335,7 +1438,7 @@
         for up in (0, 1):
             for h in range(hops[s][up]):
                 hop(s, h, up).wait_send()
-    for a in (0, 1, 2):
+    for a in (0, 1):
         held = [0]
         for mask in masks:
             for m in held:
@@ -1343,14 +1446,16 @@
             held = held + [m | mask for m in held]
     for c in locals_ + copies:
         c.wait()
-    pltpu.make_async_copy(send_ref.at[pl.ds(1, count - 1)], rest, deal_sem.at[0]).wait()
+    dealt(0, 0)
+    dealt(1, 0)
 
 
 def gather_all(x, dy, meta, dest, lens, blocks, downs, n_dp, n_f):
     streams = len(blocks)
     tok, width = x.shape
     count = n_dp * n_f
-    sent = (count, 2 * tok // count, width + 128)
+    sent_x = (count, tok // count, width + 128)
+    sent_dy = (count, tok // count, width)
     hops = max(max(d, n_f - 1 - d) for d in downs)
     any_ = pl.BlockSpec(memory_space=pl.ANY)
     vmem = pl.BlockSpec(memory_space=pltpu.VMEM)
@@ -1359,26 +1464,28 @@
     return pl.pallas_call(
         functools.partial(gather_kernel, n_dp, n_f, downs),
         in_specs=[vmem] * 5 + [any_] * streams,
-        out_specs=[any_] * 5 + [vmem] * 2 + [any_] * streams,
+        out_specs=[any_] * 4 + [vmem] * 2 + [any_] * streams,
         out_shape=[
-            rows,
             rows,
             jax.ShapeDtypeStruct((n_dp,) + lens.shape, lens.dtype),
             row,
             row,
-            jax.ShapeDtypeStruct((2 * tok, 128), F32),
+            jax.ShapeDtypeStruct((tok, 128), F32),
             jax.ShapeDtypeStruct((8, tok), F32),
         ]
-        + [jax.ShapeDtypeStruct((n_f,) + b.shape, b.dtype) for b in blocks],
+        + [jax.ShapeDtypeStruct(side_by_side(n_f, *blocks[0].shape), BF16)]
+        + [jax.ShapeDtypeStruct((n_f,) + b.shape, b.dtype) for b in blocks[1:]],
         scratch_shapes=[
-            pltpu.VMEM(sent, BF16),
-            pltpu.VMEM(sent, BF16),
+            pltpu.VMEM(sent_x, BF16),
+            pltpu.VMEM(sent_dy, BF16),
+            pltpu.VMEM(sent_x, BF16),
+            pltpu.VMEM(sent_dy, BF16),
             pltpu.VMEM((tok, width), BF16),
             pltpu.VMEM((tok, width), BF16),
-            pltpu.SemaphoreType.DMA((2,)),
-            pltpu.SemaphoreType.DMA((streams + 5,)),
-            pltpu.SemaphoreType.DMA((3, n_dp)),
-            pltpu.SemaphoreType.DMA((3, n_dp)),
+            pltpu.SemaphoreType.DMA((2, 2)),
+            pltpu.SemaphoreType.DMA((streams + 4,)),
+            pltpu.SemaphoreType.DMA((2, n_dp)),
+            pltpu.SemaphoreType.DMA((2, n_dp)),
             pltpu.SemaphoreType.DMA((streams, 2, hops)),
             pltpu.SemaphoreType.DMA((streams, 2, hops)),
         ],
@@ -1417,16 +1524,16 @@
 
 
 def spread_kernel(cs, x_ref, w_ref, out_ref, sum_ref):
-    me_d = lax.axis_index("dp")
     total = jnp.zeros(sum_ref.shape, F32)
-    for i in range(x_ref.shape[0]):
-        m = me_d + i - 2 * ((me_d // 2 % 2) * (i // 2 % 2) * 2 + (me_d % 2) * (i % 2))
-        part = x_ref[m].astype(F32)
-        cols = slice(i * cs, (i + 1) * cs)
-        out_ref[:, cols] = part
-        product = part * w_ref[:, cols].astype(F32)
-        for j in range(0, cs, 128):
-            total = total + product[:, j : j + 128]
+    n_dp = x_ref.shape[0]
+    for f in range(x_ref.shape[2] // cs):
+        for i in range(n_dp):
+            part = x_ref[i, :, f * cs : (f + 1) * cs].astype(F32)
+            cols = slice((f * n_dp + i) * cs, (f * n_dp + i + 1) * cs)
+            out_ref[:, cols] = part
+            product = part * w_ref[:, cols].astype(F32)
+            for j in range(0, cs, 128):
+                total = total + product[:, j : j + 128]
 
     @pl.when(pl.program_id(0) == 0)
     def _():
@@ -1435,29 +1542,27 @@
     sum_ref[...] += total
 
 
-def spread_columns(rel, w, cs):
-    n_dp, height, cols = rel.shape
-    if cs % 128 or n_dp != 4:
-        me_d = lax.axis_index("dp")
-        parts = [lax.dynamic_index_in_dim(rel, me_d ^ i, 0, keepdims=False) for i in range(n_dp)]
-        out = jnp.concatenate(
-            [p[:, f * cs : (f + 1) * cs] for f in range(cols // cs) for p in parts], axis=1
-        ).astype(F32)
+def spread_columns(parts, w, cs):
+    n_dp, height, cols = parts.shape
+    if cs % 128:
+        out = parts.reshape(n_dp, height, cols // cs, cs).transpose(1, 2, 0, 3).reshape(height, n_dp * cols).astype(F32)
         return out, jnp.sum(out * w.astype(F32), axis=1)
+    wide = 2 * cs
     out, sums = pl.pallas_call(
         functools.partial(spread_kernel, cs),
-        grid=(cols // cs,),
+        grid=(cols // wide,),
         in_specs=[
-            pl.BlockSpec((n_dp, height, cs), lambda f: (0, 0, f)),
-            pl.BlockSpec((height, n_dp * cs), lambda f: (0, f)),
+            pl.BlockSpec((n_dp, height, wide), lambda f: (0, 0, f)),
+            pl.BlockSpec((height, n_dp * wide), lambda f: (0, f)),
         ],
         out_specs=[
-            pl.BlockSpec((height, n_dp * cs), lambda f: (0, f)),
+            pl.BlockSpec((height, n_dp * wide), lambda f: (0, f)),
             pl.BlockSpec((height, 128), lambda f: (0, 0)),
         ],
         out_shape=[jax.ShapeDtypeStruct((height, n_dp * cols), F32), jax.ShapeDtypeStruct((height, 128), F32)],
+        compiler_params=pltpu.CompilerParams(vmem_limit_bytes=32 * 2**20),
         cost_estimate=pl.CostEstimate(flops=4 * height * cols * n_dp, bytes_accessed=8 * height * cols * n_dp, transcendentals=0),
-    )(rel, w)
+    )(parts, w)
     return out, jnp.sum(sums, axis=1)
 
 
@@ -1520,19 +1625,17 @@
     )
     wx_block, wg_block = take_columns(in_weight, 2, n_f, n_dp, cs)
     wo_block = lax.dynamic_slice_in_dim(out_weight, me_d * cs, cs, 0)
-    x_all, dy_all, lens_all, x_own, dy_own, tags, ranks, small_all, wx, wg = gather_all(
+    x_all, lens_all, x_own, dy_own, x_tags, ranks, small_all, wx, wg = gather_all(
         tokens, cotangent, meta, destination[:, None].astype(F32), lens_tile,
         [small_block, wx_block, wg_block], [n_f // 2, n_f // 2, n_f - 1 - n_f // 2], n_dp, n_f,
     )
     x_all = x_all.reshape(group, width)
     lens = lens_all[:, 0, :segs]
     from_send = (ranks[0].astype(jnp.int32)[:, None] == slots[None, :]).astype(BF16)
-    x_tags = tags.reshape(rows, 2 * pair, 128)[:, :pair].reshape(tok, 128)
-    dy_all = dy_all.reshape(group, width)
     wx = wx.reshape(width, ch)
     wg = wg.reshape(width, ch)
-    small = small_all.transpose(1, 0, 2).reshape(used + filler, ch)
-    gain = small_all[:, used - gain_rows : used].reshape(width).astype(F32)
+    small = joined(small_all)
+    gain = small[used - gain_rows : used].reshape(gain_rows, n_f, cs).transpose(1, 0, 2).reshape(width).astype(F32)
     valid = (slots < jnp.sum(lengths[0, : segs - 1])).astype(F32)
     x_own32 = x_own.astype(F32)
     square = jnp.sum(x_own32 * x_own32, axis=1)
@@ -1552,41 +1655,35 @@
     )
     dbl = dbl.reshape(group, -1)
     rate2 = rate * LOG2E
-    scan_out, states, delta, pre, wo = scan_forward(
-        lens, dbl, act, stepw, step_b.astype(F32), rate2, skip, wo_block, wo_next, n_f, tok
+    scan_out, states, delta, pre, wo, dy_all = scan_forward(
+        lens, dbl, act, stepw, step_b.astype(F32), rate2, skip, wo_block, wo_next, dy_own, n_f, tok
     )
+    dy_all = dy_all.reshape(group, width)
     wo = wo.reshape(ch, width)
     gate_silu = jax.nn.silu(gate)
     gated = (scan_out * gate_silu).astype(BF16)
-    mixed_part = flat_dot(gated, wo).astype(BF16).reshape(n_dp, tok, width)
 
     gated_grad = nt_dot(dy_all, wo)
     scan_grad = gated_grad * gate_silu
     gate_grad = (gated_grad * scan_out * silu_slope(gate)).astype(BF16)
     wg_grad = tn_dot(normed, gate_grad).astype(BF16)
-    wo_grad = tn_dot(gated, dy_all).astype(BF16)
-    pre_grad, act_grad, dbl_grad, decay_sum, sums, step_grad, wg_own, mixed = scan_backward(
+    pre_grad, act_grad, dbl_grad, decay_sum, sums, step_grad, wg_own, wo_grad, wo_half, mixed = scan_backward(
         lens, dbl, delta, pre, act, scan_grad, stepw, rate2, skip, states,
-        wg_grad.reshape(n_f, dcols, ch), mixed_part, n_f, tok,
+        wg_grad.reshape(n_f, dcols, ch), gated, dy_all, wo, n_f, tok,
     )
     lanes = lax.broadcasted_iota(jnp.int32, (1, 128), 1)
     ride = jnp.zeros((1, 128), F32)
     for j, value in enumerate(mine_sums):
         high = value.astype(BF16).astype(F32)
         ride = ride + jnp.where(lanes == 2 * j, high, 0.0) + jnp.where(lanes == 2 * j + 1, value - high, 0.0)
-    mix_back, dx_back, gx_all, gg_all, go_all, small_full = leave(
+    mix_back, dx_back, gin_all, go_all, small_full = leave(
         lens, act_grad, conv, x_in, act, dbl_grad, sel, conv_w, sums, decay_sum, rate, step_grad, normed, wx, wg,
-        gate_grad, wo_grad.reshape(n_f, cs, width), wg_own, x_own, dy_own, mixed, gain[None], x_tags, ride, n_f,
+        gate_grad, wo_grad, wo_half, wg_own, x_own, dy_own, mixed, gain[None], x_tags, ride, n_f,
     )
 
-    def in_group_order(stacked):
-        return jnp.concatenate(
-            [lax.dynamic_index_in_dim(stacked, me_d ^ i, 0, keepdims=True) for i in range(n_dp)], axis=0
-        )
-
-    grad_in_weight, gain_sum = spread_columns(jnp.concatenate([gx_all, gg_all], axis=2), in_weight, cs)
-    grad_out_weight = in_group_order(go_all).reshape(n_dp * cs, width).astype(F32)
-    small_full = in_group_order(small_full).transpose(1, 0, 2).reshape(-1, n_dp * cs)
+    grad_in_weight, gain_sum = spread_columns(gin_all, in_weight, cs)
+    grad_out_weight = go_all.reshape(n_dp * cs, width).astype(F32)
+    small_full = joined(small_full)
     grad_norm_gain = gain_sum / norm_gain.astype(F32)
     wide = select_weight.shape[0]
     at_decay = wide + rank_of

time: 579 us -> 533 us (0.921)
  Pallas kernels: 484 us -> 461 us
  local copies, waits for them, and re-layouts: 32.7 us -> 23.2 us
  matrix products: 37.8 us -> 28.5 us
    pallas_call x2, Pallas kernels: 182 us -> 152 us  [the longest x1 146 us: leave(): pl.pallas_call(functools.partial(leave_kernel, n_f, half), grid=(half + 2...]
    pallas_call x1, Pallas kernels: 76.2 us -> 96.6 us  [scan_backward(): pl.pallas_call(functools.partial(bwd_kernel, min(lanes, ch), n_f), grid=(...]
    unnamed x61 -> x58, local copies, waits for them, and re-layouts: 17.1 us -> 7.28 us
    pallas_call x1, Pallas kernels: 42.9 us -> 36.1 us  [enter(): pl.pallas_call(functools.partial(enter_kernel, n_f, half), grid=(2 * half...]
    dot_general x2 -> x1, matrix products: 12.7 us -> 6.36 us  [per_device(): lax.dot_general(a, b, (((0,), (0,)), ((), ())), preferred_element_type=F32)]
    dot_general x3 -> x2, matrix products: 12 us -> 6 us  [per_device(): flat_dot = lambda a, b: jnp.dot(a, b, preferred_element_type=F32)]
where the time goes in v6:
time: 533 us; the launch traced here: 531 us
  Pallas kernels  461 us (86%)
  matrix products  28.5 us (5%)
  local copies, waits for them, and re-layouts  23.2 us (4%)
  other arithmetic  10.5 us (2%)
  between operations  7.43 us (1%)
    pallas_call x1, Pallas kernels, leave(): pl.pallas_call(functools.partial(leave_kernel, n_f, half), grid=(half + 2...  146 us
    pallas_call x1, Pallas kernels, gather_all(): pl.pallas_call(functools.partial(gather_kernel, n_dp, n_f, downs), in_spe...  138 us
    pallas_call x1, Pallas kernels, scan_backward(): pl.pallas_call(functools.partial(bwd_kernel, min(lanes, ch), n_f), grid=(...  96.6 us
    pallas_call x1, Pallas kernels, enter(): pl.pallas_call(functools.partial(enter_kernel, n_f, half), grid=(2 * half...  36.1 us
    pallas_call x1, Pallas kernels, scan_forward(): pl.pallas_call(functools.partial(fwd_kernel, min(lanes, ch), n_f), grid=(...  35.1 us
    dot_general x1, matrix products, per_device(): lax.dot_general(a, b, (((1,), (1,)), ((), ())), preferred_element_type=F32)  16.1 us

profile of v6, /device:TPU:21, one launch (start us, length us, event | category | flops | bytes accessed | tf_op | source)
XLA Modules:
  0.0 530.9 jit_solution(17173426342128406702)
XLA Ops:
  0.7 1.4 slice_reduce_fusion
  2.1 1.2 convert_reduce_fusion.1
  10.5 1.4 concatenate.3.refs_0_
  12.0 1.1 constant_dynamic-slice_fusion.wo_ref
  13.1 4.1 shard_map.245
  17.1 1.2 copy-done.18
  20.5 137.9 %shard_map.246 = (bf16[4,256,2048]{2,1,0:T(8,128)(2,1)S(1)}, s32[4,8,128]{2,1,0:T(8,128)S(1)}, bf16[256,2048]{1,0:T(8,128)(2,1)S(1)}, bf16[256,2048]{1,0:T(8,128...) custom-call(bf16[256,2048]{1,0:T(8,128)(2,1)S(1)} %copy-done.9, ...), custom_call_target="tpu_custom_call" | custom-call | flops 10000000000 | bytes 200000000 | tf_op jit(solution)/shard_map/pallas_call | solution.py:1464
  158.4 2.0 copy-done.21
  161.7 1.2 select_reduce_fusion
  165.7 36.1 %shard_map.247 = (bf16[1024,2048]{1,0:T(8,128)(2,1)}, f32[1024,1024]{1,0:T(8,128)}, f32[1024,1024]{1,0:T(8,128)}, bf16[1024,1024]{1,0:T(8,128)(2,1)S(1)}, f32[10...) custom-call(s32[4,4]{1,0:T(4,128)S(1)} %bitcast.44, ...), custom_call_target="tpu_custom_call" | custom-call | flops 10000000000 | bytes 40000000 | tf_op jit(solution)/shard_map/pallas_call | solution.py:428
  202.0 35.1 %shard_map.248 = (f32[1024,1024]{1,0:T(8,128)S(1)}, bf16[16384,1024]{1,0:T(8,128)(2,1)}, f32[1024,1024]{1,0:T(8,128)S(1)}, f32[1024,1024]{1,0:T(8,128)S(1)}, bf1...) custom-call(s32[4,4]{1,0:T(4,128)S(1)} %bitcast.45, f32[1024,160]{1,0:T(8,128)S(1)} %bitcast.42, ...), custom_call_target="tpu_custom_call" | custom-call | flops 671088640 | bytes 54525952 | tf_op jit(solution)/shard_map/pallas_call | solution.py:623
  237.1 16.1 %multiply_convert_fusion = (bf16[1024,1024]{1,0:T(8,128)(2,1)}, bf16[1024,1024]{1,0:T(8,128)(2,1)S(1)}, f32[1024,1024]{1,0:T(8,128)}) fusion(f32[1024,1024]{1,0:T(8,128)S(1)} %get-tuple-element.73, f32[1024,1024]{1,0:T(8,128)} %get-tuple-element.70, bf16[1024,2048]{1,0:T(8,128)(2,1)} %bitcast.53, bf16[1024,2048]{1,0:T(8,128)(2,1)} %bitcast.51), kind=kOutput, calls=%fused_computation | convolution fusion | flops 4309647360 | bytes 25165824 | tf_op jit(solution)/shard_map/dot_general | solution.py:1603
  253.3 6.4 %convolution_convert_fusion = bf16[2048,1024]{1,0:T(8,128)(2,1)} fusion(bf16[1024,2048]{1,0:T(8,128)(2,1)S(1)} %copy-done.27, bf16[1024,1024]{1,0:T(8,128)(2,1)S(1)} %get-tuple-element.97.gg_ref), kind=kOutput, calls=%fused_computation.4 | convolution fusion | flops 4297064448 | bytes 10485760 | tf_op jit(solution)/shard_map/dot_general | solution.py:1604
  259.6 96.6 %shard_map.249 = (bf16[1024,1024]{1,0:T(8,128)(2,1)}, f32[1024,1024]{1,0:T(8,128)}, f32[4,256,160]{2,1,0:T(8,128)}, f32[16,1024]{1,0:T(8,128)}, f32[8,1024]{1,0:...) custom-call(s32[4,4]{1,0:T(4,128)} %bitcast.46, ...), custom_call_target="tpu_custom_call" | custom-call | flops 1342177280 | bytes 62914560 | tf_op jit(solution)/shard_map/pallas_call | solution.py:857
  356.2 146.1 %shard_map.250 = (bf16[32,8,2176]{2,1,0:T(8,128)(2,1)}, bf16[32,8,2048]{2,1,0:T(8,128)(2,1)}, bf16[4,256,2048]{2,1,0:T(8,128)(2,1)}, bf16[4,128,2048]{2,1,0:T(8,128)(2,1)}, f32[320,512]{1,0:T(8,128)}) custom-call(s32[4,4]{1,0:T(4,128)} %bitcast.47, f32[1024,1024]{1,0:T(8,128)} %get-tuple-element.74.da_ref, f32[1024,1024]{1,0:T(8,128)} %get-tuple-element.75.conv_ref, ...), custom_call_target="tpu_custom_call" | custom-call | flops 20000000000 | bytes 60000000 | tf_op jit(solution)/shard_map/pallas_call | solution.py:1168
  502.3 2.8 convolution_convert_fusion.1
  509.3 1.4 fusion.12
  510.7 1.3 slice.94
  512.1 1.4 slice.99
  513.4 1.7 slice.97
  515.1 1.7 slice.96
  516.8 3.2 fusion.11
  520.0 2.8 bitcast_convert_fusion
  523.6 5.5 %shard_map.251 = (f32[256,8192]{1,0:T(8,128)}, f32[256,128]{1,0:T(8,128)S(1)}) custom-call(bf16[4,256,2048]{2,1,0:T(8,128)(2,1)S(1)} %copy-done.5, bf16[256,8192]{1,0:T(8,128)(2,1)S(1)} %copy-done.2), custom_call_target="tpu_custom_call" | custom-call | flops 8388608 | bytes 16777216 | tf_op jit(solution)/shard_map/pallas_call | solution.py:1551
  (83 shorter events, 13.8 us)
Async XLA Ops:
  0.6 9.8 %copy-start = (bf16[160,512]{1,0:T(8,128)(2,1)S(1)}, bf16[160,512]{1,0:T(8,128)(2,1)}, u32[]{:S(2)}) copy-start(bf16[160,512]{1,0:T(8,128)(2,1)} %param.22) | copy-start | bytes 491524
  0.7 16.5 %copy-start.9 = (bf16[256,2048]{1,0:T(8,128)(2,1)S(1)}, bf16[256,2048]{1,0:T(8,128)(2,1)}, u32[]{:S(2)}) copy-start(bf16[256,2048]{1,0:T(8,128)(2,1)} %x_ref.1) | copy-start | bytes 3145732
  158.4 2.0 copy-start.21
  160.4 5.2 copy-start.24
  164.8 37.2 %copy-start.16 = (s32[4,1,4]{2,1,0:T(1,128)}, s32[4,1,4]{2,1,0:T(1,128)S(1)}, u32[]{:S(2)}) copy-start(s32[4,1,4]{2,1,0:T(1,128)S(1)} %slice.78) | copy-start | bytes 196
  164.8 37.1 %copy-start.17 = (f32[2,8,128]{2,0,1:T(2,128)}, f32[2,8,128]{2,0,1:T(2,128)S(1)}, u32[]{:S(2)}) copy-start(f32[2,8,128]{2,0,1:T(2,128)S(1)} %bitcast_convert_fusion.1) | copy-start | bytes 24580
  164.8 37.1 %copy-start.14 = (f32[1,1024]{1,0:T(1,128)}, f32[1,1024]{1,0:T(1,128)S(1)}, u32[]{:S(2)}) copy-start(f32[1,1024]{1,0:T(1,128)S(1)} %get-tuple-element.106.skip_ref) | copy-start | bytes 12292
  164.8 37.0 %copy-start.15 = (f32[4,1024]{1,0:T(4,128)}, f32[4,1024]{1,0:T(4,128)S(1)}, u32[]{:S(2)}) copy-start(f32[4,1024]{1,0:T(4,128)S(1)} %slice_convert_fusion.taps_ref) | copy-start | bytes 49156
  165.5 36.4 %copy-start.13 = (f32[16,1024]{1,0:T(8,128)}, f32[16,1024]{1,0:T(8,128)S(1)}, u32[]{:S(2)}) copy-start(f32[16,1024]{1,0:T(8,128)S(1)} %get-tuple-element.105.rate_ref) | copy-start | bytes 196612
  165.6 36.4 %copy-start.8 = (bf16[128,1024]{1,0:T(8,128)(2,1)}, bf16[128,1024]{1,0:T(8,128)(2,1)S(1)}, u32[]{:S(2)}) copy-start(bf16[128,1024]{1,0:T(8,128)(2,1)S(1)} %slice.83.stepw_ref) | copy-start | bytes 786436
  165.7 36.2 %copy-start.12 = (bf16[160,1024]{1,0:T(8,128)(2,1)}, bf16[160,1024]{1,0:T(8,128)(2,1)S(1)}, u32[]{:S(2)}) copy-start(bf16[160,1024]{1,0:T(8,128)(2,1)S(1)} %slice.82.sel_ref) | copy-start | bytes 983044
  165.7 36.3 %copy-start.23 = (bf16[256,2048]{1,0:T(8,128)(2,1)S(1)}, bf16[256,2048]{1,0:T(8,128)(2,1)}, u32[]{:S(2)}) copy-start(bf16[256,2048]{1,0:T(8,128)(2,1)} %copy-done.22) | copy-start | bytes 3145732
  201.9 35.2 %copy-start.6 = (bf16[1024,1024]{1,0:T(8,128)(2,1)}, bf16[1024,1024]{1,0:T(8,128)(2,1)S(1)}, u32[]{:S(2)}) copy-start(bf16[1024,1024]{1,0:T(8,128)(2,1)S(1)} %get-tuple-element.63.act_ref) | copy-start | bytes 6291460
  201.9 35.2 %copy-start.7 = (f32[4,256,160]{2,1,0:T(8,128)}, f32[4,256,160]{2,1,0:T(8,128)S(1)}, u32[]{:S(2)}) copy-start(f32[4,256,160]{2,1,0:T(8,128)S(1)} %get-tuple-element.62) | copy-start | bytes 1966084
  237.1 16.2 %copy-start.3 = (f32[1024,1024]{1,0:T(8,128)}, f32[1024,1024]{1,0:T(8,128)S(1)}, u32[]{:S(2)}) copy-start(f32[1024,1024]{1,0:T(8,128)S(1)} %get-tuple-element.66.delta_ref) | copy-start | bytes 12582916
  237.1 16.2 %copy-start.4 = (f32[1024,1024]{1,0:T(8,128)}, f32[1024,1024]{1,0:T(8,128)S(1)}, u32[]{:S(2)}) copy-start(f32[1024,1024]{1,0:T(8,128)S(1)} %get-tuple-element.67.pre_ref) | copy-start | bytes 12582916
  237.1 16.2 %copy-start.27 = (bf16[1024,2048]{1,0:T(8,128)(2,1)S(1)}, bf16[1024,2048]{1,0:T(8,128)(2,1)}, u32[]{:S(2)}) copy-start(bf16[1024,2048]{1,0:T(8,128)(2,1)} %get-tuple-element.72.normed_ref) | copy-start | bytes 12582916
  253.2 6.4 %copy-start.28 = (bf16[1024,1024]{1,0:T(8,128)(2,1)}, bf16[1024,1024]{1,0:T(8,128)(2,1)S(1)}, u32[]{:S(2)}) copy-start(bf16[1024,1024]{1,0:T(8,128)(2,1)S(1)} %get-tuple-element.97.gg_ref) | copy-start | bytes 6291460
  356.2 160.6 %copy-start.10 = (bf16[256,2048]{1,0:T(8,128)(2,1)S(1)}, bf16[256,2048]{1,0:T(8,128)(2,1)}, u32[]{:S(2)}) copy-start(bf16[256,2048]{1,0:T(8,128)(2,1)} %x_ref.1) | copy-start | bytes 3145732
  502.3 17.7 %copy-start.25 = (bf16[4,128,2048]{2,1,0:T(8,128)(2,1)S(1)}, bf16[4,128,2048]{2,1,0:T(8,128)(2,1)}, u32[]{:S(2)}) copy-start(bf16[4,128,2048]{2,1,0:T(8,128)(2,1)} %get-tuple-element.93) | copy-start | bytes 6291460
  516.8 6.0 %copy-start.5 = (bf16[4,256,2048]{2,1,0:T(8,128)(2,1)S(1)}, bf16[4,256,2048]{2,1,0:T(8,128)(2,1)}, u32[]{:S(2)}) copy-start(bf16[4,256,2048]{2,1,0:T(8,128)(2,1)} %get-tuple-element.89.x_ref) | copy-start | bytes 12582916
  520.0 3.6 copy-start.2
  520.0 9.8 %copy-start.1 = (bf16[160,512]{1,0:T(8,128)(2,1)S(1)}, bf16[160,512]{1,0:T(8,128)(2,1)}, u32[]{:S(2)}) copy-start(bf16[160,512]{1,0:T(8,128)(2,1)} %param.22) | copy-start | bytes 491524
  523.6 5.6 %copy-start.26 = (bf16[256]{0:T(256)(128)(2,1)S(1)}, bf16[256]{0:T(256)(128)(2,1)}, u32[]{:S(2)}) copy-start(bf16[256]{0:T(256)(128)(2,1)} %param.18) | copy-start | bytes 1540
  (5 other events, 5.6 us)

commit v7 on v6

--- a/solution.py
+++ b/solution.py
@@ -706,8 +706,6 @@
         @pl.when(now == min(4 * e, 15))
         def _(e=e):
             ring.event(e)
-            if e == 2:
-                ring_o.start()
 
     tile = 256
     parts = ch // tile
@@ -726,6 +724,14 @@
     @pl.when(now == parts - 1)
     def _():
         save.start()
+
+    @pl.when(now == 6)
+    def _():
+        ring_o.start()
+
+    @pl.when(now == 13)
+    def _():
+        ring_o.event(1)
 
     @pl.when((now >= parts) & (now < parts + n_dp))
     def _():
@@ -832,7 +838,6 @@
 
     @pl.when((j == nb - 1) & (r == n_dp - 1))
     def _():
-        ring_o.event(1)
         ring.finish(wg_own)
         group.finish()
         dbl_grad_ref[...] = total[...]
@@ -1044,6 +1049,8 @@
     @pl.when(g == steps - 2)
     def _():
         pairs[0].middle()
+        ring_s.event(1)
+        ring_x.event(1)
 
     @pl.when(g < half)
     def _():
@@ -1107,11 +1114,10 @@
         pairs[1].start()
         shares[0].relay()
         pairs[1].middle()
-        if ring_x.events > 1:
-            ring_s.event(1)
-            ring_x.event(1)
         ring_o.finish(wo_own, 2)
         shares[1].start()
+        ring_s.event(2)
+        ring_x.event(2)
         for h in (0, 1):
             pairs[h].finish(change_s.at[:, pl.ds(h * (width // 2), width // 2)])
 
@@ -1126,11 +1132,11 @@
             return 0
 
         lax.fori_loop(0, tok // 16, rows, 0)
+        for e in range(3, ring_x.events):
+            ring_s.event(e)
+            ring_x.event(e)
         ret_x.fill(pick_s[...], change_s)
         ret_x.start()
-        for e in range(2, ring_x.events):
-            ring_s.event(e)
-            ring_x.event(e)
         shares[1].relay()
         ring_s.finish(sm_own)
         shares[3].start()
@@ -1356,6 +1362,7 @@
                     hop(s, h - 1, up).wait_recv()
                     hop(s, h, up).start()
 
+    advance(1)
     dealt(0, 1)
     tag = got_x[:, :, width : width + 128].astype(F32).reshape(tok, 128)
     spots = jnp.concatenate([tag] * (tok // 128), axis=1)
@@ -1404,7 +1411,6 @@
     keep(lens_ref, lens_all.at[0])
     keep(x_own, x_all.at[0])
     keep(x_own, x_own_ref)
-    advance(1)
 
     def relay(a):
         held = [0]
@@ -1423,12 +1429,11 @@
             dealt(1, 1)
             place(got_dy, dy_own)
             keep(dy_own, dy_own_ref)
-            relay(0)
     if most <= 2:
         dealt(1, 1)
         place(got_dy, dy_own)
         keep(dy_own, dy_own_ref)
-        relay(0)
+    relay(0)
     relay(1)
     for s in range(streams):
         for up in (0, 1):

time: 533 us -> 523 us (0.981)
  Pallas kernels: 461 us -> 452 us
    pallas_call x1, Pallas kernels: 146 us -> 136 us  [leave(): pl.pallas_call(functools.partial(leave_kernel, n_f, half), grid=(half + 2...]
where the time goes in v7:
time: 523 us; the launch traced here: 521 us
  Pallas kernels  452 us (86%)
  matrix products  28.5 us (5%)
  local copies, waits for them, and re-layouts  23.2 us (4%)
  other arithmetic  10.5 us (2%)
  between operations  7.43 us (1%)
    pallas_call x1, Pallas kernels, gather_all(): pl.pallas_call(functools.partial(gather_kernel, n_dp, n_f, downs), in_spe...  138 us
    pallas_call x1, Pallas kernels, leave(): pl.pallas_call(functools.partial(leave_kernel, n_f, half), grid=(half + 2...  136 us
    pallas_call x1, Pallas kernels, scan_backward(): pl.pallas_call(functools.partial(bwd_kernel, min(lanes, ch), n_f), grid=(...  96.8 us
    pallas_call x1, Pallas kernels, enter(): pl.pallas_call(functools.partial(enter_kernel, n_f, half), grid=(2 * half...  36.1 us
    pallas_call x1, Pallas kernels, scan_forward(): pl.pallas_call(functools.partial(fwd_kernel, min(lanes, ch), n_f), grid=(...  35 us
    dot_general x1, matrix products, per_device(): lax.dot_general(a, b, (((1,), (1,)), ((), ())), preferred_element_type=F32)  16.1 us

profile of v7, /device:TPU:21, one launch (start us, length us, event | category | flops | bytes accessed | tf_op | source)
XLA Modules:
  0.0 521.4 jit_solution(11140592366220274466)
XLA Ops:
  0.7 1.4 slice_reduce_fusion
  2.1 1.2 convert_reduce_fusion.1
  10.5 1.4 concatenate.3.refs_0_
  12.0 1.1 constant_dynamic-slice_fusion.wo_ref
  13.1 4.1 shard_map.245
  17.1 1.2 copy-done.18
  20.5 138.0 %shard_map.246 = (bf16[4,256,2048]{2,1,0:T(8,128)(2,1)S(1)}, s32[4,8,128]{2,1,0:T(8,128)S(1)}, bf16[256,2048]{1,0:T(8,128)(2,1)S(1)}, bf16[256,2048]{1,0:T(8,128...) custom-call(bf16[256,2048]{1,0:T(8,128)(2,1)S(1)} %copy-done.9, ...), custom_call_target="tpu_custom_call" | custom-call | flops 10000000000 | bytes 200000000 | tf_op jit(solution)/shard_map/pallas_call | solution.py:1469
  158.4 2.0 copy-done.21
  161.8 1.2 select_reduce_fusion
  165.8 36.1 %shard_map.247 = (bf16[1024,2048]{1,0:T(8,128)(2,1)}, f32[1024,1024]{1,0:T(8,128)}, f32[1024,1024]{1,0:T(8,128)}, bf16[1024,1024]{1,0:T(8,128)(2,1)S(1)}, f32[10...) custom-call(s32[4,4]{1,0:T(4,128)S(1)} %bitcast.44, ...), custom_call_target="tpu_custom_call" | custom-call | flops 10000000000 | bytes 40000000 | tf_op jit(solution)/shard_map/pallas_call | solution.py:428
  202.0 35.0 %shard_map.248 = (f32[1024,1024]{1,0:T(8,128)S(1)}, bf16[16384,1024]{1,0:T(8,128)(2,1)}, f32[1024,1024]{1,0:T(8,128)S(1)}, f32[1024,1024]{1,0:T(8,128)S(1)}, bf1...) custom-call(s32[4,4]{1,0:T(4,128)S(1)} %bitcast.45, f32[1024,160]{1,0:T(8,128)S(1)} %bitcast.42, ...), custom_call_target="tpu_custom_call" | custom-call | flops 671088640 | bytes 54525952 | tf_op jit(solution)/shard_map/pallas_call | solution.py:623
  237.1 16.1 %multiply_convert_fusion = (bf16[1024,1024]{1,0:T(8,128)(2,1)}, bf16[1024,1024]{1,0:T(8,128)(2,1)S(1)}, f32[1024,1024]{1,0:T(8,128)}) fusion(f32[1024,1024]{1,0:T(8,128)S(1)} %get-tuple-element.73, f32[1024,1024]{1,0:T(8,128)} %get-tuple-element.70, bf16[1024,2048]{1,0:T(8,128)(2,1)} %bitcast.53, bf16[1024,2048]{1,0:T(8,128)(2,1)} %bitcast.51), kind=kOutput, calls=%fused_computation | convolution fusion | flops 4309647360 | bytes 25165824 | tf_op jit(solution)/shard_map/dot_general | solution.py:1608
  253.3 6.4 %convolution_convert_fusion = bf16[2048,1024]{1,0:T(8,128)(2,1)} fusion(bf16[1024,2048]{1,0:T(8,128)(2,1)S(1)} %copy-done.27, bf16[1024,1024]{1,0:T(8,128)(2,1)S(1)} %get-tuple-element.97.gg_ref), kind=kOutput, calls=%fused_computation.4 | convolution fusion | flops 4297064448 | bytes 10485760 | tf_op jit(solution)/shard_map/dot_general | solution.py:1609
  259.6 96.8 %shard_map.249 = (bf16[1024,1024]{1,0:T(8,128)(2,1)}, f32[1024,1024]{1,0:T(8,128)}, f32[4,256,160]{2,1,0:T(8,128)}, f32[16,1024]{1,0:T(8,128)}, f32[8,1024]{1,0:...) custom-call(s32[4,4]{1,0:T(4,128)} %bitcast.46, ...), custom_call_target="tpu_custom_call" | custom-call | flops 1342177280 | bytes 62914560 | tf_op jit(solution)/shard_map/pallas_call | solution.py:862
  356.4 136.4 %shard_map.250 = (bf16[32,8,2176]{2,1,0:T(8,128)(2,1)}, bf16[32,8,2048]{2,1,0:T(8,128)(2,1)}, bf16[4,256,2048]{2,1,0:T(8,128)(2,1)}, bf16[4,128,2048]{2,1,0:T(8,128)(2,1)}, f32[320,512]{1,0:T(8,128)}) custom-call(s32[4,4]{1,0:T(4,128)} %bitcast.47, f32[1024,1024]{1,0:T(8,128)} %get-tuple-element.74.da_ref, f32[1024,1024]{1,0:T(8,128)} %get-tuple-element.75.conv_ref, ...), custom_call_target="tpu_custom_call" | custom-call | flops 20000000000 | bytes 60000000 | tf_op jit(solution)/shard_map/pallas_call | solution.py:1174
  492.8 2.8 convolution_convert_fusion.1
  499.8 1.4 fusion.12
  501.2 1.3 slice.94
  502.5 1.4 slice.99
  503.9 1.7 slice.97
  505.6 1.7 slice.96
  507.3 3.2 fusion.11
  510.5 2.8 bitcast_convert_fusion
  514.1 5.5 %shard_map.251 = (f32[256,8192]{1,0:T(8,128)}, f32[256,128]{1,0:T(8,128)S(1)}) custom-call(bf16[4,256,2048]{2,1,0:T(8,128)(2,1)S(1)} %copy-done.5, bf16[256,8192]{1,0:T(8,128)(2,1)S(1)} %copy-done.2), custom_call_target="tpu_custom_call" | custom-call | flops 8388608 | bytes 16777216 | tf_op jit(solution)/shard_map/pallas_call | solution.py:1556
  (83 shorter events, 13.8 us)
Async XLA Ops:
  0.6 9.8 %copy-start = (bf16[160,512]{1,0:T(8,128)(2,1)S(1)}, bf16[160,512]{1,0:T(8,128)(2,1)}, u32[]{:S(2)}) copy-start(bf16[160,512]{1,0:T(8,128)(2,1)} %param.22) | copy-start | bytes 491524
  0.7 16.5 %copy-start.9 = (bf16[256,2048]{1,0:T(8,128)(2,1)S(1)}, bf16[256,2048]{1,0:T(8,128)(2,1)}, u32[]{:S(2)}) copy-start(bf16[256,2048]{1,0:T(8,128)(2,1)} %x_ref.1) | copy-start | bytes 3145732
  158.4 2.0 copy-start.21
  160.4 5.2 copy-start.24
  164.8 37.2 %copy-start.16 = (s32[4,1,4]{2,1,0:T(1,128)}, s32[4,1,4]{2,1,0:T(1,128)S(1)}, u32[]{:S(2)}) copy-start(s32[4,1,4]{2,1,0:T(1,128)S(1)} %slice.78) | copy-start | bytes 196
  164.8 37.1 %copy-start.17 = (f32[2,8,128]{2,0,1:T(2,128)}, f32[2,8,128]{2,0,1:T(2,128)S(1)}, u32[]{:S(2)}) copy-start(f32[2,8,128]{2,0,1:T(2,128)S(1)} %bitcast_convert_fusion.1) | copy-start | bytes 24580
  164.9 37.1 %copy-start.14 = (f32[1,1024]{1,0:T(1,128)}, f32[1,1024]{1,0:T(1,128)S(1)}, u32[]{:S(2)}) copy-start(f32[1,1024]{1,0:T(1,128)S(1)} %get-tuple-element.106.skip_ref) | copy-start | bytes 12292
  164.9 37.0 %copy-start.15 = (f32[4,1024]{1,0:T(4,128)}, f32[4,1024]{1,0:T(4,128)S(1)}, u32[]{:S(2)}) copy-start(f32[4,1024]{1,0:T(4,128)S(1)} %slice_convert_fusion.taps_ref) | copy-start | bytes 49156
  165.6 36.4 %copy-start.13 = (f32[16,1024]{1,0:T(8,128)}, f32[16,1024]{1,0:T(8,128)S(1)}, u32[]{:S(2)}) copy-start(f32[16,1024]{1,0:T(8,128)S(1)} %get-tuple-element.105.rate_ref) | copy-start | bytes 196612
  165.7 36.4 %copy-start.8 = (bf16[128,1024]{1,0:T(8,128)(2,1)}, bf16[128,1024]{1,0:T(8,128)(2,1)S(1)}, u32[]{:S(2)}) copy-start(bf16[128,1024]{1,0:T(8,128)(2,1)S(1)} %slice.83.stepw_ref) | copy-start | bytes 786436
  165.8 36.2 %copy-start.12 = (bf16[160,1024]{1,0:T(8,128)(2,1)}, bf16[160,1024]{1,0:T(8,128)(2,1)S(1)}, u32[]{:S(2)}) copy-start(bf16[160,1024]{1,0:T(8,128)(2,1)S(1)} %slice.82.sel_ref) | copy-start | bytes 983044
  165.8 36.3 %copy-start.23 = (bf16[256,2048]{1,0:T(8,128)(2,1)S(1)}, bf16[256,2048]{1,0:T(8,128)(2,1)}, u32[]{:S(2)}) copy-start(bf16[256,2048]{1,0:T(8,128)(2,1)} %copy-done.22) | copy-start | bytes 3145732
  202.0 35.1 %copy-start.6 = (bf16[1024,1024]{1,0:T(8,128)(2,1)}, bf16[1024,1024]{1,0:T(8,128)(2,1)S(1)}, u32[]{:S(2)}) copy-start(bf16[1024,1024]{1,0:T(8,128)(2,1)S(1)} %get-tuple-element.63.act_ref) | copy-start | bytes 6291460
  202.0 35.1 %copy-start.7 = (f32[4,256,160]{2,1,0:T(8,128)}, f32[4,256,160]{2,1,0:T(8,128)S(1)}, u32[]{:S(2)}) copy-start(f32[4,256,160]{2,1,0:T(8,128)S(1)} %get-tuple-element.62) | copy-start | bytes 1966084
  237.1 16.2 %copy-start.3 = (f32[1024,1024]{1,0:T(8,128)}, f32[1024,1024]{1,0:T(8,128)S(1)}, u32[]{:S(2)}) copy-start(f32[1024,1024]{1,0:T(8,128)S(1)} %get-tuple-element.66.delta_ref) | copy-start | bytes 12582916
  237.1 16.2 %copy-start.4 = (f32[1024,1024]{1,0:T(8,128)}, f32[1024,1024]{1,0:T(8,128)S(1)}, u32[]{:S(2)}) copy-start(f32[1024,1024]{1,0:T(8,128)S(1)} %get-tuple-element.67.pre_ref) | copy-start | bytes 12582916
  237.1 16.2 %copy-start.27 = (bf16[1024,2048]{1,0:T(8,128)(2,1)S(1)}, bf16[1024,2048]{1,0:T(8,128)(2,1)}, u32[]{:S(2)}) copy-start(bf16[1024,2048]{1,0:T(8,128)(2,1)} %get-tuple-element.72.normed_ref) | copy-start | bytes 12582916
  253.2 6.4 %copy-start.28 = (bf16[1024,1024]{1,0:T(8,128)(2,1)}, bf16[1024,1024]{1,0:T(8,128)(2,1)S(1)}, u32[]{:S(2)}) copy-start(bf16[1024,1024]{1,0:T(8,128)(2,1)S(1)} %get-tuple-element.97.gg_ref) | copy-start | bytes 6291460
  356.4 150.9 %copy-start.10 = (bf16[256,2048]{1,0:T(8,128)(2,1)S(1)}, bf16[256,2048]{1,0:T(8,128)(2,1)}, u32[]{:S(2)}) copy-start(bf16[256,2048]{1,0:T(8,128)(2,1)} %x_ref.1) | copy-start | bytes 3145732
  492.8 17.7 %copy-start.25 = (bf16[4,128,2048]{2,1,0:T(8,128)(2,1)S(1)}, bf16[4,128,2048]{2,1,0:T(8,128)(2,1)}, u32[]{:S(2)}) copy-start(bf16[4,128,2048]{2,1,0:T(8,128)(2,1)} %get-tuple-element.93) | copy-start | bytes 6291460
  507.3 6.0 %copy-start.5 = (bf16[4,256,2048]{2,1,0:T(8,128)(2,1)S(1)}, bf16[4,256,2048]{2,1,0:T(8,128)(2,1)}, u32[]{:S(2)}) copy-start(bf16[4,256,2048]{2,1,0:T(8,128)(2,1)} %get-tuple-element.89.x_ref) | copy-start | bytes 12582916
  510.5 3.6 copy-start.2
  510.5 9.8 %copy-start.1 = (bf16[160,512]{1,0:T(8,128)(2,1)S(1)}, bf16[160,512]{1,0:T(8,128)(2,1)}, u32[]{:S(2)}) copy-start(bf16[160,512]{1,0:T(8,128)(2,1)} %param.22) | copy-start | bytes 491524
  514.1 5.6 %copy-start.26 = (bf16[256]{0:T(256)(128)(2,1)S(1)}, bf16[256]{0:T(256)(128)(2,1)}, u32[]{:S(2)}) copy-start(bf16[256]{0:T(256)(128)(2,1)} %param.18) | copy-start | bytes 1540
  (5 other events, 5.6 us)

commit v8 on v7

--- a/solution.py
+++ b/solution.py
@@ -280,6 +280,10 @@
         self.local.wait()
 
 
+def my_rows(ref, height):
+    return ref.at[pl.ds(pl.multiple_of(lax.axis_index("dp") * height, height), height), :]
+
+
 def side_by_side(count, height, wide):
     return (count, height, wide) if wide % 128 else (height, count * wide)
 
@@ -343,7 +347,8 @@
     g = pl.program_id(0)
     n_dp, tok = part.shape[:2]
     rows, width = x_ref.shape
-    hops = [ring_copy(n_f, wo_ref, next_ref.at[up, 0], hop_send.at[up, 0], hop_recv.at[up, 0], up) for up in (0, 1)]
+    wo_mine = my_rows(wo_ref, next_ref.shape[2])
+    hops = [ring_copy(n_f, wo_mine, next_ref.at[up, 0], hop_send.at[up, 0], hop_recv.at[up, 0], up) for up in (0, 1)]
     hops2 = [
         ring_copy(n_f, next_ref.at[up, 0], next_ref.at[up, 1], hop_send.at[up, 1], hop_recv.at[up, 1], up)
         for up in (0, 1)
@@ -411,7 +416,7 @@
             b.wait()
 
 
-def enter(lens, x_all, gain, wx, wg, taps, bias, sel, wo_block, n_f):
+def enter(lens, x_all, gain, wx, wg, taps, bias, sel, wo, n_f):
     n_dp = lens.shape[0]
     rows, width = x_all.shape
     tok = rows // n_dp
@@ -455,7 +460,7 @@
             shaped(ch, BF16),
             shaped(ch, F32),
             jax.ShapeDtypeStruct((n_dp, tok, wide), F32),
-            jax.ShapeDtypeStruct((2, 2) + wo_block.shape, BF16),
+            jax.ShapeDtypeStruct((2, 2, wo.shape[0] // n_dp, wo.shape[1]), BF16),
         ],
         scratch_shapes=GroupSum.scratch(tok, wide)
         + [pltpu.SemaphoreType.DMA((2, 2)), pltpu.SemaphoreType.DMA((2, 2))],
@@ -463,7 +468,7 @@
             collective_id=1, has_side_effects=True, vmem_limit_bytes=48 * 2**20
         ),
         cost_estimate=pl.CostEstimate(flops=10**10, bytes_accessed=4 * 10**7, transcendentals=10**6),
-    )(lens, x_all, gain, wx, wg, taps, bias, sel, wo_block)
+    )(lens, x_all, gain, wx, wg, taps, bias, sel, wo)
 
 
 def fold_matrix(n):
@@ -549,7 +554,7 @@
     low_n = stepw_ref.shape[0]
     steps = pl.num_programs(0) * pl.num_programs(1)
     now = pl.program_id(0) * pl.num_programs(1) + pl.program_id(1)
-    ring = RingGather(n_f, wo_ref, next_ref, wo_all, local, hop_send, hop_recv)
+    ring = RingGather(n_f, my_rows(wo_ref, next_ref.shape[2]), next_ref, wo_all, local, hop_send, hop_recv)
     share = PairShare(dy_ref, lambda m: dy_all.at[m], local.at[5], sh_send, sh_recv, True)
 
     @pl.when(now == 0)
@@ -612,7 +617,7 @@
         share.finish()
 
 
-def scan_forward(lens, dbl, act, stepw, stepb, rate2, skip, wo_block, wo_next, dy_own, n_f, row_len, tblk=64, lanes=512):
+def scan_forward(lens, dbl, act, stepw, stepb, rate2, skip, wo, wo_next, dy_own, n_f, row_len, tblk=64, lanes=512):
     t, ch = act.shape
     n = rate2.shape[0]
     nb = row_len // tblk
@@ -648,7 +653,7 @@
             jax.ShapeDtypeStruct((t * n, ch), BF16),
             wide,
             wide,
-            jax.ShapeDtypeStruct((n_f,) + wo_block.shape, BF16),
+            jax.ShapeDtypeStruct((n_f,) + wo_next.shape[2:], BF16),
             jax.ShapeDtypeStruct((t // row_len,) + dy_own.shape, BF16),
         ],
         scratch_shapes=[
@@ -669,7 +674,7 @@
             collective_id=2, has_side_effects=True, vmem_limit_bytes=32 * 2**20
         ),
         cost_estimate=pl.CostEstimate(flops=t * n * ch * 40, bytes_accessed=t * ch * 52, transcendentals=t * n * ch),
-    )(lens, dbl, act, stepw, stepb, rate2, skip, wo_block, wo_next, dy_own)
+    )(lens, dbl, act, stepw, stepb, rate2, skip, wo, wo_next, dy_own)
 
 
 def bwd_kernel(lanes, n_f, lens_ref, dbl_ref, delta_ref, pre_ref, act_ref, gy_ref, stepw_ref, rate_ref, skip_ref,
@@ -1254,14 +1259,31 @@
     return jnp.where(lax.rem(f, 2) == 0, f // 2, n_f - 1 - f // 2)
 
 
-def gather_kernel(n_dp, n_f, downs, x_ref, dy_ref, meta_ref, dest_ref, lens_ref, *refs):
+def pack_kernel(cs, me_d, starts, w_ref, small_refs, gain_ref, blocks):
+    small, halves = blocks[0], blocks[1:]
+    lanes = pl.ds(pl.multiple_of(me_d * cs, 128), cs)
+    sel, step, decay, rest = small_refs[0], small_refs[1], small_refs[2], small_refs[3:]
+    at = 0
+    for ref in (sel, step, decay):
+        small[at : at + ref.shape[0], :] = ref[:, lanes]
+        at += ref.shape[0]
+    rows = [ref[:, lanes].astype(F32) for ref in rest] + [gain_ref[...].astype(F32)]
+    filler = small.shape[0] - at - sum(r.shape[0] for r in rows)
+    small[at:, :] = jnp.concatenate(rows + [jnp.zeros((filler, cs), F32)], axis=0).astype(BF16)
+    for o, out in enumerate(halves):
+        for j, start in enumerate(starts[o]):
+            out[:, j * cs : (j + 1) * cs] = w_ref[:, pl.ds(pl.multiple_of(start + me_d * cs, 128), cs)]
+
+
+def gather_kernel(n_dp, n_f, downs, segs, pack, x_ref, dy_ref, dest_row_ref, dest_ref, lens_ref, *refs):
     streams = len(downs)
-    blocks = refs[:streams]
-    x_all, lens_all, x_own_ref, dy_own_ref, tag_ref, rank_ref = refs[streams : streams + 6]
-    outs = refs[streams + 6 : 2 * streams + 6]
+    given = len(pack[1]) if pack else streams
+    x_all, lens_all, x_own_ref, dy_own_ref, tag_ref, rank_ref, ride_ref = refs[given : given + 7]
+    outs = refs[given + 7 : given + 7 + streams]
     (send_x, send_dy, got_x, got_dy, x_own, dy_own, deal_sem, loc_sem, pair_send, pair_recv, ring_send, ring_recv) = (
-        refs[2 * streams + 6 :]
+        refs[given + 7 + streams : given + 19 + streams]
     )
+    blocks = refs[given + 19 + streams :] if pack else refs[:streams]
     count = n_dp * n_f
     me_d = lax.axis_index("dp")
     me_f = lax.axis_index("fsdp")
@@ -1279,6 +1301,9 @@
         return 0
 
     lax.fori_loop(1, count, greet, 0)
+    if pack:
+        pack_kernel(pack[0], me_d, pack[2], refs[0], refs[1 : given - 1], refs[given - 1], blocks)
+
     def place_of(s, index):
         return lane_block(outs[s], index, blocks[s].shape[1]) if s == 0 else outs[s].at[index]
 
@@ -1332,7 +1357,11 @@
     tok, width = x_own.shape
     pair = got_x.shape[1]
 
-    dest_row, rel_row, abs_row, in_row = (meta_ref[i : i + 1, :] for i in range(4))
+    dest_row = dest_row_ref[...]
+    abs_row = jnp.floor((dest_row + 0.5) * (1.0 / tok))
+    in_row = dest_row - abs_row * tok
+    rel_row = abs_row - me.astype(F32)
+    rel_row = jnp.where(rel_row < 0.0, rel_row + count, rel_row)
     rank = jnp.sum((dest_ref[...] < dest_row).astype(F32), axis=0, keepdims=True)
     goal = rel_row * pair + rank - abs_row * pair
     rank_ref[...] = jnp.broadcast_to(goal, rank_ref.shape)
@@ -1411,6 +1440,21 @@
     keep(lens_ref, lens_all.at[0])
     keep(x_own, x_all.at[0])
     keep(x_own, x_own_ref)
+
+    lane = lax.broadcasted_iota(jnp.int32, (1, 128), 1)
+    limit = jnp.sum(jnp.where(lane < segs - 1, lens_ref[0:1, :], 0).astype(F32), axis=1, keepdims=True)
+
+    def squares(i, total_):
+        v = x_own[pl.ds(pl.multiple_of(i * 32, 32), 32), :].astype(F32)
+        t = (lax.broadcasted_iota(jnp.int32, (32, 1), 0) + i * 32).astype(F32)
+        each = jnp.sum(v * v, axis=1, keepdims=True)
+        return total_ + jnp.sum(jnp.where(t < limit, each, 0.0), axis=0, keepdims=True)
+
+    ride = jnp.zeros((1, 128), F32)
+    for j, value in enumerate((lax.fori_loop(0, tok // 32, squares, jnp.zeros((1, 1), F32)), limit)):
+        high = value.astype(BF16).astype(F32)
+        ride = ride + jnp.where(lane == 2 * j, high, 0.0) + jnp.where(lane == 2 * j + 1, value - high, 0.0)
+    ride_ref[...] = jnp.broadcast_to(ride, ride_ref.shape)
 
     def relay(a):
         held = [0]
@@ -1455,7 +1499,7 @@
     dealt(1, 0)
 
 
-def gather_all(x, dy, meta, dest, lens, blocks, downs, n_dp, n_f):
+def gather_all(x, dy, dest, lens, segs, blocks, pack, downs, n_dp, n_f):
     streams = len(blocks)
     tok, width = x.shape
     count = n_dp * n_f
@@ -1467,9 +1511,9 @@
     row = jax.ShapeDtypeStruct((tok, width), BF16)
     rows = jax.ShapeDtypeStruct((n_dp, tok, width), BF16)
     return pl.pallas_call(
-        functools.partial(gather_kernel, n_dp, n_f, downs),
-        in_specs=[vmem] * 5 + [any_] * streams,
-        out_specs=[any_] * 4 + [vmem] * 2 + [any_] * streams,
+        functools.partial(gather_kernel, n_dp, n_f, downs, segs, pack and (pack[0], [None] * len(pack[1]), pack[2])),
+        in_specs=[vmem] * 5 + ([vmem] * len(pack[1]) if pack else [any_] * streams),
+        out_specs=[any_] * 4 + [vmem] * 3 + [any_] * streams,
         out_shape=[
             rows,
             jax.ShapeDtypeStruct((n_dp,) + lens.shape, lens.dtype),
@@ -1477,6 +1521,7 @@
             row,
             jax.ShapeDtypeStruct((tok, 128), F32),
             jax.ShapeDtypeStruct((8, tok), F32),
+            jax.ShapeDtypeStruct((8, 128), F32),
         ]
         + [jax.ShapeDtypeStruct(side_by_side(n_f, *blocks[0].shape), BF16)]
         + [jax.ShapeDtypeStruct((n_f,) + b.shape, b.dtype) for b in blocks[1:]],
@@ -1493,42 +1538,16 @@
             pltpu.SemaphoreType.DMA((2, n_dp)),
             pltpu.SemaphoreType.DMA((streams, 2, hops)),
             pltpu.SemaphoreType.DMA((streams, 2, hops)),
-        ],
+        ]
+        + ([pltpu.VMEM(b.shape, BF16) for b in blocks] if pack else []),
         compiler_params=pltpu.CompilerParams(
             collective_id=0, has_side_effects=True, vmem_limit_bytes=40 * 2**20
         ),
         cost_estimate=pl.CostEstimate(flops=10**10, bytes_accessed=2 * 10**8, transcendentals=0),
-    )(x, dy, meta, dest, lens, *blocks)
-
-
-def columns_kernel(starts, cs, w_ref, *outs):
-    me_d = lax.axis_index("dp")
-    for o, out in enumerate(outs):
-        for j, start in enumerate(starts[o]):
-            out[:, j * cs : (j + 1) * cs] = w_ref[:, pl.ds(pl.multiple_of(start + me_d * cs, 128), cs)]
-
-
-def take_columns(w, halves, n_f, n_dp, cs):
-    inner = n_f * n_dp * cs
-    starts = [[h * inner + f * n_dp * cs for f in range(n_f)] for h in range(halves)]
-    me_d = lax.axis_index("dp")
-    if cs % 128:
-        return [
-            jnp.concatenate([lax.dynamic_slice_in_dim(w, s + me_d * cs, cs, 1) for s in group], axis=1)
-            for group in starts
-        ]
-    height = w.shape[0]
-    blk = min(height, 64)
-    return pl.pallas_call(
-        functools.partial(columns_kernel, starts, cs),
-        grid=(height // blk,),
-        in_specs=[pl.BlockSpec((blk, w.shape[1]), lambda i: (i, 0))],
-        out_specs=[pl.BlockSpec((blk, n_f * cs), lambda i: (i, 0))] * halves,
-        out_shape=[jax.ShapeDtypeStruct((height, n_f * cs), w.dtype)] * halves,
-    )(w)
-
-
-def spread_kernel(cs, x_ref, w_ref, out_ref, sum_ref):
+    )(x, dy, dest[None, :], dest[:, None], lens, *(pack[1] if pack else blocks))
+
+
+def spread_kernel(cs, x_ref, w_ref, go_ref, small_ref, out_ref, sum_ref, go_out, *small_outs):
     total = jnp.zeros(sum_ref.shape, F32)
     n_dp = x_ref.shape[0]
     for f in range(x_ref.shape[2] // cs):
@@ -1539,36 +1558,51 @@
             product = part * w_ref[:, cols].astype(F32)
             for j in range(0, cs, 128):
                 total = total + product[:, j : j + 128]
+    go_out[...] = go_ref[...].astype(F32)
 
     @pl.when(pl.program_id(0) == 0)
     def _():
         sum_ref[...] = jnp.zeros_like(sum_ref)
+        at = 0
+        for out in small_outs:
+            out[...] = small_ref[at : at + out.shape[0], :]
+            at += out.shape[0]
 
     sum_ref[...] += total
 
 
-def spread_columns(parts, w, cs):
+def spread_columns(parts, w, go, small, heights, cs):
     n_dp, height, cols = parts.shape
     if cs % 128:
         out = parts.reshape(n_dp, height, cols // cs, cs).transpose(1, 2, 0, 3).reshape(height, n_dp * cols).astype(F32)
-        return out, jnp.sum(out * w.astype(F32), axis=1)
+        cuts = [small[sum(heights[:i]) : sum(heights[: i + 1])] for i in range(len(heights))]
+        return out, jnp.sum(out * w.astype(F32), axis=1), go.astype(F32), cuts
     wide = 2 * cs
-    out, sums = pl.pallas_call(
+    steps = cols // wide
+    once = lambda f: (0, 0)
+    go_block = (go.shape[0] // steps, go.shape[1])
+    shaped = jax.ShapeDtypeStruct
+    out, sums, go, *cuts = pl.pallas_call(
         functools.partial(spread_kernel, cs),
-        grid=(cols // wide,),
+        grid=(steps,),
         in_specs=[
             pl.BlockSpec((n_dp, height, wide), lambda f: (0, 0, f)),
             pl.BlockSpec((height, n_dp * wide), lambda f: (0, f)),
+            pl.BlockSpec(go_block, lambda f: (f, 0)),
+            pl.BlockSpec(small.shape, once),
         ],
         out_specs=[
             pl.BlockSpec((height, n_dp * wide), lambda f: (0, f)),
-            pl.BlockSpec((height, 128), lambda f: (0, 0)),
-        ],
-        out_shape=[jax.ShapeDtypeStruct((height, n_dp * cols), F32), jax.ShapeDtypeStruct((height, 128), F32)],
+            pl.BlockSpec((height, 128), once),
+            pl.BlockSpec(go_block, lambda f: (f, 0)),
+        ]
+        + [pl.BlockSpec((h, small.shape[1]), once) for h in heights],
+        out_shape=[shaped((height, n_dp * cols), F32), shaped((height, 128), F32), shaped(go.shape, F32)]
+        + [shaped((h, small.shape[1]), F32) for h in heights],
         compiler_params=pltpu.CompilerParams(vmem_limit_bytes=32 * 2**20),
         cost_estimate=pl.CostEstimate(flops=4 * height * cols * n_dp, bytes_accessed=8 * height * cols * n_dp, transcendentals=0),
-    )(parts, w)
-    return out, jnp.sum(sums, axis=1)
+    )(parts, w, go, small)
+    return out, jnp.sum(sums, axis=1), go, cuts
 
 
 def per_device(
@@ -1608,31 +1642,33 @@
     nt_dot = lambda a, b: lax.dot_general(a, b, (((1,), (1,)), ((), ())), preferred_element_type=F32)
     tn_dot = lambda a, b: lax.dot_general(a, b, (((0,), (0,)), ((), ())), preferred_element_type=F32)
 
-    me = me_d * n_f + me_f
-    row_to = destination // tok
-    meta = jnp.stack(
-        [destination, (row_to - me) % rows, row_to, destination % tok] + [jnp.zeros_like(destination)] * 4
-    ).astype(F32)
     segs = lengths.shape[1]
     lens_tile = jnp.pad(lengths, ((0, 7), (0, 128 - segs)))
     slots = jnp.arange(tok, dtype=jnp.int32)
 
-    def mine(shard):
-        return lax.dynamic_slice_in_dim(shard.reshape(-1, n_dp * cs), me_d * cs, cs, 1)
-
-    smalls = [conv_weight, conv_bias, step_bias, skip_gain, decay_log, select_weight, step_weight]
-    heights = [math.prod(s.shape) // (n_dp * cs) for s in smalls]
+    flat = lambda shard: shard.reshape(-1, n_dp * cs)
+    smalls = [
+        flat(v) for v in (select_weight, step_weight, decay_log, conv_weight, conv_bias, step_bias, skip_gain)
+    ]
     gain_rows = dcols // cs
-    used = sum(heights) + gain_rows
-    filler = -used % 16
-    small_block = jnp.concatenate(
-        [mine(s) for s in smalls] + [norm_gain.reshape(gain_rows, cs), jnp.zeros((filler, cs), BF16)], axis=0
-    )
-    wx_block, wg_block = take_columns(in_weight, 2, n_f, n_dp, cs)
-    wo_block = lax.dynamic_slice_in_dim(out_weight, me_d * cs, cs, 0)
-    x_all, lens_all, x_own, dy_own, x_tags, ranks, small_all, wx, wg = gather_all(
-        tokens, cotangent, meta, destination[:, None].astype(F32), lens_tile,
-        [small_block, wx_block, wg_block], [n_f // 2, n_f // 2, n_f - 1 - n_f // 2], n_dp, n_f,
+    gain_block = norm_gain.reshape(gain_rows, cs)
+    used = sum(v.shape[0] for v in smalls) + gain_rows
+    tall = used + -used % 16
+    starts = [[h * inner + f * n_dp * cs for f in range(n_f)] for h in (0, 1)]
+    if cs % 128:
+        mine = lambda value, at: lax.dynamic_slice_in_dim(value, at + me_d * cs, cs, 1)
+        blocks = [
+            jnp.concatenate(
+                [mine(v, 0) for v in smalls] + [gain_block, jnp.zeros((tall - used, cs), BF16)], axis=0
+            )
+        ] + [jnp.concatenate([mine(in_weight, at) for at in half], axis=1) for half in starts]
+        pack = None
+    else:
+        blocks = [jax.ShapeDtypeStruct((tall, cs), BF16)] + [jax.ShapeDtypeStruct((dcols, ch), BF16)] * 2
+        pack = (cs, [in_weight] + smalls + [gain_block], starts)
+    x_all, lens_all, x_own, dy_own, x_tags, ranks, ride, small_all, wx, wg = gather_all(
+        tokens, cotangent, destination.astype(F32), lens_tile, segs, blocks, pack,
+        [n_f // 2, n_f // 2, n_f - 1 - n_f // 2], n_dp, n_f,
     )
     x_all = x_all.reshape(group, width)
     lens = lens_all[:, 0, :segs]
@@ -1640,28 +1676,25 @@
     wx = wx.reshape(width, ch)
     wg = wg.reshape(width, ch)
     small = joined(small_all)
-    gain = small[used - gain_rows : used].reshape(gain_rows, n_f, cs).transpose(1, 0, 2).reshape(width).astype(F32)
-    valid = (slots < jnp.sum(lengths[0, : segs - 1])).astype(F32)
-    x_own32 = x_own.astype(F32)
-    square = jnp.sum(x_own32 * x_own32, axis=1)
-    mine_sums = [jnp.sum(square * valid), jnp.sum(valid)]
-
-    pieces, at = [], 0
-    for height in heights:
-        pieces.append(small[at : at + height])
-        at += height
-    conv_w, conv_b, step_b, skip, dlog, sel, stepw = pieces
+    at = select_weight.shape[0]
+    sel = small[:at]
+    stepw = small[at : at + rank_of]
+    dlog = small[at + rank_of : at + rank_of + n]
+    misc = small[at + rank_of + n :]
+    conv_w, conv_b, step_b, skip = misc[:taps], misc[taps : taps + 1], misc[taps + 1 : taps + 2], misc[taps + 2 : taps + 3]
+    gain = misc[taps + 3 : taps + 3 + gain_rows]
+    gain = gain.reshape(gain_rows, n_f, cs).transpose(1, 0, 2).reshape(width).astype(F32)
     conv_w = conv_w.astype(F32)
     skip = skip.astype(F32)
     rate = -jnp.exp(dlog.astype(F32))
 
     normed, x_in, conv, act, gate, dbl, wo_next = enter(
-        lens, x_all, gain[None], wx, wg, conv_w, conv_b.astype(F32), sel, wo_block, n_f
+        lens, x_all, gain[None], wx, wg, conv_w, conv_b.astype(F32), sel, out_weight, n_f
     )
     dbl = dbl.reshape(group, -1)
     rate2 = rate * LOG2E
     scan_out, states, delta, pre, wo, dy_all = scan_forward(
-        lens, dbl, act, stepw, step_b.astype(F32), rate2, skip, wo_block, wo_next, dy_own, n_f, tok
+        lens, dbl, act, stepw, step_b.astype(F32), rate2, skip, out_weight, wo_next, dy_own, n_f, tok
     )
     dy_all = dy_all.reshape(group, width)
     wo = wo.reshape(ch, width)
@@ -1676,27 +1709,17 @@
         lens, dbl, delta, pre, act, scan_grad, stepw, rate2, skip, states,
         wg_grad.reshape(n_f, dcols, ch), gated, dy_all, wo, n_f, tok,
     )
-    lanes = lax.broadcasted_iota(jnp.int32, (1, 128), 1)
-    ride = jnp.zeros((1, 128), F32)
-    for j, value in enumerate(mine_sums):
-        high = value.astype(BF16).astype(F32)
-        ride = ride + jnp.where(lanes == 2 * j, high, 0.0) + jnp.where(lanes == 2 * j + 1, value - high, 0.0)
     mix_back, dx_back, gin_all, go_all, small_full = leave(
         lens, act_grad, conv, x_in, act, dbl_grad, sel, conv_w, sums, decay_sum, rate, step_grad, normed, wx, wg,
-        gate_grad, wo_grad, wo_half, wg_own, x_own, dy_own, mixed, gain[None], x_tags, ride, n_f,
+        gate_grad, wo_grad, wo_half, wg_own, x_own, dy_own, mixed, gain[None], x_tags, ride[:1], n_f,
     )
 
-    grad_in_weight, gain_sum = spread_columns(gin_all, in_weight, cs)
-    grad_out_weight = go_all.reshape(n_dp * cs, width).astype(F32)
-    small_full = joined(small_full)
+    grad_in_weight, gain_sum, grad_out_weight, cuts = spread_columns(
+        gin_all, in_weight, go_all.reshape(n_dp * cs, width), joined(small_full),
+        [select_weight.shape[0], rank_of, n, 8], cs,
+    )
+    grad_select, grad_step, grad_decay, misc = cuts
     grad_norm_gain = gain_sum / norm_gain.astype(F32)
-    wide = select_weight.shape[0]
-    at_decay = wide + rank_of
-    at_misc = at_decay + n
-    grad_select = small_full[:wide]
-    grad_step = small_full[wide:at_decay]
-    grad_decay = small_full[at_decay:at_misc]
-    misc = small_full[at_misc : at_misc + 8]
 
     back = mix_back.reshape(tok, width + 128)
     totals = jnp.sum(mix_back[:, 0, width : width + 4].astype(F32), axis=0)

time: 523 us -> 516 us (0.987)
  other arithmetic: 10.5 us -> 2.94 us
    unnamed x58 -> x68, local copies, waits for them, and re-layouts: 7.28 us -> 19.6 us
    pallas_call x3 -> x2, Pallas kernels: 147 us -> 146 us  [the longest x1 140 us: gather_all(): pl.pallas_call(functools.partial(gather_kernel, n_dp, n_f, downs, segs, p...]
where the time goes in v8:
time: 516 us; the launch traced here: 515 us
  Pallas kernels  451 us (87%)
  matrix products  31.3 us (6%)
  local copies, waits for them, and re-layouts  24.9 us (5%)
    pallas_call x1, Pallas kernels, gather_all(): pl.pallas_call(functools.partial(gather_kernel, n_dp, n_f, downs, segs, p...  140 us
    pallas_call x1, Pallas kernels, leave(): pl.pallas_call(functools.partial(leave_kernel, n_f, half), grid=(half + 2...  136 us
    pallas_call x1, Pallas kernels, scan_backward(): pl.pallas_call(functools.partial(bwd_kernel, min(lanes, ch), n_f), grid=(...  96.8 us
    pallas_call x1, Pallas kernels, enter(): pl.pallas_call(functools.partial(enter_kernel, n_f, half), grid=(2 * half...  36.2 us
    pallas_call x1, Pallas kernels, scan_forward(): pl.pallas_call(functools.partial(fwd_kernel, min(lanes, ch), n_f), grid=(...  35.6 us
    unnamed x68, local copies, waits for them, and re-layouts  19.6 us
    dot_general x1, matrix products, per_device(): lax.dot_general(a, b, (((1,), (1,)), ((), ())), preferred_element_type=F32)  16.3 us

profile of v8, /device:TPU:21, one launch (start us, length us, event | category | flops | bytes accessed | tf_op | source)
XLA Modules:
  0.0 515.2 jit_solution(9061082215372370455)
XLA Ops:
  4.2 1.2 copy-done.8
  6.1 1.2 copy-done.20
  7.3 0.9 copy-done.21
  8.2 0.9 copy-done.22
  9.1 0.7 copy-done.23
  10.5 139.7 %shard_map.245 = (bf16[4,256,2048]{2,1,0:T(8,128)(2,1)S(1)}, s32[4,8,128]{2,1,0:T(8,128)S(1)}, bf16[256,2048]{1,0:T(8,128)(2,1)S(1)}, bf16[256,2048]{1,0:T(8,128...) custom-call(bf16[256,2048]{1,0:T(8,128)(2,1)S(1)} %copy-done.8, ...), custom_call_target="tpu_custom_call" | custom-call | flops 10000000000 | bytes 200000000 | tf_op jit(solution)/shard_map/pallas_call | solution.py:1513
  150.3 2.0 copy-done.25
  152.3 2.0 copy-done.26
  154.3 1.0 copy-done.29
  155.3 1.0 copy-done.31
  157.6 36.2 %shard_map.246 = (bf16[1024,2048]{1,0:T(8,128)(2,1)}, f32[1024,1024]{1,0:T(8,128)}, f32[1024,1024]{1,0:T(8,128)}, bf16[1024,1024]{1,0:T(8,128)(2,1)S(1)}, f32[10...) custom-call(s32[4,4]{1,0:T(4,128)S(1)} %bitcast.34, ...), custom_call_target="tpu_custom_call" | custom-call | flops 10000000000 | bytes 40000000 | tf_op jit(solution)/shard_map/pallas_call | solution.py:433
  193.9 1.3 copy-done.27
  195.2 2.7 copy-done.28
  197.9 35.6 %shard_map.247 = (f32[1024,1024]{1,0:T(8,128)S(1)}, bf16[16384,1024]{1,0:T(8,128)(2,1)}, f32[1024,1024]{1,0:T(8,128)S(1)}, f32[1024,1024]{1,0:T(8,128)S(1)}, bf1...) custom-call(s32[4,4]{1,0:T(4,128)S(1)} %bitcast.35, f32[1024,160]{1,0:T(8,128)S(1)} %bitcast.32, ...), custom_call_target="tpu_custom_call" | custom-call | flops 671088640 | bytes 54525952 | tf_op jit(solution)/shard_map/pallas_call | solution.py:628
  233.6 16.3 %multiply_convert_fusion = (bf16[1024,1024]{1,0:T(8,128)(2,1)}, bf16[1024,1024]{1,0:T(8,128)(2,1)S(1)}, f32[1024,1024]{1,0:T(8,128)}) fusion(f32[1024,1024]{1,0:T(8,128)S(1)} %get-tuple-element.75, f32[1024,1024]{1,0:T(8,128)} %get-tuple-element.72, bf16[1024,2048]{1,0:T(8,128)(2,1)} %bitcast.48, bf16[1024,2048]{1,0:T(8,128)(2,1)} %bitcast.46), kind=kOutput, calls=%fused_computation | convolution fusion | flops 4309647360 | bytes 25165824 | tf_op jit(solution)/shard_map/dot_general | solution.py:1642
  249.9 9.1 %convolution_convert_fusion = bf16[2048,1024]{1,0:T(8,128)(2,1)} fusion(bf16[1024,2048]{1,0:T(8,128)(2,1)} %get-tuple-element.74.normed_ref, bf16[1024,1024]{1,0:T(8,128)(2,1)S(1)} %get-tuple-element.103.gg_ref), kind=kOutput, calls=%fused_computation.4 | convolution fusion | flops 4297064448 | bytes 10485760 | tf_op jit(solution)/shard_map/dot_general | solution.py:1643
  259.1 96.8 %shard_map.248 = (bf16[1024,1024]{1,0:T(8,128)(2,1)}, f32[1024,1024]{1,0:T(8,128)}, f32[4,256,160]{2,1,0:T(8,128)}, f32[16,1024]{1,0:T(8,128)}, f32[8,1024]{1,0:...) custom-call(s32[4,4]{1,0:T(4,128)} %bitcast.36, ...), custom_call_target="tpu_custom_call" | custom-call | flops 1342177280 | bytes 62914560 | tf_op jit(solution)/shard_map/pallas_call | solution.py:867
  355.9 136.3 %shard_map.249 = (bf16[32,8,2176]{2,1,0:T(8,128)(2,1)}, bf16[32,8,2048]{2,1,0:T(8,128)(2,1)}, bf16[4,256,2048]{2,1,0:T(8,128)(2,1)}, bf16[4,128,2048]{2,1,0:T(8,128)(2,1)}, f32[320,512]{1,0:T(8,128)}) custom-call(s32[4,4]{1,0:T(4,128)} %bitcast.37, f32[1024,1024]{1,0:T(8,128)} %get-tuple-element.76.da_ref, f32[1024,1024]{1,0:T(8,128)} %get-tuple-element.77.conv_ref, ...), custom_call_target="tpu_custom_call" | custom-call | flops 20000000000 | bytes 60000000 | tf_op jit(solution)/shard_map/pallas_call | solution.py:1179
  492.3 2.8 convolution_convert_fusion.1
  495.1 0.9 convert_reduce_fusion
  499.3 3.0 fusion.7
  502.3 2.2 copy-done.3
  504.5 1.1 copy-done.10
  505.6 6.6 %shard_map.250 = (f32[256,8192]{1,0:T(8,128)}, f32[256,128]{1,0:T(8,128)S(1)}, f32[512,2048]{1,0:T(8,128)}, f32[160,512]{1,0:T(8,128)}, f32[128,512]{1,0:T(8,128...) custom-call(bf16[4,256,2048]{2,1,0:T(8,128)(2,1)S(1)} %copy-done.3, bf16[256,8192]{1,0:T(8,128)(2,1)S(1)} %copy-done.2, ...), custom_call_target="tpu_custom_call" | custom-call | flops 8388608 | bytes 16777216 | tf_op jit(solution)/shard_map/pallas_call | solution.py:1585
  (75 shorter events, 8.7 us)
Async XLA Ops:
  150.3 2.0 copy-start.25
  152.3 2.0 copy-start.26
  156.2 37.6 %copy-start.32 = (f32[256,128]{1,0:T(8,128)}, f32[256,128]{1,0:T(8,128)S(1)}, u32[]{:S(2)}) copy-start(f32[256,128]{1,0:T(8,128)S(1)} %get-tuple-element.88.tags_ref) | copy-start | bytes 393220
  156.8 38.4 %copy-start.15 = (s32[4,1,4]{2,1,0:T(1,128)}, s32[4,1,4]{2,1,0:T(1,128)S(1)}, u32[]{:S(2)}) copy-start(s32[4,1,4]{2,1,0:T(1,128)S(1)} %slice.70) | copy-start | bytes 196
  156.8 37.0 %copy-start.16 = (f32[2,8,128]{2,0,1:T(2,128)}, f32[2,8,128]{2,0,1:T(2,128)S(1)}, u32[]{:S(2)}) copy-start(f32[2,8,128]{2,0,1:T(2,128)S(1)} %bitcast_convert_fusion) | copy-start | bytes 24580
  156.8 38.4 %copy-start.13 = (f32[1,1024]{1,0:T(1,128)}, f32[1,1024]{1,0:T(1,128)S(1)}, u32[]{:S(2)}) copy-start(f32[1,1024]{1,0:T(1,128)S(1)} %get-tuple-element.109.skip_ref) | copy-start | bytes 12292
  156.9 37.0 %copy-start.14 = (f32[4,1024]{1,0:T(4,128)}, f32[4,1024]{1,0:T(4,128)S(1)}, u32[]{:S(2)}) copy-start(f32[4,1024]{1,0:T(4,128)S(1)} %slice_convert_fusion.taps_ref) | copy-start | bytes 49156
  157.5 37.7 %copy-start.12 = (f32[16,1024]{1,0:T(8,128)}, f32[16,1024]{1,0:T(8,128)S(1)}, u32[]{:S(2)}) copy-start(f32[16,1024]{1,0:T(8,128)S(1)} %get-tuple-element.108.rate_ref) | copy-start | bytes 196612
  157.5 37.7 %copy-start.7 = (bf16[128,1024]{1,0:T(8,128)(2,1)}, bf16[128,1024]{1,0:T(8,128)(2,1)S(1)}, u32[]{:S(2)}) copy-start(bf16[128,1024]{1,0:T(8,128)(2,1)S(1)} %slice.75.stepw_ref) | copy-start | bytes 786436
  157.6 36.3 %copy-start.11 = (bf16[160,1024]{1,0:T(8,128)(2,1)}, bf16[160,1024]{1,0:T(8,128)(2,1)S(1)}, u32[]{:S(2)}) copy-start(bf16[160,1024]{1,0:T(8,128)(2,1)S(1)} %slice.74.sel_ref) | copy-start | bytes 983044
  157.6 37.6 %copy-start.19 = (bf16[512,2048]{1,0:T(8,128)(2,1)S(1)}, bf16[512,2048]{1,0:T(8,128)(2,1)}, u32[]{:S(2)}) copy-start(bf16[512,2048]{1,0:T(8,128)(2,1)} %wo_ref.3) | copy-start | bytes 6291460
  157.6 37.6 %copy-start.30 = (bf16[256,2048]{1,0:T(8,128)(2,1)S(1)}, bf16[256,2048]{1,0:T(8,128)(2,1)}, u32[]{:S(2)}) copy-start(bf16[256,2048]{1,0:T(8,128)(2,1)} %copy-done.29) | copy-start | bytes 3145732
  193.9 1.3 copy-start.27
  195.2 38.4 %copy-start.4 = (bf16[1024,1024]{1,0:T(8,128)(2,1)}, bf16[1024,1024]{1,0:T(8,128)(2,1)S(1)}, u32[]{:S(2)}) copy-start(bf16[1024,1024]{1,0:T(8,128)(2,1)S(1)} %get-tuple-element.65.act_ref) | copy-start | bytes 6291460
  195.2 38.4 %copy-start.6 = (f32[4,256,160]{2,1,0:T(8,128)}, f32[4,256,160]{2,1,0:T(8,128)S(1)}, u32[]{:S(2)}) copy-start(f32[4,256,160]{2,1,0:T(8,128)S(1)} %get-tuple-element.64) | copy-start | bytes 1966084
  195.2 2.7 copy-start.28
  233.6 16.3 %copy-start = (f32[1024,1024]{1,0:T(8,128)}, f32[1024,1024]{1,0:T(8,128)S(1)}, u32[]{:S(2)}) copy-start(f32[1024,1024]{1,0:T(8,128)S(1)} %get-tuple-element.68.delta_ref) | copy-start | bytes 12582916
  233.6 16.3 %copy-start.1 = (f32[1024,1024]{1,0:T(8,128)}, f32[1024,1024]{1,0:T(8,128)S(1)}, u32[]{:S(2)}) copy-start(f32[1024,1024]{1,0:T(8,128)S(1)} %get-tuple-element.69.pre_ref) | copy-start | bytes 12582916
  249.9 9.2 %copy-start.33 = (bf16[1024,1024]{1,0:T(8,128)(2,1)}, bf16[1024,1024]{1,0:T(8,128)(2,1)S(1)}, u32[]{:S(2)}) copy-start(bf16[1024,1024]{1,0:T(8,128)(2,1)S(1)} %get-tuple-element.103.gg_ref) | copy-start | bytes 6291460
  355.9 143.4 %copy-start.9 = (bf16[256,2048]{1,0:T(8,128)(2,1)S(1)}, bf16[256,2048]{1,0:T(8,128)(2,1)}, u32[]{:S(2)}) copy-start(bf16[256,2048]{1,0:T(8,128)(2,1)} %x_ref.1) | copy-start | bytes 3145732
  492.2 10.1 %copy-start.2 = (bf16[256,8192]{1,0:T(8,128)(2,1)S(1)}, bf16[256,8192]{1,0:T(8,128)(2,1)}, u32[]{:S(2)}) copy-start(bf16[256,8192]{1,0:T(8,128)(2,1)} %w_ref.1) | copy-start | bytes 12582916
  492.2 10.0 %copy-start.5 = (bf16[4,128,2048]{2,1,0:T(8,128)(2,1)S(1)}, bf16[4,128,2048]{2,1,0:T(8,128)(2,1)}, u32[]{:S(2)}) copy-start(bf16[4,128,2048]{2,1,0:T(8,128)(2,1)} %get-tuple-element.93) | copy-start | bytes 6291460
  502.3 2.2 copy-start.3
  505.6 6.7 %copy-start.18 = (bf16[256]{0:T(256)(128)(2,1)S(1)}, bf16[256]{0:T(256)(128)(2,1)}, u32[]{:S(2)}) copy-start(bf16[256]{0:T(256)(128)(2,1)} %param.18) | copy-start | bytes 1540
  (10 other events, 9.4 us)

commit v9 on v8

--- a/solution.py
+++ b/solution.py
@@ -280,10 +280,6 @@
         self.local.wait()
 
 
-def my_rows(ref, height):
-    return ref.at[pl.ds(pl.multiple_of(lax.axis_index("dp") * height, height), height), :]
-
-
 def side_by_side(count, height, wide):
     return (count, height, wide) if wide % 128 else (height, count * wide)
 
@@ -347,8 +343,7 @@
     g = pl.program_id(0)
     n_dp, tok = part.shape[:2]
     rows, width = x_ref.shape
-    wo_mine = my_rows(wo_ref, next_ref.shape[2])
-    hops = [ring_copy(n_f, wo_mine, next_ref.at[up, 0], hop_send.at[up, 0], hop_recv.at[up, 0], up) for up in (0, 1)]
+    hops = [ring_copy(n_f, wo_ref, next_ref.at[up, 0], hop_send.at[up, 0], hop_recv.at[up, 0], up) for up in (0, 1)]
     hops2 = [
         ring_copy(n_f, next_ref.at[up, 0], next_ref.at[up, 1], hop_send.at[up, 1], hop_recv.at[up, 1], up)
         for up in (0, 1)
@@ -460,7 +455,7 @@
             shaped(ch, BF16),
             shaped(ch, F32),
             jax.ShapeDtypeStruct((n_dp, tok, wide), F32),
-            jax.ShapeDtypeStruct((2, 2, wo.shape[0] // n_dp, wo.shape[1]), BF16),
+            jax.ShapeDtypeStruct((2, 2) + wo.shape, BF16),
         ],
         scratch_shapes=GroupSum.scratch(tok, wide)
         + [pltpu.SemaphoreType.DMA((2, 2)), pltpu.SemaphoreType.DMA((2, 2))],
@@ -554,7 +549,7 @@
     low_n = stepw_ref.shape[0]
     steps = pl.num_programs(0) * pl.num_programs(1)
     now = pl.program_id(0) * pl.num_programs(1) + pl.program_id(1)
-    ring = RingGather(n_f, my_rows(wo_ref, next_ref.shape[2]), next_ref, wo_all, local, hop_send, hop_recv)
+    ring = RingGather(n_f, wo_ref, next_ref, wo_all, local, hop_send, hop_recv)
     share = PairShare(dy_ref, lambda m: dy_all.at[m], local.at[5], sh_send, sh_recv, True)
 
     @pl.when(now == 0)
@@ -1666,6 +1661,7 @@
     else:
         blocks = [jax.ShapeDtypeStruct((tall, cs), BF16)] + [jax.ShapeDtypeStruct((dcols, ch), BF16)] * 2
         pack = (cs, [in_weight] + smalls + [gain_block], starts)
+    wo_block = lax.dynamic_slice_in_dim(out_weight, me_d * cs, cs, 0)
     x_all, lens_all, x_own, dy_own, x_tags, ranks, ride, small_all, wx, wg = gather_all(
         tokens, cotangent, destination.astype(F32), lens_tile, segs, blocks, pack,
         [n_f // 2, n_f // 2, n_f - 1 - n_f // 2], n_dp, n_f,
@@ -1689,12 +1685,12 @@
     rate = -jnp.exp(dlog.astype(F32))
 
     normed, x_in, conv, act, gate, dbl, wo_next = enter(
-        lens, x_all, gain[None], wx, wg, conv_w, conv_b.astype(F32), sel, out_weight, n_f
+        lens, x_all, gain[None], wx, wg, conv_w, conv_b.astype(F32), sel, wo_block, n_f
     )
     dbl = dbl.reshape(group, -1)
     rate2 = rate * LOG2E
     scan_out, states, delta, pre, wo, dy_all = scan_forward(
-        lens, dbl, act, stepw, step_b.astype(F32), rate2, skip, out_weight, wo_next, dy_own, n_f, tok
+        lens, dbl, act, stepw, step_b.astype(F32), rate2, skip, wo_block, wo_next, dy_own, n_f, tok
     )
     dy_all = dy_all.reshape(group, width)
     wo = wo.reshape(ch, width)

time: 516 us -> 513 us (level)
    unnamed x68 -> x60, local copies, waits for them, and re-layouts: 19.6 us -> 15.3 us
where the time goes in v9:
time: 513 us; the launch traced here: 512 us
  Pallas kernels  451 us (88%)
  matrix products  31.2 us (6%)
  local copies, waits for them, and re-layouts  21.6 us (4%)
    pallas_call x1, Pallas kernels, gather_all(): pl.pallas_call(functools.partial(gather_kernel, n_dp, n_f, downs, segs, p...  140 us
    pallas_call x1, Pallas kernels, leave(): pl.pallas_call(functools.partial(leave_kernel, n_f, half), grid=(half + 2...  136 us
    pallas_call x1, Pallas kernels, scan_backward(): pl.pallas_call(functools.partial(bwd_kernel, min(lanes, ch), n_f), grid=(...  96.6 us
    pallas_call x1, Pallas kernels, enter(): pl.pallas_call(functools.partial(enter_kernel, n_f, half), grid=(2 * half...  36.1 us
    pallas_call x1, Pallas kernels, scan_forward(): pl.pallas_call(functools.partial(fwd_kernel, min(lanes, ch), n_f), grid=(...  35.7 us
    dot_general x1, matrix products, per_device(): lax.dot_general(a, b, (((1,), (1,)), ((), ())), preferred_element_type=F32)  16.3 us
    unnamed x60, local copies, waits for them, and re-layouts  15.3 us

profile of v9, /device:TPU:21, one launch (start us, length us, event | category | flops | bytes accessed | tf_op | source)
XLA Modules:
  0.0 511.7 jit_solution(13830401224923094861)
XLA Ops:
  0.6 0.7 convert_element_type.77
  4.2 1.1 constant_dynamic-slice_fusion.wo_ref
  5.3 1.2 copy-done.8
  7.2 1.2 copy-done.19
  8.4 0.9 copy-done.20
  9.3 0.9 copy-done.21
  10.2 0.7 copy-done.22
  10.9 0.7 copy-done.23
  11.6 139.7 %shard_map.245 = (bf16[4,256,2048]{2,1,0:T(8,128)(2,1)S(1)}, s32[4,8,128]{2,1,0:T(8,128)S(1)}, bf16[256,2048]{1,0:T(8,128)(2,1)S(1)}, bf16[256,2048]{1,0:T(8,128...) custom-call(bf16[256,2048]{1,0:T(8,128)(2,1)S(1)} %copy-done.8, ...), custom_call_target="tpu_custom_call" | custom-call | flops 10000000000 | bytes 200000000 | tf_op jit(solution)/shard_map/pallas_call | solution.py:1508
  151.4 2.0 copy-done.24
  153.4 2.0 copy-done.25
  155.4 1.0 copy-done.27
  158.4 36.1 %shard_map.246 = (bf16[1024,2048]{1,0:T(8,128)(2,1)}, f32[1024,1024]{1,0:T(8,128)}, f32[1024,1024]{1,0:T(8,128)}, bf16[1024,1024]{1,0:T(8,128)(2,1)S(1)}, f32[10...) custom-call(s32[4,4]{1,0:T(4,128)S(1)} %bitcast.34, ...), custom_call_target="tpu_custom_call" | custom-call | flops 10000000000 | bytes 40000000 | tf_op jit(solution)/shard_map/pallas_call | solution.py:428
  194.6 35.7 %shard_map.247 = (f32[1024,1024]{1,0:T(8,128)S(1)}, bf16[16384,1024]{1,0:T(8,128)(2,1)}, f32[1024,1024]{1,0:T(8,128)S(1)}, f32[1024,1024]{1,0:T(8,128)S(1)}, bf1...) custom-call(s32[4,4]{1,0:T(4,128)S(1)} %bitcast.35, f32[1024,160]{1,0:T(8,128)S(1)} %bitcast.32, ...), custom_call_target="tpu_custom_call" | custom-call | flops 671088640 | bytes 54525952 | tf_op jit(solution)/shard_map/pallas_call | solution.py:623
  230.3 16.3 %multiply_convert_fusion = (bf16[1024,1024]{1,0:T(8,128)(2,1)}, bf16[1024,1024]{1,0:T(8,128)(2,1)S(1)}, f32[1024,1024]{1,0:T(8,128)}) fusion(f32[1024,1024]{1,0:T(8,128)S(1)} %get-tuple-element.75, f32[1024,1024]{1,0:T(8,128)} %get-tuple-element.72, bf16[1024,2048]{1,0:T(8,128)(2,1)} %bitcast.48, bf16[1024,2048]{1,0:T(8,128)(2,1)} %bitcast.46), kind=kOutput, calls=%fused_computation | convolution fusion | flops 4309647360 | bytes 25165824 | tf_op jit(solution)/shard_map/dot_general | solution.py:1637
  246.6 9.1 %convolution_convert_fusion = bf16[2048,1024]{1,0:T(8,128)(2,1)} fusion(bf16[1024,2048]{1,0:T(8,128)(2,1)} %get-tuple-element.74.normed_ref, bf16[1024,1024]{1,0:T(8,128)(2,1)S(1)} %get-tuple-element.103.gg_ref), kind=kOutput, calls=%fused_computation.4 | convolution fusion | flops 4297064448 | bytes 10485760 | tf_op jit(solution)/shard_map/dot_general | solution.py:1638
  255.8 96.6 %shard_map.248 = (bf16[1024,1024]{1,0:T(8,128)(2,1)}, f32[1024,1024]{1,0:T(8,128)}, f32[4,256,160]{2,1,0:T(8,128)}, f32[16,1024]{1,0:T(8,128)}, f32[8,1024]{1,0:...) custom-call(s32[4,4]{1,0:T(4,128)} %bitcast.36, ...), custom_call_target="tpu_custom_call" | custom-call | flops 1342177280 | bytes 62914560 | tf_op jit(solution)/shard_map/pallas_call | solution.py:862
  352.4 136.4 %shard_map.249 = (bf16[32,8,2176]{2,1,0:T(8,128)(2,1)}, bf16[32,8,2048]{2,1,0:T(8,128)(2,1)}, bf16[4,256,2048]{2,1,0:T(8,128)(2,1)}, bf16[4,128,2048]{2,1,0:T(8,128)(2,1)}, f32[320,512]{1,0:T(8,128)}) custom-call(s32[4,4]{1,0:T(4,128)} %bitcast.37, f32[1024,1024]{1,0:T(8,128)} %get-tuple-element.76.da_ref, f32[1024,1024]{1,0:T(8,128)} %get-tuple-element.77.conv_ref, ...), custom_call_target="tpu_custom_call" | custom-call | flops 20000000000 | bytes 60000000 | tf_op jit(solution)/shard_map/pallas_call | solution.py:1174
  488.7 2.8 convolution_convert_fusion.1
  491.6 0.9 convert_reduce_fusion
  495.7 3.0 fusion.7
  498.8 2.2 copy-done.3
  501.0 1.1 copy-done.10
  502.1 6.6 %shard_map.250 = (f32[256,8192]{1,0:T(8,128)}, f32[256,128]{1,0:T(8,128)S(1)}, f32[512,2048]{1,0:T(8,128)}, f32[160,512]{1,0:T(8,128)}, f32[128,512]{1,0:T(8,128...) custom-call(bf16[4,256,2048]{2,1,0:T(8,128)(2,1)S(1)} %copy-done.3, bf16[256,8192]{1,0:T(8,128)(2,1)S(1)} %copy-done.2, ...), custom_call_target="tpu_custom_call" | custom-call | flops 8388608 | bytes 16777216 | tf_op jit(solution)/shard_map/pallas_call | solution.py:1580
  (68 shorter events, 8.0 us)
Async XLA Ops:
  5.3 1.2 copy-start.8
  7.2 1.2 copy-start.19
  151.4 2.0 copy-start.24
  153.4 2.0 copy-start.25
  155.4 1.0 copy-start.27
  157.0 37.5 %copy-start.26 = (bf16[256,2048]{1,0:T(8,128)(2,1)}, bf16[256,2048]{1,0:T(8,128)(2,1)S(1)}, u32[]{:S(2)}) copy-start(bf16[256,2048]{1,0:T(8,128)(2,1)S(1)} %get-tuple-element.67.dy_ref.dy_own) | copy-start | bytes 3145732
  157.6 37.0 %copy-start.15 = (s32[4,1,4]{2,1,0:T(1,128)}, s32[4,1,4]{2,1,0:T(1,128)S(1)}, u32[]{:S(2)}) copy-start(s32[4,1,4]{2,1,0:T(1,128)S(1)} %slice.70) | copy-start | bytes 196
  157.6 36.9 %copy-start.16 = (f32[2,8,128]{2,0,1:T(2,128)}, f32[2,8,128]{2,0,1:T(2,128)S(1)}, u32[]{:S(2)}) copy-start(f32[2,8,128]{2,0,1:T(2,128)S(1)} %bitcast_convert_fusion) | copy-start | bytes 24580
  157.6 36.9 %copy-start.13 = (f32[1,1024]{1,0:T(1,128)}, f32[1,1024]{1,0:T(1,128)S(1)}, u32[]{:S(2)}) copy-start(f32[1,1024]{1,0:T(1,128)S(1)} %get-tuple-element.109.skip_ref) | copy-start | bytes 12292
  157.6 36.9 %copy-start.14 = (f32[4,1024]{1,0:T(4,128)}, f32[4,1024]{1,0:T(4,128)S(1)}, u32[]{:S(2)}) copy-start(f32[4,1024]{1,0:T(4,128)S(1)} %slice_convert_fusion.taps_ref) | copy-start | bytes 49156
  158.3 36.3 %copy-start.12 = (f32[16,1024]{1,0:T(8,128)}, f32[16,1024]{1,0:T(8,128)S(1)}, u32[]{:S(2)}) copy-start(f32[16,1024]{1,0:T(8,128)S(1)} %get-tuple-element.108.rate_ref) | copy-start | bytes 196612
  158.3 36.2 %copy-start.7 = (bf16[128,1024]{1,0:T(8,128)(2,1)}, bf16[128,1024]{1,0:T(8,128)(2,1)S(1)}, u32[]{:S(2)}) copy-start(bf16[128,1024]{1,0:T(8,128)(2,1)S(1)} %slice.75.stepw_ref) | copy-start | bytes 786436
  158.4 36.1 %copy-start.11 = (bf16[160,1024]{1,0:T(8,128)(2,1)}, bf16[160,1024]{1,0:T(8,128)(2,1)S(1)}, u32[]{:S(2)}) copy-start(bf16[160,1024]{1,0:T(8,128)(2,1)S(1)} %slice.74.sel_ref) | copy-start | bytes 983044
  194.5 35.8 %copy-start.4 = (bf16[1024,1024]{1,0:T(8,128)(2,1)}, bf16[1024,1024]{1,0:T(8,128)(2,1)S(1)}, u32[]{:S(2)}) copy-start(bf16[1024,1024]{1,0:T(8,128)(2,1)S(1)} %get-tuple-element.65.act_ref) | copy-start | bytes 6291460
  194.5 35.8 %copy-start.6 = (f32[4,256,160]{2,1,0:T(8,128)}, f32[4,256,160]{2,1,0:T(8,128)S(1)}, u32[]{:S(2)}) copy-start(f32[4,256,160]{2,1,0:T(8,128)S(1)} %get-tuple-element.64) | copy-start | bytes 1966084
  230.3 16.3 %copy-start = (f32[1024,1024]{1,0:T(8,128)}, f32[1024,1024]{1,0:T(8,128)S(1)}, u32[]{:S(2)}) copy-start(f32[1024,1024]{1,0:T(8,128)S(1)} %get-tuple-element.68.delta_ref) | copy-start | bytes 12582916
  230.3 16.3 %copy-start.1 = (f32[1024,1024]{1,0:T(8,128)}, f32[1024,1024]{1,0:T(8,128)S(1)}, u32[]{:S(2)}) copy-start(f32[1024,1024]{1,0:T(8,128)S(1)} %get-tuple-element.69.pre_ref) | copy-start | bytes 12582916
  246.6 9.1 %copy-start.29 = (bf16[1024,1024]{1,0:T(8,128)(2,1)}, bf16[1024,1024]{1,0:T(8,128)(2,1)S(1)}, u32[]{:S(2)}) copy-start(bf16[1024,1024]{1,0:T(8,128)(2,1)S(1)} %get-tuple-element.103.gg_ref) | copy-start | bytes 6291460
  352.3 143.4 %copy-start.9 = (bf16[256,2048]{1,0:T(8,128)(2,1)S(1)}, bf16[256,2048]{1,0:T(8,128)(2,1)}, u32[]{:S(2)}) copy-start(bf16[256,2048]{1,0:T(8,128)(2,1)} %x_ref.1) | copy-start | bytes 3145732
  488.7 10.1 %copy-start.2 = (bf16[256,8192]{1,0:T(8,128)(2,1)S(1)}, bf16[256,8192]{1,0:T(8,128)(2,1)}, u32[]{:S(2)}) copy-start(bf16[256,8192]{1,0:T(8,128)(2,1)} %w_ref.1) | copy-start | bytes 12582916
  488.7 10.0 %copy-start.5 = (bf16[4,128,2048]{2,1,0:T(8,128)(2,1)S(1)}, bf16[4,128,2048]{2,1,0:T(8,128)(2,1)}, u32[]{:S(2)}) copy-start(bf16[4,128,2048]{2,1,0:T(8,128)(2,1)} %get-tuple-element.93) | copy-start | bytes 6291460
  498.8 2.2 copy-start.3
  501.0 1.1 copy-start.10
  502.1 6.7 %copy-start.18 = (bf16[256]{0:T(256)(128)(2,1)S(1)}, bf16[256]{0:T(256)(128)(2,1)}, u32[]{:S(2)}) copy-start(bf16[256]{0:T(256)(128)(2,1)} %param.18) | copy-start | bytes 1540
  (6 other events, 4.5 us)

commit v10 on v9

--- a/solution.py
+++ b/solution.py
@@ -1542,7 +1542,7 @@
     )(x, dy, dest[None, :], dest[:, None], lens, *(pack[1] if pack else blocks))
 
 
-def spread_kernel(cs, x_ref, w_ref, go_ref, small_ref, out_ref, sum_ref, go_out, *small_outs):
+def spread_kernel(cs, width, x_ref, w_ref, go_ref, small_ref, ride_ref, out_ref, sum_ref, go_out, rms_ref, *small_outs):
     total = jnp.zeros(sum_ref.shape, F32)
     n_dp = x_ref.shape[0]
     for f in range(x_ref.shape[2] // cs):
@@ -1558,6 +1558,11 @@
     @pl.when(pl.program_id(0) == 0)
     def _():
         sum_ref[...] = jnp.zeros_like(sum_ref)
+        sums = jnp.sum(ride_ref[...].astype(F32), axis=0, keepdims=True)
+        lane = lax.broadcasted_iota(jnp.int32, sums.shape, 1)
+        squares = jnp.sum(jnp.where(lane < 2, sums, 0.0), axis=1, keepdims=True)
+        count = jnp.sum(jnp.where((lane >= 2) & (lane < 4), sums, 0.0), axis=1, keepdims=True)
+        rms_ref[...] = jnp.broadcast_to(jnp.sqrt(squares / (count * width)), rms_ref.shape)
         at = 0
         for out in small_outs:
             out[...] = small_ref[at : at + out.shape[0], :]
@@ -1566,38 +1571,43 @@
     sum_ref[...] += total
 
 
-def spread_columns(parts, w, go, small, heights, cs):
+def spread_columns(parts, w, go, small, heights, ride, width, cs):
     n_dp, height, cols = parts.shape
     if cs % 128:
         out = parts.reshape(n_dp, height, cols // cs, cs).transpose(1, 2, 0, 3).reshape(height, n_dp * cols).astype(F32)
         cuts = [small[sum(heights[:i]) : sum(heights[: i + 1])] for i in range(len(heights))]
-        return out, jnp.sum(out * w.astype(F32), axis=1), go.astype(F32), cuts
+        totals = jnp.sum(ride.astype(F32), axis=0)
+        rms = jnp.sqrt((totals[0] + totals[1]) / ((totals[2] + totals[3]) * width))
+        return out, jnp.sum(out * w.astype(F32), axis=1), go.astype(F32), rms, cuts
     wide = 2 * cs
     steps = cols // wide
     once = lambda f: (0, 0)
     go_block = (go.shape[0] // steps, go.shape[1])
     shaped = jax.ShapeDtypeStruct
-    out, sums, go, *cuts = pl.pallas_call(
-        functools.partial(spread_kernel, cs),
+    out, sums, go, rms, *cuts = pl.pallas_call(
+        functools.partial(spread_kernel, cs, width),
         grid=(steps,),
         in_specs=[
             pl.BlockSpec((n_dp, height, wide), lambda f: (0, 0, f)),
             pl.BlockSpec((height, n_dp * wide), lambda f: (0, f)),
             pl.BlockSpec(go_block, lambda f: (f, 0)),
             pl.BlockSpec(small.shape, once),
+            pl.BlockSpec(ride.shape, once),
         ],
         out_specs=[
             pl.BlockSpec((height, n_dp * wide), lambda f: (0, f)),
             pl.BlockSpec((height, 128), once),
             pl.BlockSpec(go_block, lambda f: (f, 0)),
+            pl.BlockSpec((8, 128), once),
         ]
         + [pl.BlockSpec((h, small.shape[1]), once) for h in heights],
         out_shape=[shaped((height, n_dp * cols), F32), shaped((height, 128), F32), shaped(go.shape, F32)]
+        + [shaped((8, 128), F32)]
         + [shaped((h, small.shape[1]), F32) for h in heights],
         compiler_params=pltpu.CompilerParams(vmem_limit_bytes=32 * 2**20),
         cost_estimate=pl.CostEstimate(flops=4 * height * cols * n_dp, bytes_accessed=8 * height * cols * n_dp, transcendentals=0),
-    )(parts, w, go, small)
-    return out, jnp.sum(sums, axis=1), go, cuts
+    )(parts, w, go, small, ride)
+    return out, jnp.sum(sums, axis=1), go, rms[0, 0], cuts
 
 
 def per_device(
@@ -1710,16 +1720,14 @@
         gate_grad, wo_grad, wo_half, wg_own, x_own, dy_own, mixed, gain[None], x_tags, ride[:1], n_f,
     )
 
-    grad_in_weight, gain_sum, grad_out_weight, cuts = spread_columns(
+    grad_in_weight, gain_sum, grad_out_weight, input_rms, cuts = spread_columns(
         gin_all, in_weight, go_all.reshape(n_dp * cs, width), joined(small_full),
-        [select_weight.shape[0], rank_of, n, 8], cs,
+        [select_weight.shape[0], rank_of, n, 8], mix_back[:, 0, width:], width, cs,
     )
     grad_select, grad_step, grad_decay, misc = cuts
     grad_norm_gain = gain_sum / norm_gain.astype(F32)
 
     back = mix_back.reshape(tok, width + 128)
-    totals = jnp.sum(mix_back[:, 0, width : width + 4].astype(F32), axis=0)
-    input_rms = jnp.sqrt((totals[0] + totals[1]) / ((totals[2] + totals[3]) * width))
     mixer_output = flat_dot(from_send, back[:, :width])
     layer_output = (tokens.astype(F32) + mixer_output).astype(BF16)
     mixer_output = mixer_output.astype(BF16)

time: 513 us -> 509 us (level)
  no operation moved by 1% of the time
where the time goes in v10:
time: 509 us; the launch traced here: 508 us
  Pallas kernels  451 us (89%)
  matrix products  31.3 us (6%)
  local copies, waits for them, and re-layouts  22.6 us (4%)
    pallas_call x1, Pallas kernels, gather_all(): pl.pallas_call(functools.partial(gather_kernel, n_dp, n_f, downs, segs, p...  140 us
    pallas_call x1, Pallas kernels, leave(): pl.pallas_call(functools.partial(leave_kernel, n_f, half), grid=(half + 2...  136 us
    pallas_call x1, Pallas kernels, scan_backward(): pl.pallas_call(functools.partial(bwd_kernel, min(lanes, ch), n_f), grid=(...  96.5 us
    pallas_call x1, Pallas kernels, enter(): pl.pallas_call(functools.partial(enter_kernel, n_f, half), grid=(2 * half...  36.1 us
    pallas_call x1, Pallas kernels, scan_forward(): pl.pallas_call(functools.partial(fwd_kernel, min(lanes, ch), n_f), grid=(...  35.7 us
    dot_general x1, matrix products, per_device(): lax.dot_general(a, b, (((1,), (1,)), ((), ())), preferred_element_type=F32)  16.3 us
    unnamed x60, local copies, waits for them, and re-layouts  14.7 us

profile of v10, /device:TPU:21, one launch (start us, length us, event | category | flops | bytes accessed | tf_op | source)
XLA Modules:
  0.0 508.0 jit_solution(6783917844290220364)
XLA Ops:
  0.6 0.7 convert_element_type.73
  4.2 1.1 constant_dynamic-slice_fusion.wo_ref
  5.3 1.2 copy-done.8
  7.2 1.2 copy-done.19
  8.4 0.9 copy-done.20
  9.3 0.9 copy-done.21
  10.2 0.7 copy-done.22
  10.9 0.7 copy-done.23
  11.6 139.7 %shard_map.245 = (bf16[4,256,2048]{2,1,0:T(8,128)(2,1)S(1)}, s32[4,8,128]{2,1,0:T(8,128)S(1)}, bf16[256,2048]{1,0:T(8,128)(2,1)S(1)}, bf16[256,2048]{1,0:T(8,128...) custom-call(bf16[256,2048]{1,0:T(8,128)(2,1)S(1)} %copy-done.8, ...), custom_call_target="tpu_custom_call" | custom-call | flops 10000000000 | bytes 200000000 | tf_op jit(solution)/shard_map/pallas_call | solution.py:1508
  151.4 2.0 copy-done.24
  153.4 2.0 copy-done.25
  155.4 1.0 copy-done.27
  158.4 36.1 %shard_map.246 = (bf16[1024,2048]{1,0:T(8,128)(2,1)}, f32[1024,1024]{1,0:T(8,128)}, f32[1024,1024]{1,0:T(8,128)}, bf16[1024,1024]{1,0:T(8,128)(2,1)S(1)}, f32[10...) custom-call(s32[4,4]{1,0:T(4,128)S(1)} %bitcast.36, ...), custom_call_target="tpu_custom_call" | custom-call | flops 10000000000 | bytes 40000000 | tf_op jit(solution)/shard_map/pallas_call | solution.py:428
  194.6 35.7 %shard_map.247 = (f32[1024,1024]{1,0:T(8,128)S(1)}, bf16[16384,1024]{1,0:T(8,128)(2,1)}, f32[1024,1024]{1,0:T(8,128)S(1)}, f32[1024,1024]{1,0:T(8,128)S(1)}, bf1...) custom-call(s32[4,4]{1,0:T(4,128)S(1)} %bitcast.37, f32[1024,160]{1,0:T(8,128)S(1)} %bitcast.34, ...), custom_call_target="tpu_custom_call" | custom-call | flops 671088640 | bytes 54525952 | tf_op jit(solution)/shard_map/pallas_call | solution.py:623
  230.4 16.3 %multiply_convert_fusion = (bf16[1024,1024]{1,0:T(8,128)(2,1)}, bf16[1024,1024]{1,0:T(8,128)(2,1)S(1)}, f32[1024,1024]{1,0:T(8,128)}) fusion(f32[1024,1024]{1,0:T(8,128)S(1)} %get-tuple-element.76, f32[1024,1024]{1,0:T(8,128)} %get-tuple-element.73, bf16[1024,2048]{1,0:T(8,128)(2,1)} %bitcast.51, bf16[1024,2048]{1,0:T(8,128)(2,1)} %bitcast.49), kind=kOutput, calls=%fused_computation | convolution fusion | flops 4309647360 | bytes 25165824 | tf_op jit(solution)/shard_map/dot_general | solution.py:1647
  246.7 9.1 %convolution_convert_fusion = bf16[2048,1024]{1,0:T(8,128)(2,1)} fusion(bf16[1024,2048]{1,0:T(8,128)(2,1)} %get-tuple-element.75.normed_ref, bf16[1024,1024]{1,0:T(8,128)(2,1)S(1)} %get-tuple-element.105.gg_ref), kind=kOutput, calls=%fused_computation.4 | convolution fusion | flops 4297064448 | bytes 10485760 | tf_op jit(solution)/shard_map/dot_general | solution.py:1648
  255.8 96.5 %shard_map.248 = (bf16[1024,1024]{1,0:T(8,128)(2,1)}, f32[1024,1024]{1,0:T(8,128)}, f32[4,256,160]{2,1,0:T(8,128)}, f32[16,1024]{1,0:T(8,128)}, f32[8,1024]{1,0:...) custom-call(s32[4,4]{1,0:T(4,128)} %bitcast.38, ...), custom_call_target="tpu_custom_call" | custom-call | flops 1342177280 | bytes 62914560 | tf_op jit(solution)/shard_map/pallas_call | solution.py:862
  352.3 136.4 %shard_map.249 = (bf16[32,8,2176]{2,1,0:T(8,128)(2,1)}, bf16[32,8,2048]{2,1,0:T(8,128)(2,1)}, bf16[4,256,2048]{2,1,0:T(8,128)(2,1)}, bf16[4,128,2048]{2,1,0:T(8,128)(2,1)}, f32[320,512]{1,0:T(8,128)}) custom-call(s32[4,4]{1,0:T(4,128)} %bitcast.39, f32[1024,1024]{1,0:T(8,128)} %get-tuple-element.77.da_ref, f32[1024,1024]{1,0:T(8,128)} %get-tuple-element.78.conv_ref, ...), custom_call_target="tpu_custom_call" | custom-call | flops 20000000000 | bytes 60000000 | tf_op jit(solution)/shard_map/pallas_call | solution.py:1174
  488.7 2.8 convolution_convert_fusion.1
  491.6 1.7 copy.32
  493.3 3.0 fusion.7
  496.3 1.6 copy-done.5
  497.9 1.1 copy-done.10
  499.0 6.7 %shard_map.250 = (f32[256,8192]{1,0:T(8,128)}, f32[256,128]{1,0:T(8,128)S(1)}, f32[512,2048]{1,0:T(8,128)}, f32[8,128]{1,0:T(8,128)S(1)}, f32[160,512]{1,0:T(8,1...) custom-call(bf16[4,256,2048]{2,1,0:T(8,128)(2,1)S(1)} %copy-done.3, ...), custom_call_target="tpu_custom_call" | custom-call | flops 8388608 | bytes 16777216 | tf_op jit(solution)/shard_map/pallas_call | solution.py:1587
  (69 shorter events, 7.9 us)
Async XLA Ops:
  5.3 1.2 copy-start.8
  7.2 1.2 copy-start.19
  151.4 2.0 copy-start.24
  153.4 2.0 copy-start.25
  155.4 1.0 copy-start.27
  157.0 37.5 %copy-start.26 = (bf16[256,2048]{1,0:T(8,128)(2,1)}, bf16[256,2048]{1,0:T(8,128)(2,1)S(1)}, u32[]{:S(2)}) copy-start(bf16[256,2048]{1,0:T(8,128)(2,1)S(1)} %get-tuple-element.68.dy_ref.dy_own) | copy-start | bytes 3145732
  157.6 37.0 %copy-start.15 = (s32[4,1,4]{2,1,0:T(1,128)}, s32[4,1,4]{2,1,0:T(1,128)S(1)}, u32[]{:S(2)}) copy-start(s32[4,1,4]{2,1,0:T(1,128)S(1)} %slice.61) | copy-start | bytes 196
  157.6 36.9 %copy-start.16 = (f32[2,8,128]{2,0,1:T(2,128)}, f32[2,8,128]{2,0,1:T(2,128)S(1)}, u32[]{:S(2)}) copy-start(f32[2,8,128]{2,0,1:T(2,128)S(1)} %bitcast_convert_fusion) | copy-start | bytes 24580
  157.6 36.9 %copy-start.13 = (f32[1,1024]{1,0:T(1,128)}, f32[1,1024]{1,0:T(1,128)S(1)}, u32[]{:S(2)}) copy-start(f32[1,1024]{1,0:T(1,128)S(1)} %get-tuple-element.111.skip_ref) | copy-start | bytes 12292
  157.6 36.9 %copy-start.14 = (f32[4,1024]{1,0:T(4,128)}, f32[4,1024]{1,0:T(4,128)S(1)}, u32[]{:S(2)}) copy-start(f32[4,1024]{1,0:T(4,128)S(1)} %slice_convert_fusion.taps_ref) | copy-start | bytes 49156
  158.3 36.3 %copy-start.12 = (f32[16,1024]{1,0:T(8,128)}, f32[16,1024]{1,0:T(8,128)S(1)}, u32[]{:S(2)}) copy-start(f32[16,1024]{1,0:T(8,128)S(1)} %get-tuple-element.110.rate_ref) | copy-start | bytes 196612
  158.3 36.3 %copy-start.7 = (bf16[128,1024]{1,0:T(8,128)(2,1)}, bf16[128,1024]{1,0:T(8,128)(2,1)S(1)}, u32[]{:S(2)}) copy-start(bf16[128,1024]{1,0:T(8,128)(2,1)S(1)} %slice.66.stepw_ref) | copy-start | bytes 786436
  158.4 36.1 %copy-start.11 = (bf16[160,1024]{1,0:T(8,128)(2,1)}, bf16[160,1024]{1,0:T(8,128)(2,1)S(1)}, u32[]{:S(2)}) copy-start(bf16[160,1024]{1,0:T(8,128)(2,1)S(1)} %slice.65.sel_ref) | copy-start | bytes 983044
  194.5 35.8 %copy-start.4 = (bf16[1024,1024]{1,0:T(8,128)(2,1)}, bf16[1024,1024]{1,0:T(8,128)(2,1)S(1)}, u32[]{:S(2)}) copy-start(bf16[1024,1024]{1,0:T(8,128)(2,1)S(1)} %get-tuple-element.66.act_ref) | copy-start | bytes 6291460
  194.5 35.8 %copy-start.6 = (f32[4,256,160]{2,1,0:T(8,128)}, f32[4,256,160]{2,1,0:T(8,128)S(1)}, u32[]{:S(2)}) copy-start(f32[4,256,160]{2,1,0:T(8,128)S(1)} %get-tuple-element.65) | copy-start | bytes 1966084
  230.3 16.3 %copy-start = (f32[1024,1024]{1,0:T(8,128)}, f32[1024,1024]{1,0:T(8,128)S(1)}, u32[]{:S(2)}) copy-start(f32[1024,1024]{1,0:T(8,128)S(1)} %get-tuple-element.69.delta_ref) | copy-start | bytes 12582916
  230.3 16.3 %copy-start.1 = (f32[1024,1024]{1,0:T(8,128)}, f32[1024,1024]{1,0:T(8,128)S(1)}, u32[]{:S(2)}) copy-start(f32[1024,1024]{1,0:T(8,128)S(1)} %get-tuple-element.70.pre_ref) | copy-start | bytes 12582916
  246.6 9.2 %copy-start.29 = (bf16[1024,1024]{1,0:T(8,128)(2,1)}, bf16[1024,1024]{1,0:T(8,128)(2,1)S(1)}, u32[]{:S(2)}) copy-start(bf16[1024,1024]{1,0:T(8,128)(2,1)S(1)} %get-tuple-element.105.gg_ref) | copy-start | bytes 6291460
  352.3 140.9 %copy-start.9 = (bf16[256,2048]{1,0:T(8,128)(2,1)S(1)}, bf16[256,2048]{1,0:T(8,128)(2,1)}, u32[]{:S(2)}) copy-start(bf16[256,2048]{1,0:T(8,128)(2,1)} %x_ref.1) | copy-start | bytes 3145732
  488.7 7.6 %copy-start.2 = (bf16[256,8192]{1,0:T(8,128)(2,1)S(1)}, bf16[256,8192]{1,0:T(8,128)(2,1)}, u32[]{:S(2)}) copy-start(bf16[256,8192]{1,0:T(8,128)(2,1)} %w_ref.1) | copy-start | bytes 12582916
  488.7 7.6 %copy-start.3 = (bf16[4,256,2048]{2,1,0:T(8,128)(2,1)S(1)}, bf16[4,256,2048]{2,1,0:T(8,128)(2,1)}, u32[]{:S(2)}) copy-start(bf16[4,256,2048]{2,1,0:T(8,128)(2,1)} %get-tuple-element.93.x_ref) | copy-start | bytes 12582916
  496.3 1.6 copy-start.5
  497.9 1.1 copy-start.10
  499.0 7.3 %copy-start.18 = (bf16[256]{0:T(256)(128)(2,1)S(1)}, bf16[256]{0:T(256)(128)(2,1)}, u32[]{:S(2)}) copy-start(bf16[256]{0:T(256)(128)(2,1)} %param.18) | copy-start | bytes 1540
  (6 other events, 4.5 us)
